TPU v7x, 32 devices: a whole 2x2x4 slice. The times are simulated.
32 devices in a mesh: dp: 8 (over z, core), cp: 4 (over y, x).
Axes of the slice: x: 2, y: 2, z: 4, core: 2. Of those that a mesh axis runs over, the one named last changes fastest.
Arguments:
- tokens: bfloat16 [8, 1152, 960], P('dp', 'cp'), may hold values from -6 to 6
- recur_depth: int32 [8, 1152], P('dp', 'cp'), may hold values from 1 to 3
- document_ids: int32 [8, 1152], P('dp', 'cp'), may hold values from 0 to 1151, as said below
- cotangent: bfloat16 [8, 1152, 960], P('dp', 'cp'), may hold values from -6 to 6
- query_weight: bfloat16 [960, 960], P('cp'), may hold values from -0.1875 to 0.1875
- key_weight: bfloat16 [960, 320], P('cp'), may hold values from -0.1875 to 0.1875
- value_weight: bfloat16 [960, 320], P('cp'), may hold values from -0.1875 to 0.1875
- output_weight: bfloat16 [960, 960], P('cp'), may hold values from -1 to 1
- gate_weight: bfloat16 [960, 2560], P('cp'), may hold values from -0.1875 to 0.1875
- up_weight: bfloat16 [960, 2560], P('cp'), may hold values from -0.1875 to 0.1875
- down_weight: bfloat16 [2560, 960], P('cp'), may hold values from -0.125 to 0.125
- router_weight: bfloat16 [3, 960], P(None, 'cp'), may hold values from -0.1875 to 0.1875
- attention_gain: bfloat16 [960], P('cp'), may hold values from 0.5 to 1.5
- feedforward_gain: bfloat16 [960], P('cp'), may hold values from 0.5 to 1.5
Outputs:
- activations: bfloat16 [8, 1152, 960], P('dp', 'cp')
- input_grad: bfloat16 [8, 1152, 960], P('dp', 'cp')
- grad_query: float32 [960, 960], P('cp')
- grad_key: float32 [960, 320], P('cp')
- grad_value: float32 [960, 320], P('cp')
- grad_output: float32 [960, 960], P('cp')
- grad_gate: float32 [960, 2560], P('cp')
- grad_up: float32 [960, 2560], P('cp')
- grad_down: float32 [2560, 960], P('cp')
- grad_router: float32 [3, 960], P(None, 'cp')
- grad_attention_gain: float32 [960], P('cp')
- grad_feedforward_gain: float32 [960], P('cp')
Inputs may be any that keep to these rules, and one draw needn't show every extreme that they name: `document_ids`: A token's id is the position within its sequence where its document begins, so ids never fall along a sequence; the first token has id 0 and the last token of every sequence is a document of its own; in every sequence one document begins on the tokens of the first device of cp and ends on those of its last.
All inputs are finite; a program needn't handle non-finite values.
Results may differ from a plain program's by a relative error of at most 0.028.
Values may be sent and summed in bfloat16 or wider, within the bound.
No kernel may reach another device: no remote copies, remote signals or barrier semaphores. Data moves between devices by JAX's collectives and lax.ppermute only.
A program may use at most 320 MiB of HBM per device.

v0:
```python
import jax
import jax.numpy as jnp
from jax import lax
from jax.sharding import PartitionSpec as P

HEAD_DIM = 64
RECUR = 3


NORM_EPSILON = 1e-05
MASKED_SCORE = -1e30
ROPE_BASE = 10000.0


def inverse_rms(matrix):
    return lax.rsqrt(jnp.mean(matrix * matrix, axis=-1, keepdims=True) + NORM_EPSILON)


def norm_back(matrix, gain_vector, upstream):
    factor = inverse_rms(matrix)
    unit_rows = matrix * factor
    scaled_up = upstream * gain_vector
    grad_rows = factor * (
        scaled_up - unit_rows * jnp.mean(scaled_up * unit_rows, axis=-1, keepdims=True)
    )
    return (grad_rows, jnp.sum(upstream * unit_rows, axis=0))


def rope_tables(offset, length, head_size):
    halfway = head_size // 2
    inverse = jnp.power(ROPE_BASE, -2.0 * jnp.arange(halfway, dtype=jnp.float32) / head_size)
    places = (offset + jnp.arange(length)).astype(jnp.float32)
    angles = places[:, None] * inverse[None, :]
    return (jnp.cos(angles), jnp.sin(angles))


def rotate_heads(matrix, cosine, sine):
    halfway = matrix.shape[-1] // 2
    front_half = matrix[..., :halfway]
    back_half = matrix[..., halfway:]
    cosine_rows = cosine[:, None, :]
    sine_rows = sine[:, None, :]
    return jnp.concatenate(
        [
            front_half * cosine_rows - back_half * sine_rows,
            back_half * cosine_rows + front_half * sine_rows,
        ],
        axis=-1,
    )


def unrotate_heads(gradient, cosine, sine):
    halfway = gradient.shape[-1] // 2
    front_half = gradient[..., :halfway]
    back_half = gradient[..., halfway:]
    cosine_rows = cosine[:, None, :]
    sine_rows = sine[:, None, :]
    return jnp.concatenate(
        [
            front_half * cosine_rows + back_half * sine_rows,
            back_half * cosine_rows - front_half * sine_rows,
        ],
        axis=-1,
    )


def build_mask(doc_rows, doc_cols, depth_cols, recursion, offset):
    row_place = offset + jnp.arange(doc_rows.shape[0])
    col_place = jnp.arange(doc_cols.shape[0])
    causal = col_place[None, :] <= row_place[:, None]
    diagonal = col_place[None, :] == row_place[:, None]
    same_doc = doc_cols[None, :] == doc_rows[:, None]
    live_keys = (depth_cols[None, :] > recursion) | diagonal
    return causal & same_doc & live_keys


def score_block(query_group, key_seq, key_mask, score_scale):
    scores = (
        jnp.einsum("ckgd,lkd->kgcl", query_group, key_seq, preferred_element_type=jnp.float32)
        * score_scale
    )
    return jnp.where(key_mask[None, None], scores, MASKED_SCORE)


def forward_level(state, weights, recursion, context):
    (
        query_weight,
        key_weight,
        value_weight,
        output_weight,
        gate_weight,
        up_weight,
        down_weight,
        router_weight,
        attention_gain,
        feedforward_gain,
    ) = weights
    cosine, sine, doc_rows, doc_cols, depth_rows, depth_cols, offset = context
    seq_count, row_count, width = state.shape
    head_count = query_weight.shape[1] // HEAD_DIM
    key_heads = key_weight.shape[1] // HEAD_DIM
    group_size = head_count // key_heads
    score_scale = HEAD_DIM ** (-0.5)
    flat_state = state.reshape(seq_count * row_count, width)
    normed = (flat_state * inverse_rms(flat_state) * attention_gain.astype(jnp.float32)).astype(
        jnp.bfloat16
    )
    query_proj = jnp.dot(normed, query_weight, preferred_element_type=jnp.float32)
    key_proj = jnp.dot(normed, key_weight, preferred_element_type=jnp.float32)
    value_rows = jnp.dot(normed, value_weight, preferred_element_type=jnp.float32).astype(
        jnp.bfloat16
    )
    value_rows = value_rows.reshape(seq_count, row_count, key_heads, HEAD_DIM)
    query_rows = rotate_heads(
        query_proj.reshape(seq_count, row_count, head_count, HEAD_DIM), cosine, sine
    ).astype(jnp.bfloat16)
    key_rows = rotate_heads(
        key_proj.reshape(seq_count, row_count, key_heads, HEAD_DIM), cosine, sine
    ).astype(jnp.bfloat16)
    key_all, value_all = (
        lax.all_gather(key_rows, "cp", axis=1, tiled=True),
        lax.all_gather(value_rows, "cp", axis=1, tiled=True),
    )

    def forward_one_sequence(sequence_items):
        query_seq, key_seq, value_seq, doc_here, doc_every, depth_every = sequence_items
        key_mask = build_mask(doc_here, doc_every, depth_every, recursion, offset)
        query_group = query_seq.reshape(row_count, key_heads, group_size, HEAD_DIM)
        scores = score_block(query_group, key_seq, key_mask, score_scale)
        row_peak = jnp.max(scores, axis=-1, keepdims=True)
        exponent = jnp.exp(scores - row_peak)
        row_total = jnp.sum(exponent, axis=-1, keepdims=True)
        attention_low = (exponent / row_total).astype(jnp.bfloat16)
        mixed_rows = jnp.einsum(
            "kgcl,lkd->ckgd", attention_low, value_seq, preferred_element_type=jnp.float32
        )
        return (
            mixed_rows.reshape(row_count, head_count * HEAD_DIM),
            row_peak[..., 0] + jnp.log(row_total[..., 0]),
        )

    mixed_all, log_totals = lax.map(
        forward_one_sequence, (query_rows, key_all, value_all, doc_rows, doc_cols, depth_cols)
    )
    attended = mixed_all.reshape(seq_count * row_count, head_count * HEAD_DIM).astype(jnp.bfloat16)
    attention_out = jnp.dot(attended, output_weight, preferred_element_type=jnp.float32)
    after_attention = flat_state + attention_out
    normed_ffn = (
        after_attention * inverse_rms(after_attention) * feedforward_gain.astype(jnp.float32)
    ).astype(jnp.bfloat16)
    gate_value = jnp.dot(normed_ffn, gate_weight, preferred_element_type=jnp.float32)
    up_value = jnp.dot(normed_ffn, up_weight, preferred_element_type=jnp.float32)
    inner_rows = (jax.nn.silu(gate_value) * up_value).astype(jnp.bfloat16)
    feedforward_out = jnp.dot(inner_rows, down_weight, preferred_element_type=jnp.float32)
    branch_sum = attention_out + feedforward_out
    router_row = router_weight[recursion].astype(jnp.float32)
    router_logit = jnp.dot(flat_state, router_row, precision=lax.Precision.HIGHEST)
    router_gate = jax.nn.sigmoid(router_logit)
    active_rows = (depth_rows.reshape(-1) > recursion).astype(jnp.float32)
    next_state = flat_state + (active_rows * router_gate)[:, None] * branch_sum
    saved_parts = (
        flat_state,
        normed,
        query_rows,
        key_all,
        value_all,
        log_totals,
        attended,
        after_attention,
        normed_ffn,
        gate_value,
        up_value,
        inner_rows,
        branch_sum,
        router_row,
        router_gate,
        active_rows,
    )
    return (next_state.reshape(state.shape), saved_parts)


def backward_level(state, weights, recursion, context, upstream):
    (
        query_weight,
        key_weight,
        value_weight,
        output_weight,
        gate_weight,
        up_weight,
        down_weight,
        router_weight,
        attention_gain,
        feedforward_gain,
    ) = weights
    cosine, sine, doc_rows, doc_cols, depth_rows, depth_cols, offset = context
    unused_state, saved_parts = forward_level(state, weights, recursion, context)
    (
        flat_state,
        normed,
        query_rows,
        key_all,
        value_all,
        log_totals,
        attended,
        after_attention,
        normed_ffn,
        gate_value,
        up_value,
        inner_rows,
        branch_sum,
        router_row,
        router_gate,
        active_rows,
    ) = saved_parts
    seq_count, row_count, width = state.shape
    head_count = query_weight.shape[1] // HEAD_DIM
    key_heads = key_weight.shape[1] // HEAD_DIM
    group_size = head_count // key_heads
    score_scale = HEAD_DIM ** (-0.5)
    grad_state = upstream.reshape(seq_count * row_count, width)
    grad_branch = grad_state * (active_rows * router_gate)[:, None]
    grad_logit = (
        jnp.sum(grad_state * branch_sum, axis=-1) * active_rows * router_gate * (1.0 - router_gate)
    )
    router_term = jnp.dot(grad_logit, flat_state, precision=lax.Precision.HIGHEST)
    grad_router = (
        jnp.zeros((router_weight.shape[0], width), jnp.float32).at[recursion].set(router_term)
    )
    grad_flat = grad_state + grad_logit[:, None] * router_row[None, :]
    grad_ffn_low = grad_branch.astype(jnp.bfloat16)
    grad_down = jnp.einsum(
        "nf,nd->fd", inner_rows, grad_ffn_low, preferred_element_type=jnp.float32
    )
    grad_inner = jnp.einsum(
        "nd,fd->nf", grad_ffn_low, down_weight, preferred_element_type=jnp.float32
    )
    sigmoid_gate = jax.nn.sigmoid(gate_value)
    grad_gate_low = (
        grad_inner * up_value * sigmoid_gate * (1.0 + gate_value * (1.0 - sigmoid_gate))
    ).astype(jnp.bfloat16)
    grad_up_low = (grad_inner * gate_value * sigmoid_gate).astype(jnp.bfloat16)
    grad_gate_w = jnp.einsum(
        "nd,nf->df", normed_ffn, grad_gate_low, preferred_element_type=jnp.float32
    )
    grad_up_w = jnp.einsum("nd,nf->df", normed_ffn, grad_up_low, preferred_element_type=jnp.float32)
    grad_normed_ffn = jnp.einsum(
        "nf,df->nd", grad_gate_low, gate_weight, preferred_element_type=jnp.float32
    )
    grad_normed_ffn = grad_normed_ffn + jnp.einsum(
        "nf,df->nd", grad_up_low, up_weight, preferred_element_type=jnp.float32
    )
    grad_after, grad_ffn_gain = norm_back(
        after_attention, feedforward_gain.astype(jnp.float32), grad_normed_ffn
    )
    grad_flat = grad_flat + grad_after
    grad_attention_low = (grad_after + grad_branch).astype(jnp.bfloat16)
    grad_output_w = jnp.einsum(
        "ne,nd->ed", attended, grad_attention_low, preferred_element_type=jnp.float32
    )
    grad_attended = jnp.einsum(
        "nd,ed->ne", grad_attention_low, output_weight, preferred_element_type=jnp.float32
    )
    grad_attended = grad_attended.astype(jnp.bfloat16).reshape(
        seq_count, row_count, head_count * HEAD_DIM
    )

    def backward_one_sequence(sequence_items):
        query_seq, key_seq, value_seq, grad_seq, log_seq, doc_here, doc_every, depth_every = (
            sequence_items
        )
        key_mask = build_mask(doc_here, doc_every, depth_every, recursion, offset)
        query_group = query_seq.reshape(row_count, key_heads, group_size, HEAD_DIM)
        grad_group = grad_seq.reshape(row_count, key_heads, group_size, HEAD_DIM)
        scores = score_block(query_group, key_seq, key_mask, score_scale)
        attention = jnp.exp(scores - log_seq[..., None])
        attention_low = attention.astype(jnp.bfloat16)
        grad_probs = jnp.einsum(
            "ckgd,lkd->kgcl", grad_group, value_seq, preferred_element_type=jnp.float32
        )
        row_dot = jnp.sum(grad_probs * attention, axis=-1, keepdims=True)
        grad_scores = (attention * (grad_probs - row_dot) * score_scale).astype(jnp.bfloat16)
        grad_query = jnp.einsum(
            "kgcl,lkd->ckgd", grad_scores, key_seq, preferred_element_type=jnp.float32
        )
        grad_key = jnp.einsum(
            "kgcl,ckgd->lkd", grad_scores, query_group, preferred_element_type=jnp.float32
        )
        grad_value = jnp.einsum(
            "kgcl,ckgd->lkd", attention_low, grad_group, preferred_element_type=jnp.float32
        )
        return (grad_query.reshape(row_count, head_count, HEAD_DIM), grad_key, grad_value)

    grad_query_all, grad_key_all, grad_value_all = lax.map(
        backward_one_sequence,
        (query_rows, key_all, value_all, grad_attended, log_totals, doc_rows, doc_cols, depth_cols),
    )
    grad_key_rows, grad_value_rows = (
        lax.psum_scatter(
            grad_key_all.astype(jnp.bfloat16), "cp", scatter_dimension=1, tiled=True
        ).astype(jnp.float32),
        lax.psum_scatter(
            grad_value_all.astype(jnp.bfloat16), "cp", scatter_dimension=1, tiled=True
        ).astype(jnp.float32),
    )
    grad_query_low = (
        unrotate_heads(grad_query_all, cosine, sine)
        .astype(jnp.bfloat16)
        .reshape(seq_count * row_count, head_count * HEAD_DIM)
    )
    grad_key_low = (
        unrotate_heads(grad_key_rows, cosine, sine)
        .astype(jnp.bfloat16)
        .reshape(seq_count * row_count, key_heads * HEAD_DIM)
    )
    grad_value_low = grad_value_rows.astype(jnp.bfloat16).reshape(
        seq_count * row_count, key_heads * HEAD_DIM
    )
    grad_query_w = jnp.einsum(
        "nd,ne->de", normed, grad_query_low, preferred_element_type=jnp.float32
    )
    grad_key_w = jnp.einsum("nd,ne->de", normed, grad_key_low, preferred_element_type=jnp.float32)
    grad_value_w = jnp.einsum(
        "nd,ne->de", normed, grad_value_low, preferred_element_type=jnp.float32
    )
    grad_normed = jnp.einsum(
        "ne,de->nd", grad_query_low, query_weight, preferred_element_type=jnp.float32
    )
    grad_normed = grad_normed + jnp.einsum(
        "ne,de->nd", grad_key_low, key_weight, preferred_element_type=jnp.float32
    )
    grad_normed = grad_normed + jnp.einsum(
        "ne,de->nd", grad_value_low, value_weight, preferred_element_type=jnp.float32
    )
    grad_input_rows, grad_attn_gain = norm_back(
        flat_state, attention_gain.astype(jnp.float32), grad_normed
    )
    grad_flat = grad_flat + grad_input_rows
    level_grads = (
        grad_query_w,
        grad_key_w,
        grad_value_w,
        grad_output_w,
        grad_gate_w,
        grad_up_w,
        grad_down,
        grad_router,
        grad_attn_gain,
        grad_ffn_gain,
    )
    return (grad_flat.reshape(state.shape), level_grads)


def local(
    tokens,
    recur_depth,
    document_ids,
    cotangent,
    query_weight,
    key_weight,
    value_weight,
    output_weight,
    gate_weight,
    up_weight,
    down_weight,
    router_weight,
    attention_gain,
    feedforward_gain,
):
    row_count = tokens.shape[1]
    offset = lax.axis_index("cp") * row_count
    doc_cols, depth_cols = (
        lax.all_gather(document_ids, "cp", axis=1, tiled=True),
        lax.all_gather(recur_depth, "cp", axis=1, tiled=True),
    )
    cosine, sine = rope_tables(offset, row_count, HEAD_DIM)
    context = (cosine, sine, document_ids, doc_cols, recur_depth, depth_cols, offset)
    gathered = (
        lax.all_gather(query_weight, "cp", axis=0, tiled=True),
        lax.all_gather(key_weight, "cp", axis=0, tiled=True),
        lax.all_gather(value_weight, "cp", axis=0, tiled=True),
        lax.all_gather(output_weight, "cp", axis=0, tiled=True),
        lax.all_gather(gate_weight, "cp", axis=0, tiled=True),
        lax.all_gather(up_weight, "cp", axis=0, tiled=True),
        lax.all_gather(down_weight, "cp", axis=0, tiled=True),
        lax.all_gather(router_weight, "cp", axis=1, tiled=True),
        lax.all_gather(attention_gain, "cp", axis=0, tiled=True),
        lax.all_gather(feedforward_gain, "cp", axis=0, tiled=True),
    )
    states = [tokens.astype(jnp.float32)]
    for recursion in range(RECUR):
        next_state, unused_parts = forward_level(states[-1], gathered, recursion, context)
        states.append(next_state)
    activations = states[-1].astype(jnp.bfloat16)
    back_weights = (
        lax.all_gather(query_weight, "cp", axis=0, tiled=True),
        lax.all_gather(key_weight, "cp", axis=0, tiled=True),
        lax.all_gather(value_weight, "cp", axis=0, tiled=True),
        lax.all_gather(output_weight, "cp", axis=0, tiled=True),
        lax.all_gather(gate_weight, "cp", axis=0, tiled=True),
        lax.all_gather(up_weight, "cp", axis=0, tiled=True),
        lax.all_gather(down_weight, "cp", axis=0, tiled=True),
        lax.all_gather(router_weight, "cp", axis=1, tiled=True),
        lax.all_gather(attention_gain, "cp", axis=0, tiled=True),
        lax.all_gather(feedforward_gain, "cp", axis=0, tiled=True),
    )
    upstream = cotangent.astype(jnp.float32)
    totals = None
    for recursion in reversed(range(RECUR)):
        upstream, level_grads = backward_level(
            states[recursion], back_weights, recursion, context, upstream
        )
        totals = level_grads if totals is None else jax.tree.map(jnp.add, totals, level_grads)
    input_grad = upstream.astype(jnp.bfloat16)
    (
        total_query,
        total_key,
        total_value,
        total_output,
        total_gate,
        total_up,
        total_down,
        total_router,
        total_attn_gain,
        total_ffn_gain,
    ) = totals
    owned = (
        lax.psum_scatter(
            total_query.astype(jnp.bfloat16), "cp", scatter_dimension=0, tiled=True
        ).astype(jnp.float32),
        lax.psum_scatter(
            total_key.astype(jnp.bfloat16), "cp", scatter_dimension=0, tiled=True
        ).astype(jnp.float32),
        lax.psum_scatter(
            total_value.astype(jnp.bfloat16), "cp", scatter_dimension=0, tiled=True
        ).astype(jnp.float32),
        lax.psum_scatter(
            total_output.astype(jnp.bfloat16), "cp", scatter_dimension=0, tiled=True
        ).astype(jnp.float32),
        lax.psum_scatter(
            total_gate.astype(jnp.bfloat16), "cp", scatter_dimension=0, tiled=True
        ).astype(jnp.float32),
        lax.psum_scatter(
            total_up.astype(jnp.bfloat16), "cp", scatter_dimension=0, tiled=True
        ).astype(jnp.float32),
        lax.psum_scatter(
            total_down.astype(jnp.bfloat16), "cp", scatter_dimension=0, tiled=True
        ).astype(jnp.float32),
        lax.psum_scatter(
            total_router.astype(jnp.bfloat16), "cp", scatter_dimension=1, tiled=True
        ).astype(jnp.float32),
        lax.psum_scatter(
            total_attn_gain.astype(jnp.bfloat16), "cp", scatter_dimension=0, tiled=True
        ).astype(jnp.float32),
        lax.psum_scatter(
            total_ffn_gain.astype(jnp.bfloat16), "cp", scatter_dimension=0, tiled=True
        ).astype(jnp.float32),
    )
    (
        own_query,
        own_key,
        own_value,
        own_output,
        own_gate,
        own_up,
        own_down,
        own_router,
        own_attn_gain,
        own_ffn_gain,
    ) = owned
    shards = (
        lax.psum(own_query.astype(jnp.bfloat16), "dp").astype(jnp.float32),
        lax.psum(own_key.astype(jnp.bfloat16), "dp").astype(jnp.float32),
        lax.psum(own_value.astype(jnp.bfloat16), "dp").astype(jnp.float32),
        lax.psum(own_output.astype(jnp.bfloat16), "dp").astype(jnp.float32),
        lax.psum(own_gate.astype(jnp.bfloat16), "dp").astype(jnp.float32),
        lax.psum(own_up.astype(jnp.bfloat16), "dp").astype(jnp.float32),
        lax.psum(own_down.astype(jnp.bfloat16), "dp").astype(jnp.float32),
        lax.psum(own_router.astype(jnp.bfloat16), "dp").astype(jnp.float32),
        lax.psum(own_attn_gain.astype(jnp.bfloat16), "dp").astype(jnp.float32),
        lax.psum(own_ffn_gain.astype(jnp.bfloat16), "dp").astype(jnp.float32),
    )
    return (
        activations,
        input_grad,
        shards[0],
        shards[1],
        shards[2],
        shards[3],
        shards[4],
        shards[5],
        shards[6],
        shards[7],
        shards[8],
        shards[9],
    )


def solution(mesh):
    in_specs = (
        P("dp", "cp", None),
        P("dp", "cp"),
        P("dp", "cp"),
        P("dp", "cp", None),
        P("cp", None),
        P("cp", None),
        P("cp", None),
        P("cp", None),
        P("cp", None),
        P("cp", None),
        P("cp", None),
        P(None, "cp"),
        P("cp"),
        P("cp"),
    )
    out_specs = (
        P("dp", "cp", None),
        P("dp", "cp", None),
        P("cp", None),
        P("cp", None),
        P("cp", None),
        P("cp", None),
        P("cp", None),
        P("cp", None),
        P("cp", None),
        P(None, "cp"),
        P("cp"),
        P("cp"),
    )
    return jax.shard_map(local, mesh=mesh, in_specs=in_specs, out_specs=out_specs, check_vma=False)
```

profile of v0, /device:TPU:0, one launch (start us, length us, event | category | flops | bytes accessed | tf_op | source)
XLA Modules:
  0.0 1347.4 jit_solution(13091218126929936947)
XLA Ops:
  11.3 9.5 all-gather
  23.2 8.9 all-reduce.14
  32.1 16.9 %all-gather.2 = bf16[4,240,320]{1,2,0:T(8,128)(2,1)S(1)} all-gather(bf16[1,240,320]{1,2,0:T(8,128)(2,1)S(1)} %bitcast.606), channel_id=1, replica_groups=mesh['dp'=8,'cp'=4] {'cp'}, dimensions={0}, use_global_device_ids=true | all-gather | bytes 768000 | tf_op jit(solution)/shard_map/all_gather | solution.py:379
  51.5 24.7 %all_gather.80 = bf16[1,1152,5,64]{3,2,0,1:T(8,128)(2,1)} all-gather(bf16[1,288,5,64]{3,2,0,1:T(8,128)(2,1)S(1)} %copy.60), channel_id=1, replica_groups=mesh['dp'=8,'cp'=4] {'cp'}, dimensions={1}, use_global_device_ids=true | all-gather | bytes 921600 | tf_op jit(solution)/shard_map/all_gather | solution.py:121
  80.5 15.4 %all-reduce.10 = (s32[1152]{0:T(1024)S(1)}, s32[1152]{0:T(1024)S(1)}) all-reduce(s32[1152]{0:T(1024)S(1)} %dynamic-update-slice.12, s32[1152]{0:T(1024)S(1)} %dynamic-update-slice.13), channel_id=1, replica_groups=mesh['dp'=8,'cp'=4] {'cp'}, use_global_device_ids=true, to_apply=%add.2 | all-reduce | flops 2304 | bytes 18432
  95.9 14.1 %all-gather.1 = bf16[4,240,320]{1,2,0:T(8,128)(2,1)S(1)} all-gather(bf16[1,240,320]{1,2,0:T(8,128)(2,1)S(1)} %bitcast.607), channel_id=1, replica_groups=mesh['dp'=8,'cp'=4] {'cp'}, dimensions={0}, use_global_device_ids=true | all-gather | bytes 768000 | tf_op jit(solution)/shard_map/all_gather | solution.py:380
  115.2 38.7 %all_gather.75 = bf16[1,1152,5,64]{3,2,0,1:T(8,128)(2,1)} all-gather(bf16[1,288,5,64]{3,2,0,1:T(8,128)(2,1)} %copy.57), channel_id=1, replica_groups=mesh['dp'=8,'cp'=4] {'cp'}, dimensions={1}, use_global_device_ids=true | all-gather | bytes 921600 | tf_op jit(solution)/shard_map/all_gather | solution.py:122
  192.8 33.0 %all-gather.15.cloned.1.call-done = bf16[960,2560]{1,0:T(8,128)(2,1)} async-done(((bf16[240,2560]{1,0:T(8,128)(2,1)}), bf16[960,2560]{1,0:T(8,128)(2,1)}) %all-gather.15.cloned.1.call-update) | async-done | bytes 4915216 | tf_op jit(solution)/shard_map/all_gather | solution.py:383
  232.9 53.3 %all-gather.17.cloned.1.call-done = bf16[2560,960]{0,1:T(8,128)(2,1)} async-done(((bf16[640,960]{0,1:T(8,128)(2,1)}), bf16[2560,960]{0,1:T(8,128)(2,1)}) %all-gather.17.cloned.1.call-update) | async-done | bytes 4915216 | tf_op jit(solution)/shard_map/all_gather | solution.py:384
  298.1 24.6 %all_gather.88 = bf16[1,1152,5,64]{3,2,0,1:T(8,128)(2,1)} all-gather(bf16[1,288,5,64]{3,2,0,1:T(8,128)(2,1)S(1)} %copy.67), channel_id=1, replica_groups=mesh['dp'=8,'cp'=4] {'cp'}, dimensions={1}, use_global_device_ids=true | all-gather | bytes 921600 | tf_op jit(solution)/shard_map/all_gather | solution.py:121
  328.2 27.0 %all_gather.87 = bf16[1,1152,5,64]{3,2,0,1:T(8,128)(2,1)} all-gather(bf16[1,288,5,64]{3,2,0,1:T(8,128)(2,1)} %copy.64), channel_id=1, replica_groups=mesh['dp'=8,'cp'=4] {'cp'}, dimensions={1}, use_global_device_ids=true | all-gather | bytes 921600 | tf_op jit(solution)/shard_map/all_gather | solution.py:122
  393.9 21.1 %all_gather.90 = bf16[1,1152,5,64]{3,2,0,1:T(8,128)(2,1)} all-gather(bf16[1,288,5,64]{3,2,0,1:T(8,128)(2,1)S(1)} %copy.74), channel_id=1, replica_groups=mesh['dp'=8,'cp'=4] {'cp'}, dimensions={1}, use_global_device_ids=true | all-gather | bytes 921600 | tf_op jit(solution)/shard_map/all_gather | solution.py:121
  420.5 25.8 %all_gather.89 = bf16[1,1152,5,64]{3,2,0,1:T(8,128)(2,1)} all-gather(bf16[1,288,5,64]{3,2,0,1:T(8,128)(2,1)} %copy.71), channel_id=1, replica_groups=mesh['dp'=8,'cp'=4] {'cp'}, dimensions={1}, use_global_device_ids=true | all-gather | bytes 921600 | tf_op jit(solution)/shard_map/all_gather | solution.py:122
  488.0 11.0 fusion.124
  499.0 42.5 %fusion.68 = bf16[1,1152,5,64]{1,3,2,0:T(8,128)(2,1)} fusion(f32[5,1152,288,3]{1,2,3,0:T(8,128)} %fusion.124, f32[5,3,288,1152]{3,2,1,0:T(8,128)} %copy-done.2, f32[5,3,288]{2,1,0:T(4,128)} %log_add_fusion.2, bf16[288,5,3,32]{0,3,2,1:T(8,128)(2,1)} %bitcast.593, bf16[288,5,3,32]{0,3,2,1:T(8,128)(2,1)S(1)} %bitcast.591), kind=kOutput, calls=%fused_computation.88 | convolution fusion | flops 673326464 | bytes 41120640 | tf_op jit(solution)/shard_map/while/body/eval_jaxpr/kgcl,ckgd->lkd/dot_general | solution.py:285
  550.3 11.2 fusion.69
  569.4 35.2 %fusion.37 = f32[5,64,3,288]{3,1,2,0:T(8,128)} fusion(f32[5,1152,288,3]{1,2,3,0:T(8,128)} %fusion.124, f32[5,3,288,1152]{3,2,1,0:T(8,128)} %copy-done.2, f32[5,3,288]{2,1,0:T(4,128)S(1)} %copy-done.121, bf16[1,1152,5,64]{1,3,2,0:T(8,128)(2,1)} %copy-done.55), kind=kOutput, calls=%fused_computation.55 | convolution fusion | flops 671851904 | bytes 41673600 | tf_op jit(solution)/shard_map/while/body/eval_jaxpr/kgcl,lkd->ckgd/dot_general | solution.py:282
  639.7 9.7 fusion.119
  649.4 34.4 %fusion.67 = bf16[1,1152,5,64]{1,3,2,0:T(8,128)(2,1)S(1)} fusion(f32[5,1152,288,3]{1,2,3,0:T(8,128)} %fusion.119, f32[5,3,288,1152]{3,2,1,0:T(8,128)} %copy-done.1, f32[5,3,288]{2,1,0:T(4,128)S(1)} %copy-done.120, bf16[288,5,3,32]{0,3,2,1:T(8,128)(2,1)} %bitcast.589, bf16[288,5,3,32]{0,3,2,1:T(8,128)(2,1)} %bitcast.587), kind=kOutput, calls=%fused_computation.87 | convolution fusion | flops 673326464 | bytes 41120640 | tf_op jit(solution)/shard_map/while/body/eval_jaxpr/kgcl,ckgd->lkd/dot_general | solution.py:285
  705.8 34.5 %fusion.39 = f32[5,64,3,288]{3,1,2,0:T(8,128)} fusion(f32[5,1152,288,3]{1,2,3,0:T(8,128)} %fusion.119, f32[5,3,288,1152]{3,2,1,0:T(8,128)} %copy-done.1, f32[5,3,288]{2,1,0:T(4,128)S(1)} %copy-done.120, bf16[1,1152,5,64]{1,3,2,0:T(8,128)(2,1)S(1)} %copy-done.52), kind=kOutput, calls=%fused_computation.57 | convolution fusion | flops 671851904 | bytes 41673600 | tf_op jit(solution)/shard_map/while/body/eval_jaxpr/kgcl,lkd->ckgd/dot_general | solution.py:282
  771.9 11.0 fusion.114
  782.9 35.2 %fusion.66 = bf16[1,1152,5,64]{1,3,2,0:T(8,128)(2,1)} fusion(f32[5,1152,288,3]{1,2,3,0:T(8,128)} %fusion.114, f32[5,3,288,1152]{3,2,1,0:T(8,128)} %copy-done, f32[5,3,288]{2,1,0:T(4,128)S(1)} %log_add_fusion, bf16[288,5,3,32]{0,3,2,1:T(8,128)(2,1)} %bitcast.585, bf16[288,5,3,32]{0,3,2,1:T(8,128)(2,1)S(1)} %bitcast.583), kind=kOutput, calls=%fused_computation.86 | convolution fusion | flops 673326464 | bytes 41120640 | tf_op jit(solution)/shard_map/while/body/eval_jaxpr/kgcl,ckgd->lkd/dot_general | solution.py:285
  826.1 9.2 fusion.75
  860.5 22.6 %reduce-scatter.47.cloned.1.call-done = bf16[288,320]{1,0:T(8,128)(2,1)} async-done(((bf16[1152,320]{1,0:T(8,128)(2,1)}), bf16[288,320]{1,0:T(8,128)(2,1)}) %reduce-scatter.47.cloned.1.call-update) | async-done | bytes 184336
  920.9 35.4 %fusion.41 = f32[5,64,3,288]{3,1,2,0:T(8,128)} fusion(f32[5,1152,288,3]{1,2,3,0:T(8,128)} %fusion.114, f32[5,3,288,1152]{3,2,1,0:T(8,128)} %copy-done, f32[5,3,288]{2,1,0:T(4,128)S(1)} %log_add_fusion, bf16[1,1152,5,64]{1,3,2,0:T(8,128)(2,1)} %copy-done.49), kind=kOutput, calls=%fused_computation.59 | convolution fusion | flops 671851904 | bytes 41673600 | tf_op jit(solution)/shard_map/while/body/eval_jaxpr/kgcl,lkd->ckgd/dot_general | solution.py:282
  1016.2 35.2 %reduce-scatter.29.cloned.1.call-done = bf16[240,960]{1,0:T(8,128)(2,1)} async-done(((bf16[960,960]{1,0:T(8,128)(2,1)}), bf16[240,960]{1,0:T(8,128)(2,1)}) %reduce-scatter.29.cloned.1.call-update) | async-done | bytes 460816 | tf_op jit(solution)/shard_map/reduce_scatter | solution.py:427
  1051.5 37.6 %reduce-scatter.31.cloned.1.call-done = bf16[240,960]{1,0:T(8,128)(2,1)} async-done(((bf16[960,960]{1,0:T(8,128)(2,1)}), bf16[240,960]{1,0:T(8,128)(2,1)}) %reduce-scatter.31.cloned.1.call-update) | async-done | bytes 460816 | tf_op jit(solution)/shard_map/reduce_scatter | solution.py:436
  1089.1 61.7 %reduce-scatter.33.cloned.1.call-done = bf16[240,2560]{1,0:T(8,128)(2,1)} async-done(((bf16[960,2560]{1,0:T(8,128)(2,1)}), bf16[240,2560]{1,0:T(8,128)(2,1)}) %reduce-scatter.33.cloned.1.call-update) | async-done | bytes 1228816 | tf_op jit(solution)/shard_map/reduce_scatter | solution.py:439
  1150.7 61.6 %reduce-scatter.35.cloned.1.call-done = bf16[240,2560]{1,0:T(8,128)(2,1)} async-done(((bf16[960,2560]{1,0:T(8,128)(2,1)}), bf16[240,2560]{1,0:T(8,128)(2,1)}) %reduce-scatter.35.cloned.1.call-update) | async-done | bytes 1228816 | tf_op jit(solution)/shard_map/reduce_scatter | solution.py:442
  1218.2 15.0 %all-reduce.13 = (bf16[3,960]{1,0:T(4,128)(2,1)S(1)}, bf16[960]{0:T(1024)(128)(2,1)S(1)}, bf16[960]{0:T(1024)(128)(2,1)S(1)}) all-reduce(bf16[3,960]{1,0:T(4,128)(2,1)S(1)} %convert_element_type.595, bf16[960]{0:T(1024)(128)(2,1)S(1)} %add_convert_fusion.19, ...), channel_id=15, replica_groups=mesh['dp'=8,'cp'=4] {'cp'}, use_global_device_ids=true, to_apply=%region_44.45.clone | all-reduce | flops 4800 | bytes 19200
  1233.4 14.6 %all-reduce.11 = (bf16[3,240]{1,0:T(4,128)(2,1)S(1)}, bf16[240]{0:T(256)(128)(2,1)S(1)}, bf16[240]{0:T(256)(128)(2,1)S(1)}) all-reduce(bf16[3,240]{1,0:T(4,128)(2,1)S(1)} %constant_dynamic-slice_fusion, bf16[240]{0:T(256)(128)(2,1)S(1)} %dynamic-slice.42, bf16[240]{0:T(256)(128)(2,1)S(1)} %dynamic-slice.44), channel_id=1, replica_groups=mesh['dp'=8,'cp'=4] {'dp'}, use_global_device_ids=true, to_apply=%region_45.46 | all-reduce | flops 1200 | bytes 4800 | tf_op jit(solution)/shard_map/psum | solution.py:478
  1253.0 77.6 %all-reduce.19.cloned.1.call-done = (bf16[240,960]{1,0:T(8,128)(2,1)}, bf16[240,320]{0,1:T(8,128)(2,1)}, bf16[240,320]{0,1:T(8,128)(2,1)}, bf16[240,960]{1,0:T(8...) async-done(((bf16[240,960]{1,0:T(8,128)(2,1)}, bf16[240,320]{0,1:T(8,128)(2,1)}, bf16[240,320]{0,1:T(8,128)(2,1)}, ...) | async-done | bytes 4915216 | tf_op jit(solution)/shard_map/psum | solution.py:471
  (681 shorter events, 420.1 us)
Async XLA Ops:
  7.2 152.1 %all-gather.9.cloned.1.call-start = ((), (), s32[]{:S(2)}) async-start(), calls=%async_computation.11 | async-start | bytes 2457600 | tf_op jit(solution)/shard_map/all_gather | solution.py:378
  7.9 175.7 %all-gather.11.cloned.1.call-start = ((), (), s32[]{:S(2)}) async-start(), calls=%async_computation.12 | async-start | bytes 2457600 | tf_op jit(solution)/shard_map/all_gather | solution.py:381
  8.7 178.0 %all-gather.13.cloned.1.call-start = ((), (), s32[]{:S(2)}) async-start(), calls=%async_computation.13 | async-start | bytes 6144000 | tf_op jit(solution)/shard_map/all_gather | solution.py:382
  9.4 216.4 %all-gather.15.cloned.1.call-start = ((), (), s32[]{:S(2)}) async-start(), calls=%async_computation.14 | async-start | bytes 6144000 | tf_op jit(solution)/shard_map/all_gather | solution.py:383
  10.0 276.2 %all-gather.17.cloned.1.call-start = ((), (), s32[]{:S(2)}) async-start(), calls=%async_computation.15 | async-start | bytes 6144000 | tf_op jit(solution)/shard_map/all_gather | solution.py:384
  10.6 598.8 %reduce-scatter.37.cloned.1.call-start = ((), (), s32[]{:S(2)}) async-start(), calls=%async_computation.20 | async-start | bytes 1105920
  11.3 147.9 %copy-start.156 = (pred[288]{0:T(512)(128)(4,1)}, pred[288]{0:T(512)(128)(4,1)S(1)}, u32[]{:S(2)}) copy-start(pred[288]{0:T(512)(128)(4,1)S(1)} %get-tuple-element.316) | copy-start | bytes 868
  11.3 365.4 %copy-start.158 = (pred[288]{0:T(512)(128)(4,1)}, pred[288]{0:T(512)(128)(4,1)S(1)}, u32[]{:S(2)}) copy-start(pred[288]{0:T(512)(128)(4,1)S(1)} %get-tuple-element.317) | copy-start | bytes 868
  21.4 137.8 %copy-start.138 = (f32[288]{0:T(512)}, f32[288]{0:T(512)S(1)}, u32[]{:S(2)}) copy-start(f32[288]{0:T(512)S(1)} %convolution_reduce_fusion) | copy-start | bytes 3460
  32.1 131.0 %copy-start.126 = (f32[288]{0:T(512)}, f32[288]{0:T(512)S(1)}, u32[]{:S(2)}) copy-start(f32[288]{0:T(512)S(1)} %add_rsqrt_fusion.5) | copy-start | bytes 3460
  50.1 567.9 %copy-start.11 = (bf16[960,320]{0,1:T(8,128)(2,1)}, bf16[960,320]{0,1:T(8,128)(2,1)S(1)}, u32[]{:S(2)}) copy-start(bf16[960,320]{0,1:T(8,128)(2,1)S(1)} %reshape.1027) | copy-start | bytes 1843204
  79.2 87.0 %copy-start.49 = (bf16[1,1152,5,64]{1,3,2,0:T(8,128)(2,1)}, bf16[1,1152,5,64]{1,3,2,0:T(8,128)(2,1)S(1)}, u32[]{:S(2)}) copy-start(bf16[1,1152,5,64]{1,3,2,0:T(8,128)(2,1)S(1)} %copy.61) | copy-start | bytes 2211844
  159.2 127.0 %copy-start.134 = (f32[288]{0:T(512)}, f32[288]{0:T(512)S(1)}, u32[]{:S(2)}) copy-start(f32[288]{0:T(512)S(1)} %broadcast_select_fusion.2) | copy-start | bytes 3460
  186.6 39.2 %copy-start.43 = (bf16[288,960]{1,0:T(8,128)(2,1)}, bf16[288,960]{1,0:T(8,128)(2,1)S(1)}, u32[]{:S(2)}) copy-start(bf16[288,960]{1,0:T(8,128)(2,1)S(1)} %multiply_convert_fusion.13) | copy-start | bytes 1658884
  292.2 92.4 %copy-start.5 = (f32[288,960]{1,0:T(8,128)}, f32[288,960]{1,0:T(8,128)S(1)}, u32[]{:S(2)}) copy-start(f32[288,960]{1,0:T(8,128)S(1)} %get-tuple-element.384) | copy-start | bytes 3317764
  292.9 83.8 %copy-start.142 = (f32[288]{0:T(512)}, f32[288]{0:T(512)S(1)}, u32[]{:S(2)}) copy-start(f32[288]{0:T(512)S(1)} %convolution_reduce_fusion.2) | copy-start | bytes 3460
  325.6 33.3 %copy-start.51 = (bf16[1,1152,5,64]{1,3,2,0:T(8,128)(2,1)}, bf16[1,1152,5,64]{1,3,2,0:T(8,128)(2,1)S(1)}, u32[]{:S(2)}) copy-start(bf16[1,1152,5,64]{1,3,2,0:T(8,128)(2,1)S(1)} %copy.68) | copy-start | bytes 2211844
  387.6 233.6 %copy-start.7 = (f32[288,960]{1,0:T(8,128)}, f32[288,960]{1,0:T(8,128)S(1)}, u32[]{:S(2)}) copy-start(f32[288,960]{1,0:T(8,128)S(1)} %get-tuple-element.367) | copy-start | bytes 3317764
  467.4 153.8 %copy-start.146 = (f32[288]{0:T(512)}, f32[288]{0:T(512)S(1)}, u32[]{:S(2)}) copy-start(f32[288]{0:T(512)S(1)} %get-tuple-element.453) | copy-start | bytes 3460
  549.6 64.0 %reduce-scatter.39.cloned.1.call-start = ((), (), s32[]{:S(2)}) async-start(), calls=%async_computation.21 | async-start | bytes 1105920
  569.4 175.7 %reduce-scatter.41.cloned.1.call-start = ((), (), s32[]{:S(2)}) async-start(), calls=%async_computation.22 | async-start | bytes 1105920
  690.5 57.3 %reduce-scatter.43.cloned.1.call-start = ((), (), s32[]{:S(2)}) async-start(), calls=%async_computation.23 | async-start | bytes 1105920
  705.7 150.6 %reduce-scatter.45.cloned.1.call-start = ((), (), s32[]{:S(2)}) async-start(), calls=%async_computation.24 | async-start | bytes 1105920
  826.0 57.1 %reduce-scatter.47.cloned.1.call-start = ((), (), s32[]{:S(2)}) async-start(), calls=%async_computation.25 | async-start | bytes 1105920
  843.3 166.9 %all-reduce.21.cloned.1.call-start = ((), (), s32[]{:S(2)}) async-start(), calls=%async_computation.28 | async-start | bytes 2621440
  892.4 121.4 %reduce-scatter.49.cloned.1.call-start = ((), (), s32[]{:S(2)}) async-start(), calls=%async_computation.26 | async-start | bytes 6553600
  913.0 138.4 %reduce-scatter.29.cloned.1.call-start = ((), (), s32[]{:S(2)}) async-start(), calls=%async_computation.16 | async-start | bytes 2457600 | tf_op jit(solution)/shard_map/reduce_scatter | solution.py:427
  965.0 124.0 %reduce-scatter.31.cloned.1.call-start = ((), (), s32[]{:S(2)}) async-start(), calls=%async_computation.17 | async-start | bytes 2457600 | tf_op jit(solution)/shard_map/reduce_scatter | solution.py:436
  972.3 178.5 %reduce-scatter.33.cloned.1.call-start = ((), (), s32[]{:S(2)}) async-start(), calls=%async_computation.18 | async-start | bytes 6144000 | tf_op jit(solution)/shard_map/reduce_scatter | solution.py:439
  990.3 222.1 %reduce-scatter.35.cloned.1.call-start = ((), (), s32[]{:S(2)}) async-start(), calls=%async_computation.19 | async-start | bytes 6144000 | tf_op jit(solution)/shard_map/reduce_scatter | solution.py:442
  1007.2 323.4 %all-reduce.19.cloned.1.call-start = ((), (), s32[]{:S(2)}) async-start(), calls=%async_computation.27 | async-start | bytes 9994240 | tf_op jit(solution)/shard_map/psum | solution.py:471
  1216.5 33.3 %copy-start.24 = (f32[288,960]{1,0:T(8,128)S(1)}, f32[288,960]{1,0:T(8,128)}, u32[]{:S(2)}) copy-start(f32[288,960]{1,0:T(8,128)} %copy-done.22) | copy-start | bytes 3317764
  (182 other events, 794.9 us)
Sparse Core Ops, SparseCore 0:
  9.9 41.6 all-gather.8
  53.4 38.3 all-gather.10
  93.7 71.4 all-gather.12
  166.8 58.8 all-gather.14
  227.5 58.6 all-gather.16
  549.7 26.6 reduce-scatter.36
  579.9 26.8 reduce-scatter.38
  690.6 26.7 reduce-scatter.40
  720.9 26.8 reduce-scatter.42
  826.1 26.6 reduce-scatter.44
  856.4 26.6 reduce-scatter.46
  892.5 56.7 all-reduce.20
  952.3 61.4 reduce-scatter.48
  1017.3 34.0 reduce-scatter.28
  1055.0 34.0 reduce-scatter.30
  1092.0 58.7 reduce-scatter.32
  1153.6 58.7 reduce-scatter.34
  1215.8 114.7 all-reduce.18
where the time goes:
time: 1360 us; the launch traced here: 1350 us
  matrix products  486 us (36%)
  waiting for transfers between devices  387 us (28%)
  blocking collectives  256 us (19%)
  local copies, waits for them, and re-layouts  149 us (11%)
  other arithmetic  47.8 us (4%)
  between operations  19 us (1%)
    dot_general x3, matrix products, backward_one_sequence(): jnp.einsum('kgcl,ckgd->lkd', grad_scores, query_group, preferred_element_...  112 us
    unnamed x435, local copies, waits for them, and re-layouts  109 us
    dot_general x3, matrix products, backward_one_sequence(): jnp.einsum('kgcl,lkd->ckgd', grad_scores, key_seq, preferred_element_type...  105 us
    all_gather x3, blocking collectives, forward_level(): lax.all_gather(value_rows, 'cp', axis=1, tiled=True)  91.4 us
    psum x1, waiting for transfers between devices, local(): lax.psum(own_query.astype(jnp.bfloat16), 'dp').astype(jnp.float32)  77.6 us
    all_gather x3, blocking collectives, forward_level(): lax.all_gather(key_rows, 'cp', axis=1, tiled=True)  70.4 us
    reduce_scatter x1, waiting for transfers between devices, local(): lax.psum_scatter(total_gate.astype(jnp.bfloat16), 'cp', scatter_dimension...  61.7 us
    reduce_scatter x1, waiting for transfers between devices, local(): lax.psum_scatter(total_up.astype(jnp.bfloat16), 'cp', scatter_dimension=0...  61.6 us
  transfers between devices with their start and end apart: 18, of which 10 were waited for; matrix products, arithmetic and copies ran while one was open for 25% of the time, Pallas kernels for 0%

commit v1 on v0

v1 whole, which is shorter than its diff:
```python
import functools

import jax
import jax.numpy as jnp
from jax import lax
from jax.experimental import pallas as pl
from jax.experimental.pallas import tpu as pltpu
from jax.sharding import PartitionSpec as P

HEAD_DIM = 64
LANES = 128
GROUP = 3
RECUR = 3
NORM_EPSILON = 1e-05
MASKED_SCORE = -1e30
ROPE_BASE = 10000.0
SCALE = HEAD_DIM ** (-0.5)
MIB = 2**20
F32, BF16 = jnp.float32, jnp.bfloat16
NN = (((1,), (0,)), ((), ()))
NT = (((1,), (1,)), ((), ()))
TN = (((0,), (0,)), ((), ()))


def dotf(a, b, dims=NN):
    return lax.dot_general(a, b, dims, preferred_element_type=F32)


def whole(*shape):
    return pl.BlockSpec(shape, lambda g: (0,) * len(shape))


def turn(u):
    lane = lax.broadcasted_iota(jnp.int32, u.shape, 1) % HEAD_DIM
    return jnp.where(lane < HEAD_DIM // 2, pltpu.roll(u, LANES - 32, 1), pltpu.roll(u, 32, 1))


def qkv_kernel(x_ref, gain_ref, wq_ref, wkv_ref, cq_ref, sq_ref, ck_ref, sk_ref, q_ref, kv_ref, normed_ref):
    x = x_ref[...]
    factor = lax.rsqrt(jnp.mean(x * x, axis=-1, keepdims=True) + NORM_EPSILON)
    normed_ref[...] = (x * factor * gain_ref[...]).astype(BF16)
    normed = normed_ref[...]
    kv = dotf(normed, wkv_ref[...])
    cos, sin = ck_ref[...], sk_ref[...]
    for at in range(0, kv_ref.shape[1], LANES):
        u = kv[:, at : at + LANES]
        kv_ref[:, at : at + LANES] = (u * cos + turn(u) * sin).astype(BF16)
    q = dotf(normed, wq_ref[...])
    cos, sin = cq_ref[...], sq_ref[...]
    width = q_ref.shape[1]
    for at in range(0, width, LANES):
        if at + LANES <= width:
            u = q[:, at : at + LANES]
        else:
            u = jnp.concatenate([q[:, at:], jnp.zeros((q.shape[0], at + LANES - width), F32)], axis=1)
        r = (u * cos + turn(u) * sin).astype(BF16)
        q_ref[:, at : min(at + LANES, width)] = r[:, : min(LANES, width - at)]


def qkv_call(x, gain, wq, wkv, tables):
    rows, width = x.shape
    heads, both = wq.shape[1], wkv.shape[1]
    return pl.pallas_call(
        qkv_kernel,
        grid=(1,),
        in_specs=[whole(rows, width), whole(1, width), whole(width, heads), whole(width, both)]
        + [whole(rows, LANES)] * 4,
        out_specs=[whole(rows, heads), whole(rows, both), whole(rows, width)],
        out_shape=[
            jax.ShapeDtypeStruct((rows, heads), BF16),
            jax.ShapeDtypeStruct((rows, both), BF16),
            jax.ShapeDtypeStruct((rows, width), BF16),
        ],
        compiler_params=pltpu.CompilerParams(vmem_limit_bytes=32 * MIB),
        cost_estimate=pl.CostEstimate(
            flops=2 * rows * width * (heads + both),
            bytes_accessed=2 * width * (heads + both) + 8 * rows * width,
            transcendentals=0,
        ),
        name="norm_qkv_rope",
    )(x, gain, wq, wkv, *tables)


def make_bias(row_info, col_info, recursion):
    doc_r, pos_r = row_info[:, 0:1], row_info[:, 1:2]
    doc_c, pos_c, depth_c = col_info[0:1, :], col_info[1:2, :], col_info[2:3, :]
    live = (depth_c > recursion) | (pos_c == pos_r)
    allowed = (pos_c <= pos_r) & (doc_c == doc_r) & live
    return jnp.where(allowed, 0.0, MASKED_SCORE).astype(F32)


def split_pairs(packed, out, to_left):
    rows, width = packed.shape
    lane = lax.broadcasted_iota(jnp.int32, (rows, LANES), 1)
    for at in range(0, width, LANES):
        h = at // HEAD_DIM
        if at + LANES <= width:
            u = packed[:, at : at + LANES].astype(F32)
        else:
            u = jnp.concatenate([packed[:, at:].astype(F32), jnp.zeros((rows, at + LANES - width), F32)], axis=1)
        v = pltpu.roll(u, HEAD_DIM, 1)
        first, second = (u, v) if to_left else (v, u)
        keep = (lane < HEAD_DIM) if to_left else (lane >= HEAD_DIM)
        out[h] = jnp.where(keep, first, 0.0).astype(out.dtype)
        if at + LANES <= width:
            out[h + 1] = jnp.where(keep, second, 0.0).astype(out.dtype)


def join_pairs(scr, out_ref, from_left):
    heads = scr.shape[0]
    lane = lax.broadcasted_iota(jnp.int32, scr.shape[1:], 1)
    for h in range(0, heads, 2):
        at = h * HEAD_DIM
        a = scr[h] if from_left else pltpu.roll(scr[h], HEAD_DIM, 1)
        if h + 1 < heads:
            b = pltpu.roll(scr[h + 1], HEAD_DIM, 1) if from_left else scr[h + 1]
            out_ref[:, at : at + LANES] = jnp.where(lane < HEAD_DIM, a, b).astype(out_ref.dtype)
        else:
            out_ref[:, at : at + HEAD_DIM] = a[:, :HEAD_DIM].astype(out_ref.dtype)


def attend_kernel(recursion, count, q_ref, *refs):
    key_refs, (row_ref, col_ref, att_ref, lse_ref, bias, q_all, o_all) = refs[:count], refs[count:]
    g = pl.program_id(0)

    @pl.when(g == 0)
    def _():
        bias[...] = make_bias(row_ref[...], col_ref[...], recursion)
        split_pairs(q_ref[...], q_all, True)

    kv = jnp.concatenate([k[...] for k in key_refs], axis=0)
    for j in range(GROUP):
        h = g * GROUP + j
        s = dotf(q_all[h], kv, NT) * SCALE + bias[...]
        peak = jnp.max(s, axis=1, keepdims=True)
        e = jnp.exp(s - peak)
        total = jnp.sum(e, axis=1, keepdims=True)
        o_all[h] = dotf(e.astype(BF16), kv) / total
        lse_ref[0, :, j : j + 1] = peak + jnp.log(total)

    @pl.when(g == pl.num_programs(0) - 1)
    def _():
        join_pairs(o_all, att_ref, False)


def attend_call(recursion, q, kvs, row_info, col_info):
    rows, width = q.shape
    keys = sum(k.shape[0] for k in kvs)
    groups = kvs[0].shape[1] // LANES
    heads = groups * GROUP
    return pl.pallas_call(
        functools.partial(attend_kernel, recursion, len(kvs)),
        grid=(groups,),
        in_specs=[whole(rows, width)]
        + [pl.BlockSpec((k.shape[0], LANES), lambda g: (0, g)) for k in kvs]
        + [whole(rows, 2), whole(3, keys)],
        out_specs=[whole(rows, width), pl.BlockSpec((1, rows, GROUP), lambda g: (g, 0, 0))],
        out_shape=[
            jax.ShapeDtypeStruct((rows, width), BF16),
            jax.ShapeDtypeStruct((groups, rows, GROUP), F32),
        ],
        scratch_shapes=[
            pltpu.VMEM((rows, keys), F32),
            pltpu.VMEM((heads, rows, LANES), BF16),
            pltpu.VMEM((heads, rows, LANES), F32),
        ],
        compiler_params=pltpu.CompilerParams(vmem_limit_bytes=40 * MIB),
        cost_estimate=pl.CostEstimate(
            flops=4 * rows * keys * LANES * heads,
            bytes_accessed=4 * q.size + 2 * keys * groups * LANES,
            transcendentals=heads * rows * keys,
        ),
        name="attend",
    )(q, *kvs, row_info, col_info)


def attend_back_kernel(recursion, count, q_ref, do_ref, att_ref, *refs):
    key_refs, refs = refs[:count], refs[count:]
    lse_ref, row_ref, col_ref, cos_ref, sin_ref, dq_ref, dkv_ref, bias, q_all, do_all, dot_all, p3, ds3, dq_all = refs
    g = pl.program_id(0)
    rows, width = q_ref.shape

    @pl.when(g == 0)
    def _():
        bias[...] = make_bias(row_ref[...], col_ref[...], recursion)
        split_pairs(q_ref[...], q_all, True)
        split_pairs(do_ref[...], do_all, False)
        prod = do_ref[...].astype(F32) * att_ref[...].astype(F32)
        for h in range(width // HEAD_DIM):
            dot_all[h] = jnp.sum(prod[:, h * HEAD_DIM : (h + 1) * HEAD_DIM], axis=1, keepdims=True)

    kv = jnp.concatenate([k[...] for k in key_refs], axis=0)
    for j in range(GROUP):
        h = g * GROUP + j
        here = slice(j * rows, (j + 1) * rows)
        s = dotf(q_all[h], kv, NT) * SCALE + bias[...]
        p = jnp.exp(s - lse_ref[0, :, j : j + 1])
        dp = dotf(do_all[h], kv, NT)
        ds = (p * (dp - dot_all[h])).astype(BF16)
        p3[here, :] = p.astype(BF16)
        ds3[here, :] = ds
        dq = dotf(ds, kv) * SCALE
        dq_all[h] = dq * cos_ref[...] - turn(dq) * sin_ref[...]
    q3 = jnp.concatenate([q_all[g * GROUP + j] for j in range(GROUP)], axis=0)
    do3 = jnp.concatenate([do_all[g * GROUP + j] for j in range(GROUP)], axis=0)
    dkv = dotf(q3, ds3[...], TN) * SCALE + dotf(do3, p3[...], TN)
    dkv_ref[...] = dkv.T.astype(BF16)

    @pl.when(g == pl.num_programs(0) - 1)
    def _():
        join_pairs(dq_all, dq_ref, True)


def attend_back_call(recursion, q, do, att, kvs, lse, row_info, col_info, cos, sin):
    rows, width = q.shape
    keys = sum(k.shape[0] for k in kvs)
    groups = kvs[0].shape[1] // LANES
    heads = groups * GROUP
    return pl.pallas_call(
        functools.partial(attend_back_kernel, recursion, len(kvs)),
        grid=(groups,),
        in_specs=[whole(rows, width)] * 3
        + [pl.BlockSpec((k.shape[0], LANES), lambda g: (0, g)) for k in kvs]
        + [pl.BlockSpec((1, rows, GROUP), lambda g: (g, 0, 0)), whole(rows, 2), whole(3, keys)]
        + [whole(rows, LANES)] * 2,
        out_specs=[whole(rows, width), pl.BlockSpec((keys, LANES), lambda g: (0, g))],
        out_shape=[
            jax.ShapeDtypeStruct((rows, width), BF16),
            jax.ShapeDtypeStruct((keys, groups * LANES), BF16),
        ],
        scratch_shapes=[
            pltpu.VMEM((rows, keys), F32),
            pltpu.VMEM((heads, rows, LANES), BF16),
            pltpu.VMEM((heads, rows, LANES), BF16),
            pltpu.VMEM((heads, rows, 1), F32),
            pltpu.VMEM((GROUP * rows, keys), BF16),
            pltpu.VMEM((GROUP * rows, keys), BF16),
            pltpu.VMEM((heads, rows, LANES), F32),
        ],
        compiler_params=pltpu.CompilerParams(vmem_limit_bytes=48 * MIB),
        cost_estimate=pl.CostEstimate(
            flops=10 * rows * keys * LANES * heads,
            bytes_accessed=8 * q.size + 4 * keys * groups * LANES,
            transcendentals=heads * rows * keys,
        ),
        name="attend_back",
    )(q, do, att, *kvs, lse, row_info, col_info, cos, sin)


class Place:
    def __init__(self, dp, cp):
        self.dp, self.cp, self.square = dp, cp, cp == 4
        dp_at, cp_at = lax.axis_index("dp"), lax.axis_index("cp")
        self.core, self.z = dp_at % 2, dp_at // 2
        self.y, self.x = cp_at // 2, cp_at % 2

    def over_x(self, a):
        return lax.ppermute(a, "cp", [(i, i ^ 1) for i in range(self.cp)])

    def over_y(self, a):
        return lax.ppermute(a, "cp", [(i, i ^ 2) for i in range(self.cp)])

    def over_core(self, a):
        return lax.ppermute(a, "dp", [(i, i ^ 1) for i in range(self.dp)])

    def move_tokens(self, a):
        if not self.square:
            return a
        pairs = []
        for d in range(self.dp):
            for c in range(self.cp):
                z, core, y, x = d // 2, d % 2, c // 2, c % 2
                pairs.append((d * self.cp + c, (2 * z + y) * self.cp + 2 * core + x))
        return lax.ppermute(a, ("dp", "cp"), pairs)

    def key_blocks(self):
        if not self.square:
            return list(range(self.cp)), lax.axis_index("cp")
        own = 2 * self.core + self.x
        return [own ^ k for k in range(4)], own

    def gather_keys(self, a):
        if not self.square:
            return (lax.all_gather(a, "cp", axis=0, tiled=True),)
        from_x, from_core = self.over_x(a), self.over_core(a)
        return a, from_x, from_core, self.over_core(from_x)

    def scatter_keys(self, a):
        if not self.square:
            return lax.psum_scatter(a, "cp", scatter_dimension=0, tiled=True).astype(F32)
        rows = a.shape[0] // 4
        got = self.over_core(a[2 * rows :])
        pair = (a[: 2 * rows].astype(F32) + got.astype(F32)).astype(BF16)
        return pair[:rows].astype(F32) + self.over_x(pair[rows:]).astype(F32)

    def sum_z(self, a):
        n = self.dp // 2

        def hop(b, moves):
            return lax.ppermute(b, "dp", [(2 * s + c, 2 * t + c) for s, t in moves for c in range(2)])

        def add(b, c):
            return (b.astype(F32) + c.astype(F32)).astype(BF16)

        if n == 1:
            return a
        half = n // 2
        for t in range(half - 1):
            a = add(a, hop(a, [(t, t + 1), (n - 1 - t, n - 2 - t)]))
        a = add(a, hop(a, [(half - 1, half), (half, half - 1)]))
        for t in reversed(range(half - 1)):
            back = hop(a, [(t + 1, t), (n - 2 - t, n - 1 - t)])
            a = jnp.where((self.z == t) | (self.z == n - 1 - t), back, a)
        return a

    def scatter_sum(self, blocks, cut):
        _, rows, width = blocks.shape
        if not self.square:
            return lax.psum_scatter(blocks, "cp", scatter_dimension=0, tiled=False)

        def step(b, at, axis, over):
            away = lax.dynamic_index_in_dim(b, 1 - at, axis, keepdims=False)
            kept = lax.dynamic_index_in_dim(b, at, axis, keepdims=False)
            return (kept.astype(F32) + over(away).astype(F32)).astype(BF16)

        blocks = blocks.reshape(2, 2, rows, width)
        first = step(blocks[:, :, :cut], self.x, 1, self.over_x)
        second = step(blocks[:, :, cut:], self.y, 0, self.over_y)
        first = step(first, self.y, 0, self.over_y)
        second = step(second, self.x, 0, self.over_x)
        return jnp.concatenate([first, second], axis=0)

    def pick(self, a, b):
        return jnp.where(self.core == 0, a, b)


def inverse_rms(matrix):
    return lax.rsqrt(jnp.mean(matrix * matrix, axis=-1, keepdims=True) + NORM_EPSILON)


def norm_back(matrix, gain, upstream):
    factor = inverse_rms(matrix)
    unit = matrix * factor
    scaled = upstream * gain
    grad = factor * (scaled - unit * jnp.mean(scaled * unit, axis=-1, keepdims=True))
    return grad, jnp.sum(upstream * unit, axis=0)


def rope_tables(places):
    half = HEAD_DIM // 2
    inverse = jnp.power(ROPE_BASE, -2.0 * jnp.arange(half, dtype=F32) / HEAD_DIM)
    angles = places.astype(F32)[:, None] * inverse[None, :]
    cos, sin = jnp.cos(angles), jnp.sin(angles)
    cos, sin = jnp.concatenate([cos, cos], 1), jnp.concatenate([-sin, sin], 1)
    one, zero = jnp.ones_like(cos), jnp.zeros_like(sin)
    both = lambda a, b: jnp.concatenate([a, b], 1)
    return both(cos, cos), both(sin, sin), both(cos, one), both(sin, zero)


def gather_weights(place, shards):
    wq, wk, wv, wo, gate, up, down, router, gain_a, gain_f = shards
    rows, kv_heads = wk.shape[0], wk.shape[1] // HEAD_DIM
    gather = lambda a: lax.all_gather(a, "cp", axis=0, tiled=True)
    wkv = jnp.stack([wk.reshape(rows, kv_heads, HEAD_DIM), wv.reshape(rows, kv_heads, HEAD_DIM)], axis=2)
    wkv = wkv.reshape(rows, 2 * kv_heads * HEAD_DIM)
    both, width = wkv.shape[1], wq.shape[1]
    small = jnp.concatenate([gain_a[:, None], gain_f[:, None], router.T], axis=1)
    total = jnp.concatenate([wkv, wq, wo], axis=1)
    half = total.shape[1] // 2
    mine = gather(jnp.concatenate([place.pick(total[:, :half], total[:, half:]), small], axis=1))
    theirs = place.over_core(mine)
    total = jnp.concatenate([place.pick(mine, theirs)[:, :half], place.pick(theirs, mine)[:, :half]], axis=1)
    small = mine[:, half:]
    wkv, wq, wo = total[:, :both], total[:, both : both + width], total[:, both + width :]
    mine = gather(place.pick(gate, up))
    theirs = place.over_core(mine)
    gate, up = place.pick(mine, theirs), place.pick(theirs, mine)
    each, wide = down.shape
    mine = gather(place.pick(down[: each // 2], down[each // 2 :]))
    theirs = place.over_core(mine)
    down = jnp.stack(
        [
            place.pick(mine, theirs).reshape(place.cp, each // 2, wide),
            place.pick(theirs, mine).reshape(place.cp, each // 2, wide),
        ],
        axis=1,
    ).reshape(place.cp * each, wide)
    return wkv, wq, wo, gate, up, down, small


def forward_level(state, weights, recursion, context):
    wkv, wq, wo, gate_w, up_w, down_w, small = weights
    place, tables, row_info, col_info, depth = context
    gain_a, gain_f = small[:, 0].astype(F32), small[:, 1].astype(F32)
    q, kv, normed = qkv_call(state, gain_a[None, :], wq, wkv, tables)
    kvs = place.gather_keys(kv)
    att, lse = attend_call(recursion, q, kvs, row_info, col_info)
    attn = dotf(att, wo)
    after = state + attn
    normed2 = (after * inverse_rms(after) * gain_f).astype(BF16)
    gate = dotf(normed2, gate_w)
    up = dotf(normed2, up_w)
    inner = (jax.nn.silu(gate) * up).astype(BF16)
    branch = attn + dotf(inner, down_w)
    router_row = small[:, 2 + recursion].astype(F32)
    router = jax.nn.sigmoid(jnp.sum(state * router_row, axis=-1, keepdims=True))
    active = (depth[:, None] > recursion).astype(F32)
    following = state + active * router * branch
    saved = (state, normed, q, kvs, lse, att, after, normed2, gate.astype(BF16), up.astype(BF16), inner, branch, router_row, router, active)
    return following, saved


def backward_level(saved, weights, recursion, context, grad):
    wkv, wq, wo, gate_w, up_w, down_w, small = weights
    place, tables, row_info, col_info, _ = context
    cos_q, sin_q, cos_k, sin_k = tables
    gain_a, gain_f = small[:, 0].astype(F32), small[:, 1].astype(F32)
    state, normed, q, kvs, lse, att, after, normed2, gate, up, inner, branch, router_row, router, active = saved
    rows = state.shape[0]
    g_branch = grad * (active * router)
    g_logit = jnp.sum(grad * branch, axis=-1, keepdims=True) * active * router * (1.0 - router)
    g_router = jnp.sum(g_logit * state, axis=0)
    g_state = grad + g_logit * router_row
    g_ffn = g_branch.astype(BF16)
    g_inner = dotf(g_ffn, down_w, NT)
    gate, up = gate.astype(F32), up.astype(F32)
    sig = jax.nn.sigmoid(gate)
    g_gate = (g_inner * up * sig * (1.0 + gate * (1.0 - sig))).astype(BF16)
    g_up = (g_inner * gate * sig).astype(BF16)
    g_normed2 = dotf(g_gate, gate_w, NT) + dotf(g_up, up_w, NT)
    g_after, g_gain_f = norm_back(after, gain_f, g_normed2)
    g_state = g_state + g_after
    g_attn = (g_after + g_branch).astype(BF16)
    g_att = dotf(g_attn, wo, NT).astype(BF16)
    dq, dkv = attend_back_call(recursion, q, g_att, att, kvs, lse, row_info, col_info, cos_q, sin_q)
    dkv = place.scatter_keys(dkv)
    parts = dkv.reshape(rows, -1, 2, 2, HEAD_DIM // 2)
    swapped = parts[:, :, :, ::-1, :].reshape(rows, -1)
    spread = lambda t: jnp.tile(t, (1, dkv.shape[1] // LANES))
    dkv = (dkv * spread(cos_k) - swapped * spread(sin_k)).astype(BF16)
    g_normed = dotf(dq, wq, NT) + dotf(dkv, wkv, NT)
    g_rows, g_gain_a = norm_back(state, gain_a, g_normed)
    g_state = g_state + g_rows
    return g_state, (g_ffn, inner), (g_gate, g_up, normed2), (g_attn, att), (dq, dkv, normed), (g_router, g_gain_a, g_gain_f)


def local(tokens, recur_depth, document_ids, cotangent, *shards, dp, cp):
    place = Place(dp, cp)
    rows = tokens.shape[1]
    ids = jnp.stack([document_ids[0], recur_depth[0]])
    ids = place.move_tokens(ids)
    state = place.move_tokens(tokens[0]).astype(F32)
    grad = place.move_tokens(cotangent[0]).astype(F32)
    steps = jnp.arange(rows, dtype=jnp.int32)
    blocks, block = place.key_blocks()
    every = jnp.concatenate(place.gather_keys(ids.T), axis=0)
    spots = jnp.concatenate([b * rows + steps for b in blocks])
    col_info = jnp.stack([every[:, 0], spots, every[:, 1]])
    row_info = jnp.stack([ids[0], block * rows + steps], axis=1)
    tables = rope_tables(row_info[:, 1])
    context = (place, tables, row_info, col_info, ids[1])
    weights = gather_weights(place, shards)
    saved = []
    for recursion in range(RECUR):
        state, kept = forward_level(state, weights, recursion, context)
        saved.append(kept)
    activations = place.move_tokens(state.astype(BF16))[None]
    downs, ups, outs, ins, smalls = [], [], [], [], []
    for recursion in reversed(range(RECUR)):
        grad, a, b, c, d, e = backward_level(saved[recursion], weights, recursion, context, grad)
        for group, item in zip((downs, ups, outs, ins, smalls), (a, b, c, d, e)):
            group.append(item)
    input_grad = place.move_tokens(grad.astype(BF16))[None]
    column = lambda group, i: jnp.concatenate([item[i] for item in group], axis=0)
    width = shards[0].shape[0] * cp

    def reduce(left, away, kept):
        got = place.over_core(dotf(left, away, TN).astype(BF16))
        own = (dotf(left, kept, TN) + got.astype(F32)).astype(BF16)
        own = own.reshape(cp, -1, own.shape[1])
        cut = -(-own.shape[1] // 32) * 16
        return place.sum_z(place.scatter_sum(own, cut))

    def halves(right):
        n = right.shape[1] // 2
        return place.pick(right[:, n:], right[:, :n]), place.pick(right[:, :n], right[:, n:])

    def finish(own):
        other = place.over_core(own)
        return place.pick(own, other).astype(F32), place.pick(other, own).astype(F32)

    own_down = reduce(column(downs, 1), *halves(column(downs, 0)))
    g_gate, g_up = column(ups, 0), column(ups, 1)
    own_up = reduce(column(ups, 2), place.pick(g_up, g_gate), place.pick(g_gate, g_up))
    own_out = reduce(column(outs, 1), *halves(column(outs, 0)))
    own_in = reduce(column(ins, 2), *halves(jnp.concatenate([column(ins, 0), column(ins, 1)], axis=1)))
    grad_down = jnp.concatenate(finish(own_down), axis=1)
    grad_gate, grad_up = finish(own_up)
    grad_out = jnp.concatenate(finish(own_out), axis=1)
    grad_in = jnp.concatenate(finish(own_in), axis=1)
    grad_query = grad_in[:, :width]
    grad_kv = grad_in[:, width:].reshape(grad_in.shape[0], -1, 2, HEAD_DIM)
    grad_key = grad_kv[:, :, 0].reshape(grad_in.shape[0], -1)
    grad_value = grad_kv[:, :, 1].reshape(grad_in.shape[0], -1)
    vectors = [smalls[RECUR - 1 - r][0] for r in range(RECUR)]
    vectors += [sum(s[1] for s in smalls), sum(s[2] for s in smalls)]
    vectors = lax.psum(jnp.stack(vectors), ("dp", "cp"))
    vectors = lax.dynamic_slice_in_dim(vectors, lax.axis_index("cp") * (width // cp), width // cp, axis=1)
    return (
        activations,
        input_grad,
        grad_query,
        grad_key,
        grad_value,
        grad_out,
        grad_gate,
        grad_up,
        grad_down,
        vectors[:RECUR],
        vectors[RECUR],
        vectors[RECUR + 1],
    )


def solution(mesh):
    by_token = P("dp", "cp", None)
    by_row = P("cp", None)
    in_specs = (by_token, P("dp", "cp"), P("dp", "cp"), by_token) + (by_row,) * 7 + (P(None, "cp"), P("cp"), P("cp"))
    out_specs = (by_token, by_token) + (by_row,) * 7 + (P(None, "cp"), P("cp"), P("cp"))
    step = functools.partial(local, dp=mesh.shape["dp"], cp=mesh.shape["cp"])
    return jax.shard_map(step, mesh=mesh, in_specs=in_specs, out_specs=out_specs, check_vma=False)
```

time: 1360 us -> 889 us (0.65)
  matrix products: 486 us -> 128 us
  blocking collectives: 256 us -> 37.9 us
  Pallas kernels: 0 us -> 100 us
  starting transfers between devices: 1.52 us -> 74.3 us
  waiting for transfers between devices: 387 us -> 320 us
  other arithmetic: 47.8 us -> 67.9 us
    dot_general x87 -> x38, matrix products: 486 us -> 128 us  [dotf(): return lax.dot_general(a, b, dims, preferred_element_type=F32)]
    all_gather x9 -> x0, blocking collectives: 202 us -> none  [the longest x3 91.4 us: forward_level(): lax.all_gather(value_rows, 'cp', axis=1, tiled=True)]
    reduce_scatter x4 -> x0, waiting for transfers between devices: 196 us -> none  [the longest x1 61.7 us: local(): lax.psum_scatter(total_gate.astype(jnp.bfloat16), 'cp', scatter_dimension...]
    ppermute x0 -> x62, waiting for transfers between devices: none -> 188 us  [the longest x15 85.5 us: over_x(): return lax.ppermute(a, 'cp', [(i, i ^ 1) for i in range(self.cp)])]
    pallas_call x0 -> x9, Pallas kernels: none -> 100 us  [the longest x3 55.1 us: attend_back_call(): pl.pallas_call(functools.partial(attend_back_kernel, recursion, len(kvs))...]
    psum x1 -> x0, waiting for transfers between devices: 77.6 us -> none  [local(): lax.psum(own_query.astype(jnp.bfloat16), 'dp').astype(jnp.float32)]
    ppermute x0 -> x62, starting transfers between devices: none -> 74.2 us  [the longest x12 26.5 us: hop(): lax.ppermute(b, 'dp', [(2 * s + c, 2 * t + c) for s, t in moves for c in...]
    unnamed x435 -> x399, local copies, waits for them, and re-layouts: 109 us -> 52.2 us
  transfers between devices with their start and end apart: 18 -> 65, of which waited for: 10 -> 25; matrix products, arithmetic and copies ran while one was open for 25% -> 19% of each run, Pallas kernels for 0% -> 2%
where the time goes in v1:
time: 889 us; the launch traced here: 883 us
  waiting for transfers between devices  320 us (36%)
  local copies, waits for them, and re-layouts  136 us (15%)
  matrix products  128 us (14%)
  Pallas kernels  100 us (11%)
  starting transfers between devices  74.3 us (8%)
  other arithmetic  67.9 us (8%)
  blocking collectives  37.9 us (4%)
  between operations  17.2 us (2%)
    all_gather x3, waiting for transfers between devices, gather_weights(): gather = lambda a: lax.all_gather(a, 'cp', axis=0, tiled=True)  132 us
    dot_general x38, matrix products, dotf(): return lax.dot_general(a, b, dims, preferred_element_type=F32)  128 us
    ppermute x15, waiting for transfers between devices, over_x(): return lax.ppermute(a, 'cp', [(i, i ^ 1) for i in range(self.cp)])  85.5 us
    ppermute x12, waiting for transfers between devices, hop(): lax.ppermute(b, 'dp', [(2 * s + c, 2 * t + c) for s, t in moves for c in...  60.1 us
    pallas_call x3, Pallas kernels, attend_back_call(): pl.pallas_call(functools.partial(attend_back_kernel, recursion, len(kvs))...  55.1 us
    unnamed x399, local copies, waits for them, and re-layouts  52.2 us
    pallas_call x3, Pallas kernels, attend_call(): pl.pallas_call(functools.partial(attend_kernel, recursion, len(kvs)), gri...  40.1 us
    ppermute x8, waiting for transfers between devices, over_y(): return lax.ppermute(a, 'cp', [(i, i ^ 2) for i in range(self.cp)])  38.8 us
  transfers between devices with their start and end apart: 65, of which 25 were waited for; matrix products, arithmetic and copies ran while one was open for 19% of the time, Pallas kernels for 2%

profile of v1, /device:TPU:0, one launch (start us, length us, event | category | flops | bytes accessed | tf_op | source)
XLA Modules:
  0.0 882.5 jit_solution(14839704796095197697)
XLA Ops:
  17.6 38.2 %all-gather.9.cloned.1.call-done = bf16[4,240,1285]{1,2,0:T(8,128)(2,1)} async-done(((bf16[1,240,1285]{1,2,0:T(8,128)(2,1)}), bf16[4,240,1285]{1,2,0:T(8,128)(2,1)}) %all-gather.9.cloned.1.call-update) | async-done | bytes 2467216 | tf_op jit(solution)/shard_map/all_gather | solution.py:363
  62.8 6.5 collective-permute-start
  71.8 51.5 %all-gather.5.cloned.1.call-done = bf16[960,2560]{1,0:T(8,128)(2,1)} async-done(((bf16[240,2560]{1,0:T(8,128)(2,1)}), bf16[960,2560]{1,0:T(8,128)(2,1)}) %all-gather.5.cloned.1.call-update) | async-done | bytes 4915216 | tf_op jit(solution)/shard_map/all_gather | solution.py:363
  123.3 42.1 %all-gather.7.cloned.1.call-done = bf16[1280,960]{1,0:T(8,128)(2,1)} async-done(((bf16[320,960]{1,0:T(8,128)(2,1)}), bf16[1280,960]{1,0:T(8,128)(2,1)}) %all-gather.7.cloned.1.call-update) | async-done | bytes 2457616 | tf_op jit(solution)/shard_map/all_gather | solution.py:363
  210.0 14.0 %attend.3 = (bf16[288,960]{1,0:T(8,128)(2,1)S(1)}, f32[5,288,3]{2,1,0:T(8,128)S(1)}) custom-call(bf16[288,960]{1,0:T(8,128)(2,1)S(1)} %copy-done.28, bf16[288,640]{1,0:T(8,128)(2,1)} %get-tuple-element.34.refs_0_, bf16[288,640]{1,0:T(8,128)(2,1)} %collective-permute-done.3.refs_1_, bf16[288,640]{1,0:T(8,128)(2,1)S(1)} %collective-permute-done.4.refs_2_, ...), custom_call_target="tpu_custom_call" | custom-call | flops 2548039680 | bytes 2580480 | tf_op jit(solution)/shard_map/attend/pallas_call | solution.py:151
  229.2 8.5 broadcast_select_fusion.1
  245.0 5.1 multiply_reduce_fusion.10
  253.5 9.3 %collective-permute-done.11.refs_1_ = bf16[288,640]{1,0:T(8,128)(2,1)S(1)} collective-permute-done((bf16[288,640]{1,0:T(8,128)(2,1)S(1)}, bf16[288,640]{1,0:T(8,128)(2,1)S(1)}, u32[]{:S(2)}, u32[]{:S(2)}) %collective-permute-start.11) | collective-permute-done | bytes 368672 | tf_op jit(solution)/shard_map/ppermute | solution.py:258
  264.5 13.0 %attend.4 = (bf16[288,960]{1,0:T(8,128)(2,1)S(1)}, f32[5,288,3]{2,1,0:T(8,128)S(1)}) custom-call(bf16[288,960]{1,0:T(8,128)(2,1)S(1)} %get-tuple-element.36.q_ref, bf16[288,640]{1,0:T(8,128)(2,1)S(1)} %get-tuple-element.37.refs_0_, bf16[288,640]{1,0:T(8,128)(2,1)S(1)} %collective-permute-done.11.refs_1_, ...), custom_call_target="tpu_custom_call" | custom-call | flops 2548039680 | bytes 2580480 | tf_op jit(solution)/shard_map/attend/pallas_call | solution.py:151
  296.3 6.5 collective-permute-done.14.refs_1_
  304.5 13.2 %attend.5 = (bf16[288,960]{1,0:T(8,128)(2,1)S(1)}, f32[5,288,3]{2,1,0:T(8,128)S(1)}) custom-call(bf16[288,960]{1,0:T(8,128)(2,1)S(1)} %get-tuple-element.39.q_ref, bf16[288,640]{1,0:T(8,128)(2,1)S(1)} %get-tuple-element.40.refs_0_, bf16[288,640]{1,0:T(8,128)(2,1)S(1)} %collective-permute-done.14.refs_1_, ...), custom_call_target="tpu_custom_call" | custom-call | flops 2548039680 | bytes 2580480 | tf_op jit(solution)/shard_map/attend/pallas_call | solution.py:151
  327.3 6.9 fusion.12
  348.1 18.3 %attend_back.3 = (bf16[288,960]{1,0:T(8,128)(2,1)S(1)}, bf16[1152,640]{1,0:T(8,128)(2,1)}) custom-call(bf16[288,960]{1,0:T(8,128)(2,1)S(1)} %get-tuple-element.39.q_ref, bf16[288,960]{1,0:T(8,128)(2,1)S(1)} %convolution_convert_fusion.6.do_ref, bf16[288,960]{1,0:T(8,128)(2,1)S(1)} %get-tuple-element.41.att_ref, ...), custom_call_target="tpu_custom_call" | custom-call | flops 6370099200 | bytes 5160960 | tf_op jit(solution)/shard_map/attend_back/pallas_call | solution.py:219
  379.7 9.4 %collective-permute-done.20 = bf16[288,640]{1,0:T(8,128)(2,1)S(1)} collective-permute-done((bf16[288,640]{1,0:T(8,128)(2,1)S(1)}, bf16[288,640]{1,0:T(8,128)(2,1)S(1)}, u32[]{:S(2)}, u32[]{:S(2)}) %collective-permute-start.20) | collective-permute-done | bytes 368672 | tf_op jit(solution)/shard_map/ppermute | solution.py:258
  420.2 18.0 %attend_back.4 = (bf16[288,960]{1,0:T(8,128)(2,1)S(1)}, bf16[1152,640]{1,0:T(8,128)(2,1)}) custom-call(bf16[288,960]{1,0:T(8,128)(2,1)S(1)} %copy-done.31, bf16[288,960]{1,0:T(8,128)(2,1)S(1)} %convolution_convert_fusion.5.do_ref, bf16[288,960]{1,0:T(8,128)(2,1)S(1)} %copy-done.12, bf16[288,640]{1,0:T(8,128)(2,1)S(1)} %copy-done.37, ...), custom_call_target="tpu_custom_call" | custom-call | flops 6370099200 | bytes 5160960 | tf_op jit(solution)/shard_map/attend_back/pallas_call | solution.py:219
  445.5 8.4 collective-permute-done.22
  486.3 9.0 %convolution_convert_fusion = bf16[960,2560]{1,0:T(8,128)(2,1)} fusion(pred[]{:T(512)S(6)} %eq.9, bf16[288,2560]{1,0:T(8,128)(2,1)} %copy-done.164, bf16[288,2560]{1,0:T(8,128)(2,1)} %copy-done.163, bf16[288,2560]{1,0:T(8,128)(2,1)S(1)} %copy-done.162, bf16[288,2560]{1,0:T(8,128)(2,1)S(1)} %get-tuple-element.132, bf16[288,2560]{1,0:T(8,128)(2,1)S(1)} %copy-done.159, ...), kind=kOutput, calls=%fused_computation.1 | convolution fusion | flops 4282920960 | bytes 15421441 | tf_op jit(solution)/shard_map/dot_general | solution.py:26
  497.7 18.7 %attend_back.5 = (bf16[288,960]{1,0:T(8,128)(2,1)S(1)}, bf16[1152,640]{1,0:T(8,128)(2,1)}) custom-call(bf16[288,960]{1,0:T(8,128)(2,1)S(1)} %copy-done.29, bf16[288,960]{1,0:T(8,128)(2,1)S(1)} %convolution_convert_fusion.4.do_ref, bf16[288,960]{1,0:T(8,128)(2,1)S(1)} %copy-done.17, bf16[288,640]{1,0:T(8,128)(2,1)} %get-tuple-element.34.refs_0_, ...), custom_call_target="tpu_custom_call" | custom-call | flops 6370099200 | bytes 5160960 | tf_op jit(solution)/shard_map/attend_back/pallas_call | solution.py:219
  556.8 6.1 collective-permute-start.25
  562.9 5.2 convolution_convert_fusion.2
  574.7 5.1 collective-permute-done.37
  583.4 37.9 %psum.7 = f32[5,960]{1,0:T(8,128)S(1)} all-reduce(f32[5,960]{1,0:T(8,128)S(1)} %stack.42), channel_id=1, replica_groups=mesh['dp'=8,'cp'=4] {'dp','cp'}, use_global_device_ids=true, to_apply=%region_27.28 | all-reduce | flops 4800 | bytes 38400 | tf_op jit(solution)/shard_map/psum | solution.py:507
  622.7 6.5 add_convert_fusion.1
  669.2 8.4 add_convert_fusion
  682.9 19.9 %collective-permute-done.47 = bf16[2,112,2560]{2,1,0:T(8,128)(2,1)S(1)} collective-permute-done((bf16[2,112,2560]{2,1,0:T(8,128)(2,1)S(1)}, bf16[2,112,2560]{2,1,0:T(8,128)(2,1)S(1)}, u32[]{:S(2)}, u32[]{:S(2)}) %collective-permute-start.47) | collective-permute-done | bytes 1146912 | tf_op jit(solution)/shard_map/ppermute | solution.py:261
  704.5 20.3 %collective-permute-done.45 = bf16[2,128,2560]{2,1,0:T(8,128)(2,1)S(1)} collective-permute-done((bf16[2,128,2560]{2,1,0:T(8,128)(2,1)S(1)}, bf16[2,128,2560]{2,1,0:T(8,128)(2,1)S(1)}, u32[]{:S(2)}, u32[]{:S(2)}) %collective-permute-start.45) | collective-permute-done | bytes 1310752 | tf_op jit(solution)/shard_map/ppermute | solution.py:258
  725.8 12.5 %collective-permute-done.48 = bf16[112,2560]{1,0:T(8,128)(2,1)S(1)} collective-permute-done((bf16[112,2560]{1,0:T(8,128)(2,1)S(1)}, bf16[112,2560]{1,0:T(8,128)(2,1)S(1)}, u32[]{:S(2)}, u32[]{:S(2)}) %collective-permute-start.48) | collective-permute-done | bytes 573472 | tf_op jit(solution)/shard_map/ppermute | solution.py:258
  739.4 13.8 %collective-permute-done.46 = bf16[128,2560]{1,0:T(8,128)(2,1)S(1)} collective-permute-done((bf16[128,2560]{1,0:T(8,128)(2,1)S(1)}, bf16[128,2560]{1,0:T(8,128)(2,1)S(1)}, u32[]{:S(2)}, u32[]{:S(2)}) %collective-permute-start.46) | collective-permute-done | bytes 655392 | tf_op jit(solution)/shard_map/ppermute | solution.py:261
  754.5 5.9 collective-permute-start.49
  770.0 17.8 %collective-permute-done.49 = bf16[240,2560]{1,0:T(8,128)(2,1)S(1)} collective-permute-done((bf16[240,2560]{1,0:T(8,128)(2,1)S(1)}, bf16[240,2560]{1,0:T(8,128)(2,1)S(1)}, u32[]{:S(2)}, u32[]{:S(2)}) %collective-permute-start.49) | collective-permute-done | bytes 1228832 | tf_op jit(solution)/shard_map/ppermute | solution.py:300
  816.0 36.6 %collective-permute-done.33 = bf16[240,800]{0,1:T(8,128)(2,1)} collective-permute-done((bf16[240,800]{0,1:T(8,128)(2,1)S(1)}, bf16[240,800]{0,1:T(8,128)(2,1)}, u32[]{:S(2)}, u32[]{:S(2)}) %collective-permute-start.33) | collective-permute-done | bytes 384032 | tf_op jit(solution)/shard_map/ppermute | solution.py:300
  853.7 5.3 collective-permute-done.60
  (748 shorter events, 367.6 us)
Async XLA Ops:
  7.2 48.6 %all-gather.9.cloned.1.call-start = ((), (), s32[]{:S(2)}) async-start(), calls=%async_computation.2 | async-start | bytes 3297280 | tf_op jit(solution)/shard_map/all_gather | solution.py:363
  13.2 110.1 %all-gather.5.cloned.1.call-start = ((), (), s32[]{:S(2)}) async-start(), calls=%async_computation | async-start | bytes 6144000 | tf_op jit(solution)/shard_map/all_gather | solution.py:363
  14.5 150.9 %all-gather.7.cloned.1.call-start = ((), (), s32[]{:S(2)}) async-start(), calls=%async_computation.1 | async-start | bytes 3276800 | tf_op jit(solution)/shard_map/all_gather | solution.py:363
  62.1 116.8 %collective-permute-start.2 = (bf16[960,1285]{0,1:T(8,128)(2,1)}, bf16[960,1285]{0,1:T(8,128)(2,1)}, u32[]{:S(2)}, u32[]{:S(2)}) collective-permute-start(bf16[960,1285]{0,1:T(8,128)(2,1)} %copy.111), channel_id=1, source_target_pairs={{0,4},{4,0},{8,12},{12,8},{16,20},{20,16},{24,28},{28,24},{1,5},{5... | collective-permute-start | bytes 7401608 | tf_op jit(solution)/shard_map/ppermute | solution.py:264
  62.1 107.7 %collective-permute-start.1 = (s32[2,288]{1,0:T(2,128)S(1)}, s32[2,288]{1,0:T(2,128)S(1)}, u32[]{:S(2)}, u32[]{:S(2)}) collective-permute-start(s32[2,288]{1,0:T(2,128)S(1)} %pad_add_fusion.1), channel_id=1, source_target_pairs={{0,0},{1,1},{2,4},{3,5},{4,2},{5,3},{6,6},{7,7},{8,8},{9,9},{10,12... | collective-permute-start | bytes 6920 | tf_op jit(solution)/shard_map/ppermute | solution.py:274
  62.8 113.1 %collective-permute-start = (bf16[288,960]{1,0:T(8,128)(2,1)}, bf16[288,960]{1,0:T(8,128)(2,1)}, u32[]{:S(2)}, u32[]{:S(2)}) collective-permute-start(bf16[288,960]{1,0:T(8,128)(2,1)} %bitcast), channel_id=1, source_target_pairs={{0,0},{1,1},{2,4},{3,5},{4,2},{5,3},{6,6},{7,7},{8,8},{9,9},{10,12... | collective-permute-start | bytes 1658888 | tf_op jit(solution)/shard_map/ppermute | solution.py:274
  123.3 105.8 %collective-permute-start.9 = (bf16[960,2560]{1,0:T(8,128)(2,1)}, bf16[960,2560]{1,0:T(8,128)(2,1)}, u32[]{:S(2)}, u32[]{:S(2)}) collective-permute-start(bf16[960,2560]{1,0:T(8,128)(2,1)} %all-gather.5.cloned.1.call-done), channel_id=1, source_target_pairs={{0,4},{4,0},{8,12},{12,8},{16,20},{20,16},{24,28},{28,24},{1,5},{5... | collective-permute-start | bytes 14745608 | tf_op jit(solution)/shard_map/ppermute | solution.py:264
  169.7 24.5 %collective-permute-start.10 = (bf16[1280,960]{0,1:T(8,128)(2,1)}, bf16[1280,960]{0,1:T(8,128)(2,1)}, u32[]{:S(2)}, u32[]{:S(2)}) collective-permute-start(bf16[1280,960]{0,1:T(8,128)(2,1)} %copy.117), channel_id=1, source_target_pairs={{0,4},{4,0},{8,12},{12,8},{16,20},{20,16},{24,28},{28,24},{1,5},{5... | collective-permute-start | bytes 7372808 | tf_op jit(solution)/shard_map/ppermute | solution.py:264
  520.4 147.2 %collective-permute-start.44 = (bf16[960,2560]{1,0:T(8,128)(2,1)}, bf16[960,2560]{1,0:T(8,128)(2,1)}, u32[]{:S(2)}, u32[]{:S(2)}) collective-permute-start(bf16[960,2560]{1,0:T(8,128)(2,1)} %convolution_convert_fusion), channel_id=1, source_target_pairs={{0,4},{4,0},{8,12},{12,8},{16,20},{20,16},{24,28},{28,24},{1,5},{5... | collective-permute-start | bytes 14745608 | tf_op jit(solution)/shard_map/ppermute | solution.py:264
  525.9 96.8 %collective-permute-start.53 = (bf16[2560,480]{0,1:T(8,128)(2,1)}, bf16[2560,480]{0,1:T(8,128)(2,1)}, u32[]{:S(2)}, u32[]{:S(2)}) collective-permute-start(bf16[2560,480]{0,1:T(8,128)(2,1)} %convolution_convert_fusion.1), channel_id=1, source_target_pairs={{0,4},{4,0},{8,12},{12,8},{16,20},{20,16},{24,28},{28,24},{1,5},{5... | collective-permute-start | bytes 7372808 | tf_op jit(solution)/shard_map/ppermute | solution.py:264
  531.7 36.4 %collective-permute-start.38 = (bf16[2,112,480]{2,1,0:T(8,128)(2,1)}, bf16[2,112,480]{2,1,0:T(8,128)(2,1)}, u32[]{:S(2)}, u32[]{:S(2)}) collective-permute-start(bf16[2,112,480]{2,1,0:T(8,128)(2,1)} %dynamic-slice_bitcast_fusion.7), channel_id=1, source_target_pairs={{0,2},{1,3},{2,0},{3,1},{4,6},{5,7},{6,4},{7,5},{8,10},{9,11},{10,... | collective-permute-start | bytes 645128 | tf_op jit(solution)/shard_map/ppermute | solution.py:261
  532.8 36.3 %collective-permute-start.36 = (bf16[2,128,480]{2,1,0:T(8,128)(2,1)S(1)}, bf16[2,128,480]{2,1,0:T(8,128)(2,1)}, u32[]{:S(2)}, u32[]{:S(2)}) collective-permute-start(bf16[2,128,480]{2,1,0:T(8,128)(2,1)S(1)} %dynamic-slice_bitcast_fusion.6), channel_id=1, source_target_pairs={{0,1},{1,0},{2,3},{3,2},{4,5},{5,4},{6,7},{7,6},{8,9},{9,8},{10,11... | collective-permute-start | bytes 737288 | tf_op jit(solution)/shard_map/ppermute | solution.py:258
  556.8 240.2 %collective-permute-start.25 = (bf16[288,960]{1,0:T(8,128)(2,1)}, bf16[288,960]{1,0:T(8,128)(2,1)}, u32[]{:S(2)}, u32[]{:S(2)}) collective-permute-start(bf16[288,960]{1,0:T(8,128)(2,1)} %fusion.53), channel_id=1, source_target_pairs={{0,0},{1,1},{2,4},{3,5},{4,2},{5,3},{6,6},{7,7},{8,8},{9,9},{10,12... | collective-permute-start | bytes 1658888 | tf_op jit(solution)/shard_map/ppermute | solution.py:274
  568.0 87.5 %collective-permute-start.26 = (bf16[960,800]{0,1:T(8,128)(2,1)}, bf16[960,800]{0,1:T(8,128)(2,1)}, u32[]{:S(2)}, u32[]{:S(2)}) collective-permute-start(bf16[960,800]{0,1:T(8,128)(2,1)} %convolution_convert_fusion.2), channel_id=1, source_target_pairs={{0,4},{4,0},{8,12},{12,8},{16,20},{20,16},{24,28},{28,24},{1,5},{5... | collective-permute-start | bytes 4608008 | tf_op jit(solution)/shard_map/ppermute | solution.py:264
  579.9 41.4 %collective-permute-start.40 = (bf16[240,480]{1,0:T(8,128)(2,1)S(1)}, bf16[240,480]{1,0:T(8,128)(2,1)S(1)}, u32[]{:S(2)}, u32[]{:S(2)}) collective-permute-start(bf16[240,480]{1,0:T(8,128)(2,1)S(1)} %pad_maximum_fusion.28), channel_id=1, source_target_pairs={{0,8},{4,12},{24,16},{28,20},{1,9},{5,13},{25,17},{29,21},{2,10},{... | collective-permute-start | bytes 691208 | tf_op jit(solution)/shard_map/ppermute | solution.py:300
  621.3 175.7 %collective-permute-start.41 = (bf16[240,480]{1,0:T(8,128)(2,1)S(1)}, bf16[240,480]{1,0:T(8,128)(2,1)}, u32[]{:S(2)}, u32[]{:S(2)}) collective-permute-start(bf16[240,480]{1,0:T(8,128)(2,1)S(1)} %add_convert_fusion.17), channel_id=1, source_target_pairs={{8,16},{12,20},{16,8},{20,12},{9,17},{13,21},{17,9},{21,13},{10,18... | collective-permute-start | bytes 691208 | tf_op jit(solution)/shard_map/ppermute | solution.py:300
  639.3 40.7 %collective-permute-start.56 = (bf16[2,320,480]{2,1,0:T(8,128)(2,1)}, bf16[2,320,480]{2,1,0:T(8,128)(2,1)}, u32[]{:S(2)}, u32[]{:S(2)}) collective-permute-start(bf16[2,320,480]{2,1,0:T(8,128)(2,1)} %bitcast.241), channel_id=1, source_target_pairs={{0,2},{1,3},{2,0},{3,1},{4,6},{5,7},{6,4},{7,5},{8,10},{9,11},{10,... | collective-permute-start | bytes 1843208 | tf_op jit(solution)/shard_map/ppermute | solution.py:261
  664.7 13.2 %collective-permute-start.29 = (bf16[2,112,800]{1,2,0:T(8,128)(2,1)S(1)}, bf16[2,112,800]{1,2,0:T(8,128)(2,1)S(1)}, u32[]{:S(2)}, u32[]{:S(2)}) collective-permute-start(bf16[2,112,800]{1,2,0:T(8,128)(2,1)S(1)} %bitcast.244), channel_id=1, source_target_pairs={{0,2},{1,3},{2,0},{3,1},{4,6},{5,7},{6,4},{7,5},{8,10},{9,11},{10,... | collective-permute-start | bytes 1075208 | tf_op jit(solution)/shard_map/ppermute | solution.py:261
  677.9 24.9 %collective-permute-start.47 = (bf16[2,112,2560]{2,1,0:T(8,128)(2,1)S(1)}, bf16[2,112,2560]{2,1,0:T(8,128)(2,1)S(1)}, u32[]{:S(2)}, u32[]{:S(2)}) collective-permute-start(bf16[2,112,2560]{2,1,0:T(8,128)(2,1)S(1)} %dynamic-slice_bitcast_fusion.1), channel_id=1, source_target_pairs={{0,2},{1,3},{2,0},{3,1},{4,6},{5,7},{6,4},{7,5},{8,10},{9,11},{10,... | collective-permute-start | bytes 3440648 | tf_op jit(solution)/shard_map/ppermute | solution.py:261
  679.0 75.5 %collective-permute-start.54 = (bf16[2,320,480]{2,1,0:T(8,128)(2,1)S(1)}, bf16[2,320,480]{2,1,0:T(8,128)(2,1)S(1)}, u32[]{:S(2)}, u32[]{:S(2)}) collective-permute-start(bf16[2,320,480]{2,1,0:T(8,128)(2,1)S(1)} %bitcast.240), channel_id=1, source_target_pairs={{0,1},{1,0},{2,3},{3,2},{4,5},{5,4},{6,7},{7,6},{8,9},{9,8},{10,11... | collective-permute-start | bytes 1843208 | tf_op jit(solution)/shard_map/ppermute | solution.py:258
  680.1 44.8 %collective-permute-start.45 = (bf16[2,128,2560]{2,1,0:T(8,128)(2,1)S(1)}, bf16[2,128,2560]{2,1,0:T(8,128)(2,1)S(1)}, u32[]{:S(2)}, u32[]{:S(2)}) collective-permute-start(bf16[2,128,2560]{2,1,0:T(8,128)(2,1)S(1)} %dynamic-slice_bitcast_fusion), channel_id=1, source_target_pairs={{0,1},{1,0},{2,3},{3,2},{4,5},{5,4},{6,7},{7,6},{8,9},{9,8},{10,11... | collective-permute-start | bytes 3932168 | tf_op jit(solution)/shard_map/ppermute | solution.py:258
  702.8 57.9 %collective-permute-start.30 = (bf16[112,800]{0,1:T(8,128)(2,1)S(1)}, bf16[112,800]{0,1:T(8,128)(2,1)S(1)}, u32[]{:S(2)}, u32[]{:S(2)}) collective-permute-start(bf16[112,800]{0,1:T(8,128)(2,1)S(1)} %dynamic-slice_bitcast_fusion.8), channel_id=1, source_target_pairs={{0,1},{1,0},{2,3},{3,2},{4,5},{5,4},{6,7},{7,6},{8,9},{9,8},{10,11... | collective-permute-start | bytes 537608 | tf_op jit(solution)/shard_map/ppermute | solution.py:258
  724.8 13.4 %collective-permute-start.48 = (bf16[112,2560]{1,0:T(8,128)(2,1)S(1)}, bf16[112,2560]{1,0:T(8,128)(2,1)S(1)}, u32[]{:S(2)}, u32[]{:S(2)}) collective-permute-start(bf16[112,2560]{1,0:T(8,128)(2,1)S(1)} %dynamic-slice_bitcast_fusion.3), channel_id=1, source_target_pairs={{0,1},{1,0},{2,3},{3,2},{4,5},{5,4},{6,7},{7,6},{8,9},{9,8},{10,11... | collective-permute-start | bytes 1720328 | tf_op jit(solution)/shard_map/ppermute | solution.py:258
  738.3 14.9 %collective-permute-start.46 = (bf16[128,2560]{1,0:T(8,128)(2,1)S(1)}, bf16[128,2560]{1,0:T(8,128)(2,1)S(1)}, u32[]{:S(2)}, u32[]{:S(2)}) collective-permute-start(bf16[128,2560]{1,0:T(8,128)(2,1)S(1)} %dynamic-slice_bitcast_fusion.2), channel_id=1, source_target_pairs={{0,2},{1,3},{2,0},{3,1},{4,6},{5,7},{6,4},{7,5},{8,10},{9,11},{10,... | collective-permute-start | bytes 1966088 | tf_op jit(solution)/shard_map/ppermute | solution.py:261
  754.5 33.3 %collective-permute-start.49 = (bf16[240,2560]{1,0:T(8,128)(2,1)S(1)}, bf16[240,2560]{1,0:T(8,128)(2,1)S(1)}, u32[]{:S(2)}, u32[]{:S(2)}) collective-permute-start(bf16[240,2560]{1,0:T(8,128)(2,1)S(1)} %pad_maximum_fusion.19), channel_id=1, source_target_pairs={{0,8},{4,12},{24,16},{28,20},{1,9},{5,13},{25,17},{29,21},{2,10},{... | collective-permute-start | bytes 3686408 | tf_op jit(solution)/shard_map/ppermute | solution.py:300
  761.9 27.9 %collective-permute-start.55 = (bf16[320,480]{1,0:T(8,128)(2,1)S(1)}, bf16[320,480]{1,0:T(8,128)(2,1)S(1)}, u32[]{:S(2)}, u32[]{:S(2)}) collective-permute-start(bf16[320,480]{1,0:T(8,128)(2,1)S(1)} %dynamic-slice_bitcast_fusion.5), channel_id=1, source_target_pairs={{0,2},{1,3},{2,0},{3,1},{4,6},{5,7},{6,4},{7,5},{8,10},{9,11},{10,... | collective-permute-start | bytes 921608 | tf_op jit(solution)/shard_map/ppermute | solution.py:261
  767.8 32.2 %collective-permute-start.31 = (bf16[240,800]{0,1:T(8,128)(2,1)}, bf16[240,800]{0,1:T(8,128)(2,1)}, u32[]{:S(2)}, u32[]{:S(2)}) collective-permute-start(bf16[240,800]{0,1:T(8,128)(2,1)} %pad_maximum_fusion.26), channel_id=1, source_target_pairs={{0,8},{4,12},{24,16},{28,20},{1,9},{5,13},{25,17},{29,21},{2,10},{... | collective-permute-start | bytes 1152008 | tf_op jit(solution)/shard_map/ppermute | solution.py:300
  788.1 17.2 %collective-permute-start.50 = (bf16[240,2560]{1,0:T(8,128)(2,1)S(1)}, bf16[240,2560]{1,0:T(8,128)(2,1)}, u32[]{:S(2)}, u32[]{:S(2)}) collective-permute-start(bf16[240,2560]{1,0:T(8,128)(2,1)S(1)} %add_convert_fusion.4), channel_id=1, source_target_pairs={{8,16},{12,20},{16,8},{20,12},{9,17},{13,21},{17,9},{21,13},{10,18... | collective-permute-start | bytes 3686408 | tf_op jit(solution)/shard_map/ppermute | solution.py:300
  791.0 12.6 %collective-permute-start.58 = (bf16[640,480]{0,1:T(8,128)(2,1)}, bf16[640,480]{0,1:T(8,128)(2,1)S(1)}, u32[]{:S(2)}, u32[]{:S(2)}) collective-permute-start(bf16[640,480]{0,1:T(8,128)(2,1)} %copy.144), channel_id=1, source_target_pairs={{0,8},{4,12},{24,16},{28,20},{1,9},{5,13},{25,17},{29,21},{2,10},{... | collective-permute-start | bytes 1843208 | tf_op jit(solution)/shard_map/ppermute | solution.py:300
  807.9 51.5 %collective-permute-start.51 = (bf16[240,2560]{1,0:T(8,128)(2,1)}, bf16[240,2560]{1,0:T(8,128)(2,1)}, u32[]{:S(2)}, u32[]{:S(2)}) collective-permute-start(bf16[240,2560]{1,0:T(8,128)(2,1)} %add_convert_fusion.3), channel_id=1, source_target_pairs={{8,0},{12,4},{16,24},{20,28},{9,1},{13,5},{17,25},{21,29},{10,2},{... | collective-permute-start | bytes 3686408 | tf_op jit(solution)/shard_map/ppermute | solution.py:300
  810.5 42.1 %collective-permute-start.33 = (bf16[240,800]{0,1:T(8,128)(2,1)S(1)}, bf16[240,800]{0,1:T(8,128)(2,1)}, u32[]{:S(2)}, u32[]{:S(2)}) collective-permute-start(bf16[240,800]{0,1:T(8,128)(2,1)S(1)} %add_convert_fusion.14), channel_id=1, source_target_pairs={{8,0},{12,4},{16,24},{20,28},{9,1},{13,5},{17,25},{21,29},{10,2},{... | collective-permute-start | bytes 1152008 | tf_op jit(solution)/shard_map/ppermute | solution.py:300
  812.6 46.5 %collective-permute-start.60 = (bf16[640,480]{0,1:T(8,128)(2,1)S(1)}, bf16[640,480]{0,1:T(8,128)(2,1)S(1)}, u32[]{:S(2)}, u32[]{:S(2)}) collective-permute-start(bf16[640,480]{0,1:T(8,128)(2,1)S(1)} %copy.148), channel_id=1, source_target_pairs={{8,0},{12,4},{16,24},{20,28},{9,1},{13,5},{17,25},{21,29},{10,2},{... | collective-permute-start | bytes 1843208 | tf_op jit(solution)/shard_map/ppermute | solution.py:300
  (223 other events, 1409.8 us)
Sparse Core Ops, SparseCore 0:
  13.3 42.4 all-gather.8
  58.2 65.0 all-gather.4
  125.7 39.6 all-gather.6

commit v2 on v1

--- a/solution.py
+++ b/solution.py
@@ -247,6 +247,172 @@
     )(q, do, att, *kvs, lse, row_info, col_info, cos, sin)
 
 
+def qkv_back_kernel(
+    dq_ref, mine_ref, got_ref, wq_ref, wkv_ref, x_ref, gain_ref, up_ref, ck_ref, sk_ref, dkv_ref, out_ref, gain_grad_ref
+):
+    cos, sin = ck_ref[...], sk_ref[...]
+    for at in range(0, dkv_ref.shape[1], LANES):
+        cols = slice(at, at + LANES)
+        u = mine_ref[:, cols].astype(F32) + got_ref[:, cols].astype(F32)
+        dkv_ref[:, cols] = (u * cos - turn(u) * sin).astype(BF16)
+    g = dotf(dq_ref[...], wq_ref[...], NT) + dotf(dkv_ref[...], wkv_ref[...], NT)
+    x = x_ref[...]
+    factor = lax.rsqrt(jnp.mean(x * x, axis=-1, keepdims=True) + NORM_EPSILON)
+    unit = x * factor
+    gain_grad_ref[...] = jnp.sum(g * unit, axis=0, keepdims=True)
+    scaled = g * gain_ref[...]
+    out_ref[...] = up_ref[...] + factor * (scaled - unit * jnp.mean(scaled * unit, axis=-1, keepdims=True))
+
+
+def qkv_back_call(dq, mine, got, wq, wkv, x, gain, upstream, cos, sin):
+    rows, width = x.shape
+    heads, both = wq.shape[1], wkv.shape[1]
+    return pl.pallas_call(
+        qkv_back_kernel,
+        grid=(1,),
+        in_specs=[
+            whole(rows, heads),
+            whole(rows, both),
+            whole(rows, both),
+            whole(width, heads),
+            whole(width, both),
+            whole(rows, width),
+            whole(1, width),
+            whole(rows, width),
+            whole(rows, LANES),
+            whole(rows, LANES),
+        ],
+        out_specs=[whole(rows, both), whole(rows, width), whole(1, width)],
+        out_shape=[
+            jax.ShapeDtypeStruct((rows, both), BF16),
+            jax.ShapeDtypeStruct((rows, width), F32),
+            jax.ShapeDtypeStruct((1, width), F32),
+        ],
+        compiler_params=pltpu.CompilerParams(vmem_limit_bytes=32 * MIB),
+        cost_estimate=pl.CostEstimate(
+            flops=2 * rows * width * (heads + both),
+            bytes_accessed=2 * width * (heads + both) + 16 * rows * width,
+            transcendentals=0,
+        ),
+        name="qkv_back",
+    )(dq, mine, got, wq, wkv, x, gain, upstream, cos, sin)
+
+
+def weight_grad_kernel(fill, counts, stride, spot_ref, *refs):
+    c = pl.program_id(0)
+    n_left, n_right, n_extra, levels = counts
+    sources, refs = refs[: n_left * levels], refs[n_left * levels :]
+    rights, refs = refs[: n_right * levels], refs[n_right * levels :]
+    extra, outs, scratch = refs[:n_extra], refs[n_extra : n_extra + 5], refs[n_extra + 5 :]
+    staged, turned, values, sem = scratch[:n_left], scratch[n_left : 2 * n_left], scratch[-3:-1], scratch[-1]
+
+    @pl.when(c == 0)
+    def _():
+        copies = []
+        for i, source in enumerate(sources):
+            rows = source.shape[0]
+            target = staged[i // levels].at[pl.ds(i % levels * rows, rows), :]
+            copies.append(pltpu.make_async_copy(source, target, sem.at[i]))
+            copies[-1].start()
+        for i, copy in enumerate(copies):
+            copy.wait()
+            if i % levels == levels - 1:
+                turned[i // levels][...] = staged[i // levels][...].T
+
+    def product(left, right):
+        stacked = jnp.concatenate([a[...] for a in rights[right * levels : (right + 1) * levels]], axis=0)
+        return dotf(turned[left][...], stacked)
+
+    core = spot_ref[1]
+    fill(core, c, product, values, extra)
+    each, cut = outs[4].shape[1], outs[0].shape[1]
+    kept, away = values
+    for r in range(4):
+        mine = other = pl.multiple_of((spot_ref[0] ^ r) * stride, 16)
+        source = away
+        if stride != each:
+            other = pl.multiple_of(mine + (1 - core) * each, 16)
+            mine = pl.multiple_of(mine + core * each, 16)
+            source = kept
+        outs[r % 2][r // 2] = kept[pl.ds(mine, cut), :]
+        outs[2 + r // 2][r % 2] = kept[pl.ds(pl.multiple_of(mine + cut, 16), each - cut), :]
+        outs[4][r] = source[pl.ds(other, each), :]
+
+
+def fill_rows(core, c, product, values, extra):
+    values[0][...] = product(0, 0).astype(BF16)
+
+
+def fill_roles(core, c, product, values, extra):
+    for i, value in enumerate(values):
+        value[...] = product(0, i).astype(BF16)
+
+
+def fill_choice(core, c, product, values, extra):
+    kept, away = values
+    first, second = product(0, 0).astype(BF16), product(1, 1).astype(BF16)
+    kept[...] = jnp.where(core == 0, first, second)
+    away[...] = jnp.where(core == 0, second, first)
+
+
+def fill_groups(core, c, product, values, extra):
+    kept, away = values
+    v = product(0, 0)
+    part = kept.shape[1] - LANES
+    low, high = v[:, :part].astype(BF16), v[:, v.shape[1] - part :].astype(BF16)
+    kept[:, :part] = jnp.where(core == 0, low, high)
+    away[:, :part] = jnp.where(core == 0, high, low)
+    vectors = extra[0][...].T
+    rest = jnp.zeros((vectors.shape[0], LANES - vectors.shape[1]), F32)
+    vectors = jnp.concatenate([vectors, rest], axis=1).astype(BF16)
+    kept[:, part:] = vectors
+    away[:, part:] = vectors
+
+
+def weight_grad(spot, fill, lefts, rights, stride, each, n, step, extra=()):
+    levels, rows = len(lefts[0]), lefts[0][0].shape[0]
+    depth = levels * rows
+    cut = -(-each // 32) * 16
+    shapes = [(2, cut, n), (2, cut, n), (2, each - cut, n), (2, each - cut, n), (4, each, n)]
+    flops = 2 * depth * 4 * stride * sum(right[0].shape[1] for right in rights)
+    sources, moving = [a for group in lefts for a in group], [a for group in rights for a in group]
+    by_step = pl.BlockSpec((rows, step), lambda c, s: (0, c))
+    at_once = lambda a: pl.BlockSpec(a.shape, lambda c, s: (0, 0))
+    return pl.pallas_call(
+        functools.partial(weight_grad_kernel, fill, (len(lefts), len(rights), len(extra), levels), stride),
+        grid_spec=pltpu.PrefetchScalarGridSpec(
+            num_scalar_prefetch=1,
+            grid=(-(-n // step),),
+            in_specs=[pl.BlockSpec(memory_space=pl.ANY)] * len(sources)
+            + [by_step if n > step else at_once(a) for a in moving]
+            + [at_once(a) for a in extra],
+            out_specs=[pl.BlockSpec(s[:2] + (step,), lambda c, s: (0, 0, c)) for s in shapes],
+            scratch_shapes=[pltpu.VMEM((depth, group[0].shape[1]), BF16) for group in lefts]
+            + [pltpu.VMEM((group[0].shape[1], depth), BF16) for group in lefts]
+            + [pltpu.VMEM((4 * stride, step), BF16)] * 2
+            + [pltpu.SemaphoreType.DMA((len(sources),))],
+        ),
+        out_shape=[jax.ShapeDtypeStruct(s, BF16) for s in shapes],
+        compiler_params=pltpu.CompilerParams(vmem_limit_bytes=60 * MIB),
+        cost_estimate=pl.CostEstimate(
+            flops=flops, bytes_accessed=2 * sum(a.size for a in sources + moving) + 16 * each * n, transcendentals=0
+        ),
+        name="weight_grad",
+    )(spot, *sources, *moving, *extra)
+
+
+def tie(*trees):
+    return lax.optimization_barrier(trees)
+
+
+def add(*terms):
+    return sum(a.astype(F32) for a in terms).astype(BF16)
+
+
+def at(a, index, axis):
+    return lax.dynamic_index_in_dim(a, index, axis, keepdims=False)
+
+
 class Place:
     def __init__(self, dp, cp):
         self.dp, self.cp, self.square = dp, cp, cp == 4
@@ -279,56 +445,160 @@
         own = 2 * self.core + self.x
         return [own ^ k for k in range(4)], own
 
-    def gather_keys(self, a):
-        if not self.square:
-            return (lax.all_gather(a, "cp", axis=0, tiled=True),)
+    def gather_keys(self, a, axis=0):
+        if not self.square:
+            return (lax.all_gather(a, "cp", axis=axis, tiled=True),)
         from_x, from_core = self.over_x(a), self.over_core(a)
         return a, from_x, from_core, self.over_core(from_x)
 
-    def scatter_keys(self, a):
-        if not self.square:
-            return lax.psum_scatter(a, "cp", scatter_dimension=0, tiled=True).astype(F32)
+    def scatter_keys_first(self, a):
+        if not self.square:
+            own = lax.psum_scatter(a, "cp", scatter_dimension=0, tiled=True)
+            return own, jnp.zeros_like(own)
         rows = a.shape[0] // 4
-        got = self.over_core(a[2 * rows :])
-        pair = (a[: 2 * rows].astype(F32) + got.astype(F32)).astype(BF16)
-        return pair[:rows].astype(F32) + self.over_x(pair[rows:]).astype(F32)
-
-    def sum_z(self, a):
+        return a[: 2 * rows], self.over_core(a[2 * rows :])
+
+    def scatter_keys_second(self, pair):
+        if not self.square:
+            return pair
+        rows = pair[0].shape[0] // 2
+        pair = add(*pair)
+        return pair[:rows], self.over_x(pair[rows:])
+
+
+    def gather_first(self, a):
+        if not self.square:
+            return (lax.all_gather(a, "cp", axis=0, tiled=True),)
+        cut = -(-a.shape[0] // 32) * 16
+        top, low = a[:cut], a[cut:]
+        return top, low, self.over_x(top), self.over_y(low)
+
+    def pair_up(self, spot, mine, got, axis=0):
+        return jnp.where(spot == 0, jnp.stack([mine, got], axis), jnp.stack([got, mine], axis))
+
+    def gather_pairs(self, parts):
+        if not self.square:
+            return parts
+        top, low, from_x, from_y = parts
+        return self.pair_up(self.x, top, from_x), self.pair_up(self.y, low, from_y)
+
+    def gather_second(self, pairs):
+        if not self.square:
+            return pairs
+        top, low = pairs
+        return top, low, self.over_y(top), self.over_x(low)
+
+    def gather_whole(self, parts):
+        if not self.square:
+            return parts[0]
+        top, low, from_y, from_x = parts
+        a = jnp.concatenate([self.pair_up(self.y, top, from_y), self.pair_up(self.x, low, from_x, 1)], axis=2)
+        return a.reshape(-1, a.shape[-1])
+
+
+    def halves(self, fill, lefts, rights, stride, each, n, step, extra=()):
+        if self.square:
+            spot = jnp.stack([lax.axis_index("cp"), self.core]).astype(jnp.int32)
+            return weight_grad(spot, fill, lefts, rights, stride, each, n, step, extra)
+        products = []
+
+        def product(left, right):
+            a, b = (jnp.concatenate(group, axis=0) for group in (lefts[left], rights[right]))
+            return dotf(a, b, TN).astype(BF16)
+
+        if fill is fill_rows:
+            both = product(0, 0).reshape(self.cp, 2, each, n)
+            products = at(both, self.core, 1), at(both, 1 - self.core, 1)
+        elif fill is fill_roles:
+            products = product(0, 0), product(0, 1)
+        elif fill is fill_choice:
+            first, second = product(0, 0), product(1, 1)
+            products = self.pick(first, second), self.pick(second, first)
+        else:
+            kv, part = product(0, 0), n - LANES
+            low, high = kv[:, :part], kv[:, kv.shape[1] - part :]
+            vectors = jnp.pad(extra[0].T, ((0, 0), (0, LANES - extra[0].shape[0]))).astype(BF16)
+            products = [jnp.concatenate([self.pick(*pair), vectors], axis=1) for pair in ((low, high), (high, low))]
+        return [a.reshape(self.cp, each, n) for a in products]
+
+    def scatter_ready(self, pieces, got, apart=False):
+        if not self.square:
+            return (add(pieces[0], got),)
+        top, top_out, low, low_out = pieces[:4]
+        got = got.reshape((2, 2) + got.shape[1:])
+        cut = top.shape[1]
+        if apart:
+            over_x = [add(top_out[i], got[i, 1, :cut]) for i in range(2)]
+            over_y = [add(low_out[i], got[1, i, cut:]) for i in range(2)]
+            return top, low, got, over_x, over_y
+        return top, low, got, add(top_out, got[:, 1, :cut]), add(low_out, got[1, :, cut:])
+
+    def scatter_first(self, parts):
+        if not self.square:
+            return (lax.psum_scatter(parts[0], "cp", scatter_dimension=0, tiled=False),)
+        return parts[:3] + (self.over_x(parts[3]), self.over_y(parts[4]))
+
+    def scatter_open(self, parts):
+        if not self.square:
+            return self.scatter_first(parts)
+        return parts + ([self.over_x(parts[3][1])], [self.over_y(parts[4][1])])
+
+    def scatter_more(self, parts):
+        if not self.square:
+            return parts
+        over_x, over_y, from_x, from_y = parts[3:]
+        return parts[:3] + ([self.over_x(over_x[0])] + from_x, [self.over_y(over_y[0])] + from_y)
+
+    def scatter_second(self, parts):
+        if not self.square:
+            return parts
+        top, low, got, from_x, from_y = parts
+        cut = top.shape[1]
+        top_out = add(top[1], got[1, 0, :cut], from_x[1])
+        low_out = add(low[1], got[0, 1, cut:], from_y[1])
+        return parts + (self.over_y(top_out), self.over_x(low_out))
+
+    def scatter_rows(self, parts):
+        if not self.square:
+            half = parts[0].shape[0] // 2
+            return parts[0][:half], parts[0][half:]
+        top, low, got, from_x, from_y, last_y, last_x = parts
+        cut = top.shape[1]
+        return add(top[0], got[0, 0, :cut], from_x[0], last_y), add(low[0], got[0, 0, cut:], from_y[0], last_x)
+
+    def scatter_whole(self, parts):
+        return jnp.concatenate(self.scatter_rows(parts), axis=0)
+
+
+    def hop(self, a, moves):
+        return lax.ppermute(a, "dp", [(2 * s + c, 2 * t + c) for s, t in moves for c in range(2)])
+
+    def z_first(self, a):
+        n, got = self.dp // 2, jnp.zeros_like(a)
+        for t in range(n // 2 - 1):
+            if t:
+                a = add(a, got)
+            got = self.hop(a, [(t, t + 1), (n - 1 - t, n - 2 - t)])
+        return a, got
+
+    def z_second(self, pair):
+        n, a = self.dp // 2, add(*pair)
+        return a, self.hop(a, [(n // 2 - 1, n // 2), (n // 2, n // 2 - 1)])
+
+    def z_third(self, pair):
+        n, a = self.dp // 2, add(*pair)
+        back = a
+        for t in reversed(range(n // 2 - 1)):
+            if t < n // 2 - 2:
+                a = jnp.where((self.z == t + 1) | (self.z == n - 2 - t), back, a)
+            back = self.hop(a, [(t + 1, t), (n - 2 - t, n - 1 - t)])
+        return a, back
+
+    def z_whole(self, pair):
         n = self.dp // 2
-
-        def hop(b, moves):
-            return lax.ppermute(b, "dp", [(2 * s + c, 2 * t + c) for s, t in moves for c in range(2)])
-
-        def add(b, c):
-            return (b.astype(F32) + c.astype(F32)).astype(BF16)
-
-        if n == 1:
-            return a
-        half = n // 2
-        for t in range(half - 1):
-            a = add(a, hop(a, [(t, t + 1), (n - 1 - t, n - 2 - t)]))
-        a = add(a, hop(a, [(half - 1, half), (half, half - 1)]))
-        for t in reversed(range(half - 1)):
-            back = hop(a, [(t + 1, t), (n - 2 - t, n - 1 - t)])
-            a = jnp.where((self.z == t) | (self.z == n - 1 - t), back, a)
-        return a
-
-    def scatter_sum(self, blocks, cut):
-        _, rows, width = blocks.shape
-        if not self.square:
-            return lax.psum_scatter(blocks, "cp", scatter_dimension=0, tiled=False)
-
-        def step(b, at, axis, over):
-            away = lax.dynamic_index_in_dim(b, 1 - at, axis, keepdims=False)
-            kept = lax.dynamic_index_in_dim(b, at, axis, keepdims=False)
-            return (kept.astype(F32) + over(away).astype(F32)).astype(BF16)
-
-        blocks = blocks.reshape(2, 2, rows, width)
-        first = step(blocks[:, :, :cut], self.x, 1, self.over_x)
-        second = step(blocks[:, :, cut:], self.y, 0, self.over_y)
-        first = step(first, self.y, 0, self.over_y)
-        second = step(second, self.x, 0, self.over_x)
-        return jnp.concatenate([first, second], axis=0)
+        if n < 4:
+            return pair[0]
+        return jnp.where((self.z == 0) | (self.z == n - 1), pair[1], pair[0])
 
     def pick(self, a, b):
         return jnp.where(self.core == 0, a, b)
@@ -343,7 +613,7 @@
     unit = matrix * factor
     scaled = upstream * gain
     grad = factor * (scaled - unit * jnp.mean(scaled * unit, axis=-1, keepdims=True))
-    return grad, jnp.sum(upstream * unit, axis=0)
+    return grad, jnp.sum(upstream * unit, axis=0, keepdims=True)
 
 
 def rope_tables(places):
@@ -357,162 +627,240 @@
     return both(cos, cos), both(sin, sin), both(cos, one), both(sin, zero)
 
 
-def gather_weights(place, shards):
-    wq, wk, wv, wo, gate, up, down, router, gain_a, gain_f = shards
-    rows, kv_heads = wk.shape[0], wk.shape[1] // HEAD_DIM
-    gather = lambda a: lax.all_gather(a, "cp", axis=0, tiled=True)
-    wkv = jnp.stack([wk.reshape(rows, kv_heads, HEAD_DIM), wv.reshape(rows, kv_heads, HEAD_DIM)], axis=2)
-    wkv = wkv.reshape(rows, 2 * kv_heads * HEAD_DIM)
-    both, width = wkv.shape[1], wq.shape[1]
-    small = jnp.concatenate([gain_a[:, None], gain_f[:, None], router.T], axis=1)
-    total = jnp.concatenate([wkv, wq, wo], axis=1)
-    half = total.shape[1] // 2
-    mine = gather(jnp.concatenate([place.pick(total[:, :half], total[:, half:]), small], axis=1))
-    theirs = place.over_core(mine)
-    total = jnp.concatenate([place.pick(mine, theirs)[:, :half], place.pick(theirs, mine)[:, :half]], axis=1)
-    small = mine[:, half:]
-    wkv, wq, wo = total[:, :both], total[:, both : both + width], total[:, both + width :]
-    mine = gather(place.pick(gate, up))
-    theirs = place.over_core(mine)
-    gate, up = place.pick(mine, theirs), place.pick(theirs, mine)
-    each, wide = down.shape
-    mine = gather(place.pick(down[: each // 2], down[each // 2 :]))
-    theirs = place.over_core(mine)
-    down = jnp.stack(
-        [
-            place.pick(mine, theirs).reshape(place.cp, each // 2, wide),
-            place.pick(theirs, mine).reshape(place.cp, each // 2, wide),
-        ],
-        axis=1,
-    ).reshape(place.cp * each, wide)
-    return wkv, wq, wo, gate, up, down, small
-
-
-def forward_level(state, weights, recursion, context):
-    wkv, wq, wo, gate_w, up_w, down_w, small = weights
-    place, tables, row_info, col_info, depth = context
-    gain_a, gain_f = small[:, 0].astype(F32), small[:, 1].astype(F32)
-    q, kv, normed = qkv_call(state, gain_a[None, :], wq, wkv, tables)
-    kvs = place.gather_keys(kv)
-    att, lse = attend_call(recursion, q, kvs, row_info, col_info)
-    attn = dotf(att, wo)
-    after = state + attn
-    normed2 = (after * inverse_rms(after) * gain_f).astype(BF16)
-    gate = dotf(normed2, gate_w)
-    up = dotf(normed2, up_w)
-    inner = (jax.nn.silu(gate) * up).astype(BF16)
-    branch = attn + dotf(inner, down_w)
-    router_row = small[:, 2 + recursion].astype(F32)
-    router = jax.nn.sigmoid(jnp.sum(state * router_row, axis=-1, keepdims=True))
-    active = (depth[:, None] > recursion).astype(F32)
-    following = state + active * router * branch
-    saved = (state, normed, q, kvs, lse, att, after, normed2, gate.astype(BF16), up.astype(BF16), inner, branch, router_row, router, active)
-    return following, saved
-
-
-def backward_level(saved, weights, recursion, context, grad):
-    wkv, wq, wo, gate_w, up_w, down_w, small = weights
-    place, tables, row_info, col_info, _ = context
-    cos_q, sin_q, cos_k, sin_k = tables
-    gain_a, gain_f = small[:, 0].astype(F32), small[:, 1].astype(F32)
-    state, normed, q, kvs, lse, att, after, normed2, gate, up, inner, branch, router_row, router, active = saved
-    rows = state.shape[0]
-    g_branch = grad * (active * router)
-    g_logit = jnp.sum(grad * branch, axis=-1, keepdims=True) * active * router * (1.0 - router)
-    g_router = jnp.sum(g_logit * state, axis=0)
-    g_state = grad + g_logit * router_row
-    g_ffn = g_branch.astype(BF16)
-    g_inner = dotf(g_ffn, down_w, NT)
-    gate, up = gate.astype(F32), up.astype(F32)
-    sig = jax.nn.sigmoid(gate)
-    g_gate = (g_inner * up * sig * (1.0 + gate * (1.0 - sig))).astype(BF16)
-    g_up = (g_inner * gate * sig).astype(BF16)
-    g_normed2 = dotf(g_gate, gate_w, NT) + dotf(g_up, up_w, NT)
-    g_after, g_gain_f = norm_back(after, gain_f, g_normed2)
-    g_state = g_state + g_after
-    g_attn = (g_after + g_branch).astype(BF16)
-    g_att = dotf(g_attn, wo, NT).astype(BF16)
-    dq, dkv = attend_back_call(recursion, q, g_att, att, kvs, lse, row_info, col_info, cos_q, sin_q)
-    dkv = place.scatter_keys(dkv)
-    parts = dkv.reshape(rows, -1, 2, 2, HEAD_DIM // 2)
-    swapped = parts[:, :, :, ::-1, :].reshape(rows, -1)
-    spread = lambda t: jnp.tile(t, (1, dkv.shape[1] // LANES))
-    dkv = (dkv * spread(cos_k) - swapped * spread(sin_k)).astype(BF16)
-    g_normed = dotf(dq, wq, NT) + dotf(dkv, wkv, NT)
-    g_rows, g_gain_a = norm_back(state, gain_a, g_normed)
-    g_state = g_state + g_rows
-    return g_state, (g_ffn, inner), (g_gate, g_up, normed2), (g_attn, att), (dq, dkv, normed), (g_router, g_gain_a, g_gain_f)
+class Level:
+    def __init__(self, recursion, place, context):
+        self.recursion, self.place = recursion, place
+        self.tables, self.row_info, self.col_info, self.depth = context
+
+    def project(self, state, w):
+        self.state = state
+        self.q, self.kv, self.normed = qkv_call(state, w["gain_a"], w["q"], w["kv"], self.tables)
+
+    def attend(self, kvs, w):
+        self.kvs = kvs
+        self.att, self.lse = attend_call(self.recursion, self.q, kvs, self.row_info, self.col_info)
+        self.attn = dotf(self.att, w["o"])
+        self.after = self.state + self.attn
+        self.normed2 = (self.after * inverse_rms(self.after) * w["gain_f"]).astype(BF16)
+
+    def expand(self, w):
+        mine, theirs = dotf(self.normed2, w["mine"]), dotf(self.normed2, w["theirs"])
+        gate, up = self.place.pick(mine, theirs), self.place.pick(theirs, mine)
+        self.inner = (jax.nn.silu(gate) * up).astype(BF16)
+        self.gate, self.up = gate.astype(BF16), up.astype(BF16)
+
+    def close(self, w):
+        self.branch = self.attn + dotf(self.inner, w["down"])
+        self.router_row = w["router"][self.recursion]
+        self.router = jax.nn.sigmoid(jnp.sum(self.state * self.router_row, axis=-1, keepdims=True))
+        self.active = (self.depth[:, None] > self.recursion).astype(F32)
+        return self.state + self.active * self.router * self.branch
+
+    def back_open(self, grad):
+        self.g_branch = grad * (self.active * self.router)
+        g_logit = jnp.sum(grad * self.branch, axis=-1, keepdims=True)
+        g_logit = g_logit * self.active * self.router * (1.0 - self.router)
+        self.g_router = jnp.sum(g_logit * self.state, axis=0, keepdims=True)
+        self.g_state = grad + g_logit * self.router_row
+        self.g_ffn = self.g_branch.astype(BF16)
+
+    def back_expand(self, w):
+        g_inner = dotf(self.g_ffn, w["down"], NT)
+        gate, up = self.gate.astype(F32), self.up.astype(F32)
+        sig = jax.nn.sigmoid(gate)
+        g_gate = (g_inner * up * sig * (1.0 + gate * (1.0 - sig))).astype(BF16)
+        g_up = (g_inner * gate * sig).astype(BF16)
+        self.g_mine, self.g_theirs = self.place.pick(g_gate, g_up), self.place.pick(g_up, g_gate)
+
+    def back_norm(self, w):
+        g_normed2 = dotf(self.g_mine, w["mine"], NT) + dotf(self.g_theirs, w["theirs"], NT)
+        g_after, self.g_gain_f = norm_back(self.after, w["gain_f"], g_normed2)
+        self.g_state = self.g_state + g_after
+        self.g_attn = (g_after + self.g_branch).astype(BF16)
+        self.g_att = dotf(self.g_attn, w["o"], NT).astype(BF16)
+
+    def back_attend(self):
+        cos, sin = self.tables[:2]
+        self.dq, dkv = attend_back_call(
+            self.recursion, self.q, self.g_att, self.att, self.kvs, self.lse, self.row_info, self.col_info, cos, sin
+        )
+        return dkv
+
+    def back_project(self, mine, got, w):
+        cos, sin = self.tables[2:]
+        self.dkv, grad, self.g_gain_a = qkv_back_call(
+            self.dq, mine, got, w["q"], w["kv"], self.state, w["gain_a"], self.g_state, cos, sin
+        )
+        return grad
 
 
 def local(tokens, recur_depth, document_ids, cotangent, *shards, dp, cp):
     place = Place(dp, cp)
-    rows = tokens.shape[1]
-    ids = jnp.stack([document_ids[0], recur_depth[0]])
-    ids = place.move_tokens(ids)
-    state = place.move_tokens(tokens[0]).astype(F32)
-    grad = place.move_tokens(cotangent[0]).astype(F32)
+    wq, wk, wv, wo, gate, up, down, router, gain_a, gain_f = shards
+    rows, each = tokens.shape[1], wq.shape[0]
+    width, kv_heads = each * cp, wk.shape[1] // HEAD_DIM
+
+    wkv = jnp.stack([wk.reshape(each, kv_heads, HEAD_DIM), wv.reshape(each, kv_heads, HEAD_DIM)], axis=2)
+    wkv = wkv.reshape(each, -1)
+    small = jnp.concatenate([gain_a[:, None], gain_f[:, None], router.T], axis=1)
+    blend = jnp.concatenate([wkv, wq, wo], axis=1)
+    half, both = blend.shape[1] // 2, wkv.shape[1]
+    blend = jnp.concatenate([place.pick(blend[:, :half], blend[:, half:]), small], axis=1)
+    part = place.gather_first(blend)
+    ids = place.move_tokens(jnp.stack([document_ids[0], recur_depth[0]]))
+    state = place.move_tokens(tokens[0])
+    gates = place.pick(gate, up)
+    downs = place.pick(down[: down.shape[0] // 2], down[down.shape[0] // 2 :])
+    part, ids, state, gates, downs = tie(part, ids, state, gates, downs)
+
+    part = place.gather_second(place.gather_pairs(part))
     steps = jnp.arange(rows, dtype=jnp.int32)
     blocks, block = place.key_blocks()
-    every = jnp.concatenate(place.gather_keys(ids.T), axis=0)
+    every = jnp.concatenate(place.gather_keys(ids, 1), axis=1)
     spots = jnp.concatenate([b * rows + steps for b in blocks])
-    col_info = jnp.stack([every[:, 0], spots, every[:, 1]])
+    col_info = jnp.stack([every[0], spots, every[1]])
     row_info = jnp.stack([ids[0], block * rows + steps], axis=1)
     tables = rope_tables(row_info[:, 1])
-    context = (place, tables, row_info, col_info, ids[1])
-    weights = gather_weights(place, shards)
-    saved = []
-    for recursion in range(RECUR):
-        state, kept = forward_level(state, weights, recursion, context)
-        saved.append(kept)
+    context = (tables, row_info, col_info, ids[1])
+    part, context, state, gates = tie(part, context, state.astype(F32), gates)
+
+    g_part = place.gather_first(gates)
+    mine = place.gather_whole(part)
+    theirs = place.over_core(mine)
+    w = {"gain_a": mine[:, half][None, :].astype(F32), "gain_f": mine[:, half + 1][None, :].astype(F32)}
+    w["router"] = mine[:, half + 2 :].T.astype(F32)
+    blend = jnp.concatenate([place.pick(mine, theirs)[:, :half], place.pick(theirs, mine)[:, :half]], axis=1)
+    w["kv"], w["q"], w["o"] = blend[:, :both], blend[:, both : both + width], blend[:, both + width :]
+    levels = [Level(r, place, context) for r in range(RECUR)]
+    first = levels[0]
+    first.project(state, w)
+    g_part = place.gather_pairs(g_part)
+    first.kv, g_part, downs = tie(first.kv, g_part, downs)
+
+    kvs = place.gather_keys(first.kv)
+    kvs, g_part, downs = tie(kvs, g_part, downs)
+
+    g_part = place.gather_second(g_part)
+    d_part = place.gather_first(downs)
+    first.attend(kvs, w)
+    first.normed2, g_part, d_part = tie(first.normed2, g_part, d_part)
+
+    d_part = place.gather_second(place.gather_pairs(d_part))
+    w["mine"] = place.gather_whole(g_part)
+    w["theirs"] = place.over_core(w["mine"])
+    first.expand(w)
+    first.inner, d_part = tie(first.inner, d_part)
+
+    mine = place.gather_whole(d_part)
+    theirs = place.over_core(mine)
+    mine, theirs = (a.reshape(cp, -1, width) for a in (mine, theirs))
+    w["down"] = jnp.stack([place.pick(mine, theirs), place.pick(theirs, mine)], axis=1).reshape(-1, width)
+    state = first.close(w)
+
+    for level in levels[1:]:
+        level.project(state, w)
+        level.attend(place.gather_keys(level.kv), w)
+        level.expand(w)
+        state = level.close(w)
     activations = place.move_tokens(state.astype(BF16))[None]
-    downs, ups, outs, ins, smalls = [], [], [], [], []
-    for recursion in reversed(range(RECUR)):
-        grad, a, b, c, d, e = backward_level(saved[recursion], weights, recursion, context, grad)
-        for group, item in zip((downs, ups, outs, ins, smalls), (a, b, c, d, e)):
-            group.append(item)
+    grad = place.move_tokens(cotangent[0]).astype(F32)
+
+    for level in levels[:0:-1]:
+        level.back_open(grad)
+        level.back_expand(w)
+        level.back_norm(w)
+        pair = place.scatter_keys_second(place.scatter_keys_first(level.back_attend()))
+        grad = level.back_project(*pair, w)
+
+    every = lambda name: [getattr(level, name) for level in levels]
+    ff = gate.shape[1]
+    part = -(-both // (2 * LANES)) * LANES
+
+    grad, activations = tie(grad, activations)
+    first.back_open(grad)
+    d = place.halves(fill_rows, [every("inner")], [every("g_ffn")], ff // cp, ff // cp // 2, width, 512)
+    d_got = place.over_core(d[-1])
+    first.back_expand(w)
+    d = place.scatter_ready(d, d_got)
+    d, first.g_mine, first.g_theirs = tie(d, first.g_mine, first.g_theirs)
+
+    d = place.scatter_first(d)
+    u = place.halves(fill_roles, [every("normed2")], [every("g_mine"), every("g_theirs")], each, each, ff, 512)
+    d, u = tie(d, u)
+
+    u_got = place.over_core(u[-1])
+    d = place.scatter_second(d)
+    first.back_norm(w)
+    u = place.scatter_ready(u, u_got, True)
+    d, u, first.g_att = tie(d, u, first.g_att)
+
+    u = place.scatter_open(u)
+    d = place.z_first(place.scatter_whole(d))
+    dkv = first.back_attend()
+    u, d, dkv = tie(u, d, dkv)
+
+    u = place.scatter_more(u)
+    pair = place.scatter_keys_first(dkv)
+    (pair,) = tie(pair)
+    pair = place.scatter_keys_second(pair)
+    lefts, rights = [every("att"), every("normed")], [every("g_attn"), every("dq")]
+    p = place.halves(fill_choice, lefts, rights, each, each, width, 512)
+    u, pair, p = tie(u, pair, p)
+
+    u = place.scatter_second(u)
+    p_got = place.over_core(p[-1])
+    d = place.z_second(d)
+    grad = first.back_project(*pair, w)
+    vectors = every("g_router") + [sum(every("g_gain_a")), sum(every("g_gain_f"))]
+    vectors = jnp.concatenate(vectors + [jnp.zeros((8 - len(vectors), width), F32)], axis=0)
+    k = place.halves(fill_groups, [every("normed")], [every("dkv")], each, each, part + LANES, part + LANES, (vectors,))
+    p = place.scatter_ready(p, p_got)
+    u, d, p, k, grad = tie(u, d, p, k, grad)
+
+    p = place.scatter_first(p)
+    k_got = place.over_core(k[-1])
+    u, v = place.scatter_rows(u)
+    u = place.z_first(u)
+    k = place.scatter_ready(k, k_got)
+    u, v, p, k = tie(u, v, p, k)
+
+    p, k = place.scatter_second(p), place.scatter_first(k)
+    u, v = place.z_second(u), place.z_first(v)
+    u, v, p, k = tie(u, v, p, k)
+
+    k = place.scatter_second(k)
+    u, v = place.z_third(u), place.z_second(v)
+    a = place.z_first(jnp.concatenate([place.scatter_whole(k), place.scatter_whole(p)], axis=1))
+    u, v, a = tie(u, v, a)
+
+    a, v = place.z_second(a), place.z_third(v)
+    d = place.z_third(d)
     input_grad = place.move_tokens(grad.astype(BF16))[None]
-    column = lambda group, i: jnp.concatenate([item[i] for item in group], axis=0)
-    width = shards[0].shape[0] * cp
-
-    def reduce(left, away, kept):
-        got = place.over_core(dotf(left, away, TN).astype(BF16))
-        own = (dotf(left, kept, TN) + got.astype(F32)).astype(BF16)
-        own = own.reshape(cp, -1, own.shape[1])
-        cut = -(-own.shape[1] // 32) * 16
-        return place.sum_z(place.scatter_sum(own, cut))
-
-    def halves(right):
-        n = right.shape[1] // 2
-        return place.pick(right[:, n:], right[:, :n]), place.pick(right[:, :n], right[:, n:])
-
-    def finish(own):
-        other = place.over_core(own)
-        return place.pick(own, other).astype(F32), place.pick(other, own).astype(F32)
-
-    own_down = reduce(column(downs, 1), *halves(column(downs, 0)))
-    g_gate, g_up = column(ups, 0), column(ups, 1)
-    own_up = reduce(column(ups, 2), place.pick(g_up, g_gate), place.pick(g_gate, g_up))
-    own_out = reduce(column(outs, 1), *halves(column(outs, 0)))
-    own_in = reduce(column(ins, 2), *halves(jnp.concatenate([column(ins, 0), column(ins, 1)], axis=1)))
-    grad_down = jnp.concatenate(finish(own_down), axis=1)
-    grad_gate, grad_up = finish(own_up)
-    grad_out = jnp.concatenate(finish(own_out), axis=1)
-    grad_in = jnp.concatenate(finish(own_in), axis=1)
-    grad_query = grad_in[:, :width]
-    grad_kv = grad_in[:, width:].reshape(grad_in.shape[0], -1, 2, HEAD_DIM)
-    grad_key = grad_kv[:, :, 0].reshape(grad_in.shape[0], -1)
-    grad_value = grad_kv[:, :, 1].reshape(grad_in.shape[0], -1)
-    vectors = [smalls[RECUR - 1 - r][0] for r in range(RECUR)]
-    vectors += [sum(s[1] for s in smalls), sum(s[2] for s in smalls)]
-    vectors = lax.psum(jnp.stack(vectors), ("dp", "cp"))
-    vectors = lax.dynamic_slice_in_dim(vectors, lax.axis_index("cp") * (width // cp), width // cp, axis=1)
+    a, v, d, input_grad = tie(a, v, d, input_grad)
+
+    a = place.z_third(a)
+    d_own = place.z_whole(d)
+    d_other = place.over_core(d_own)
+    u_own = jnp.concatenate([place.z_whole(u), place.z_whole(v)], axis=0)
+    u_other = place.over_core(u_own)
+    grad_gate, grad_up = place.pick(u_own, u_other).astype(F32), place.pick(u_other, u_own).astype(F32)
+    d_own, d_other = (b.reshape(-1, width) for b in (d_own, d_other))
+    grad_down = jnp.concatenate([place.pick(d_own, d_other), place.pick(d_other, d_own)], axis=0).astype(F32)
+    a, grad_gate, grad_up, grad_down = tie(a, grad_gate, grad_up, grad_down)
+
+    own = place.z_whole(a)
+    other = place.over_core(own)
+    low, high = place.pick(own, other).astype(F32), place.pick(other, own).astype(F32)
+    grad_kv = jnp.concatenate([low[:, :part], high[:, 2 * part - both : part]], axis=1)
+    grad_kv = grad_kv.reshape(each, -1, 2, HEAD_DIM)
+    vectors = low[:, part : part + RECUR + 2].T
     return (
         activations,
         input_grad,
-        grad_query,
-        grad_key,
-        grad_value,
-        grad_out,
+        high[:, part + LANES :],
+        grad_kv[:, :, 0].reshape(each, -1),
+        grad_kv[:, :, 1].reshape(each, -1),
+        low[:, part + LANES :],
         grad_gate,
         grad_up,
         grad_down,

time: 889 us -> 646 us (0.73)
  waiting for transfers between devices: 320 us -> 175 us
  local copies, waits for them, and re-layouts: 136 us -> 67.6 us
  Pallas kernels: 100 us -> 154 us
  matrix products: 128 us -> 75.4 us
  blocking collectives: 37.9 us -> 0 us
  between operations: 17.2 us -> 3.89 us
  other arithmetic: 67.9 us -> 79.1 us
  starting transfers between devices: 74.3 us -> 85.1 us
    all_gather x3 -> x0, waiting for transfers between devices: 132 us -> none  [gather_weights(): gather = lambda a: lax.all_gather(a, 'cp', axis=0, tiled=True)]
    pallas_call x0 -> x7, Pallas kernels: none -> 54 us  [the longest x4 47.2 us: weight_grad(): pl.pallas_call(functools.partial(weight_grad_kernel, fill, (len(lefts), l...]
    dot_general x38 -> x24, matrix products: 128 us -> 75.4 us  [dotf(): return lax.dot_general(a, b, dims, preferred_element_type=F32)]
    psum x1 -> x0, blocking collectives: 37.9 us -> none  [local(): vectors = lax.psum(jnp.stack(vectors), ('dp', 'cp'))]
    ppermute x12, waiting for transfers between devices: 60.1 us -> 33.2 us  [hop(): lax.ppermute(a, 'dp', [(2 * s + c, 2 * t + c) for s, t in moves for c in...]
    unnamed x399 -> x313, local copies, waits for them, and re-layouts: 52.2 us -> 25.8 us
    another operation x12 -> x4, local copies, waits for them, and re-layouts: 15.1 us -> 1.91 us  [the longest x2 1.32 us: pair_up(): jnp.stack([mine, got], axis)]
    ppermute x15 -> x22, starting transfers between devices: 19.7 us -> 28.1 us  [over_x(): return lax.ppermute(a, 'cp', [(i, i ^ 1) for i in range(self.cp)])]
  transfers between devices with their start and end apart: 65 -> 75, of which waited for: 25 -> 33; matrix products, arithmetic and copies ran while one was open for 19% -> 16% of each run, Pallas kernels for 2% -> 13%
where the time goes in v2:
time: 646 us; the launch traced here: 640 us
  waiting for transfers between devices  175 us (27%)
  Pallas kernels  154 us (24%)
  starting transfers between devices  85.1 us (13%)
  other arithmetic  79.1 us (12%)
  matrix products  75.4 us (12%)
  local copies, waits for them, and re-layouts  67.6 us (10%)
    ppermute x22, waiting for transfers between devices, over_x(): return lax.ppermute(a, 'cp', [(i, i ^ 1) for i in range(self.cp)])  88.8 us
    dot_general x24, matrix products, dotf(): return lax.dot_general(a, b, dims, preferred_element_type=F32)  75.4 us
    pallas_call x3, Pallas kernels, attend_back_call(): pl.pallas_call(functools.partial(attend_back_kernel, recursion, len(kvs))...  55.2 us
    pallas_call x4, Pallas kernels, weight_grad(): pl.pallas_call(functools.partial(weight_grad_kernel, fill, (len(lefts), l...  47.2 us
    ppermute x15, waiting for transfers between devices, over_y(): return lax.ppermute(a, 'cp', [(i, i ^ 2) for i in range(self.cp)])  40 us
    pallas_call x3, Pallas kernels, attend_call(): pl.pallas_call(functools.partial(attend_kernel, recursion, len(kvs)), gri...  40 us
    ppermute x12, waiting for transfers between devices, hop(): lax.ppermute(a, 'dp', [(2 * s + c, 2 * t + c) for s, t in moves for c in...  33.2 us
    convert_element_type x32, other arithmetic, add(): return sum((a.astype(F32) for a in terms)).astype(BF16)  30.5 us
  transfers between devices with their start and end apart: 75, of which 33 were waited for; matrix products, arithmetic and copies ran while one was open for 16% of the time, Pallas kernels for 13%

profile of v2, /device:TPU:0, one launch (start us, length us, event | category | flops | bytes accessed | tf_op | source)
XLA Modules:
  0.0 639.8 jit_solution(6782719757242181472)
XLA Ops:
  11.1 6.0 collective-permute-start.3
  34.4 12.6 %collective-permute-done.5 = bf16[2,112,1285]{2,1,0:T(8,128)(2,1)} collective-permute-done((bf16[2,112,1285]{2,1,0:T(8,128)(2,1)S(1)}, bf16[2,112,1285]{2,1,0:T(8,128)(2,1)}, u32[]{:S(2)}, u32[]{:S(2)}) %collective-permute-start.5) | collective-permute-done | bytes 575712 | tf_op jit(solution)/shard_map/ppermute | solution.py:424
  57.5 13.1 %collective-permute-done.11 = bf16[112,2560]{1,0:T(8,128)(2,1)S(1)} collective-permute-done((bf16[112,2560]{1,0:T(8,128)(2,1)S(1)}, bf16[112,2560]{1,0:T(8,128)(2,1)S(1)}, u32[]{:S(2)}, u32[]{:S(2)}) %collective-permute-start.11) | collective-permute-done | bytes 573472 | tf_op jit(solution)/shard_map/ppermute | solution.py:427
  89.3 7.8 %collective-permute-done.12.refs_1_ = bf16[288,640]{1,0:T(8,128)(2,1)} collective-permute-done((bf16[288,640]{1,0:T(8,128)(2,1)}, bf16[288,640]{1,0:T(8,128)(2,1)}, u32[]{:S(2)}, u32[]{:S(2)}) %collective-permute-start.12) | collective-permute-done | bytes 368672 | tf_op jit(solution)/shard_map/ppermute | solution.py:424
  103.3 13.9 %attend.3 = (bf16[288,960]{1,0:T(8,128)(2,1)S(1)}, f32[5,288,3]{2,1,0:T(8,128)S(1)}) custom-call(bf16[288,960]{1,0:T(8,128)(2,1)S(1)} %copy-done.26, bf16[288,640]{1,0:T(8,128)(2,1)} %get-tuple-element.260.refs_0_, bf16[288,640]{1,0:T(8,128)(2,1)} %collective-permute-done.12.refs_1_, bf16[288,640]{1,0:T(8,128)(2,1)S(1)} %collective-permute-done.13.refs_2_, ...), custom_call_target="tpu_custom_call" | custom-call | flops 2548039680 | bytes 2580480 | tf_op jit(solution)/shard_map/attend/pallas_call | solution.py:151
  119.7 15.8 %collective-permute-done.17 = bf16[160,960]{1,0:T(8,128)(2,1)S(1)} collective-permute-done((bf16[160,960]{1,0:T(8,128)(2,1)S(1)}, bf16[160,960]{1,0:T(8,128)(2,1)S(1)}, u32[]{:S(2)}, u32[]{:S(2)}) %collective-permute-start.17) | collective-permute-done | bytes 307232 | tf_op jit(solution)/shard_map/ppermute | solution.py:424
  189.6 9.1 %collective-permute-done.23.refs_1_ = bf16[288,640]{1,0:T(8,128)(2,1)S(1)} collective-permute-done((bf16[288,640]{1,0:T(8,128)(2,1)S(1)}, bf16[288,640]{1,0:T(8,128)(2,1)S(1)}, u32[]{:S(2)}, u32[]{:S(2)}) %collective-permute-start.23) | collective-permute-done | bytes 368672 | tf_op jit(solution)/shard_map/ppermute | solution.py:424
  200.4 13.2 %attend.4 = (bf16[288,960]{1,0:T(8,128)(2,1)S(1)}, f32[5,288,3]{2,1,0:T(8,128)S(1)}) custom-call(bf16[288,960]{1,0:T(8,128)(2,1)S(1)} %get-tuple-element.284.q_ref, bf16[288,640]{1,0:T(8,128)(2,1)S(1)} %get-tuple-element.285.refs_0_, bf16[288,640]{1,0:T(8,128)(2,1)S(1)} %collective-permute-done.23.refs_1_, ...), custom_call_target="tpu_custom_call" | custom-call | flops 2548039680 | bytes 2580480 | tf_op jit(solution)/shard_map/attend/pallas_call | solution.py:151
  215.0 4.8 fusion.99
  229.3 9.1 %collective-permute-done.26.refs_1_ = bf16[288,640]{1,0:T(8,128)(2,1)S(1)} collective-permute-done((bf16[288,640]{1,0:T(8,128)(2,1)S(1)}, bf16[288,640]{1,0:T(8,128)(2,1)S(1)}, u32[]{:S(2)}, u32[]{:S(2)}) %collective-permute-start.26) | collective-permute-done | bytes 368672 | tf_op jit(solution)/shard_map/ppermute | solution.py:424
  240.2 12.9 %attend.5 = (bf16[288,960]{1,0:T(8,128)(2,1)S(1)}, f32[5,288,3]{2,1,0:T(8,128)S(1)}) custom-call(bf16[288,960]{1,0:T(8,128)(2,1)S(1)} %get-tuple-element.287.q_ref, bf16[288,640]{1,0:T(8,128)(2,1)S(1)} %get-tuple-element.288.refs_0_, bf16[288,640]{1,0:T(8,128)(2,1)S(1)} %collective-permute-done.26.refs_1_, ...), custom_call_target="tpu_custom_call" | custom-call | flops 2548039680 | bytes 2580480 | tf_op jit(solution)/shard_map/attend/pallas_call | solution.py:151
  265.2 6.6 %broadcast_select_fusion.8 = (bf16[288,2560]{1,0:T(8,128)(2,1)}, bf16[288,2560]{1,0:T(8,128)(2,1)}, bf16[288,2560]{1,0:T(8,128)(2,1)}) fusion(pred[]{:T(512)S(6)} %eq.14, f32[288,2560]{1,0:T(8,128)} %copy-done.137, bf16[288,2560]{1,0:T(8,128)(2,1)} %get-tuple-element.632, bf16[288,960]{1,0:T(8,128)(2,1)S(1)} %fusion.25.refs_5_, ...), kind=kOutput, calls=%fused_computation.60 | convolution fusion | flops 1428848640 | bytes 14315521 | tf_op jit(solution)/shard_map/dot_general | solution.py:26
  275.2 4.7 fusion.101
  284.6 18.1 %attend_back.3 = (bf16[288,960]{1,0:T(8,128)(2,1)S(1)}, bf16[1152,640]{1,0:T(8,128)(2,1)}) custom-call(bf16[288,960]{1,0:T(8,128)(2,1)S(1)} %get-tuple-element.287.q_ref, bf16[288,960]{1,0:T(8,128)(2,1)S(1)} %convolution_convert_fusion.2.do_ref, bf16[288,960]{1,0:T(8,128)(2,1)S(1)} %get-tuple-element.289.att_ref.refs_2_, ...), custom_call_target="tpu_custom_call" | custom-call | flops 6370099200 | bytes 5160960 | tf_op jit(solution)/shard_map/attend_back/pallas_call | solution.py:219
  309.6 9.4 %collective-permute-done.31.got_ref = bf16[288,640]{1,0:T(8,128)(2,1)S(1)} collective-permute-done((bf16[288,640]{1,0:T(8,128)(2,1)S(1)}, bf16[288,640]{1,0:T(8,128)(2,1)S(1)}, u32[]{:S(2)}, u32[]{:S(2)}) %collective-permute-start.31) | collective-permute-done | bytes 368672 | tf_op jit(solution)/shard_map/ppermute | solution.py:424
  339.4 18.3 %attend_back.4 = (bf16[288,960]{1,0:T(8,128)(2,1)S(1)}, bf16[1152,640]{1,0:T(8,128)(2,1)}) custom-call(bf16[288,960]{1,0:T(8,128)(2,1)S(1)} %get-tuple-element.284.q_ref, bf16[288,960]{1,0:T(8,128)(2,1)S(1)} %convolution_convert_fusion.1.do_ref, bf16[288,960]{1,0:T(8,128)(2,1)S(1)} %get-tuple-element.286.att_ref.refs_1_, ...), custom_call_target="tpu_custom_call" | custom-call | flops 6370099200 | bytes 5160960 | tf_op jit(solution)/shard_map/attend_back/pallas_call | solution.py:219
  363.9 9.0 %collective-permute-done.33.got_ref = bf16[288,640]{1,0:T(8,128)(2,1)S(1)} collective-permute-done((bf16[288,640]{1,0:T(8,128)(2,1)S(1)}, bf16[288,640]{1,0:T(8,128)(2,1)S(1)}, u32[]{:S(2)}, u32[]{:S(2)}) %collective-permute-start.33) | collective-permute-done | bytes 368672 | tf_op jit(solution)/shard_map/ppermute | solution.py:424
  376.4 13.2 %weight_grad.4 = (bf16[2,160,960]{2,1,0:T(8,128)(2,1)}, bf16[2,160,960]{2,1,0:T(8,128)(2,1)}, bf16[2,160,960]{2,1,0:T(8,128)(2,1)}, bf16[2,160,960]{2,1,0:T(8,128)(2,1)}, bf16[4,320,960]{2,1,0:T(8,128)(2,1)}) custom-call(s32[2]{0:T(128)} %pad_add_fusion.3.spot_ref, bf16[288,2560]{1,0:T(8,128)(2,1)} %get-tuple-element.279.refs_0_, ...), custom_call_target="tpu_custom_call" | custom-call | flops 4246732800 | bytes 10997760 | tf_op jit(solution)/shard_map/weight_grad/pallas_call | solution.py:381
  402.1 17.0 %weight_grad.5 = (bf16[2,128,2560]{2,1,0:T(8,128)(2,1)}, bf16[2,128,2560]{2,1,0:T(8,128)(2,1)}, bf16[2,112,2560]{2,1,0:T(8,128)(2,1)}, bf16[2,112,2560]{2,1,0:T(8,128)(2,1)}, bf16[4,240,2560]{2,1,0:T(8,128)(2,1)}) custom-call(s32[2]{0:T(128)} %pad_add_fusion.3.spot_ref, bf16[288,960]{1,0:T(8,128)(2,1)} %copy-done.104, bf16[288,960]{1,0:T(8,128)(2,1)} %copy-done.106, ...), custom_call_target="tpu_custom_call" | custom-call | flops 8493465600 | bytes 20336640 | tf_op jit(solution)/shard_map/weight_grad/pallas_call | solution.py:381
  419.2 4.7 fusion.104
  452.3 18.8 %attend_back.5 = (bf16[288,960]{1,0:T(8,128)(2,1)S(1)}, bf16[1152,640]{1,0:T(8,128)(2,1)}) custom-call(bf16[288,960]{1,0:T(8,128)(2,1)S(1)} %copy-done.27, bf16[288,960]{1,0:T(8,128)(2,1)S(1)} %convolution_convert_fusion.do_ref, bf16[288,960]{1,0:T(8,128)(2,1)S(1)} %copy-done.15, bf16[288,640]{1,0:T(8,128)(2,1)} %get-tuple-element.260.refs_0_, ...), custom_call_target="tpu_custom_call" | custom-call | flops 6370099200 | bytes 5160960 | tf_op jit(solution)/shard_map/attend_back/pallas_call | solution.py:219
  478.7 10.6 %weight_grad.6 = (bf16[2,128,960]{2,1,0:T(8,128)(2,1)}, bf16[2,128,960]{2,1,0:T(8,128)(2,1)}, bf16[2,112,960]{2,1,0:T(8,128)(2,1)}, bf16[2,112,960]{2,1,0:T(8,128)(2,1)}, bf16[4,240,960]{2,1,0:T(8,128)(2,1)}) custom-call(s32[2]{0:T(128)} %pad_add_fusion.3.spot_ref, bf16[288,960]{1,0:T(8,128)(2,1)} %copy-done.14, bf16[288,960]{1,0:T(8,128)(2,1)} %copy-done.20, ...), custom_call_target="tpu_custom_call" | custom-call | flops 3185049600 | bytes 10321920 | tf_op jit(solution)/shard_map/weight_grad/pallas_call | solution.py:381
  493.9 5.5 collective-permute-done.47.got_ref
  512.1 6.4 %weight_grad.7 = (bf16[2,128,512]{2,1,0:T(8,128)(2,1)}, bf16[2,128,512]{2,1,0:T(8,128)(2,1)}, bf16[2,112,512]{2,1,0:T(8,128)(2,1)}, bf16[2,112,512]{2,1,0:T(8,128)(2,1)}, bf16[4,240,512]{2,1,0:T(8,128)(2,1)}) custom-call(s32[2]{0:T(128)} %pad_add_fusion.3.spot_ref, bf16[288,960]{1,0:T(8,128)(2,1)} %copy-done.24, bf16[288,960]{1,0:T(8,128)(2,1)} %copy-done.28, ...), custom_call_target="tpu_custom_call" | custom-call | flops 1061683200 | bytes 4730880 | tf_op jit(solution)/shard_map/weight_grad/pallas_call | solution.py:381
  528.0 10.2 %collective-permute-done.54 = bf16[2,112,960]{2,1,0:T(8,128)(2,1)S(1)} collective-permute-done((bf16[2,112,960]{2,1,0:T(8,128)(2,1)S(1)}, bf16[2,112,960]{2,1,0:T(8,128)(2,1)S(1)}, u32[]{:S(2)}, u32[]{:S(2)}) %collective-permute-start.54) | collective-permute-done | bytes 430112 | tf_op jit(solution)/shard_map/ppermute | solution.py:427
  540.3 7.2 %collective-permute-start.57 = (bf16[112,2560]{1,0:T(8,128)(2,1)S(1)}, bf16[112,2560]{1,0:T(8,128)(2,1)S(1)}, u32[]{:S(2)}, u32[]{:S(2)}) collective-permute-start(bf16[112,2560]{1,0:T(8,128)(2,1)S(1)} %fusion.43), channel_id=1, source_target_pairs={{0,8},{4,12},{24,16},{28,20},{1,9},{5,13},{25,17},{29,21},{2,10},{... | collective-permute-start | bytes 1720328 | tf_op jit(solution)/shard_map/ppermute | solution.py:574
  552.4 4.8 collective-permute-done.59
  557.7 6.0 collective-permute-done.61
  571.5 6.4 collective-permute-start.66
  583.2 5.8 collective-permute-done.66
  596.3 11.3 %collective-permute-done.68 = bf16[112,2560]{1,0:T(8,128)(2,1)S(1)} collective-permute-done((bf16[112,2560]{1,0:T(8,128)(2,1)S(1)}, bf16[112,2560]{1,0:T(8,128)(2,1)S(1)}, u32[]{:S(2)}, u32[]{:S(2)}) %collective-permute-start.68) | collective-permute-done | bytes 573472 | tf_op jit(solution)/shard_map/ppermute | solution.py:574
  615.0 14.0 %collective-permute-done.71 = bf16[240,1472]{1,0:T(8,128)(2,1)S(1)} collective-permute-done((bf16[240,1472]{1,0:T(8,128)(2,1)S(1)}, bf16[240,1472]{1,0:T(8,128)(2,1)S(1)}, u32[]{:S(2)}, u32[]{:S(2)}) %collective-permute-start.71) | collective-permute-done | bytes 706592 | tf_op jit(solution)/shard_map/ppermute | solution.py:574
  (637 shorter events, 309.6 us)
Async XLA Ops:
  5.1 18.9 %collective-permute-start = (bf16[128,1285]{1,0:T(8,128)(2,1)S(1)}, bf16[128,1285]{1,0:T(8,128)(2,1)}, u32[]{:S(2)}, u32[]{:S(2)}) collective-permute-start(bf16[128,1285]{1,0:T(8,128)(2,1)S(1)} %slice.424), channel_id=1, source_target_pairs={{0,1},{1,0},{2,3},{3,2},{4,5},{5,4},{6,7},{7,6},{8,9},{9,8},{10,11... | collective-permute-start | bytes 986888 | tf_op jit(solution)/shard_map/ppermute | solution.py:424
  27.0 19.9 %collective-permute-start.4 = (bf16[2,128,1285]{1,0,2:T(2,128)(2,1)S(1)}, bf16[2,128,1285]{1,0,2:T(2,128)(2,1)S(1)}, u32[]{:S(2)}, u32[]{:S(2)}) collective-permute-start(bf16[2,128,1285]{1,0,2:T(2,128)(2,1)S(1)} %copy.117), channel_id=1, source_target_pairs={{0,2},{1,3},{2,0},{3,1},{4,6},{5,7},{6,4},{7,5},{8,10},{9,11},{10,... | collective-permute-start | bytes 1973768 | tf_op jit(solution)/shard_map/ppermute | solution.py:427
  30.4 16.5 %collective-permute-start.5 = (bf16[2,112,1285]{2,1,0:T(8,128)(2,1)S(1)}, bf16[2,112,1285]{2,1,0:T(8,128)(2,1)}, u32[]{:S(2)}, u32[]{:S(2)}) collective-permute-start(bf16[2,112,1285]{2,1,0:T(8,128)(2,1)S(1)} %maximum_select_fusion.11), channel_id=1, source_target_pairs={{0,1},{1,0},{2,3},{3,2},{4,5},{5,4},{6,7},{7,6},{8,9},{9,8},{10,11... | collective-permute-start | bytes 1727048 | tf_op jit(solution)/shard_map/ppermute | solution.py:424
  54.0 19.8 %collective-permute-start.9 = (bf16[960,1285]{0,1:T(8,128)(2,1)}, bf16[960,1285]{0,1:T(8,128)(2,1)}, u32[]{:S(2)}, u32[]{:S(2)}) collective-permute-start(bf16[960,1285]{0,1:T(8,128)(2,1)} %copy.120), channel_id=1, source_target_pairs={{0,4},{4,0},{8,12},{12,8},{16,20},{20,16},{24,28},{28,24},{1,5},{5... | collective-permute-start | bytes 7401608 | tf_op jit(solution)/shard_map/ppermute | solution.py:430
  55.7 16.9 %collective-permute-start.10 = (bf16[128,2560]{1,0:T(8,128)(2,1)S(1)}, bf16[128,2560]{1,0:T(8,128)(2,1)S(1)}, u32[]{:S(2)}, u32[]{:S(2)}) collective-permute-start(bf16[128,2560]{1,0:T(8,128)(2,1)S(1)} %get-tuple-element.587), channel_id=1, source_target_pairs={{0,1},{1,0},{2,3},{3,2},{4,5},{5,4},{6,7},{7,6},{8,9},{9,8},{10,11... | collective-permute-start | bytes 1966088 | tf_op jit(solution)/shard_map/ppermute | solution.py:424
  99.0 38.3 %collective-permute-start.15 = (bf16[2,128,2560]{2,1,0:T(8,128)(2,1)S(1)}, bf16[2,128,2560]{2,1,0:T(8,128)(2,1)S(1)}, u32[]{:S(2)}, u32[]{:S(2)}) collective-permute-start(bf16[2,128,2560]{2,1,0:T(8,128)(2,1)S(1)} %copy-done.53), channel_id=1, source_target_pairs={{0,2},{1,3},{2,0},{3,1},{4,6},{5,7},{6,4},{7,5},{8,10},{9,11},{10,... | collective-permute-start | bytes 3932168 | tf_op jit(solution)/shard_map/ppermute | solution.py:427
  100.8 36.5 %collective-permute-start.16 = (bf16[2,112,2560]{2,1,0:T(8,128)(2,1)}, bf16[2,112,2560]{2,1,0:T(8,128)(2,1)S(1)}, u32[]{:S(2)}, u32[]{:S(2)}) collective-permute-start(bf16[2,112,2560]{2,1,0:T(8,128)(2,1)} %maximum_select_fusion.7), channel_id=1, source_target_pairs={{0,1},{1,0},{2,3},{3,2},{4,5},{5,4},{6,7},{7,6},{8,9},{9,8},{10,11... | collective-permute-start | bytes 3440648 | tf_op jit(solution)/shard_map/ppermute | solution.py:424
  102.4 33.1 %collective-permute-start.17 = (bf16[160,960]{1,0:T(8,128)(2,1)S(1)}, bf16[160,960]{1,0:T(8,128)(2,1)S(1)}, u32[]{:S(2)}, u32[]{:S(2)}) collective-permute-start(bf16[160,960]{1,0:T(8,128)(2,1)S(1)} %get-tuple-element.275), channel_id=1, source_target_pairs={{0,1},{1,0},{2,3},{3,2},{4,5},{5,4},{6,7},{7,6},{8,9},{9,8},{10,11... | collective-permute-start | bytes 921608 | tf_op jit(solution)/shard_map/ppermute | solution.py:424
  103.0 34.3 %collective-permute-start.18 = (bf16[160,960]{1,0:T(8,128)(2,1)S(1)}, bf16[160,960]{1,0:T(8,128)(2,1)S(1)}, u32[]{:S(2)}, u32[]{:S(2)}) collective-permute-start(bf16[160,960]{1,0:T(8,128)(2,1)S(1)} %get-tuple-element.277), channel_id=1, source_target_pairs={{0,2},{1,3},{2,0},{3,1},{4,6},{5,7},{6,4},{7,5},{8,10},{9,11},{10,... | collective-permute-start | bytes 921608 | tf_op jit(solution)/shard_map/ppermute | solution.py:427
  139.4 17.2 %collective-permute-start.20 = (bf16[2,160,960]{2,1,0:T(8,128)(2,1)S(1)}, bf16[2,160,960]{2,1,0:T(8,128)(2,1)S(1)}, u32[]{:S(2)}, u32[]{:S(2)}) collective-permute-start(bf16[2,160,960]{2,1,0:T(8,128)(2,1)S(1)} %maximum_select_fusion.9), channel_id=1, source_target_pairs={{0,2},{1,3},{2,0},{3,1},{4,6},{5,7},{6,4},{7,5},{8,10},{9,11},{10,... | collective-permute-start | bytes 1843208 | tf_op jit(solution)/shard_map/ppermute | solution.py:427
  141.3 16.9 %collective-permute-start.21 = (bf16[2,160,960]{2,1,0:T(8,128)(2,1)S(1)}, bf16[2,160,960]{2,1,0:T(8,128)(2,1)S(1)}, u32[]{:S(2)}, u32[]{:S(2)}) collective-permute-start(bf16[2,160,960]{2,1,0:T(8,128)(2,1)S(1)} %maximum_select_fusion.10), channel_id=1, source_target_pairs={{0,1},{1,0},{2,3},{3,2},{4,5},{5,4},{6,7},{7,6},{8,9},{9,8},{10,11... | collective-permute-start | bytes 1843208 | tf_op jit(solution)/shard_map/ppermute | solution.py:424
  238.5 23.7 %collective-permute-start.29 = (bf16[288,960]{1,0:T(8,128)(2,1)}, bf16[288,960]{1,0:T(8,128)(2,1)S(1)}, u32[]{:S(2)}, u32[]{:S(2)}) collective-permute-start(bf16[288,960]{1,0:T(8,128)(2,1)} %bitcast.40), channel_id=1, source_target_pairs={{0,0},{1,1},{2,4},{3,5},{4,2},{5,3},{6,6},{7,7},{8,8},{9,9},{10,12... | collective-permute-start | bytes 1658888 | tf_op jit(solution)/shard_map/ppermute | solution.py:440
  400.3 18.7 %collective-permute-start.36 = (bf16[2,160,960]{2,1,0:T(8,128)(2,1)}, bf16[2,160,960]{2,1,0:T(8,128)(2,1)}, u32[]{:S(2)}, u32[]{:S(2)}) collective-permute-start(bf16[2,160,960]{2,1,0:T(8,128)(2,1)} %get-tuple-element.308), channel_id=1, source_target_pairs={{0,1},{1,0},{2,3},{3,2},{4,5},{5,4},{6,7},{7,6},{8,9},{9,8},{10,11... | collective-permute-start | bytes 1843208 | tf_op jit(solution)/shard_map/ppermute | solution.py:424
  401.8 17.3 %collective-permute-start.37 = (bf16[2,160,960]{2,1,0:T(8,128)(2,1)}, bf16[2,160,960]{2,1,0:T(8,128)(2,1)}, u32[]{:S(2)}, u32[]{:S(2)}) collective-permute-start(bf16[2,160,960]{2,1,0:T(8,128)(2,1)} %get-tuple-element.309), channel_id=1, source_target_pairs={{0,2},{1,3},{2,0},{3,1},{4,6},{5,7},{6,4},{7,5},{8,10},{9,11},{10,... | collective-permute-start | bytes 1843208 | tf_op jit(solution)/shard_map/ppermute | solution.py:427
  419.1 17.5 %collective-permute-start.40 = (bf16[4,240,2560]{2,1,0:T(8,128)(2,1)}, bf16[4,240,2560]{2,1,0:T(8,128)(2,1)S(1)}, u32[]{:S(2)}, u32[]{:S(2)}) collective-permute-start(bf16[4,240,2560]{2,1,0:T(8,128)(2,1)} %get-tuple-element.324), channel_id=1, source_target_pairs={{0,4},{4,0},{8,12},{12,8},{16,20},{20,16},{24,28},{28,24},{1,5},{5... | collective-permute-start | bytes 14745608 | tf_op jit(solution)/shard_map/ppermute | solution.py:430
  445.9 25.2 %collective-permute-start.41 = (bf16[128,2560]{1,0:T(8,128)(2,1)}, bf16[128,2560]{1,0:T(8,128)(2,1)S(1)}, u32[]{:S(2)}, u32[]{:S(2)}) collective-permute-start(bf16[128,2560]{1,0:T(8,128)(2,1)} %get-tuple-element.331), channel_id=1, source_target_pairs={{0,1},{1,0},{2,3},{3,2},{4,5},{5,4},{6,7},{7,6},{8,9},{9,8},{10,11... | collective-permute-start | bytes 1966088 | tf_op jit(solution)/shard_map/ppermute | solution.py:424
  448.3 22.8 %collective-permute-start.43 = (bf16[320,960]{1,0:T(8,128)(2,1)S(1)}, bf16[320,960]{1,0:T(8,128)(2,1)S(1)}, u32[]{:S(2)}, u32[]{:S(2)}) collective-permute-start(bf16[320,960]{1,0:T(8,128)(2,1)S(1)} %pad_maximum_fusion.7), channel_id=1, source_target_pairs={{0,8},{4,12},{24,16},{28,20},{1,9},{5,13},{25,17},{29,21},{2,10},{... | collective-permute-start | bytes 1843208 | tf_op jit(solution)/shard_map/ppermute | solution.py:574
  451.8 19.3 %collective-permute-start.42 = (bf16[112,2560]{1,0:T(8,128)(2,1)}, bf16[112,2560]{1,0:T(8,128)(2,1)S(1)}, u32[]{:S(2)}, u32[]{:S(2)}) collective-permute-start(bf16[112,2560]{1,0:T(8,128)(2,1)} %get-tuple-element.333), channel_id=1, source_target_pairs={{0,2},{1,3},{2,0},{3,1},{4,6},{5,7},{6,4},{7,5},{8,10},{9,11},{10,... | collective-permute-start | bytes 1720328 | tf_op jit(solution)/shard_map/ppermute | solution.py:427
  474.0 19.9 %collective-permute-start.44 = (bf16[128,2560]{1,0:T(8,128)(2,1)}, bf16[128,2560]{1,0:T(8,128)(2,1)}, u32[]{:S(2)}, u32[]{:S(2)}) collective-permute-start(bf16[128,2560]{1,0:T(8,128)(2,1)} %get-tuple-element.347), channel_id=1, source_target_pairs={{0,1},{1,0},{2,3},{3,2},{4,5},{5,4},{6,7},{7,6},{8,9},{9,8},{10,11... | collective-permute-start | bytes 1966088 | tf_op jit(solution)/shard_map/ppermute | solution.py:424
  475.4 18.5 %collective-permute-start.45 = (bf16[112,2560]{1,0:T(8,128)(2,1)}, bf16[112,2560]{1,0:T(8,128)(2,1)}, u32[]{:S(2)}, u32[]{:S(2)}) collective-permute-start(bf16[112,2560]{1,0:T(8,128)(2,1)} %get-tuple-element.349), channel_id=1, source_target_pairs={{0,2},{1,3},{2,0},{3,1},{4,6},{5,7},{6,4},{7,5},{8,10},{9,11},{10,... | collective-permute-start | bytes 1720328 | tf_op jit(solution)/shard_map/ppermute | solution.py:427
  478.0 21.3 %collective-permute-start.47 = (bf16[288,640]{1,0:T(8,128)(2,1)}, bf16[288,640]{1,0:T(8,128)(2,1)}, u32[]{:S(2)}, u32[]{:S(2)}) collective-permute-start(bf16[288,640]{1,0:T(8,128)(2,1)} %get-tuple-element.597), channel_id=1, source_target_pairs={{0,1},{1,0},{2,3},{3,2},{4,5},{5,4},{6,7},{7,6},{8,9},{9,8},{10,11... | collective-permute-start | bytes 1105928 | tf_op jit(solution)/shard_map/ppermute | solution.py:424
  491.9 29.3 %collective-permute-start.50 = (bf16[320,960]{1,0:T(8,128)(2,1)}, bf16[320,960]{1,0:T(8,128)(2,1)}, u32[]{:S(2)}, u32[]{:S(2)}) collective-permute-start(bf16[320,960]{1,0:T(8,128)(2,1)} %add_convert_fusion.8), channel_id=1, source_target_pairs={{8,16},{12,20},{16,8},{20,12},{9,17},{13,21},{17,9},{21,13},{10,18... | collective-permute-start | bytes 1843208 | tf_op jit(solution)/shard_map/ppermute | solution.py:574
  499.3 19.2 %collective-permute-start.51 = (bf16[4,240,960]{2,1,0:T(8,128)(2,1)}, bf16[4,240,960]{2,1,0:T(8,128)(2,1)}, u32[]{:S(2)}, u32[]{:S(2)}) collective-permute-start(bf16[4,240,960]{2,1,0:T(8,128)(2,1)} %get-tuple-element.374), channel_id=1, source_target_pairs={{0,4},{4,0},{8,12},{12,8},{16,20},{20,16},{24,28},{28,24},{1,5},{5... | collective-permute-start | bytes 5529608 | tf_op jit(solution)/shard_map/ppermute | solution.py:430
  501.7 19.5 %collective-permute-start.48 = (bf16[128,2560]{1,0:T(8,128)(2,1)}, bf16[128,2560]{1,0:T(8,128)(2,1)}, u32[]{:S(2)}, u32[]{:S(2)}) collective-permute-start(bf16[128,2560]{1,0:T(8,128)(2,1)} %fusion.30), channel_id=1, source_target_pairs={{0,2},{1,3},{2,0},{3,1},{4,6},{5,7},{6,4},{7,5},{8,10},{9,11},{10,... | collective-permute-start | bytes 1966088 | tf_op jit(solution)/shard_map/ppermute | solution.py:427
  505.4 15.8 %collective-permute-start.49 = (bf16[112,2560]{1,0:T(8,128)(2,1)}, bf16[112,2560]{1,0:T(8,128)(2,1)}, u32[]{:S(2)}, u32[]{:S(2)}) collective-permute-start(bf16[112,2560]{1,0:T(8,128)(2,1)} %fusion.45), channel_id=1, source_target_pairs={{0,1},{1,0},{2,3},{3,2},{4,5},{5,4},{6,7},{7,6},{8,9},{9,8},{10,11... | collective-permute-start | bytes 1720328 | tf_op jit(solution)/shard_map/ppermute | solution.py:424
  523.2 16.3 %collective-permute-start.52 = (bf16[128,2560]{1,0:T(8,128)(2,1)S(1)}, bf16[128,2560]{1,0:T(8,128)(2,1)S(1)}, u32[]{:S(2)}, u32[]{:S(2)}) collective-permute-start(bf16[128,2560]{1,0:T(8,128)(2,1)S(1)} %fusion.28), channel_id=1, source_target_pairs={{0,8},{4,12},{24,16},{28,20},{1,9},{5,13},{25,17},{29,21},{2,10},{... | collective-permute-start | bytes 1966088 | tf_op jit(solution)/shard_map/ppermute | solution.py:574
  539.6 24.1 %collective-permute-start.56 = (bf16[128,2560]{1,0:T(8,128)(2,1)S(1)}, bf16[128,2560]{1,0:T(8,128)(2,1)S(1)}, u32[]{:S(2)}, u32[]{:S(2)}) collective-permute-start(bf16[128,2560]{1,0:T(8,128)(2,1)S(1)} %add_convert_fusion.7), channel_id=1, source_target_pairs={{8,16},{12,20},{16,8},{20,12},{9,17},{13,21},{17,9},{21,13},{10,18... | collective-permute-start | bytes 1966088 | tf_op jit(solution)/shard_map/ppermute | solution.py:574
  540.3 23.4 %collective-permute-start.57 = (bf16[112,2560]{1,0:T(8,128)(2,1)S(1)}, bf16[112,2560]{1,0:T(8,128)(2,1)S(1)}, u32[]{:S(2)}, u32[]{:S(2)}) collective-permute-start(bf16[112,2560]{1,0:T(8,128)(2,1)S(1)} %fusion.43), channel_id=1, source_target_pairs={{0,8},{4,12},{24,16},{28,20},{1,9},{5,13},{25,17},{29,21},{2,10},{... | collective-permute-start | bytes 1720328 | tf_op jit(solution)/shard_map/ppermute | solution.py:574
  563.9 19.3 %collective-permute-start.62 = (bf16[128,2560]{1,0:T(8,128)(2,1)S(1)}, bf16[128,2560]{1,0:T(8,128)(2,1)}, u32[]{:S(2)}, u32[]{:S(2)}) collective-permute-start(bf16[128,2560]{1,0:T(8,128)(2,1)S(1)} %add_convert_fusion.6), channel_id=1, source_target_pairs={{8,0},{12,4},{16,24},{20,28},{9,1},{13,5},{17,25},{21,29},{10,2},{... | collective-permute-start | bytes 1966088 | tf_op jit(solution)/shard_map/ppermute | solution.py:574
  571.5 17.5 %collective-permute-start.66 = (bf16[240,1472]{1,0:T(8,128)(2,1)S(1)}, bf16[240,1472]{1,0:T(8,128)(2,1)}, u32[]{:S(2)}, u32[]{:S(2)}) collective-permute-start(bf16[240,1472]{1,0:T(8,128)(2,1)S(1)} %maximum_maximum_fusion), channel_id=1, source_target_pairs={{0,8},{4,12},{24,16},{28,20},{1,9},{5,13},{25,17},{29,21},{2,10},{... | collective-permute-start | bytes 2119688 | tf_op jit(solution)/shard_map/ppermute | solution.py:574
  590.3 17.4 %collective-permute-start.67 = (bf16[240,1472]{1,0:T(8,128)(2,1)S(1)}, bf16[240,1472]{1,0:T(8,128)(2,1)S(1)}, u32[]{:S(2)}, u32[]{:S(2)}) collective-permute-start(bf16[240,1472]{1,0:T(8,128)(2,1)S(1)} %add_convert_fusion.1), channel_id=1, source_target_pairs={{8,16},{12,20},{16,8},{20,12},{9,17},{13,21},{17,9},{21,13},{10,18... | collective-permute-start | bytes 2119688 | tf_op jit(solution)/shard_map/ppermute | solution.py:574
  608.7 20.3 %collective-permute-start.71 = (bf16[240,1472]{1,0:T(8,128)(2,1)S(1)}, bf16[240,1472]{1,0:T(8,128)(2,1)S(1)}, u32[]{:S(2)}, u32[]{:S(2)}) collective-permute-start(bf16[240,1472]{1,0:T(8,128)(2,1)S(1)} %add_convert_fusion), channel_id=1, source_target_pairs={{8,0},{12,4},{16,24},{20,28},{9,1},{13,5},{17,25},{21,29},{10,2},{... | collective-permute-start | bytes 2119688 | tf_op jit(solution)/shard_map/ppermute | solution.py:574
  (196 other events, 1545.4 us)

commit v3 on v2

--- a/solution.py
+++ b/solution.py
@@ -26,63 +26,105 @@
     return lax.dot_general(a, b, dims, preferred_element_type=F32)
 
 
-def whole(*shape):
-    return pl.BlockSpec(shape, lambda g: (0,) * len(shape))
-
-
 def turn(u):
     lane = lax.broadcasted_iota(jnp.int32, u.shape, 1) % HEAD_DIM
     return jnp.where(lane < HEAD_DIM // 2, pltpu.roll(u, LANES - 32, 1), pltpu.roll(u, 32, 1))
 
 
-def qkv_kernel(x_ref, gain_ref, wq_ref, wkv_ref, cq_ref, sq_ref, ck_ref, sk_ref, q_ref, kv_ref, normed_ref):
-    x = x_ref[...]
-    factor = lax.rsqrt(jnp.mean(x * x, axis=-1, keepdims=True) + NORM_EPSILON)
-    normed_ref[...] = (x * factor * gain_ref[...]).astype(BF16)
-    normed = normed_ref[...]
-    kv = dotf(normed, wkv_ref[...])
-    cos, sin = ck_ref[...], sk_ref[...]
-    for at in range(0, kv_ref.shape[1], LANES):
-        u = kv[:, at : at + LANES]
-        kv_ref[:, at : at + LANES] = (u * cos + turn(u) * sin).astype(BF16)
-    q = dotf(normed, wq_ref[...])
-    cos, sin = cq_ref[...], sq_ref[...]
+def variants_of(rows, keys):
+    pick = lambda count, third, unit: (count * third // 3 // unit + 1) * unit
+    return tuple((pick(rows, k, 32), pick(keys, k, LANES)) for k in (1, 2)) + ((rows, keys),)
+
+
+def choose(meta_ref, variants, body):
+    if len(variants) == 1:
+        body(*variants[0])
+    else:
+        for i, variant in enumerate(variants):
+            pl.when(meta_ref[0] == i)(functools.partial(body, *variant))
+
+
+def clear(m, *refs):
+    for ref in refs:
+        if m < ref.shape[0]:
+            ref[m:, :] = jnp.zeros((ref.shape[0] - m, ref.shape[1]), ref.dtype)
+
+
+def call(kernel, name, meta, grid, inputs, in_specs, out_specs, out_shape, scratch, vmem, flops, traffic):
+    return pl.pallas_call(
+        kernel,
+        grid_spec=pltpu.PrefetchScalarGridSpec(
+            num_scalar_prefetch=1, grid=grid, in_specs=in_specs, out_specs=out_specs, scratch_shapes=scratch
+        ),
+        out_shape=out_shape,
+        compiler_params=pltpu.CompilerParams(vmem_limit_bytes=vmem * MIB),
+        cost_estimate=pl.CostEstimate(flops=flops, bytes_accessed=traffic, transcendentals=0),
+        name=name,
+    )(meta, *inputs)
+
+
+def whole(*shape):
+    return pl.BlockSpec(shape, lambda g, s: (0,) * len(shape))
+
+
+def turns(table, keys):
+    cos, sin = table[:, :LANES], table[:, LANES : 2 * LANES]
+    if not keys:
+        return cos, sin
+    lane = lax.broadcasted_iota(jnp.int32, cos.shape, 1)
+    return jnp.where(lane < HEAD_DIM, cos, 1.0), jnp.where(lane < HEAD_DIM, sin, 0.0)
+
+
+def qkv_kernel(
+    variants, meta_ref, x_ref, gain_ref, wq_ref, wkv_ref, table_ref, q_ref, kv_ref, normed_ref
+):
     width = q_ref.shape[1]
-    for at in range(0, width, LANES):
-        if at + LANES <= width:
-            u = q[:, at : at + LANES]
-        else:
-            u = jnp.concatenate([q[:, at:], jnp.zeros((q.shape[0], at + LANES - width), F32)], axis=1)
-        r = (u * cos + turn(u) * sin).astype(BF16)
-        q_ref[:, at : min(at + LANES, width)] = r[:, : min(LANES, width - at)]
-
-
-def qkv_call(x, gain, wq, wkv, tables):
+
+    def body(m, _):
+        x = x_ref[:m]
+        factor = lax.rsqrt(jnp.mean(x * x, axis=-1, keepdims=True) + NORM_EPSILON)
+        normed = (x * factor * gain_ref[...]).astype(BF16)
+        normed_ref[:m, :] = normed
+        kv = dotf(normed, wkv_ref[...])
+        cos, sin = turns(table_ref[:m], True)
+        for at in range(0, kv_ref.shape[1], LANES):
+            u = kv[:, at : at + LANES]
+            kv_ref[:m, at : at + LANES] = (u * cos + turn(u) * sin).astype(BF16)
+        q = dotf(normed, wq_ref[:, :width])
+        cos, sin = turns(table_ref[:m], False)
+        for at in range(0, width, LANES):
+            if at + LANES <= width:
+                u = q[:, at : at + LANES]
+            else:
+                u = jnp.concatenate([q[:, at:], jnp.zeros((m, at + LANES - width), F32)], axis=1)
+            r = (u * cos + turn(u) * sin).astype(BF16)
+            q_ref[:m, at : min(at + LANES, width)] = r[:, : min(LANES, width - at)]
+        clear(m, q_ref, kv_ref, normed_ref)
+
+    choose(meta_ref, variants, body)
+
+
+def qkv_call(variants, meta, x, gain, wq, wkv, table):
     rows, width = x.shape
-    heads, both = wq.shape[1], wkv.shape[1]
-    return pl.pallas_call(
-        qkv_kernel,
-        grid=(1,),
-        in_specs=[whole(rows, width), whole(1, width), whole(width, heads), whole(width, both)]
-        + [whole(rows, LANES)] * 4,
-        out_specs=[whole(rows, heads), whole(rows, both), whole(rows, width)],
-        out_shape=[
-            jax.ShapeDtypeStruct((rows, heads), BF16),
-            jax.ShapeDtypeStruct((rows, both), BF16),
-            jax.ShapeDtypeStruct((rows, width), BF16),
-        ],
-        compiler_params=pltpu.CompilerParams(vmem_limit_bytes=32 * MIB),
-        cost_estimate=pl.CostEstimate(
-            flops=2 * rows * width * (heads + both),
-            bytes_accessed=2 * width * (heads + both) + 8 * rows * width,
-            transcendentals=0,
-        ),
-        name="norm_qkv_rope",
-    )(x, gain, wq, wkv, *tables)
-
-
-def make_bias(row_info, col_info, recursion):
-    doc_r, pos_r = row_info[:, 0:1], row_info[:, 1:2]
+    both = wkv.shape[1]
+    return call(
+        functools.partial(qkv_kernel, variants),
+        "norm_qkv_rope",
+        meta,
+        (1,),
+        (x, gain, wq, wkv, table),
+        [whole(rows, width), whole(1, width), whole(*wq.shape), whole(width, both), whole(*table.shape)],
+        [whole(rows, width), whole(rows, both), whole(rows, width)],
+        [jax.ShapeDtypeStruct((rows, k), BF16) for k in (width, both, width)],
+        [],
+        32,
+        2 * rows * width * (width + both),
+        2 * width * (width + both) + 8 * rows * width,
+    )
+
+
+def make_bias(row_table, col_info, recursion):
+    doc_r, pos_r = (row_table[:, k : k + 1].astype(jnp.int32) for k in (2 * LANES + HEAD_DIM, 3 * LANES + HEAD_DIM))
     doc_c, pos_c, depth_c = col_info[0:1, :], col_info[1:2, :], col_info[2:3, :]
     live = (depth_c > recursion) | (pos_c == pos_r)
     allowed = (pos_c <= pos_r) & (doc_c == doc_r) & live
@@ -119,117 +161,153 @@
             out_ref[:, at : at + HEAD_DIM] = a[:, :HEAD_DIM].astype(out_ref.dtype)
 
 
-def attend_kernel(recursion, count, q_ref, *refs):
-    key_refs, (row_ref, col_ref, att_ref, lse_ref, bias, q_all, o_all) = refs[:count], refs[count:]
+def compact_keys(meta_ref, key_refs, rows, keys):
+    block = 0
+    for ref in key_refs:
+        for first in range(0, ref.shape[0], rows):
+            keys[pl.ds(pl.multiple_of(meta_ref[2 + 2 * block], 16), rows), :] = ref[first : first + rows, :]
+            block += 1
+
+
+def attend_kernel(recursion, variants, count, meta_ref, q_ref, *refs):
+    key_refs, (row_ref, col_ref, att_ref, lse_ref, keys, bias, q_all, o_all) = refs[:count], refs[count:]
     g = pl.program_id(0)
+    rows = q_ref.shape[0]
 
     @pl.when(g == 0)
     def _():
-        bias[...] = make_bias(row_ref[...], col_ref[...], recursion)
+        lse_ref[...] = jnp.zeros_like(lse_ref)
         split_pairs(q_ref[...], q_all, True)
 
-    kv = jnp.concatenate([k[...] for k in key_refs], axis=0)
-    for j in range(GROUP):
-        h = g * GROUP + j
-        s = dotf(q_all[h], kv, NT) * SCALE + bias[...]
-        peak = jnp.max(s, axis=1, keepdims=True)
-        e = jnp.exp(s - peak)
-        total = jnp.sum(e, axis=1, keepdims=True)
-        o_all[h] = dotf(e.astype(BF16), kv) / total
-        lse_ref[0, :, j : j + 1] = peak + jnp.log(total)
+    keys[...] = jnp.zeros_like(keys)
+    compact_keys(meta_ref, key_refs, rows, keys)
+
+    def body(m, n):
+        @pl.when(g == 0)
+        def _():
+            bias[:m, :n] = make_bias(row_ref[:m], col_ref[:, :n], recursion)
+
+        kv = keys[:n, :]
+        for j in range(GROUP):
+            h = g * GROUP + j
+            s = dotf(q_all[h, :m], kv, NT) * SCALE + bias[:m, :n]
+            peak = jnp.max(s, axis=1, keepdims=True)
+            e = jnp.exp(s - peak)
+            total = jnp.sum(e, axis=1, keepdims=True)
+            o_all[h, :m] = dotf(e.astype(BF16), kv) / total
+            lane = lax.broadcasted_iota(jnp.int32, (m, LANES), 1)
+            lse_ref[:m, :] = jnp.where(lane == h, peak + jnp.log(total), lse_ref[:m, :])
+            if m < rows:
+                o_all[h, m:] = jnp.zeros((rows - m, LANES), F32)
+
+    choose(meta_ref, variants, body)
 
     @pl.when(g == pl.num_programs(0) - 1)
     def _():
         join_pairs(o_all, att_ref, False)
 
 
-def attend_call(recursion, q, kvs, row_info, col_info):
+def attend_call(recursion, variants, meta, q, kvs, row_info, col_info):
     rows, width = q.shape
     keys = sum(k.shape[0] for k in kvs)
     groups = kvs[0].shape[1] // LANES
     heads = groups * GROUP
-    return pl.pallas_call(
-        functools.partial(attend_kernel, recursion, len(kvs)),
-        grid=(groups,),
-        in_specs=[whole(rows, width)]
-        + [pl.BlockSpec((k.shape[0], LANES), lambda g: (0, g)) for k in kvs]
-        + [whole(rows, 2), whole(3, keys)],
-        out_specs=[whole(rows, width), pl.BlockSpec((1, rows, GROUP), lambda g: (g, 0, 0))],
-        out_shape=[
+    return call(
+        functools.partial(attend_kernel, recursion, variants, len(kvs)),
+        "attend",
+        meta,
+        (groups,),
+        (q, *kvs, row_info, col_info),
+        [whole(rows, width)]
+        + [pl.BlockSpec((k.shape[0], LANES), lambda g, s: (0, g)) for k in kvs]
+        + [whole(*row_info.shape), whole(3, keys)],
+        [whole(rows, width), whole(rows, LANES), pl.BlockSpec((keys, LANES), lambda g, s: (0, g))],
+        [
             jax.ShapeDtypeStruct((rows, width), BF16),
-            jax.ShapeDtypeStruct((groups, rows, GROUP), F32),
+            jax.ShapeDtypeStruct((rows, LANES), F32),
+            jax.ShapeDtypeStruct((keys, groups * LANES), BF16),
         ],
-        scratch_shapes=[
+        [
             pltpu.VMEM((rows, keys), F32),
             pltpu.VMEM((heads, rows, LANES), BF16),
             pltpu.VMEM((heads, rows, LANES), F32),
         ],
-        compiler_params=pltpu.CompilerParams(vmem_limit_bytes=40 * MIB),
-        cost_estimate=pl.CostEstimate(
-            flops=4 * rows * keys * LANES * heads,
-            bytes_accessed=4 * q.size + 2 * keys * groups * LANES,
-            transcendentals=heads * rows * keys,
-        ),
-        name="attend",
-    )(q, *kvs, row_info, col_info)
-
-
-def attend_back_kernel(recursion, count, q_ref, do_ref, att_ref, *refs):
-    key_refs, refs = refs[:count], refs[count:]
-    lse_ref, row_ref, col_ref, cos_ref, sin_ref, dq_ref, dkv_ref, bias, q_all, do_all, dot_all, p3, ds3, dq_all = refs
+        24,
+        4 * rows * keys * LANES * heads,
+        4 * q.size + 2 * keys * groups * LANES,
+    )
+
+
+def attend_back_kernel(
+    recursion, variants, meta_ref, q_ref, do_ref, att_ref, keys, lse_ref, row_ref, col_ref, dq_ref, dkv_ref,
+    bias, back, q_all, do_all, dot_all, p3, ds3, dq_all,
+):
     g = pl.program_id(0)
     rows, width = q_ref.shape
 
     @pl.when(g == 0)
     def _():
-        bias[...] = make_bias(row_ref[...], col_ref[...], recursion)
         split_pairs(q_ref[...], q_all, True)
         split_pairs(do_ref[...], do_all, False)
         prod = do_ref[...].astype(F32) * att_ref[...].astype(F32)
         for h in range(width // HEAD_DIM):
             dot_all[h] = jnp.sum(prod[:, h * HEAD_DIM : (h + 1) * HEAD_DIM], axis=1, keepdims=True)
 
-    kv = jnp.concatenate([k[...] for k in key_refs], axis=0)
-    for j in range(GROUP):
-        h = g * GROUP + j
-        here = slice(j * rows, (j + 1) * rows)
-        s = dotf(q_all[h], kv, NT) * SCALE + bias[...]
-        p = jnp.exp(s - lse_ref[0, :, j : j + 1])
-        dp = dotf(do_all[h], kv, NT)
-        ds = (p * (dp - dot_all[h])).astype(BF16)
-        p3[here, :] = p.astype(BF16)
-        ds3[here, :] = ds
-        dq = dotf(ds, kv) * SCALE
-        dq_all[h] = dq * cos_ref[...] - turn(dq) * sin_ref[...]
-    q3 = jnp.concatenate([q_all[g * GROUP + j] for j in range(GROUP)], axis=0)
-    do3 = jnp.concatenate([do_all[g * GROUP + j] for j in range(GROUP)], axis=0)
-    dkv = dotf(q3, ds3[...], TN) * SCALE + dotf(do3, p3[...], TN)
-    dkv_ref[...] = dkv.T.astype(BF16)
+    def body(m, n):
+        @pl.when(g == 0)
+        def _():
+            bias[:m, :n] = make_bias(row_ref[:m], col_ref[:, :n], recursion)
+
+        kv = keys[:n, :]
+        cos, sin = turns(row_ref[:m], False)
+        for j in range(GROUP):
+            h = g * GROUP + j
+            here = slice(j * m, (j + 1) * m)
+            s = dotf(q_all[h, :m], kv, NT) * SCALE + bias[:m, :n]
+            lane = lax.broadcasted_iota(jnp.int32, (m, LANES), 1)
+            p = jnp.exp(s - jnp.sum(jnp.where(lane == h, lse_ref[:m], 0.0), axis=1, keepdims=True))
+            dp = dotf(do_all[h, :m], kv, NT)
+            ds = (p * (dp - dot_all[h, :m])).astype(BF16)
+            p3[here, :n] = p.astype(BF16)
+            ds3[here, :n] = ds
+            dq = dotf(ds, kv) * SCALE
+            dq_all[h, :m] = dq * cos - turn(dq) * sin
+            if m < rows:
+                dq_all[h, m:] = jnp.zeros((rows - m, LANES), F32)
+        q3 = jnp.concatenate([q_all[g * GROUP + j, :m] for j in range(GROUP)], axis=0)
+        do3 = jnp.concatenate([do_all[g * GROUP + j, :m] for j in range(GROUP)], axis=0)
+        dkv = dotf(q3, ds3[: GROUP * m, :n], TN) * SCALE + dotf(do3, p3[: GROUP * m, :n], TN)
+        back[:n, :] = dkv.T
+
+    choose(meta_ref, variants, body)
+    spot = lax.broadcasted_iota(jnp.int32, (rows, LANES), 0)
+    for block in range(dkv_ref.shape[0] // rows):
+        part = back[pl.ds(pl.multiple_of(meta_ref[2 + 2 * block], 16), rows), :]
+        part = jnp.where(spot < meta_ref[3 + 2 * block], part, 0.0)
+        dkv_ref[block * rows : (block + 1) * rows, :] = part.astype(BF16)
 
     @pl.when(g == pl.num_programs(0) - 1)
     def _():
         join_pairs(dq_all, dq_ref, True)
 
 
-def attend_back_call(recursion, q, do, att, kvs, lse, row_info, col_info, cos, sin):
+def attend_back_call(recursion, variants, meta, q, do, att, kv, lse, row_info, col_info):
     rows, width = q.shape
-    keys = sum(k.shape[0] for k in kvs)
-    groups = kvs[0].shape[1] // LANES
+    keys, groups = kv.shape[0], kv.shape[1] // LANES
     heads = groups * GROUP
-    return pl.pallas_call(
-        functools.partial(attend_back_kernel, recursion, len(kvs)),
-        grid=(groups,),
-        in_specs=[whole(rows, width)] * 3
-        + [pl.BlockSpec((k.shape[0], LANES), lambda g: (0, g)) for k in kvs]
-        + [pl.BlockSpec((1, rows, GROUP), lambda g: (g, 0, 0)), whole(rows, 2), whole(3, keys)]
-        + [whole(rows, LANES)] * 2,
-        out_specs=[whole(rows, width), pl.BlockSpec((keys, LANES), lambda g: (0, g))],
-        out_shape=[
-            jax.ShapeDtypeStruct((rows, width), BF16),
-            jax.ShapeDtypeStruct((keys, groups * LANES), BF16),
-        ],
-        scratch_shapes=[
+    return call(
+        functools.partial(attend_back_kernel, recursion, variants),
+        "attend_back",
+        meta,
+        (groups,),
+        (q, do, att, kv, lse, row_info, col_info),
+        [whole(rows, width)] * 3
+        + [pl.BlockSpec((keys, LANES), lambda g, s: (0, g)), whole(rows, LANES), whole(*row_info.shape), whole(3, keys)],
+        [whole(rows, width), pl.BlockSpec((keys, LANES), lambda g, s: (0, g))],
+        [jax.ShapeDtypeStruct((rows, width), BF16), jax.ShapeDtypeStruct((keys, groups * LANES), BF16)],
+        [
             pltpu.VMEM((rows, keys), F32),
+            pltpu.VMEM((keys, LANES), F32),
             pltpu.VMEM((heads, rows, LANES), BF16),
             pltpu.VMEM((heads, rows, LANES), BF16),
             pltpu.VMEM((heads, rows, 1), F32),
@@ -237,65 +315,271 @@
             pltpu.VMEM((GROUP * rows, keys), BF16),
             pltpu.VMEM((heads, rows, LANES), F32),
         ],
-        compiler_params=pltpu.CompilerParams(vmem_limit_bytes=48 * MIB),
-        cost_estimate=pl.CostEstimate(
-            flops=10 * rows * keys * LANES * heads,
-            bytes_accessed=8 * q.size + 4 * keys * groups * LANES,
-            transcendentals=heads * rows * keys,
-        ),
-        name="attend_back",
-    )(q, do, att, *kvs, lse, row_info, col_info, cos, sin)
+        32,
+        10 * rows * keys * LANES * heads,
+        8 * q.size + 4 * keys * groups * LANES,
+    )
+
+
+IN_VMEM = pl.BlockSpec(memory_space=pltpu.VMEM)
+
+
+def inverse(x):
+    return lax.rsqrt(jnp.mean(x * x, axis=-1, keepdims=True) + NORM_EPSILON)
+
+
+def sigmoid(x):
+    return 1.0 / (1.0 + jnp.exp(-x))
+
+
+def roles(core, a, b):
+    return jnp.where(core == 0, a, b), jnp.where(core == 0, b, a)
+
+
+def by_steps(width, step, do):
+    def one(c, _):
+        do(pl.ds(pl.multiple_of(c * step, step), step))
+        return 0
+
+    lax.fori_loop(0, width // step, one, 0)
+
+
+def post_kernel(variants, step, meta_ref, att, state, wo, gain, router_row, active, mine, theirs, down, *refs):
+    following, after, normed2, branch, router, gate_ref, up_ref, inner_ref = refs
+    core, width = meta_ref[1], state.shape[1]
+
+    def body(m, _):
+        attn = dotf(att[:m], wo[:, :width])
+        x = state[:m] + attn
+        after[:m, :] = x
+        normed2[:m, :] = (x * inverse(x) * gain[...]).astype(BF16)
+        branch[:m, :] = attn
+
+        def part(cols):
+            n2 = normed2[:m, :]
+            gate, up = roles(core, dotf(n2, mine[:, cols]), dotf(n2, theirs[:, cols]))
+            inner = (gate * sigmoid(gate) * up).astype(BF16)
+            inner_ref[:m, cols] = inner
+            gate_ref[:m, cols] = gate.astype(BF16)
+            up_ref[:m, cols] = up.astype(BF16)
+            branch[:m, :] += dotf(inner, down[cols, :])
+
+        by_steps(inner_ref.shape[1], step, part)
+        clear(m, after, normed2, branch, inner_ref, gate_ref, up_ref)
+
+    choose(meta_ref, variants, body)
+    x = state[...]
+    router[...] = sigmoid(jnp.sum(x * router_row[...], axis=-1, keepdims=True))
+    following[...] = x + active[...] * router[...] * branch[...]
+
+
+def post_call(variants, meta, att, state, w, router_row, active, step=512):
+    rows, width = state.shape
+    ff = w["mine"].shape[1]
+    shape = jax.ShapeDtypeStruct
+    inputs = (att, state, w["wide_o"], w["gain_f"], router_row, active, w["mine"], w["theirs"], w["down"])
+    outputs = [shape((rows, width), F32), shape((rows, width), F32), shape((rows, width), BF16), shape((rows, width), F32)]
+    outputs += [shape((rows, 1), F32)] + [shape((rows, ff), BF16)] * 3
+    return call(
+        functools.partial(post_kernel, variants, step),
+        "post",
+        meta,
+        (1,),
+        inputs,
+        [IN_VMEM] * len(inputs),
+        [IN_VMEM] * len(outputs),
+        outputs,
+        [],
+        16,
+        2 * rows * width * (width + 3 * ff),
+        2 * width * (width + 3 * ff),
+    )
+
+
+def post_back_kernel(
+    variants, step, meta_ref, grad, branch, state, after, router, active, router_row, gain, wo, gate_ref, up_ref, mine, theirs,
+    down, g_ffn, g_state, g_attn, g_att, g_router, g_gain, g_mine_ref, g_theirs_ref, g_branch, g_normed2,
+):
+    core, width = meta_ref[1], state.shape[1]
+
+    def body(m, _):
+        g = grad[:m]
+        weight = active[:m] * router[:m]
+        logit = jnp.sum(g * branch[:m], axis=-1, keepdims=True) * weight * (1.0 - router[:m])
+        g_router[...] = jnp.sum(logit * state[:m], axis=0, keepdims=True)
+        g_state[:m, :] = g + logit * router_row[...]
+        if m < grad.shape[0]:
+            g_state[m:, :] = grad[m:]
+        low = g * weight
+        g_branch[:m, :] = low
+        g_ffn[:m, :] = low.astype(BF16)
+        g_normed2[:m, :] = jnp.zeros((m, width), F32)
+
+        def part(cols):
+            g_inner = dotf(g_ffn[:m, :], down[cols, :], NT)
+            gate, up = gate_ref[:m, cols].astype(F32), up_ref[:m, cols].astype(F32)
+            sig = sigmoid(gate)
+            g_gate = (g_inner * up * sig * (1.0 + gate * (1.0 - sig))).astype(BF16)
+            g_up = (g_inner * gate * sig).astype(BF16)
+            g_mine, g_theirs = roles(core, g_gate, g_up)
+            g_mine_ref[:m, cols] = g_mine
+            g_theirs_ref[:m, cols] = g_theirs
+            g_normed2[:m, :] += dotf(g_mine, mine[:, cols], NT) + dotf(g_theirs, theirs[:, cols], NT)
+
+        by_steps(gate_ref.shape[1], step, part)
+        x, g = after[:m], g_normed2[:m, :]
+        factor = inverse(x)
+        unit = x * factor
+        g_gain[...] = jnp.sum(g * unit, axis=0, keepdims=True)
+        scaled = g * gain[...]
+        g_after = factor * (scaled - unit * jnp.mean(scaled * unit, axis=-1, keepdims=True))
+        g_state[:m, :] += g_after
+        low = (g_after + g_branch[:m, :]).astype(BF16)
+        g_attn[:m, :] = low
+        g_att[:m, :] = dotf(low, wo[:, :width], NT).astype(BF16)
+        clear(m, g_ffn, g_attn, g_att, g_mine_ref, g_theirs_ref)
+
+    choose(meta_ref, variants, body)
+
+
+def expand_back_kernel(step, meta_ref, g_ffn, gate_ref, up_ref, down, g_mine_ref, g_theirs_ref):
+    core = meta_ref[1]
+
+    def part(cols):
+        g_inner = dotf(g_ffn[...], down[cols, :], NT)
+        gate, up = gate_ref[:, cols].astype(F32), up_ref[:, cols].astype(F32)
+        sig = sigmoid(gate)
+        g_gate = (g_inner * up * sig * (1.0 + gate * (1.0 - sig))).astype(BF16)
+        g_up = (g_inner * gate * sig).astype(BF16)
+        g_mine_ref[:, cols], g_theirs_ref[:, cols] = roles(core, g_gate, g_up)
+
+    by_steps(gate_ref.shape[1], step, part)
+
+
+def expand_back_call(meta, g_ffn, gate, up, w, step=512):
+    inputs = (g_ffn, gate, up, w["down"])
+    return call(
+        functools.partial(expand_back_kernel, step),
+        "expand_back",
+        meta,
+        (1,),
+        inputs,
+        [IN_VMEM] * len(inputs),
+        [IN_VMEM] * 2,
+        [jax.ShapeDtypeStruct(gate.shape, BF16)] * 2,
+        [],
+        16,
+        2 * gate.size * g_ffn.shape[1],
+        2 * w["down"].size,
+    )
+
+
+def norm_back_kernel(step, meta_ref, g_mine, g_theirs, mine, theirs, after, gain, g_branch, grad, wo, g_state, g_attn, g_att, g_gain):
+    width = after.shape[1]
+    g = dotf(g_mine[...], mine[...], NT) + dotf(g_theirs[...], theirs[...], NT)
+    x = after[...]
+    factor = inverse(x)
+    unit = x * factor
+    g_gain[...] = jnp.sum(g * unit, axis=0, keepdims=True)
+    scaled = g * gain[...]
+    g_after = factor * (scaled - unit * jnp.mean(scaled * unit, axis=-1, keepdims=True))
+    g_state[...] = grad[...] + g_after
+    low = (g_after + g_branch[...]).astype(BF16)
+    g_attn[...] = low
+    g_att[...] = dotf(low, wo[:, :width], NT).astype(BF16)
+
+
+def norm_back_call(meta, g_mine, g_theirs, after, g_branch, grad, w, step=512):
+    rows, width = after.shape
+    inputs = (g_mine, g_theirs, w["mine"], w["theirs"], after, w["gain_f"], g_branch, grad, w["wide_o"])
+    shape = jax.ShapeDtypeStruct
+    outputs = [shape((rows, width), k) for k in (F32, BF16, BF16)] + [shape((1, width), F32)]
+    return call(
+        functools.partial(norm_back_kernel, step),
+        "norm_back",
+        meta,
+        (1,),
+        inputs,
+        [IN_VMEM] * len(inputs),
+        [IN_VMEM] * len(outputs),
+        outputs,
+        [],
+        16,
+        2 * rows * width * (width + 2 * g_mine.shape[1]),
+        2 * width * (width + 2 * g_mine.shape[1]),
+    )
+
+
+def post_back_call(variants, meta, grad, branch, state, after, router, active, router_row, gate, up, w, step=512):
+    rows, width = state.shape
+    ff = w["mine"].shape[1]
+    shape = jax.ShapeDtypeStruct
+    inputs = (grad, branch, state, after, router, active, router_row, w["gain_f"], w["wide_o"], gate, up)
+    inputs += (w["mine"], w["theirs"], w["down"])
+    outputs = [shape((rows, width), k) for k in (BF16, F32, BF16, BF16)]
+    outputs += [shape((1, width), F32)] * 2 + [shape((rows, ff), BF16)] * 2
+    return call(
+        functools.partial(post_back_kernel, variants, step),
+        "post_back",
+        meta,
+        (1,),
+        inputs,
+        [IN_VMEM] * len(inputs),
+        [IN_VMEM] * len(outputs),
+        outputs,
+        [pltpu.VMEM((rows, width), F32)] * 2,
+        16,
+        2 * rows * width * (width + 3 * ff),
+        2 * width * (width + 3 * ff),
+    )
 
 
 def qkv_back_kernel(
-    dq_ref, mine_ref, got_ref, wq_ref, wkv_ref, x_ref, gain_ref, up_ref, ck_ref, sk_ref, dkv_ref, out_ref, gain_grad_ref
+    variants, meta_ref, dq_ref, mine_ref, got_ref, wq_ref, wkv_ref, x_ref, gain_ref, up_ref, table_ref,
+    dkv_ref, out_ref, gain_grad_ref,
 ):
-    cos, sin = ck_ref[...], sk_ref[...]
-    for at in range(0, dkv_ref.shape[1], LANES):
-        cols = slice(at, at + LANES)
-        u = mine_ref[:, cols].astype(F32) + got_ref[:, cols].astype(F32)
-        dkv_ref[:, cols] = (u * cos - turn(u) * sin).astype(BF16)
-    g = dotf(dq_ref[...], wq_ref[...], NT) + dotf(dkv_ref[...], wkv_ref[...], NT)
-    x = x_ref[...]
-    factor = lax.rsqrt(jnp.mean(x * x, axis=-1, keepdims=True) + NORM_EPSILON)
-    unit = x * factor
-    gain_grad_ref[...] = jnp.sum(g * unit, axis=0, keepdims=True)
-    scaled = g * gain_ref[...]
-    out_ref[...] = up_ref[...] + factor * (scaled - unit * jnp.mean(scaled * unit, axis=-1, keepdims=True))
-
-
-def qkv_back_call(dq, mine, got, wq, wkv, x, gain, upstream, cos, sin):
+    def body(m, _):
+        cos, sin = turns(table_ref[:m], True)
+        for at in range(0, dkv_ref.shape[1], LANES):
+            cols = slice(at, at + LANES)
+            u = mine_ref[:m, cols].astype(F32) + got_ref[:m, cols].astype(F32)
+            dkv_ref[:m, cols] = (u * cos - turn(u) * sin).astype(BF16)
+        clear(m, dkv_ref)
+        g = dotf(dq_ref[:m], wq_ref[:, : dq_ref.shape[1]], NT) + dotf(dkv_ref[:m, :], wkv_ref[...], NT)
+        x = x_ref[:m]
+        factor = inverse(x)
+        unit = x * factor
+        gain_grad_ref[...] = jnp.sum(g * unit, axis=0, keepdims=True)
+        scaled = g * gain_ref[...]
+        out_ref[:m, :] = up_ref[:m] + factor * (scaled - unit * jnp.mean(scaled * unit, axis=-1, keepdims=True))
+        if m < up_ref.shape[0]:
+            out_ref[m:, :] = up_ref[m:]
+
+    choose(meta_ref, variants, body)
+
+
+def qkv_back_call(variants, meta, dq, mine, got, wq, wkv, x, gain, upstream, table):
     rows, width = x.shape
-    heads, both = wq.shape[1], wkv.shape[1]
-    return pl.pallas_call(
-        qkv_back_kernel,
-        grid=(1,),
-        in_specs=[
-            whole(rows, heads),
-            whole(rows, both),
-            whole(rows, both),
-            whole(width, heads),
-            whole(width, both),
-            whole(rows, width),
-            whole(1, width),
-            whole(rows, width),
-            whole(rows, LANES),
-            whole(rows, LANES),
-        ],
-        out_specs=[whole(rows, both), whole(rows, width), whole(1, width)],
-        out_shape=[
+    both = wkv.shape[1]
+    full, row, keys = whole(rows, width), whole(1, width), whole(rows, both)
+    return call(
+        functools.partial(qkv_back_kernel, variants),
+        "qkv_back",
+        meta,
+        (1,),
+        (dq, mine, got, wq, wkv, x, gain, upstream, table),
+        [full, keys, keys, whole(*wq.shape), whole(width, both), full, row, full, whole(*table.shape)],
+        [keys, full, row],
+        [
             jax.ShapeDtypeStruct((rows, both), BF16),
             jax.ShapeDtypeStruct((rows, width), F32),
             jax.ShapeDtypeStruct((1, width), F32),
         ],
-        compiler_params=pltpu.CompilerParams(vmem_limit_bytes=32 * MIB),
-        cost_estimate=pl.CostEstimate(
-            flops=2 * rows * width * (heads + both),
-            bytes_accessed=2 * width * (heads + both) + 16 * rows * width,
-            transcendentals=0,
-        ),
-        name="qkv_back",
-    )(dq, mine, got, wq, wkv, x, gain, upstream, cos, sin)
+        [],
+        32,
+        2 * rows * width * (width + both),
+        2 * width * (width + both) + 16 * rows * width,
+    )
 
 
 def weight_grad_kernel(fill, counts, stride, spot_ref, *refs):
@@ -393,12 +677,60 @@
             + [pltpu.SemaphoreType.DMA((len(sources),))],
         ),
         out_shape=[jax.ShapeDtypeStruct(s, BF16) for s in shapes],
-        compiler_params=pltpu.CompilerParams(vmem_limit_bytes=60 * MIB),
+        compiler_params=pltpu.CompilerParams(vmem_limit_bytes=24 * MIB),
         cost_estimate=pl.CostEstimate(
             flops=flops, bytes_accessed=2 * sum(a.size for a in sources + moving) + 16 * each * n, transcendentals=0
         ),
         name="weight_grad",
     )(spot, *sources, *moving, *extra)
+
+
+def settle_kernel(moves, spot_ref, *refs):
+    out = refs[-1]
+    for i, first, rows, place in moves:
+        out[pl.ds(pl.multiple_of(place(spot_ref), 16), rows), :] = refs[i][first : first + rows, : out.shape[1]]
+
+
+def copy_call(kernel, name, spot, arrays, shapes):
+    return pl.pallas_call(
+        kernel,
+        grid_spec=pltpu.PrefetchScalarGridSpec(
+            num_scalar_prefetch=1,
+            grid=(1,),
+            in_specs=[pl.BlockSpec(a.shape, lambda g, s: (0, 0)) for a in arrays],
+            out_specs=[pl.BlockSpec(shape, lambda g, s: (0, 0)) for shape in shapes],
+        ),
+        out_shape=[jax.ShapeDtypeStruct(shape, arrays[0].dtype) for shape in shapes],
+        compiler_params=pltpu.CompilerParams(vmem_limit_bytes=32 * MIB),
+        cost_estimate=pl.CostEstimate(flops=0, bytes_accessed=4 * sum(a.size for a in arrays), transcendentals=0),
+        name=name,
+    )(spot, *arrays)
+
+
+def settle_call(spot, arrays, moves, rows, width=None):
+    shape = (rows, width or arrays[0].shape[1])
+    (out,) = copy_call(functools.partial(settle_kernel, moves), "settle", spot, arrays, [shape])
+    return out
+
+
+def unpack_kernel(part, spot_ref, mine, theirs, q_out, o_out, kv_out, tail_out):
+    both = kv_out.shape[1]
+    tail_out[...] = mine[:, mine.shape[1] - LANES :]
+
+    def go(first, second):
+        q_out[...] = first[:, part:]
+        o_out[...] = second[:, part:]
+        kv_out[:, :part] = first[:, :part]
+        kv_out[:, part:] = second[:, 2 * part - both : part]
+
+    pl.when(spot_ref[1] == 0)(lambda: go(mine, theirs))
+    pl.when(spot_ref[1] == 1)(lambda: go(theirs, mine))
+
+
+def unpack_call(spot, mine, theirs, part, both):
+    rows, width = mine.shape
+    shapes = [(rows, width - part), (rows, width - part), (rows, both), (rows, LANES)]
+    return copy_call(functools.partial(unpack_kernel, part), "unpack", spot, (mine, theirs), shapes)
 
 
 def tie(*trees):
@@ -419,6 +751,7 @@
         dp_at, cp_at = lax.axis_index("dp"), lax.axis_index("cp")
         self.core, self.z = dp_at % 2, dp_at // 2
         self.y, self.x = cp_at // 2, cp_at % 2
+        self.spot = jnp.stack([cp_at, self.core]).astype(jnp.int32)
 
     def over_x(self, a):
         return lax.ppermute(a, "cp", [(i, i ^ 1) for i in range(self.cp)])
@@ -439,11 +772,8 @@
                 pairs.append((d * self.cp + c, (2 * z + y) * self.cp + 2 * core + x))
         return lax.ppermute(a, ("dp", "cp"), pairs)
 
-    def key_blocks(self):
-        if not self.square:
-            return list(range(self.cp)), lax.axis_index("cp")
-        own = 2 * self.core + self.x
-        return [own ^ k for k in range(4)], own
+    def key_block(self):
+        return 2 * self.core + self.x if self.square else lax.axis_index("cp")
 
     def gather_keys(self, a, axis=0):
         if not self.square:
@@ -473,37 +803,53 @@
         top, low = a[:cut], a[cut:]
         return top, low, self.over_x(top), self.over_y(low)
 
-    def pair_up(self, spot, mine, got, axis=0):
-        return jnp.where(spot == 0, jnp.stack([mine, got], axis), jnp.stack([got, mine], axis))
-
-    def gather_pairs(self, parts):
+    def gather_second(self, parts):
         if not self.square:
             return parts
         top, low, from_x, from_y = parts
-        return self.pair_up(self.x, top, from_x), self.pair_up(self.y, low, from_y)
-
-    def gather_second(self, pairs):
-        if not self.square:
-            return pairs
-        top, low = pairs
-        return top, low, self.over_y(top), self.over_x(low)
+        over_y = self.over_y(jnp.concatenate([top, from_x], axis=0))
+        over_x = self.over_x(jnp.concatenate([low, from_y], axis=0))
+        return parts + (over_y, over_x)
 
     def gather_whole(self, parts):
         if not self.square:
             return parts[0]
-        top, low, from_y, from_x = parts
-        a = jnp.concatenate([self.pair_up(self.y, top, from_y), self.pair_up(self.x, low, from_x, 1)], axis=2)
-        return a.reshape(-1, a.shape[-1])
+        cut, rest = parts[0].shape[0], parts[1].shape[0]
+        rows = cut + rest
+
+        def move(i, first, count, block, offset):
+            return i, first, count, lambda spot: (spot[0] ^ block) * rows + offset
+
+        moves = [
+            move(0, 0, cut, 0, 0),
+            move(1, 0, rest, 0, cut),
+            move(2, 0, cut, 1, 0),
+            move(3, 0, rest, 2, cut),
+            move(4, 0, cut, 2, 0),
+            move(4, cut, cut, 3, 0),
+            move(5, 0, rest, 1, cut),
+            move(5, rest, rest, 3, cut),
+        ]
+        return settle_call(self.spot, parts, moves, 4 * rows)
+
+    def interleave(self, mine, theirs, width):
+        half = mine.shape[0] // self.cp
+
+        def move(i, block):
+            return i, block * half, half, lambda spot: (2 * block + (spot[1] if i == 0 else 1 - spot[1])) * half
+
+        moves = [move(i, block) for block in range(self.cp) for i in range(2)]
+        return settle_call(self.spot, (mine, theirs), moves, 2 * mine.shape[0], width)
 
 
     def halves(self, fill, lefts, rights, stride, each, n, step, extra=()):
         if self.square:
-            spot = jnp.stack([lax.axis_index("cp"), self.core]).astype(jnp.int32)
-            return weight_grad(spot, fill, lefts, rights, stride, each, n, step, extra)
+            return weight_grad(self.spot, fill, lefts, rights, stride, each, n, step, extra)
         products = []
 
         def product(left, right):
             a, b = (jnp.concatenate(group, axis=0) for group in (lefts[left], rights[right]))
+            b = jnp.pad(b, ((0, 0), (0, max(n - b.shape[1], 0)))) if fill is not fill_groups else b
             return dotf(a, b, TN).astype(BF16)
 
         if fill is fill_rows:
@@ -608,37 +954,78 @@
     return lax.rsqrt(jnp.mean(matrix * matrix, axis=-1, keepdims=True) + NORM_EPSILON)
 
 
-def norm_back(matrix, gain, upstream):
-    factor = inverse_rms(matrix)
-    unit = matrix * factor
-    scaled = upstream * gain
-    grad = factor * (scaled - unit * jnp.mean(scaled * unit, axis=-1, keepdims=True))
-    return grad, jnp.sum(upstream * unit, axis=0, keepdims=True)
-
-
-def rope_tables(places):
+def row_table(documents, places):
     half = HEAD_DIM // 2
     inverse = jnp.power(ROPE_BASE, -2.0 * jnp.arange(half, dtype=F32) / HEAD_DIM)
     angles = places.astype(F32)[:, None] * inverse[None, :]
     cos, sin = jnp.cos(angles), jnp.sin(angles)
-    cos, sin = jnp.concatenate([cos, cos], 1), jnp.concatenate([-sin, sin], 1)
-    one, zero = jnp.ones_like(cos), jnp.zeros_like(sin)
-    both = lambda a, b: jnp.concatenate([a, b], 1)
-    return both(cos, cos), both(sin, sin), both(cos, one), both(sin, zero)
+    spread = lambda a: jnp.broadcast_to(a.astype(F32)[:, None], (a.shape[0], LANES))
+    return jnp.concatenate([cos] * 4 + [-sin, sin] * 2 + [spread(documents), spread(places)], axis=1)
+
+
+def depth_order(depth):
+    steps = jnp.arange(depth.shape[0])
+    before = (depth[:, None] > depth[None, :]) | ((depth[:, None] == depth[None, :]) & (steps[:, None] < steps[None, :]))
+    return jnp.sum(before, axis=0)[None, :] == steps[:, None]
+
+
+def reorder(order, rows):
+    return dotf(order.astype(BF16), rows).astype(BF16)
+
+
+def all_keys(every, rows, core):
+    blocks = every.shape[1] // rows
+    spots = jnp.stack([rows * jnp.arange(blocks), jnp.full((blocks,), rows)], axis=1).reshape(-1)
+    return jnp.concatenate([jnp.stack([0, core]), spots]).astype(jnp.int32), every
+
+
+def active_keys(every, rows, core, square):
+    keys = every.shape[1]
+    blocks, steps = keys // rows, jnp.arange(rows)
+    levels = jnp.arange(1, RECUR)[:, None]
+    counts = jnp.sum((every[2][None] > levels).reshape(RECUR - 1, blocks, rows), axis=2)
+    taken = (counts + 15) // 16 * 16
+    ahead = jnp.arange(blocks)[:, None] < jnp.arange(blocks)[None, :]
+    starts = jnp.sum(jnp.where(ahead[None], taken[:, :, None], 0), axis=1)
+    target = jnp.where(steps < taken[:, :, None], starts[:, :, None] + steps, -1).reshape(RECUR - 1, 1, keys, 1)
+    hit = target == jnp.arange(keys)
+    cols = jnp.sum(jnp.where(hit, every[None, :, :, None] + 1, 0), axis=2) - 1
+    total = jnp.sum(taken, axis=1)
+    own = counts[:, 0] if square else jnp.max(counts, axis=1)
+    (m, n), (wide_m, wide_n), _ = variants_of(rows, keys)
+    body = jnp.where((own <= m) & (total <= n), 0, jnp.where((own <= wide_m) & (total <= wide_n), 1, 2))
+    spots = jnp.stack([starts, counts], axis=2).reshape(RECUR - 1, -1)
+    metas = jnp.concatenate([body[:, None], jnp.full_like(body, core)[:, None], spots], axis=1).astype(jnp.int32)
+    return [(metas[i], cols[i].astype(jnp.int32)) for i in range(RECUR - 1)]
 
 
 class Level:
-    def __init__(self, recursion, place, context):
-        self.recursion, self.place = recursion, place
-        self.tables, self.row_info, self.col_info, self.depth = context
+    def __init__(self, recursion, place, context, meta, col_info):
+        self.recursion, self.place, self.meta, self.col_info = recursion, place, meta, col_info
+        self.table, depth = context
+        rows, keys = self.table.shape[0], self.col_info.shape[1]
+        self.variants = variants_of(rows, keys) if recursion else ((rows, keys),)
+        self.active = (depth[:, None] > recursion).astype(F32)
 
     def project(self, state, w):
         self.state = state
-        self.q, self.kv, self.normed = qkv_call(state, w["gain_a"], w["q"], w["kv"], self.tables)
-
-    def attend(self, kvs, w):
-        self.kvs = kvs
-        self.att, self.lse = attend_call(self.recursion, self.q, kvs, self.row_info, self.col_info)
+        self.q, self.kv, self.normed = qkv_call(
+            self.variants, self.meta, state, w["gain_a"], w["q"], w["kv"], self.table
+        )
+
+    def attend(self, kvs):
+        self.att, self.lse, self.keys = attend_call(
+            self.recursion, self.variants, self.meta, self.q, kvs, self.table, self.col_info
+        )
+
+    def post(self, w):
+        self.router_row = w["router"][self.recursion][None, :]
+        state, self.after, self.normed2, self.branch, self.router, self.gate, self.up, self.inner = post_call(
+            self.variants, self.meta, self.att, self.state, w, self.router_row, self.active
+        )
+        return state
+
+    def widen(self, w):
         self.attn = dotf(self.att, w["o"])
         self.after = self.state + self.attn
         self.normed2 = (self.after * inverse_rms(self.after) * w["gain_f"]).astype(BF16)
@@ -651,9 +1038,8 @@
 
     def close(self, w):
         self.branch = self.attn + dotf(self.inner, w["down"])
-        self.router_row = w["router"][self.recursion]
+        self.router_row = w["router"][self.recursion][None, :]
         self.router = jax.nn.sigmoid(jnp.sum(self.state * self.router_row, axis=-1, keepdims=True))
-        self.active = (self.depth[:, None] > self.recursion).astype(F32)
         return self.state + self.active * self.router * self.branch
 
     def back_open(self, grad):
@@ -665,31 +1051,30 @@
         self.g_ffn = self.g_branch.astype(BF16)
 
     def back_expand(self, w):
-        g_inner = dotf(self.g_ffn, w["down"], NT)
-        gate, up = self.gate.astype(F32), self.up.astype(F32)
-        sig = jax.nn.sigmoid(gate)
-        g_gate = (g_inner * up * sig * (1.0 + gate * (1.0 - sig))).astype(BF16)
-        g_up = (g_inner * gate * sig).astype(BF16)
-        self.g_mine, self.g_theirs = self.place.pick(g_gate, g_up), self.place.pick(g_up, g_gate)
+        self.g_mine, self.g_theirs = expand_back_call(self.meta, self.g_ffn, self.gate, self.up, w)
 
     def back_norm(self, w):
-        g_normed2 = dotf(self.g_mine, w["mine"], NT) + dotf(self.g_theirs, w["theirs"], NT)
-        g_after, self.g_gain_f = norm_back(self.after, w["gain_f"], g_normed2)
-        self.g_state = self.g_state + g_after
-        self.g_attn = (g_after + self.g_branch).astype(BF16)
-        self.g_att = dotf(self.g_attn, w["o"], NT).astype(BF16)
+        self.g_state, self.g_attn, self.g_att, self.g_gain_f = norm_back_call(
+            self.meta, self.g_mine, self.g_theirs, self.after, self.g_branch, self.g_state, w
+        )
+
+    def post_back(self, grad, w):
+        out = post_back_call(
+            self.variants, self.meta, grad, self.branch, self.state, self.after, self.router, self.active, self.router_row,
+            self.gate, self.up, w,
+        )
+        self.g_ffn, self.g_state, self.g_attn, self.g_att, self.g_router, self.g_gain_f, self.g_mine, self.g_theirs = out
 
     def back_attend(self):
-        cos, sin = self.tables[:2]
         self.dq, dkv = attend_back_call(
-            self.recursion, self.q, self.g_att, self.att, self.kvs, self.lse, self.row_info, self.col_info, cos, sin
+            self.recursion, self.variants, self.meta, self.q, self.g_att, self.att, self.keys, self.lse, self.table,
+            self.col_info,
         )
         return dkv
 
     def back_project(self, mine, got, w):
-        cos, sin = self.tables[2:]
         self.dkv, grad, self.g_gain_a = qkv_back_call(
-            self.dq, mine, got, w["q"], w["kv"], self.state, w["gain_a"], self.g_state, cos, sin
+            self.variants, self.meta, self.dq, mine, got, w["q"], w["kv"], self.state, w["gain_a"], self.g_state, self.table
         )
         return grad
 
@@ -703,82 +1088,81 @@
     wkv = jnp.stack([wk.reshape(each, kv_heads, HEAD_DIM), wv.reshape(each, kv_heads, HEAD_DIM)], axis=2)
     wkv = wkv.reshape(each, -1)
     small = jnp.concatenate([gain_a[:, None], gain_f[:, None], router.T], axis=1)
-    blend = jnp.concatenate([wkv, wq, wo], axis=1)
-    half, both = blend.shape[1] // 2, wkv.shape[1]
-    blend = jnp.concatenate([place.pick(blend[:, :half], blend[:, half:]), small], axis=1)
-    part = place.gather_first(blend)
+    both = wkv.shape[1]
+    part = -(-both // (2 * LANES)) * LANES
+    spare = -(part + width + small.shape[1]) % LANES
+    blend = [place.pick(wkv[:, :part], wkv[:, both - part :]), place.pick(wq, wo), small, jnp.zeros((each, spare), BF16)]
+    blend = place.gather_first(jnp.concatenate(blend, axis=1))
     ids = place.move_tokens(jnp.stack([document_ids[0], recur_depth[0]]))
     state = place.move_tokens(tokens[0])
     gates = place.pick(gate, up)
     downs = place.pick(down[: down.shape[0] // 2], down[down.shape[0] // 2 :])
-    part, ids, state, gates, downs = tie(part, ids, state, gates, downs)
-
-    part = place.gather_second(place.gather_pairs(part))
+    padded = -(-width // LANES) * LANES
+    downs = jnp.pad(downs, ((0, 0), (0, padded - width)))
+    blend, ids, state, gates, downs = tie(blend, ids, state, gates, downs)
+
+    blend = place.gather_second(blend)
     steps = jnp.arange(rows, dtype=jnp.int32)
-    blocks, block = place.key_blocks()
+    order = depth_order(ids[1])
+    ids = jnp.stack([ids[0], place.key_block() * rows + steps, ids[1]])
+    ids = jnp.sum(jnp.where(order[None], ids[:, None, :], 0), axis=2)
     every = jnp.concatenate(place.gather_keys(ids, 1), axis=1)
-    spots = jnp.concatenate([b * rows + steps for b in blocks])
-    col_info = jnp.stack([every[0], spots, every[1]])
-    row_info = jnp.stack([ids[0], block * rows + steps], axis=1)
-    tables = rope_tables(row_info[:, 1])
-    context = (tables, row_info, col_info, ids[1])
-    part, context, state, gates = tie(part, context, state.astype(F32), gates)
+    table = row_table(ids[0], ids[1])
+    state = reorder(order, state)
+    context = (table, ids[2])
+    blend, context, order, state, gates, every = tie(blend, context, order, state.astype(F32), gates, every)
 
     g_part = place.gather_first(gates)
-    mine = place.gather_whole(part)
+    mine = place.gather_whole(blend)
     theirs = place.over_core(mine)
-    w = {"gain_a": mine[:, half][None, :].astype(F32), "gain_f": mine[:, half + 1][None, :].astype(F32)}
-    w["router"] = mine[:, half + 2 :].T.astype(F32)
-    blend = jnp.concatenate([place.pick(mine, theirs)[:, :half], place.pick(theirs, mine)[:, :half]], axis=1)
-    w["kv"], w["q"], w["o"] = blend[:, :both], blend[:, both : both + width], blend[:, both + width :]
-    levels = [Level(r, place, context) for r in range(RECUR)]
-    first = levels[0]
+    w = dict(zip(("q", "o", "kv", "tail"), unpack_call(place.spot, mine, theirs, part, both)))
+    edge = width % LANES
+    small = w["tail"][:, edge : edge + small.shape[1]].T.astype(F32)
+    w["wide_o"], w["o"] = w["o"], w["o"][:, :width]
+    w["gain_a"], w["gain_f"], w["router"] = small[:1], small[1:2], small[2:]
+    first = Level(0, place, context, *all_keys(every, rows, place.core))
     first.project(state, w)
-    g_part = place.gather_pairs(g_part)
     first.kv, g_part, downs = tie(first.kv, g_part, downs)
 
     kvs = place.gather_keys(first.kv)
-    kvs, g_part, downs = tie(kvs, g_part, downs)
+    kvs, g_part, downs, every = tie(kvs, g_part, downs, every)
 
     g_part = place.gather_second(g_part)
     d_part = place.gather_first(downs)
-    first.attend(kvs, w)
-    first.normed2, g_part, d_part = tie(first.normed2, g_part, d_part)
-
-    d_part = place.gather_second(place.gather_pairs(d_part))
+    first.attend(kvs)
+    first.widen(w)
+    later = active_keys(every, rows, place.core, place.square)
+    first.normed2, g_part, d_part, later = tie(first.normed2, g_part, d_part, later)
+    levels = [first] + [Level(r + 1, place, context, *found) for r, found in enumerate(later)]
+
+    d_part = place.gather_second(d_part)
     w["mine"] = place.gather_whole(g_part)
     w["theirs"] = place.over_core(w["mine"])
     first.expand(w)
     first.inner, d_part = tie(first.inner, d_part)
 
     mine = place.gather_whole(d_part)
-    theirs = place.over_core(mine)
-    mine, theirs = (a.reshape(cp, -1, width) for a in (mine, theirs))
-    w["down"] = jnp.stack([place.pick(mine, theirs), place.pick(theirs, mine)], axis=1).reshape(-1, width)
+    w["down"] = place.interleave(mine, place.over_core(mine), width)
     state = first.close(w)
 
     for level in levels[1:]:
         level.project(state, w)
-        level.attend(place.gather_keys(level.kv), w)
-        level.expand(w)
-        state = level.close(w)
-    activations = place.move_tokens(state.astype(BF16))[None]
-    grad = place.move_tokens(cotangent[0]).astype(F32)
+        level.attend(place.gather_keys(level.kv))
+        state = level.post(w)
+    activations = place.move_tokens(reorder(order.T, state.astype(BF16)))[None]
+    grad = reorder(order, place.move_tokens(cotangent[0])).astype(F32)
 
     for level in levels[:0:-1]:
-        level.back_open(grad)
-        level.back_expand(w)
-        level.back_norm(w)
+        level.post_back(grad, w)
         pair = place.scatter_keys_second(place.scatter_keys_first(level.back_attend()))
         grad = level.back_project(*pair, w)
 
     every = lambda name: [getattr(level, name) for level in levels]
     ff = gate.shape[1]
-    part = -(-both // (2 * LANES)) * LANES
 
     grad, activations = tie(grad, activations)
     first.back_open(grad)
-    d = place.halves(fill_rows, [every("inner")], [every("g_ffn")], ff // cp, ff // cp // 2, width, 512)
+    d = place.halves(fill_rows, [every("inner")], [every("g_ffn")], ff // cp, ff // cp // 2, padded, 512)
     d_got = place.over_core(d[-1])
     first.back_expand(w)
     d = place.scatter_ready(d, d_got)
@@ -804,7 +1188,7 @@
     (pair,) = tie(pair)
     pair = place.scatter_keys_second(pair)
     lefts, rights = [every("att"), every("normed")], [every("g_attn"), every("dq")]
-    p = place.halves(fill_choice, lefts, rights, each, each, width, 512)
+    p = place.halves(fill_choice, lefts, rights, each, each, padded, 512)
     u, pair, p = tie(u, pair, p)
 
     u = place.scatter_second(u)
@@ -835,7 +1219,7 @@
 
     a, v = place.z_second(a), place.z_third(v)
     d = place.z_third(d)
-    input_grad = place.move_tokens(grad.astype(BF16))[None]
+    input_grad = place.move_tokens(reorder(order.T, grad.astype(BF16)))[None]
     a, v, d, input_grad = tie(a, v, d, input_grad)
 
     a = place.z_third(a)
@@ -844,7 +1228,7 @@
     u_own = jnp.concatenate([place.z_whole(u), place.z_whole(v)], axis=0)
     u_other = place.over_core(u_own)
     grad_gate, grad_up = place.pick(u_own, u_other).astype(F32), place.pick(u_other, u_own).astype(F32)
-    d_own, d_other = (b.reshape(-1, width) for b in (d_own, d_other))
+    d_own, d_other = d_own[:, :width], d_other[:, :width]
     grad_down = jnp.concatenate([place.pick(d_own, d_other), place.pick(d_other, d_own)], axis=0).astype(F32)
     a, grad_gate, grad_up, grad_down = tie(a, grad_gate, grad_up, grad_down)
 
@@ -857,10 +1241,10 @@
     return (
         activations,
         input_grad,
-        high[:, part + LANES :],
+        high[:, part + LANES : part + LANES + width],
         grad_kv[:, :, 0].reshape(each, -1),
         grad_kv[:, :, 1].reshape(each, -1),
-        low[:, part + LANES :],
+        low[:, part + LANES : part + LANES + width],
         grad_gate,
         grad_up,
         grad_down,

time: 646 us -> 589 us (0.912)
  matrix products: 75.4 us -> 13.6 us
  local copies, waits for them, and re-layouts: 67.6 us -> 89.4 us
  other arithmetic: 79.1 us -> 59.1 us
  Pallas kernels: 154 us -> 172 us
  waiting for transfers between devices: 175 us -> 164 us
    dot_general x24 -> x8, matrix products: 75.4 us -> 13.6 us  [dotf(): return lax.dot_general(a, b, dims, preferred_element_type=F32)]
    unnamed x313 -> x393, local copies, waits for them, and re-layouts: 25.8 us -> 69 us
    pallas_call x12 -> x23, Pallas kernels: 107 us -> 136 us  [the longest x18 126 us: call(): pl.pallas_call(kernel, grid_spec=pltpu.PrefetchScalarGridSpec(num_scalar_...]
    ppermute x15, waiting for transfers between devices: 40 us -> 17.9 us  [over_y(): return lax.ppermute(a, 'cp', [(i, i ^ 2) for i in range(self.cp)])]
    select_n x10 -> x5, other arithmetic: 18.1 us -> 2.51 us  [pick(): return jnp.where(self.core == 0, a, b)]
    ppermute x12, waiting for transfers between devices: 33.2 us -> 44.8 us  [hop(): lax.ppermute(a, 'dp', [(2 * s + c, 2 * t + c) for s, t in moves for c in...]
    pallas_call x4, Pallas kernels: 47.2 us -> 36.2 us  [weight_grad(): pl.pallas_call(functools.partial(weight_grad_kernel, fill, (len(lefts), l...]
    ppermute x2 -> x0, local copies, waits for them, and re-layouts: 8.96 us -> none  [over_core(): return lax.ppermute(a, 'dp', [(i, i ^ 1) for i in range(self.dp)])]
  transfers between devices with their start and end apart: 75 -> 75, of which waited for: 33 -> 36; matrix products, arithmetic and copies ran while one was open for 16% -> 13% of each run, Pallas kernels for 13% -> 17%
where the time goes in v3:
time: 589 us; the launch traced here: 581 us
  Pallas kernels  172 us (29%)
  waiting for transfers between devices  164 us (28%)
  local copies, waits for them, and re-layouts  89.4 us (15%)
  starting transfers between devices  79.3 us (13%)
  other arithmetic  59.1 us (10%)
  matrix products  13.6 us (2%)
    pallas_call x18, Pallas kernels, call(): pl.pallas_call(kernel, grid_spec=pltpu.PrefetchScalarGridSpec(num_scalar_...  126 us
    ppermute x22, waiting for transfers between devices, over_x(): return lax.ppermute(a, 'cp', [(i, i ^ 1) for i in range(self.cp)])  85.4 us
    unnamed x393, local copies, waits for them, and re-layouts  69 us
    ppermute x12, waiting for transfers between devices, hop(): lax.ppermute(a, 'dp', [(2 * s + c, 2 * t + c) for s, t in moves for c in...  44.8 us
    pallas_call x4, Pallas kernels, weight_grad(): pl.pallas_call(functools.partial(weight_grad_kernel, fill, (len(lefts), l...  36.2 us
    ppermute x12, starting transfers between devices, hop(): lax.ppermute(a, 'dp', [(2 * s + c, 2 * t + c) for s, t in moves for c in...  26.9 us
    convert_element_type x32, other arithmetic, add(): return sum((a.astype(F32) for a in terms)).astype(BF16)  26.4 us
    ppermute x22, starting transfers between devices, over_x(): return lax.ppermute(a, 'cp', [(i, i ^ 1) for i in range(self.cp)])  21.5 us
  transfers between devices with their start and end apart: 75, of which 36 were waited for; matrix products, arithmetic and copies ran while one was open for 13% of the time, Pallas kernels for 17%

profile of v3, /device:TPU:0, one launch (start us, length us, event | category | flops | bytes accessed | tf_op | source)
XLA Modules:
  0.0 581.3 jit_solution(8363761964483726655)
XLA Ops:
  12.4 6.1 %collective-permute-start.3 = (bf16[288,960]{1,0:T(8,128)(2,1)}, bf16[288,960]{1,0:T(8,128)(2,1)}, u32[]{:S(2)}, u32[]{:S(2)}) collective-permute-start(bf16[288,960]{1,0:T(8,128)(2,1)} %bitcast.6), channel_id=1, source_target_pairs={{0,0},{1,1},{2,4},{3,5},{4,2},{5,3},{6,6},{7,7},{8,8},{9,9},{10,12... | collective-permute-start | bytes 1658888 | tf_op jit(solution)/shard_map/ppermute | solution.py:773
  34.7 8.2 %collective-permute-done.6 = s32[3,288]{1,0:T(4,128)S(1)} collective-permute-done((s32[3,288]{1,0:T(4,128)S(1)}, s32[3,288]{1,0:T(4,128)S(1)}, u32[]{:S(2)}, u32[]{:S(2)}) %collective-permute-start.6) | collective-permute-done | bytes 3488 | tf_op jit(solution)/shard_map/ppermute | solution.py:757
  74.6 8.9 %collective-permute-done.12.refs_1_ = bf16[288,640]{1,0:T(8,128)(2,1)} collective-permute-done((bf16[288,640]{1,0:T(8,128)(2,1)}, bf16[288,640]{1,0:T(8,128)(2,1)}, u32[]{:S(2)}, u32[]{:S(2)}) %collective-permute-start.12) | collective-permute-done | bytes 368672 | tf_op jit(solution)/shard_map/ppermute | solution.py:757
  100.4 15.0 %attend.3 = (bf16[288,960]{1,0:T(8,128)(2,1)S(1)}, f32[288,128]{1,0:T(8,128)S(1)}, bf16[1152,640]{1,0:T(8,128)(2,1)S(1)}) custom-call(s32[10]{0:T(128)S(1)} %copy-done.92, bf16[288,960]{1,0:T(8,128)(2,1)S(1)} %copy-done.112, bf16[288,640]{1,0:T(8,128)(2,1)} %get-tuple-element.321.refs_0_, bf16[288,640]{1,0:T(8,128)(2,1)} %collective-permute-done.12.refs_1_, ...), custom_call_target="tpu_custom_call" | custom-call | flops 2548039680 | bytes 2580480 | tf_op jit(solution)/shard_map/attend/pallas_call | solution.py:54
  120.6 5.5 select_reduce_fusion
  137.3 4.7 collective-permute-done.19.theirs
  155.1 4.8 collective-permute-done.22.refs_1_
  166.5 10.0 %collective-permute-done.23.refs_1_ = bf16[288,640]{1,0:T(8,128)(2,1)S(1)} collective-permute-done((bf16[288,640]{1,0:T(8,128)(2,1)S(1)}, bf16[288,640]{1,0:T(8,128)(2,1)S(1)}, u32[]{:S(2)}, u32[]{:S(2)}) %collective-permute-start.23) | collective-permute-done | bytes 368672 | tf_op jit(solution)/shard_map/ppermute | solution.py:757
  178.2 9.9 %attend.4 = (bf16[288,960]{1,0:T(8,128)(2,1)S(1)}, f32[288,128]{1,0:T(8,128)S(1)}, bf16[1152,640]{1,0:T(8,128)(2,1)S(1)}) custom-call(s32[10]{0:T(128)S(1)} %get-tuple-element.333.meta_ref, bf16[288,960]{1,0:T(8,128)(2,1)S(1)} %get-tuple-element.353.q_ref, bf16[288,640]{1,0:T(8,128)(2,1)S(1)} %get-tuple-element.355.refs_0_, ...), custom_call_target="tpu_custom_call" | custom-call | flops 2548039680 | bytes 2580480 | tf_op jit(solution)/shard_map/attend/pallas_call | solution.py:54
  189.9 7.3 %post.2 = (f32[288,960]{1,0:T(8,128)S(1)}, f32[288,960]{1,0:T(8,128)S(1)}, bf16[288,960]{1,0:T(8,128)(2,1)S(1)}, f32[288,960]{1,0:T(8,128)S(1)}, f32[288,1]{1,0:...) custom-call(s32[10]{0:T(128)S(1)} %get-tuple-element.333.meta_ref, ...), custom_call_target="tpu_custom_call" | custom-call | flops 4777574400 | bytes 16588800 | tf_op jit(solution)/shard_map/post/pallas_call | solution.py:54
  204.8 9.6 %collective-permute-done.27.refs_1_ = bf16[288,640]{1,0:T(8,128)(2,1)S(1)} collective-permute-done((bf16[288,640]{1,0:T(8,128)(2,1)S(1)}, bf16[288,640]{1,0:T(8,128)(2,1)S(1)}, u32[]{:S(2)}, u32[]{:S(2)}) %collective-permute-start.27) | collective-permute-done | bytes 368672 | tf_op jit(solution)/shard_map/ppermute | solution.py:757
  216.1 6.9 %attend.5 = (bf16[288,960]{1,0:T(8,128)(2,1)S(1)}, f32[288,128]{1,0:T(8,128)S(1)}, bf16[1152,640]{1,0:T(8,128)(2,1)S(1)}) custom-call(s32[10]{0:T(128)S(1)} %get-tuple-element.354.meta_ref, bf16[288,960]{1,0:T(8,128)(2,1)S(1)} %get-tuple-element.359.q_ref, bf16[288,640]{1,0:T(8,128)(2,1)S(1)} %get-tuple-element.361.refs_0_, ...), custom_call_target="tpu_custom_call" | custom-call | flops 2548039680 | bytes 2580480 | tf_op jit(solution)/shard_map/attend/pallas_call | solution.py:54
  223.0 5.7 post.3
  231.8 8.2 %post_back.2 = (bf16[288,960]{1,0:T(8,128)(2,1)S(1)}, f32[288,960]{1,0:T(8,128)S(1)}, bf16[288,960]{1,0:T(8,128)(2,1)S(1)}, bf16[288,960]{1,0:T(8,128)(2,1)S(1)}...) custom-call(s32[10]{0:T(128)S(1)} %get-tuple-element.354.meta_ref, ...), custom_call_target="tpu_custom_call" | custom-call | flops 4777574400 | bytes 16588800 | tf_op jit(solution)/shard_map/post_back/pallas_call | solution.py:54
  241.5 9.1 %attend_back.3 = (bf16[288,960]{1,0:T(8,128)(2,1)S(1)}, bf16[1152,640]{1,0:T(8,128)(2,1)S(1)}) custom-call(s32[10]{0:T(128)S(1)} %get-tuple-element.354.meta_ref, bf16[288,960]{1,0:T(8,128)(2,1)S(1)} %get-tuple-element.359.q_ref, bf16[288,960]{1,0:T(8,128)(2,1)S(1)} %get-tuple-element.369.do_ref, bf16[288,960]{1,0:T(8,128)(2,1)S(1)} %copy-done.74, ...), custom_call_target="tpu_custom_call" | custom-call | flops 6370099200 | bytes 5160960 | tf_op jit(solution)/shard_map/attend_back/pallas_call | solution.py:54
  254.1 9.9 %collective-permute-done.31.got_ref = bf16[288,640]{1,0:T(8,128)(2,1)S(1)} collective-permute-done((bf16[288,640]{1,0:T(8,128)(2,1)S(1)}, bf16[288,640]{1,0:T(8,128)(2,1)S(1)}, u32[]{:S(2)}, u32[]{:S(2)}) %collective-permute-start.31) | collective-permute-done | bytes 368672 | tf_op jit(solution)/shard_map/ppermute | solution.py:757
  275.0 8.7 %post_back.3 = (bf16[288,960]{1,0:T(8,128)(2,1)S(1)}, f32[288,960]{1,0:T(8,128)S(1)}, bf16[288,960]{1,0:T(8,128)(2,1)S(1)}, bf16[288,960]{1,0:T(8,128)(2,1)S(1)}...) custom-call(s32[10]{0:T(128)S(1)} %get-tuple-element.333.meta_ref, ...), custom_call_target="tpu_custom_call" | custom-call | flops 4777574400 | bytes 16588800 | tf_op jit(solution)/shard_map/post_back/pallas_call | solution.py:54
  289.0 13.7 %attend_back.4 = (bf16[288,960]{1,0:T(8,128)(2,1)S(1)}, bf16[1152,640]{1,0:T(8,128)(2,1)S(1)}) custom-call(s32[10]{0:T(128)S(1)} %get-tuple-element.333.meta_ref, bf16[288,960]{1,0:T(8,128)(2,1)S(1)} %copy-done.129, bf16[288,960]{1,0:T(8,128)(2,1)S(1)} %get-tuple-element.381.do_ref, bf16[288,960]{1,0:T(8,128)(2,1)S(1)} %copy-done.71, ...), custom_call_target="tpu_custom_call" | custom-call | flops 6370099200 | bytes 5160960 | tf_op jit(solution)/shard_map/attend_back/pallas_call | solution.py:54
  306.7 10.2 %collective-permute-done.33.got_ref = bf16[288,640]{1,0:T(8,128)(2,1)S(1)} collective-permute-done((bf16[288,640]{1,0:T(8,128)(2,1)S(1)}, bf16[288,640]{1,0:T(8,128)(2,1)S(1)}, u32[]{:S(2)}, u32[]{:S(2)}) %collective-permute-start.33) | collective-permute-done | bytes 368672 | tf_op jit(solution)/shard_map/ppermute | solution.py:757
  324.2 9.5 %weight_grad.4 = (bf16[2,160,1024]{2,1,0:T(8,128)(2,1)S(1)}, bf16[2,160,1024]{2,1,0:T(8,128)(2,1)S(1)}, bf16[2,160,1024]{2,1,0:T(8,128)(2,1)S(1)}, bf16[2,160,10...) custom-call(s32[2]{0:T(128)S(1)} %copy-done.94, bf16[288,2560]{1,0:T(8,128)(2,1)S(1)} %copy-done.141, ...), custom_call_target="tpu_custom_call" | custom-call | flops 4246732800 | bytes 11325440 | tf_op jit(solution)/shard_map/weight_grad/pallas_call | solution.py:665
  346.4 15.2 %weight_grad.5 = (bf16[2,128,2560]{2,1,0:T(8,128)(2,1)S(1)}, bf16[2,128,2560]{2,1,0:T(8,128)(2,1)S(1)}, bf16[2,112,2560]{2,1,0:T(8,128)(2,1)S(1)}, bf16[2,112,25...) custom-call(s32[2]{0:T(128)S(1)} %copy-done.94, bf16[288,960]{1,0:T(8,128)(2,1)S(1)} %copy-done.81, ...), custom_call_target="tpu_custom_call" | custom-call | flops 8493465600 | bytes 20336640 | tf_op jit(solution)/shard_map/weight_grad/pallas_call | solution.py:665
  366.3 4.9 norm_back.1
  376.6 5.0 collective-permute-done.39
  387.9 18.8 %attend_back.5 = (bf16[288,960]{1,0:T(8,128)(2,1)S(1)}, bf16[1152,640]{1,0:T(8,128)(2,1)S(1)}) custom-call(s32[10]{0:T(128)S(1)} %copy-done.92, bf16[288,960]{1,0:T(8,128)(2,1)S(1)} %copy-done.113, bf16[288,960]{1,0:T(8,128)(2,1)S(1)} %get-tuple-element.445.do_ref, bf16[288,960]{1,0:T(8,128)(2,1)S(1)} %copy-done.69, bf16[1152,640]{1,0:T(8,128)(2,1)S(1)} %copy-done.143, ...), custom_call_target="tpu_custom_call" | custom-call | flops 6370099200 | bytes 5160960 | tf_op jit(solution)/shard_map/attend_back/pallas_call | solution.py:54
  411.5 8.6 %weight_grad.6 = (bf16[2,128,1024]{2,1,0:T(8,128)(2,1)S(1)}, bf16[2,128,1024]{2,1,0:T(8,128)(2,1)S(1)}, bf16[2,112,1024]{2,1,0:T(8,128)(2,1)S(1)}, bf16[2,112,10...) custom-call(s32[2]{0:T(128)S(1)} %copy-done.94, bf16[288,960]{1,0:T(8,128)(2,1)S(1)} %copy-done.69, ...), custom_call_target="tpu_custom_call" | custom-call | flops 3185049600 | bytes 10567680 | tf_op jit(solution)/shard_map/weight_grad/pallas_call | solution.py:665
  426.4 7.1 %collective-permute-done.47.got_ref = bf16[288,640]{1,0:T(8,128)(2,1)S(1)} collective-permute-done((bf16[288,640]{1,0:T(8,128)(2,1)S(1)}, bf16[288,640]{1,0:T(8,128)(2,1)S(1)}, u32[]{:S(2)}, u32[]{:S(2)}) %collective-permute-start.47) | collective-permute-done | bytes 368672 | tf_op jit(solution)/shard_map/ppermute | solution.py:757
  473.1 7.3 %collective-permute-done.52 = bf16[128,2560]{1,0:T(8,128)(2,1)S(1)} collective-permute-done((bf16[128,2560]{1,0:T(8,128)(2,1)S(1)}, bf16[128,2560]{1,0:T(8,128)(2,1)S(1)}, u32[]{:S(2)}, u32[]{:S(2)}) %collective-permute-start.52) | collective-permute-done | bytes 655392 | tf_op jit(solution)/shard_map/ppermute | solution.py:920
  496.0 5.4 collective-permute-done.61
  507.6 5.9 %collective-permute-start.66 = (bf16[240,1536]{1,0:T(8,128)(2,1)S(1)}, bf16[240,1536]{1,0:T(8,128)(2,1)}, u32[]{:S(2)}, u32[]{:S(2)}) collective-permute-start(bf16[240,1536]{1,0:T(8,128)(2,1)S(1)} %maximum_maximum_fusion), channel_id=1, source_target_pairs={{0,8},{4,12},{24,16},{28,20},{1,9},{5,13},{25,17},{29,21},{2,10},{... | collective-permute-start | bytes 2211848 | tf_op jit(solution)/shard_map/ppermute | solution.py:920
  519.2 6.2 %collective-permute-done.66 = bf16[240,1536]{1,0:T(8,128)(2,1)} collective-permute-done((bf16[240,1536]{1,0:T(8,128)(2,1)S(1)}, bf16[240,1536]{1,0:T(8,128)(2,1)}, u32[]{:S(2)}, u32[]{:S(2)}) %collective-permute-start.66) | collective-permute-done | bytes 737312 | tf_op jit(solution)/shard_map/ppermute | solution.py:920
  535.6 12.4 %collective-permute-done.68 = bf16[112,2560]{1,0:T(8,128)(2,1)S(1)} collective-permute-done((bf16[112,2560]{1,0:T(8,128)(2,1)S(1)}, bf16[112,2560]{1,0:T(8,128)(2,1)S(1)}, u32[]{:S(2)}, u32[]{:S(2)}) %collective-permute-start.68) | collective-permute-done | bytes 573472 | tf_op jit(solution)/shard_map/ppermute | solution.py:920
  556.5 14.3 %collective-permute-done.71 = bf16[240,1536]{1,0:T(8,128)(2,1)S(1)} collective-permute-done((bf16[240,1536]{1,0:T(8,128)(2,1)S(1)}, bf16[240,1536]{1,0:T(8,128)(2,1)S(1)}, u32[]{:S(2)}, u32[]{:S(2)}) %collective-permute-start.71) | collective-permute-done | bytes 737312 | tf_op jit(solution)/shard_map/ppermute | solution.py:920
  (693 shorter events, 295.0 us)
Async XLA Ops:
  1.4 23.1 %collective-permute-start.2 = (s32[2,288]{1,0:T(2,128)S(1)}, s32[2,288]{1,0:T(2,128)S(1)}, u32[]{:S(2)}, u32[]{:S(2)}) collective-permute-start(s32[2,288]{1,0:T(2,128)S(1)} %pad_add_fusion.1), channel_id=1, source_target_pairs={{0,0},{1,1},{2,4},{3,5},{4,2},{5,3},{6,6},{7,7},{8,8},{9,9},{10,12... | collective-permute-start | bytes 6920 | tf_op jit(solution)/shard_map/ppermute | solution.py:773
  6.5 18.0 %collective-permute-start.1 = (bf16[112,1408]{1,0:T(8,128)(2,1)S(1)}, bf16[112,1408]{1,0:T(8,128)(2,1)S(1)}, u32[]{:S(2)}, u32[]{:S(2)}) collective-permute-start(bf16[112,1408]{1,0:T(8,128)(2,1)S(1)} %slice.448.refs_1_), channel_id=1, source_target_pairs={{0,2},{1,3},{2,0},{3,1},{4,6},{5,7},{6,4},{7,5},{8,10},{9,11},{10,... | collective-permute-start | bytes 946184 | tf_op jit(solution)/shard_map/ppermute | solution.py:760
  25.6 19.3 %collective-permute-start.5 = (bf16[224,1408]{1,0:T(8,128)(2,1)}, bf16[224,1408]{1,0:T(8,128)(2,1)S(1)}, u32[]{:S(2)}, u32[]{:S(2)}) collective-permute-start(bf16[224,1408]{1,0:T(8,128)(2,1)} %pad_maximum_fusion.7), channel_id=1, source_target_pairs={{0,1},{1,0},{2,3},{3,2},{4,5},{5,4},{6,7},{7,6},{8,9},{9,8},{10,11... | collective-permute-start | bytes 1892360 | tf_op jit(solution)/shard_map/ppermute | solution.py:757
  27.1 19.8 %collective-permute-start.4 = (bf16[256,1408]{1,0:T(8,128)(2,1)}, bf16[256,1408]{1,0:T(8,128)(2,1)S(1)}, u32[]{:S(2)}, u32[]{:S(2)}) collective-permute-start(bf16[256,1408]{1,0:T(8,128)(2,1)} %pad_maximum_fusion.3), channel_id=1, source_target_pairs={{0,2},{1,3},{2,0},{3,1},{4,6},{5,7},{6,4},{7,5},{8,10},{9,11},{10,... | collective-permute-start | bytes 2162696 | tf_op jit(solution)/shard_map/ppermute | solution.py:760
  55.2 18.0 %collective-permute-start.10 = (bf16[128,2560]{1,0:T(8,128)(2,1)}, bf16[128,2560]{1,0:T(8,128)(2,1)}, u32[]{:S(2)}, u32[]{:S(2)}) collective-permute-start(bf16[128,2560]{1,0:T(8,128)(2,1)} %slice.348.refs_0_), channel_id=1, source_target_pairs={{0,1},{1,0},{2,3},{3,2},{4,5},{5,4},{6,7},{7,6},{8,9},{9,8},{10,11... | collective-permute-start | bytes 1966088 | tf_op jit(solution)/shard_map/ppermute | solution.py:757
  91.4 35.1 %collective-permute-start.18 = (bf16[160,1024]{1,0:T(8,128)(2,1)S(1)}, bf16[160,1024]{1,0:T(8,128)(2,1)}, u32[]{:S(2)}, u32[]{:S(2)}) collective-permute-start(bf16[160,1024]{1,0:T(8,128)(2,1)S(1)} %get-tuple-element.348.refs_1_), channel_id=1, source_target_pairs={{0,2},{1,3},{2,0},{3,1},{4,6},{5,7},{6,4},{7,5},{8,10},{9,11},{10,... | collective-permute-start | bytes 983048 | tf_op jit(solution)/shard_map/ppermute | solution.py:760
  93.2 33.3 %collective-permute-start.17 = (bf16[160,1024]{1,0:T(8,128)(2,1)S(1)}, bf16[160,1024]{1,0:T(8,128)(2,1)S(1)}, u32[]{:S(2)}, u32[]{:S(2)}) collective-permute-start(bf16[160,1024]{1,0:T(8,128)(2,1)S(1)} %get-tuple-element.347.refs_0_), channel_id=1, source_target_pairs={{0,1},{1,0},{2,3},{3,2},{4,5},{5,4},{6,7},{7,6},{8,9},{9,8},{10,11... | collective-permute-start | bytes 983048 | tf_op jit(solution)/shard_map/ppermute | solution.py:757
  97.1 30.3 %collective-permute-start.16 = (bf16[224,2560]{1,0:T(8,128)(2,1)}, bf16[224,2560]{1,0:T(8,128)(2,1)}, u32[]{:S(2)}, u32[]{:S(2)}) collective-permute-start(bf16[224,2560]{1,0:T(8,128)(2,1)} %pad_maximum_fusion.2), channel_id=1, source_target_pairs={{0,1},{1,0},{2,3},{3,2},{4,5},{5,4},{6,7},{7,6},{8,9},{9,8},{10,11... | collective-permute-start | bytes 3440648 | tf_op jit(solution)/shard_map/ppermute | solution.py:757
  100.0 30.4 %collective-permute-start.15 = (bf16[256,2560]{1,0:T(8,128)(2,1)}, bf16[256,2560]{1,0:T(8,128)(2,1)}, u32[]{:S(2)}, u32[]{:S(2)}) collective-permute-start(bf16[256,2560]{1,0:T(8,128)(2,1)} %pad_maximum_fusion), channel_id=1, source_target_pairs={{0,2},{1,3},{2,0},{3,1},{4,6},{5,7},{6,4},{7,5},{8,10},{9,11},{10,... | collective-permute-start | bytes 3932168 | tf_op jit(solution)/shard_map/ppermute | solution.py:760
  134.9 17.1 %collective-permute-start.21 = (bf16[320,1024]{1,0:T(8,128)(2,1)S(1)}, bf16[320,1024]{1,0:T(8,128)(2,1)S(1)}, u32[]{:S(2)}, u32[]{:S(2)}) collective-permute-start(bf16[320,1024]{1,0:T(8,128)(2,1)S(1)} %pad_maximum_fusion.5), channel_id=1, source_target_pairs={{0,1},{1,0},{2,3},{3,2},{4,5},{5,4},{6,7},{7,6},{8,9},{9,8},{10,11... | collective-permute-start | bytes 1966088 | tf_op jit(solution)/shard_map/ppermute | solution.py:757
  136.4 16.9 %collective-permute-start.20 = (bf16[320,1024]{1,0:T(8,128)(2,1)S(1)}, bf16[320,1024]{1,0:T(8,128)(2,1)S(1)}, u32[]{:S(2)}, u32[]{:S(2)}) collective-permute-start(bf16[320,1024]{1,0:T(8,128)(2,1)S(1)} %pad_maximum_fusion.4), channel_id=1, source_target_pairs={{0,2},{1,3},{2,0},{3,1},{4,6},{5,7},{6,4},{7,5},{8,10},{9,11},{10,... | collective-permute-start | bytes 1966088 | tf_op jit(solution)/shard_map/ppermute | solution.py:760
  176.5 38.1 %collective-permute-start.26 = (bf16[288,960]{1,0:T(8,128)(2,1)S(1)}, bf16[288,960]{1,0:T(8,128)(2,1)S(1)}, u32[]{:S(2)}, u32[]{:S(2)}) collective-permute-start(bf16[288,960]{1,0:T(8,128)(2,1)S(1)} %bitcast.279), channel_id=1, source_target_pairs={{0,0},{1,1},{2,4},{3,5},{4,2},{5,3},{6,6},{7,7},{8,8},{9,9},{10,12... | collective-permute-start | bytes 1658888 | tf_op jit(solution)/shard_map/ppermute | solution.py:773
  341.4 22.4 %collective-permute-start.36 = (bf16[2,160,1024]{2,1,0:T(8,128)(2,1)}, bf16[2,160,1024]{2,1,0:T(8,128)(2,1)S(1)}, u32[]{:S(2)}, u32[]{:S(2)}) collective-permute-start(bf16[2,160,1024]{2,1,0:T(8,128)(2,1)} %get-tuple-element.405), channel_id=1, source_target_pairs={{0,1},{1,0},{2,3},{3,2},{4,5},{5,4},{6,7},{7,6},{8,9},{9,8},{10,11... | collective-permute-start | bytes 1966088 | tf_op jit(solution)/shard_map/ppermute | solution.py:757
  342.2 21.5 %collective-permute-start.37 = (bf16[2,160,1024]{2,1,0:T(8,128)(2,1)}, bf16[2,160,1024]{2,1,0:T(8,128)(2,1)S(1)}, u32[]{:S(2)}, u32[]{:S(2)}) collective-permute-start(bf16[2,160,1024]{2,1,0:T(8,128)(2,1)} %get-tuple-element.406), channel_id=1, source_target_pairs={{0,2},{1,3},{2,0},{3,1},{4,6},{5,7},{6,4},{7,5},{8,10},{9,11},{10,... | collective-permute-start | bytes 1966088 | tf_op jit(solution)/shard_map/ppermute | solution.py:760
  382.6 24.1 %collective-permute-start.43 = (bf16[320,1024]{1,0:T(8,128)(2,1)S(1)}, bf16[320,1024]{1,0:T(8,128)(2,1)S(1)}, u32[]{:S(2)}, u32[]{:S(2)}) collective-permute-start(bf16[320,1024]{1,0:T(8,128)(2,1)S(1)} %pad_maximum_fusion.6), channel_id=1, source_target_pairs={{0,8},{4,12},{24,16},{28,20},{1,9},{5,13},{25,17},{29,21},{2,10},{... | collective-permute-start | bytes 1966088 | tf_op jit(solution)/shard_map/ppermute | solution.py:920
  386.3 20.5 %collective-permute-start.41 = (bf16[128,2560]{1,0:T(8,128)(2,1)S(1)}, bf16[128,2560]{1,0:T(8,128)(2,1)S(1)}, u32[]{:S(2)}, u32[]{:S(2)}) collective-permute-start(bf16[128,2560]{1,0:T(8,128)(2,1)S(1)} %get-tuple-element.435), channel_id=1, source_target_pairs={{0,1},{1,0},{2,3},{3,2},{4,5},{5,4},{6,7},{7,6},{8,9},{9,8},{10,11... | collective-permute-start | bytes 1966088 | tf_op jit(solution)/shard_map/ppermute | solution.py:757
  387.6 19.1 %collective-permute-start.42 = (bf16[112,2560]{1,0:T(8,128)(2,1)S(1)}, bf16[112,2560]{1,0:T(8,128)(2,1)S(1)}, u32[]{:S(2)}, u32[]{:S(2)}) collective-permute-start(bf16[112,2560]{1,0:T(8,128)(2,1)S(1)} %get-tuple-element.437), channel_id=1, source_target_pairs={{0,2},{1,3},{2,0},{3,1},{4,6},{5,7},{6,4},{7,5},{8,10},{9,11},{10,... | collective-permute-start | bytes 1720328 | tf_op jit(solution)/shard_map/ppermute | solution.py:760
  408.8 17.6 %collective-permute-start.44 = (bf16[128,2560]{1,0:T(8,128)(2,1)S(1)}, bf16[128,2560]{1,0:T(8,128)(2,1)S(1)}, u32[]{:S(2)}, u32[]{:S(2)}) collective-permute-start(bf16[128,2560]{1,0:T(8,128)(2,1)S(1)} %get-tuple-element.452), channel_id=1, source_target_pairs={{0,1},{1,0},{2,3},{3,2},{4,5},{5,4},{6,7},{7,6},{8,9},{9,8},{10,11... | collective-permute-start | bytes 1966088 | tf_op jit(solution)/shard_map/ppermute | solution.py:757
  409.8 23.7 %collective-permute-start.47 = (bf16[288,640]{1,0:T(8,128)(2,1)S(1)}, bf16[288,640]{1,0:T(8,128)(2,1)S(1)}, u32[]{:S(2)}, u32[]{:S(2)}) collective-permute-start(bf16[288,640]{1,0:T(8,128)(2,1)S(1)} %get-tuple-element.656), channel_id=1, source_target_pairs={{0,1},{1,0},{2,3},{3,2},{4,5},{5,4},{6,7},{7,6},{8,9},{9,8},{10,11... | collective-permute-start | bytes 1105928 | tf_op jit(solution)/shard_map/ppermute | solution.py:757
  433.5 21.8 %collective-permute-start.51 = (bf16[4,240,1024]{2,1,0:T(8,128)(2,1)}, bf16[4,240,1024]{2,1,0:T(8,128)(2,1)}, u32[]{:S(2)}, u32[]{:S(2)}) collective-permute-start(bf16[4,240,1024]{2,1,0:T(8,128)(2,1)} %get-tuple-element.482), channel_id=1, source_target_pairs={{0,4},{4,0},{8,12},{12,8},{16,20},{20,16},{24,28},{28,24},{1,5},{5... | collective-permute-start | bytes 5898248 | tf_op jit(solution)/shard_map/ppermute | solution.py:763
  434.6 23.4 %collective-permute-start.50 = (bf16[320,1024]{1,0:T(8,128)(2,1)}, bf16[320,1024]{1,0:T(8,128)(2,1)}, u32[]{:S(2)}, u32[]{:S(2)}) collective-permute-start(bf16[320,1024]{1,0:T(8,128)(2,1)} %add_convert_fusion.8), channel_id=1, source_target_pairs={{8,16},{12,20},{16,8},{20,12},{9,17},{13,21},{17,9},{21,13},{10,18... | collective-permute-start | bytes 1966088 | tf_op jit(solution)/shard_map/ppermute | solution.py:920
  438.4 19.6 %collective-permute-start.49 = (bf16[112,2560]{1,0:T(8,128)(2,1)}, bf16[112,2560]{1,0:T(8,128)(2,1)}, u32[]{:S(2)}, u32[]{:S(2)}) collective-permute-start(bf16[112,2560]{1,0:T(8,128)(2,1)} %fusion.19), channel_id=1, source_target_pairs={{0,1},{1,0},{2,3},{3,2},{4,5},{5,4},{6,7},{7,6},{8,9},{9,8},{10,11... | collective-permute-start | bytes 1720328 | tf_op jit(solution)/shard_map/ppermute | solution.py:757
  441.3 17.2 %collective-permute-start.48 = (bf16[128,2560]{1,0:T(8,128)(2,1)}, bf16[128,2560]{1,0:T(8,128)(2,1)}, u32[]{:S(2)}, u32[]{:S(2)}) collective-permute-start(bf16[128,2560]{1,0:T(8,128)(2,1)} %fusion.8), channel_id=1, source_target_pairs={{0,2},{1,3},{2,0},{3,1},{4,6},{5,7},{6,4},{7,5},{8,10},{9,11},{10,... | collective-permute-start | bytes 1966088 | tf_op jit(solution)/shard_map/ppermute | solution.py:760
  462.5 17.9 %collective-permute-start.52 = (bf16[128,2560]{1,0:T(8,128)(2,1)S(1)}, bf16[128,2560]{1,0:T(8,128)(2,1)S(1)}, u32[]{:S(2)}, u32[]{:S(2)}) collective-permute-start(bf16[128,2560]{1,0:T(8,128)(2,1)S(1)} %fusion.6), channel_id=1, source_target_pairs={{0,8},{4,12},{24,16},{28,20},{1,9},{5,13},{25,17},{29,21},{2,10},{... | collective-permute-start | bytes 1966088 | tf_op jit(solution)/shard_map/ppermute | solution.py:920
  480.4 21.0 %collective-permute-start.57 = (bf16[112,2560]{1,0:T(8,128)(2,1)S(1)}, bf16[112,2560]{1,0:T(8,128)(2,1)S(1)}, u32[]{:S(2)}, u32[]{:S(2)}) collective-permute-start(bf16[112,2560]{1,0:T(8,128)(2,1)S(1)} %fusion.17), channel_id=1, source_target_pairs={{0,8},{4,12},{24,16},{28,20},{1,9},{5,13},{25,17},{29,21},{2,10},{... | collective-permute-start | bytes 1720328 | tf_op jit(solution)/shard_map/ppermute | solution.py:920
  485.0 16.4 %collective-permute-start.56 = (bf16[128,2560]{1,0:T(8,128)(2,1)S(1)}, bf16[128,2560]{1,0:T(8,128)(2,1)S(1)}, u32[]{:S(2)}, u32[]{:S(2)}) collective-permute-start(bf16[128,2560]{1,0:T(8,128)(2,1)S(1)} %add_convert_fusion.7), channel_id=1, source_target_pairs={{8,16},{12,20},{16,8},{20,12},{9,17},{13,21},{17,9},{21,13},{10,18... | collective-permute-start | bytes 1966088 | tf_op jit(solution)/shard_map/ppermute | solution.py:920
  503.3 15.9 %collective-permute-start.62 = (bf16[128,2560]{1,0:T(8,128)(2,1)S(1)}, bf16[128,2560]{1,0:T(8,128)(2,1)}, u32[]{:S(2)}, u32[]{:S(2)}) collective-permute-start(bf16[128,2560]{1,0:T(8,128)(2,1)S(1)} %add_convert_fusion.6), channel_id=1, source_target_pairs={{8,0},{12,4},{16,24},{20,28},{9,1},{13,5},{17,25},{21,29},{10,2},{... | collective-permute-start | bytes 1966088 | tf_op jit(solution)/shard_map/ppermute | solution.py:920
  507.6 17.8 %collective-permute-start.66 = (bf16[240,1536]{1,0:T(8,128)(2,1)S(1)}, bf16[240,1536]{1,0:T(8,128)(2,1)}, u32[]{:S(2)}, u32[]{:S(2)}) collective-permute-start(bf16[240,1536]{1,0:T(8,128)(2,1)S(1)} %maximum_maximum_fusion), channel_id=1, source_target_pairs={{0,8},{4,12},{24,16},{28,20},{1,9},{5,13},{25,17},{29,21},{2,10},{... | collective-permute-start | bytes 2211848 | tf_op jit(solution)/shard_map/ppermute | solution.py:920
  517.9 17.7 %collective-permute-start.69 = (bf16[320,1024]{1,0:T(8,128)(2,1)S(1)}, bf16[320,1024]{1,0:T(8,128)(2,1)S(1)}, u32[]{:S(2)}, u32[]{:S(2)}) collective-permute-start(bf16[320,1024]{1,0:T(8,128)(2,1)S(1)} %add_convert_fusion.5), channel_id=1, source_target_pairs={{8,0},{12,4},{16,24},{20,28},{9,1},{13,5},{17,25},{21,29},{10,2},{... | collective-permute-start | bytes 1966088 | tf_op jit(solution)/shard_map/ppermute | solution.py:920
  526.7 21.3 %collective-permute-start.67 = (bf16[240,1536]{1,0:T(8,128)(2,1)S(1)}, bf16[240,1536]{1,0:T(8,128)(2,1)S(1)}, u32[]{:S(2)}, u32[]{:S(2)}) collective-permute-start(bf16[240,1536]{1,0:T(8,128)(2,1)S(1)} %add_convert_fusion.1), channel_id=1, source_target_pairs={{8,16},{12,20},{16,8},{20,12},{9,17},{13,21},{17,9},{21,13},{10,18... | collective-permute-start | bytes 2211848 | tf_op jit(solution)/shard_map/ppermute | solution.py:920
  528.6 19.4 %collective-permute-start.68 = (bf16[112,2560]{1,0:T(8,128)(2,1)S(1)}, bf16[112,2560]{1,0:T(8,128)(2,1)S(1)}, u32[]{:S(2)}, u32[]{:S(2)}) collective-permute-start(bf16[112,2560]{1,0:T(8,128)(2,1)S(1)} %add_convert_fusion.9), channel_id=1, source_target_pairs={{8,0},{12,4},{16,24},{20,28},{9,1},{13,5},{17,25},{21,29},{10,2},{... | collective-permute-start | bytes 1720328 | tf_op jit(solution)/shard_map/ppermute | solution.py:920
  550.1 20.8 %collective-permute-start.71 = (bf16[240,1536]{1,0:T(8,128)(2,1)S(1)}, bf16[240,1536]{1,0:T(8,128)(2,1)S(1)}, u32[]{:S(2)}, u32[]{:S(2)}) collective-permute-start(bf16[240,1536]{1,0:T(8,128)(2,1)S(1)} %add_convert_fusion), channel_id=1, source_target_pairs={{8,0},{12,4},{16,24},{20,28},{9,1},{13,5},{17,25},{21,29},{10,2},{... | collective-permute-start | bytes 2211848 | tf_op jit(solution)/shard_map/ppermute | solution.py:920
  (235 other events, 1553.2 us)

commit v4 on v3

--- a/solution.py
+++ b/solution.py
@@ -65,6 +65,9 @@
 
 def whole(*shape):
     return pl.BlockSpec(shape, lambda g, s: (0,) * len(shape))
+
+
+IN_VMEM = pl.BlockSpec(memory_space=pltpu.VMEM)
 
 
 def turns(table, keys):
@@ -113,11 +116,11 @@
         meta,
         (1,),
         (x, gain, wq, wkv, table),
-        [whole(rows, width), whole(1, width), whole(*wq.shape), whole(width, both), whole(*table.shape)],
-        [whole(rows, width), whole(rows, both), whole(rows, width)],
+        [IN_VMEM] * 5,
+        [IN_VMEM] * 3,
         [jax.ShapeDtypeStruct((rows, k), BF16) for k in (width, both, width)],
         [],
-        32,
+        16,
         2 * rows * width * (width + both),
         2 * width * (width + both) + 8 * rows * width,
     )
@@ -132,36 +135,37 @@
 
 
 def split_pairs(packed, out, to_left):
-    rows, width = packed.shape
-    lane = lax.broadcasted_iota(jnp.int32, (rows, LANES), 1)
+    m, width = packed.shape
+    lane = lax.broadcasted_iota(jnp.int32, (m, LANES), 1)
     for at in range(0, width, LANES):
         h = at // HEAD_DIM
         if at + LANES <= width:
             u = packed[:, at : at + LANES].astype(F32)
         else:
-            u = jnp.concatenate([packed[:, at:].astype(F32), jnp.zeros((rows, at + LANES - width), F32)], axis=1)
+            u = jnp.concatenate([packed[:, at:].astype(F32), jnp.zeros((m, at + LANES - width), F32)], axis=1)
         v = pltpu.roll(u, HEAD_DIM, 1)
         first, second = (u, v) if to_left else (v, u)
         keep = (lane < HEAD_DIM) if to_left else (lane >= HEAD_DIM)
-        out[h] = jnp.where(keep, first, 0.0).astype(out.dtype)
+        out[h, :m] = jnp.where(keep, first, 0.0).astype(out.dtype)
         if at + LANES <= width:
-            out[h + 1] = jnp.where(keep, second, 0.0).astype(out.dtype)
-
-
-def join_pairs(scr, out_ref, from_left):
+            out[h + 1, :m] = jnp.where(keep, second, 0.0).astype(out.dtype)
+
+
+def join_pairs(scr, out_ref, from_left, m):
     heads = scr.shape[0]
-    lane = lax.broadcasted_iota(jnp.int32, scr.shape[1:], 1)
+    lane = lax.broadcasted_iota(jnp.int32, (m, LANES), 1)
     for h in range(0, heads, 2):
         at = h * HEAD_DIM
-        a = scr[h] if from_left else pltpu.roll(scr[h], HEAD_DIM, 1)
+        a = scr[h, :m] if from_left else pltpu.roll(scr[h, :m], HEAD_DIM, 1)
         if h + 1 < heads:
-            b = pltpu.roll(scr[h + 1], HEAD_DIM, 1) if from_left else scr[h + 1]
-            out_ref[:, at : at + LANES] = jnp.where(lane < HEAD_DIM, a, b).astype(out_ref.dtype)
+            b = pltpu.roll(scr[h + 1, :m], HEAD_DIM, 1) if from_left else scr[h + 1, :m]
+            out_ref[:m, at : at + LANES] = jnp.where(lane < HEAD_DIM, a, b).astype(out_ref.dtype)
         else:
-            out_ref[:, at : at + HEAD_DIM] = a[:, :HEAD_DIM].astype(out_ref.dtype)
+            out_ref[:m, at : at + HEAD_DIM] = a[:, :HEAD_DIM].astype(out_ref.dtype)
 
 
 def compact_keys(meta_ref, key_refs, rows, keys):
+    keys[...] = jnp.zeros_like(keys)
     block = 0
     for ref in key_refs:
         for first in range(0, ref.shape[0], rows):
@@ -169,159 +173,156 @@
             block += 1
 
 
+def by_group(count, do):
+    def one(g, _):
+        do(g, pl.ds(pl.multiple_of(g * LANES, LANES), LANES))
+        return 0
+
+    lax.fori_loop(0, count, one, 0)
+
+
+def stacked(m):
+    return GROUP if GROUP * m <= 400 else 1
+
+
 def attend_kernel(recursion, variants, count, meta_ref, q_ref, *refs):
     key_refs, (row_ref, col_ref, att_ref, lse_ref, keys, bias, q_all, o_all) = refs[:count], refs[count:]
-    g = pl.program_id(0)
-    rows = q_ref.shape[0]
-
-    @pl.when(g == 0)
-    def _():
-        lse_ref[...] = jnp.zeros_like(lse_ref)
-        split_pairs(q_ref[...], q_all, True)
-
-    keys[...] = jnp.zeros_like(keys)
+    rows, groups = q_ref.shape[0], keys.shape[1] // LANES
     compact_keys(meta_ref, key_refs, rows, keys)
+    lse_ref[...] = jnp.zeros_like(lse_ref)
 
     def body(m, n):
-        @pl.when(g == 0)
-        def _():
-            bias[:m, :n] = make_bias(row_ref[:m], col_ref[:, :n], recursion)
-
-        kv = keys[:n, :]
-        for j in range(GROUP):
-            h = g * GROUP + j
-            s = dotf(q_all[h, :m], kv, NT) * SCALE + bias[:m, :n]
-            peak = jnp.max(s, axis=1, keepdims=True)
-            e = jnp.exp(s - peak)
-            total = jnp.sum(e, axis=1, keepdims=True)
-            o_all[h, :m] = dotf(e.astype(BF16), kv) / total
+        bias[:m, :n] = make_bias(row_ref[:m], col_ref[:, :n], recursion)
+        split_pairs(q_ref[:m] * jnp.bfloat16(SCALE), q_all, True)
+        at_once = stacked(m)
+
+        def group(g, cols):
+            kv = keys[:n, cols]
             lane = lax.broadcasted_iota(jnp.int32, (m, LANES), 1)
-            lse_ref[:m, :] = jnp.where(lane == h, peak + jnp.log(total), lse_ref[:m, :])
-            if m < rows:
-                o_all[h, m:] = jnp.zeros((rows - m, LANES), F32)
+            for first in range(0, GROUP, at_once):
+                heads = [g * GROUP + first + j for j in range(at_once)]
+                queries = jnp.concatenate([q_all[h, :m] for h in heads], axis=0)
+                s = dotf(queries, kv, NT) + jnp.concatenate([bias[:m, :n]] * at_once, axis=0)
+                peak = jnp.max(s, axis=1, keepdims=True)
+                e = jnp.exp(s - peak)
+                total = jnp.sum(e, axis=1, keepdims=True)
+                o = dotf(e.astype(BF16), kv) / total
+                log = peak + jnp.log(total)
+                for j, h in enumerate(heads):
+                    here = slice(j * m, (j + 1) * m)
+                    o_all[h, :m] = o[here]
+                    lse_ref[:m, :] = jnp.where(lane == h, log[here], lse_ref[:m, :])
+
+        by_group(groups, group)
+        join_pairs(o_all, att_ref, False, m)
+        clear(m, att_ref)
 
     choose(meta_ref, variants, body)
-
-    @pl.when(g == pl.num_programs(0) - 1)
-    def _():
-        join_pairs(o_all, att_ref, False)
 
 
 def attend_call(recursion, variants, meta, q, kvs, row_info, col_info):
     rows, width = q.shape
-    keys = sum(k.shape[0] for k in kvs)
-    groups = kvs[0].shape[1] // LANES
-    heads = groups * GROUP
+    keys, both = sum(k.shape[0] for k in kvs), kvs[0].shape[1]
+    heads = both // LANES * GROUP
+    shape = jax.ShapeDtypeStruct
+    inputs = (q, *kvs, row_info, col_info)
     return call(
         functools.partial(attend_kernel, recursion, variants, len(kvs)),
         "attend",
         meta,
-        (groups,),
-        (q, *kvs, row_info, col_info),
-        [whole(rows, width)]
-        + [pl.BlockSpec((k.shape[0], LANES), lambda g, s: (0, g)) for k in kvs]
-        + [whole(*row_info.shape), whole(3, keys)],
-        [whole(rows, width), whole(rows, LANES), pl.BlockSpec((keys, LANES), lambda g, s: (0, g))],
-        [
-            jax.ShapeDtypeStruct((rows, width), BF16),
-            jax.ShapeDtypeStruct((rows, LANES), F32),
-            jax.ShapeDtypeStruct((keys, groups * LANES), BF16),
-        ],
+        (1,),
+        inputs,
+        [IN_VMEM] * len(inputs),
+        [IN_VMEM] * 3,
+        [shape((rows, width), BF16), shape((rows, LANES), F32), shape((keys, both), BF16)],
         [
             pltpu.VMEM((rows, keys), F32),
             pltpu.VMEM((heads, rows, LANES), BF16),
             pltpu.VMEM((heads, rows, LANES), F32),
         ],
-        24,
+        16,
         4 * rows * keys * LANES * heads,
-        4 * q.size + 2 * keys * groups * LANES,
+        4 * q.size + 2 * keys * both,
     )
 
 
 def attend_back_kernel(
     recursion, variants, meta_ref, q_ref, do_ref, att_ref, keys, lse_ref, row_ref, col_ref, dq_ref, dkv_ref,
-    bias, back, q_all, do_all, dot_all, p3, ds3, dq_all,
+    bias, back, q_all, do_all, p3, ds3, dq_all,
 ):
-    g = pl.program_id(0)
-    rows, width = q_ref.shape
-
-    @pl.when(g == 0)
-    def _():
-        split_pairs(q_ref[...], q_all, True)
-        split_pairs(do_ref[...], do_all, False)
-        prod = do_ref[...].astype(F32) * att_ref[...].astype(F32)
-        for h in range(width // HEAD_DIM):
-            dot_all[h] = jnp.sum(prod[:, h * HEAD_DIM : (h + 1) * HEAD_DIM], axis=1, keepdims=True)
+    rows, groups = q_ref.shape[0], keys.shape[1] // LANES
 
     def body(m, n):
-        @pl.when(g == 0)
-        def _():
-            bias[:m, :n] = make_bias(row_ref[:m], col_ref[:, :n], recursion)
-
-        kv = keys[:n, :]
-        cos, sin = turns(row_ref[:m], False)
-        for j in range(GROUP):
-            h = g * GROUP + j
-            here = slice(j * m, (j + 1) * m)
-            s = dotf(q_all[h, :m], kv, NT) * SCALE + bias[:m, :n]
+        bias[:m, :n] = make_bias(row_ref[:m], col_ref[:, :n], recursion)
+        split_pairs(q_ref[:m] * jnp.bfloat16(SCALE), q_all, True)
+        split_pairs(do_ref[:m], do_all, False)
+        split_pairs(do_ref[:m].astype(F32) * att_ref[:m].astype(F32), dq_all, True)
+        at_once = stacked(m)
+
+        def group(g, cols):
+            kv = keys[:n, cols]
+            cos, sin = turns(row_ref[:m], False)
             lane = lax.broadcasted_iota(jnp.int32, (m, LANES), 1)
-            p = jnp.exp(s - jnp.sum(jnp.where(lane == h, lse_ref[:m], 0.0), axis=1, keepdims=True))
-            dp = dotf(do_all[h, :m], kv, NT)
-            ds = (p * (dp - dot_all[h, :m])).astype(BF16)
-            p3[here, :n] = p.astype(BF16)
-            ds3[here, :n] = ds
-            dq = dotf(ds, kv) * SCALE
-            dq_all[h, :m] = dq * cos - turn(dq) * sin
-            if m < rows:
-                dq_all[h, m:] = jnp.zeros((rows - m, LANES), F32)
-        q3 = jnp.concatenate([q_all[g * GROUP + j, :m] for j in range(GROUP)], axis=0)
-        do3 = jnp.concatenate([do_all[g * GROUP + j, :m] for j in range(GROUP)], axis=0)
-        dkv = dotf(q3, ds3[: GROUP * m, :n], TN) * SCALE + dotf(do3, p3[: GROUP * m, :n], TN)
-        back[:n, :] = dkv.T
+            for first in range(0, GROUP, at_once):
+                heads = [g * GROUP + first + j for j in range(at_once)]
+                here = slice(first * m, (first + at_once) * m)
+                stack = lambda parts: jnp.concatenate(parts, axis=0)
+                logs = stack([jnp.sum(jnp.where(lane == h, lse_ref[:m], 0.0), axis=1, keepdims=True) for h in heads])
+                dots = stack([jnp.sum(dq_all[h, :m], axis=1, keepdims=True) for h in heads])
+                s = dotf(stack([q_all[h, :m] for h in heads]), kv, NT) + stack([bias[:m, :n]] * at_once)
+                p = jnp.exp(s - logs)
+                dp = dotf(stack([do_all[h, :m] for h in heads]), kv, NT)
+                ds = (p * (dp - dots)).astype(BF16)
+                p3[here, :n] = p.astype(BF16)
+                ds3[here, :n] = ds
+                dq = dotf(ds, kv) * SCALE
+                for j, h in enumerate(heads):
+                    one = dq[j * m : (j + 1) * m]
+                    dq_all[h, :m] = one * cos - turn(one) * sin
+            q3 = jnp.concatenate([q_all[g * GROUP + j, :m] for j in range(GROUP)], axis=0)
+            do3 = jnp.concatenate([do_all[g * GROUP + j, :m] for j in range(GROUP)], axis=0)
+            dkv = dotf(q3, ds3[: GROUP * m, :n], TN) + dotf(do3, p3[: GROUP * m, :n], TN)
+            back[:n, cols] = dkv.T
+
+        by_group(groups, group)
+        join_pairs(dq_all, dq_ref, True, m)
+        clear(m, dq_ref)
 
     choose(meta_ref, variants, body)
-    spot = lax.broadcasted_iota(jnp.int32, (rows, LANES), 0)
+    spot = lax.broadcasted_iota(jnp.int32, (rows, back.shape[1]), 0)
     for block in range(dkv_ref.shape[0] // rows):
         part = back[pl.ds(pl.multiple_of(meta_ref[2 + 2 * block], 16), rows), :]
         part = jnp.where(spot < meta_ref[3 + 2 * block], part, 0.0)
         dkv_ref[block * rows : (block + 1) * rows, :] = part.astype(BF16)
 
-    @pl.when(g == pl.num_programs(0) - 1)
-    def _():
-        join_pairs(dq_all, dq_ref, True)
-
 
 def attend_back_call(recursion, variants, meta, q, do, att, kv, lse, row_info, col_info):
     rows, width = q.shape
-    keys, groups = kv.shape[0], kv.shape[1] // LANES
-    heads = groups * GROUP
+    keys, both = kv.shape
+    heads = both // LANES * GROUP
+    inputs = (q, do, att, kv, lse, row_info, col_info)
     return call(
         functools.partial(attend_back_kernel, recursion, variants),
         "attend_back",
         meta,
-        (groups,),
-        (q, do, att, kv, lse, row_info, col_info),
-        [whole(rows, width)] * 3
-        + [pl.BlockSpec((keys, LANES), lambda g, s: (0, g)), whole(rows, LANES), whole(*row_info.shape), whole(3, keys)],
-        [whole(rows, width), pl.BlockSpec((keys, LANES), lambda g, s: (0, g))],
-        [jax.ShapeDtypeStruct((rows, width), BF16), jax.ShapeDtypeStruct((keys, groups * LANES), BF16)],
+        (1,),
+        inputs,
+        [IN_VMEM] * len(inputs),
+        [IN_VMEM] * 2,
+        [jax.ShapeDtypeStruct((rows, width), BF16), jax.ShapeDtypeStruct((keys, both), BF16)],
         [
             pltpu.VMEM((rows, keys), F32),
-            pltpu.VMEM((keys, LANES), F32),
+            pltpu.VMEM((keys, both), F32),
             pltpu.VMEM((heads, rows, LANES), BF16),
             pltpu.VMEM((heads, rows, LANES), BF16),
-            pltpu.VMEM((heads, rows, 1), F32),
             pltpu.VMEM((GROUP * rows, keys), BF16),
             pltpu.VMEM((GROUP * rows, keys), BF16),
             pltpu.VMEM((heads, rows, LANES), F32),
         ],
-        32,
+        24,
         10 * rows * keys * LANES * heads,
-        8 * q.size + 4 * keys * groups * LANES,
+        8 * q.size + 4 * keys * both,
     )
-
-
-IN_VMEM = pl.BlockSpec(memory_space=pltpu.VMEM)
 
 
 def inverse(x):
@@ -561,54 +562,66 @@
 def qkv_back_call(variants, meta, dq, mine, got, wq, wkv, x, gain, upstream, table):
     rows, width = x.shape
     both = wkv.shape[1]
-    full, row, keys = whole(rows, width), whole(1, width), whole(rows, both)
     return call(
         functools.partial(qkv_back_kernel, variants),
         "qkv_back",
         meta,
         (1,),
         (dq, mine, got, wq, wkv, x, gain, upstream, table),
-        [full, keys, keys, whole(*wq.shape), whole(width, both), full, row, full, whole(*table.shape)],
-        [keys, full, row],
+        [IN_VMEM] * 9,
+        [IN_VMEM] * 3,
         [
             jax.ShapeDtypeStruct((rows, both), BF16),
             jax.ShapeDtypeStruct((rows, width), F32),
             jax.ShapeDtypeStruct((1, width), F32),
         ],
         [],
-        32,
+        16,
         2 * rows * width * (width + both),
         2 * width * (width + both) + 16 * rows * width,
     )
 
 
-def weight_grad_kernel(fill, counts, stride, spot_ref, *refs):
+def weight_grad_kernel(fill, counts, hand, choices, stride, spot_ref, *refs):
     c = pl.program_id(0)
-    n_left, n_right, n_extra, levels = counts
+    n_left, n_right, n_extra, n_ready, levels = counts
     sources, refs = refs[: n_left * levels], refs[n_left * levels :]
     rights, refs = refs[: n_right * levels], refs[n_right * levels :]
-    extra, outs, scratch = refs[:n_extra], refs[n_extra : n_extra + 5], refs[n_extra + 5 :]
-    staged, turned, values, sem = scratch[:n_left], scratch[n_left : 2 * n_left], scratch[-3:-1], scratch[-1]
-
-    @pl.when(c == 0)
-    def _():
-        copies = []
-        for i, source in enumerate(sources):
-            rows = source.shape[0]
-            target = staged[i // levels].at[pl.ds(i % levels * rows, rows), :]
-            copies.append(pltpu.make_async_copy(source, target, sem.at[i]))
-            copies[-1].start()
-        for i, copy in enumerate(copies):
-            copy.wait()
-            if i % levels == levels - 1:
-                turned[i // levels][...] = staged[i // levels][...].T
-
-    def product(left, right):
-        stacked = jnp.concatenate([a[...] for a in rights[right * levels : (right + 1) * levels]], axis=0)
-        return dotf(turned[left][...], stacked)
+    extra, ready, refs = refs[:n_extra], refs[n_extra : n_extra + n_ready], refs[n_extra + n_ready :]
+    outs, handed = refs[:5], refs[5 : 5 + (hand is not None)]
+    scratch = refs[5 + len(handed) :]
+    staged, turned, values, sem = scratch[:n_left], list(scratch[n_left : 2 * n_left]), scratch[-3:-1], scratch[-1]
+    if handed:
+        turned[hand] = handed[0]
+    turned += ready
+
+    def run(sizes):
+        starts = [sum(sizes[:i]) for i in range(levels)]
+        depth = sum(sizes)
+
+        @pl.when(c == 0)
+        def _():
+            copies = []
+            for i, source in enumerate(sources):
+                size = sizes[i % levels]
+                target = staged[i // levels].at[pl.ds(starts[i % levels], size), :]
+                copies.append(pltpu.make_async_copy(source.at[pl.ds(0, size), :], target, sem.at[i]))
+                copies[-1].start()
+            for i, copy in enumerate(copies):
+                copy.wait()
+                if i % levels == levels - 1:
+                    turned[i // levels][:, :depth] = staged[i // levels][:depth, :].T
+
+        def product(left, right):
+            group = rights[right * levels : (right + 1) * levels]
+            stacked = jnp.concatenate([a[:size, :] for a, size in zip(group, sizes)], axis=0)
+            return dotf(turned[left][:, :depth], stacked)
+
+        fill(spot_ref[1], c, product, values, extra)
 
     core = spot_ref[1]
-    fill(core, c, product, values, extra)
+    for i, sizes in enumerate(choices):
+        pl.when(spot_ref[2] == i)(functools.partial(run, sizes))
     each, cut = outs[4].shape[1], outs[0].shape[1]
     kept, away = values
     for r in range(4):
@@ -653,36 +666,38 @@
     away[:, part:] = vectors
 
 
-def weight_grad(spot, fill, lefts, rights, stride, each, n, step, extra=()):
-    levels, rows = len(lefts[0]), lefts[0][0].shape[0]
+def weight_grad(spot, fill, lefts, rights, stride, each, n, step, choices, extra=(), ready=(), hand=None):
+    levels, rows = len(rights[0]), rights[0][0].shape[0]
     depth = levels * rows
     cut = -(-each // 32) * 16
     shapes = [(2, cut, n), (2, cut, n), (2, each - cut, n), (2, each - cut, n), (4, each, n)]
     flops = 2 * depth * 4 * stride * sum(right[0].shape[1] for right in rights)
     sources, moving = [a for group in lefts for a in group], [a for group in rights for a in group]
     by_step = pl.BlockSpec((rows, step), lambda c, s: (0, c))
+    given = [] if hand is None else [(lefts[hand][0].shape[1], depth)]
     at_once = lambda a: pl.BlockSpec(a.shape, lambda c, s: (0, 0))
     return pl.pallas_call(
-        functools.partial(weight_grad_kernel, fill, (len(lefts), len(rights), len(extra), levels), stride),
+        functools.partial(weight_grad_kernel, fill, (len(lefts), len(rights), len(extra), len(ready), levels), hand, choices, stride),
         grid_spec=pltpu.PrefetchScalarGridSpec(
             num_scalar_prefetch=1,
             grid=(-(-n // step),),
             in_specs=[pl.BlockSpec(memory_space=pl.ANY)] * len(sources)
             + [by_step if n > step else at_once(a) for a in moving]
-            + [at_once(a) for a in extra],
-            out_specs=[pl.BlockSpec(s[:2] + (step,), lambda c, s: (0, 0, c)) for s in shapes],
+            + [at_once(a) for a in extra]
+            + [IN_VMEM] * len(ready),
+            out_specs=[pl.BlockSpec(s[:2] + (step,), lambda c, s: (0, 0, c)) for s in shapes] + [IN_VMEM] * len(given),
             scratch_shapes=[pltpu.VMEM((depth, group[0].shape[1]), BF16) for group in lefts]
             + [pltpu.VMEM((group[0].shape[1], depth), BF16) for group in lefts]
             + [pltpu.VMEM((4 * stride, step), BF16)] * 2
-            + [pltpu.SemaphoreType.DMA((len(sources),))],
+            + [pltpu.SemaphoreType.DMA((max(len(sources), 1),))],
         ),
-        out_shape=[jax.ShapeDtypeStruct(s, BF16) for s in shapes],
+        out_shape=[jax.ShapeDtypeStruct(s, BF16) for s in shapes + given],
         compiler_params=pltpu.CompilerParams(vmem_limit_bytes=24 * MIB),
         cost_estimate=pl.CostEstimate(
             flops=flops, bytes_accessed=2 * sum(a.size for a in sources + moving) + 16 * each * n, transcendentals=0
         ),
         name="weight_grad",
-    )(spot, *sources, *moving, *extra)
+    )(spot, *sources, *moving, *extra, *ready)
 
 
 def settle_kernel(moves, spot_ref, *refs):
@@ -697,11 +712,11 @@
         grid_spec=pltpu.PrefetchScalarGridSpec(
             num_scalar_prefetch=1,
             grid=(1,),
-            in_specs=[pl.BlockSpec(a.shape, lambda g, s: (0, 0)) for a in arrays],
-            out_specs=[pl.BlockSpec(shape, lambda g, s: (0, 0)) for shape in shapes],
+            in_specs=[IN_VMEM] * len(arrays),
+            out_specs=[IN_VMEM] * len(shapes),
         ),
         out_shape=[jax.ShapeDtypeStruct(shape, arrays[0].dtype) for shape in shapes],
-        compiler_params=pltpu.CompilerParams(vmem_limit_bytes=32 * MIB),
+        compiler_params=pltpu.CompilerParams(vmem_limit_bytes=16 * MIB),
         cost_estimate=pl.CostEstimate(flops=0, bytes_accessed=4 * sum(a.size for a in arrays), transcendentals=0),
         name=name,
     )(spot, *arrays)
@@ -731,6 +746,69 @@
     rows, width = mine.shape
     shapes = [(rows, width - part), (rows, width - part), (rows, both), (rows, LANES)]
     return copy_call(functools.partial(unpack_kernel, part), "unpack", spot, (mine, theirs), shapes)
+
+
+def finish_kernel(part, both, spot_ref, own, other, query, key, value, out, vectors):
+    width = query.shape[1]
+
+    def go(low, high):
+        out[...] = low[:, part + LANES : part + LANES + width].astype(F32)
+        query[...] = high[:, part + LANES : part + LANES + width].astype(F32)
+        vectors[...] = low[:, part : part + LANES].astype(F32).T[: vectors.shape[0], :]
+        groups = [low[:, at : at + LANES] for at in range(0, part, LANES)]
+        groups += [high[:, at : at + LANES] for at in range(2 * part - both, part, LANES)]
+        groups = [group.astype(F32) for group in groups]
+        lane = lax.broadcasted_iota(jnp.int32, groups[0].shape, 1)
+        for i in range(0, len(groups), 2):
+            at = i * HEAD_DIM
+            a, turned = groups[i], pltpu.roll(groups[i], HEAD_DIM, 1)
+            if i + 1 < len(groups):
+                b = groups[i + 1]
+                key[at : at + LANES, :] = jnp.where(lane < HEAD_DIM, a, pltpu.roll(b, HEAD_DIM, 1)).T
+                value[at : at + LANES, :] = jnp.where(lane < HEAD_DIM, turned, b).T
+            else:
+                key[at : at + HEAD_DIM, :] = a.T[:HEAD_DIM, :]
+                value[at : at + HEAD_DIM, :] = turned.T[:HEAD_DIM, :]
+
+    pl.when(spot_ref[1] == 0)(lambda: go(own, other))
+    pl.when(spot_ref[1] == 1)(lambda: go(other, own))
+
+
+def finish_rows_kernel(spot_ref, own, other, out):
+    half, width = own.shape[0], out.shape[0]
+
+    def go(low, high):
+        out[:, :half] = low[:, :width].astype(F32).T
+        out[:, half:] = high[:, :width].astype(F32).T
+
+    pl.when(spot_ref[1] == 0)(lambda: go(own, other))
+    pl.when(spot_ref[1] == 1)(lambda: go(other, own))
+
+
+def finish_rows_call(spot, own, other, width):
+    shape = jax.ShapeDtypeStruct((width, 2 * own.shape[0]), F32)
+    return call(
+        finish_rows_kernel, "finish_rows", spot, (1,), (own, other), [IN_VMEM] * 2, IN_VMEM, shape, [], 16, 0, 8 * own.size
+    )
+
+
+def finish_call(spot, own, other, part, both, width):
+    rows = own.shape[0]
+    shapes = [(rows, width), (both // 2, rows), (both // 2, rows), (rows, width), (8, rows)]
+    return call(
+        functools.partial(finish_kernel, part, both),
+        "finish",
+        spot,
+        (1,),
+        (own, other),
+        [IN_VMEM] * 2,
+        [IN_VMEM] * len(shapes),
+        [jax.ShapeDtypeStruct(shape, F32) for shape in shapes],
+        [],
+        16,
+        0,
+        8 * own.size,
+    )
 
 
 def tie(*trees):
@@ -772,6 +850,17 @@
                 pairs.append((d * self.cp + c, (2 * z + y) * self.cp + 2 * core + x))
         return lax.ppermute(a, ("dp", "cp"), pairs)
 
+    def move_wide(self, a):
+        return self.move_tokens(jnp.pad(a, ((0, 0), (0, -a.shape[1] % LANES))))
+
+    def fit(self, rows, later):
+        sizes = [m for m, _ in variants_of(rows, later[0][1].shape[1])]
+        self.choices = (tuple(reversed(sizes)), (rows,) * RECUR)
+        fits = jnp.bool_(True)
+        for r, (meta, _) in enumerate(later):
+            fits = fits & (meta[0] <= RECUR - 2 - r)
+        self.grad_spot = jnp.concatenate([self.spot, jnp.where(fits, 0, 1)[None].astype(jnp.int32)])
+
     def key_block(self):
         return 2 * self.core + self.x if self.square else lax.axis_index("cp")
 
@@ -799,37 +888,25 @@
     def gather_first(self, a):
         if not self.square:
             return (lax.all_gather(a, "cp", axis=0, tiled=True),)
-        cut = -(-a.shape[0] // 32) * 16
-        top, low = a[:cut], a[cut:]
-        return top, low, self.over_x(top), self.over_y(low)
+        return a, self.over_x(a), self.over_y(a)
 
     def gather_second(self, parts):
         if not self.square:
             return parts
-        top, low, from_x, from_y = parts
-        over_y = self.over_y(jnp.concatenate([top, from_x], axis=0))
-        over_x = self.over_x(jnp.concatenate([low, from_y], axis=0))
-        return parts + (over_y, over_x)
+        own, from_x, from_y = parts
+        cut = -(-own.shape[0] // 32) * 16
+        return parts + (self.over_y(from_x[:cut]), self.over_x(from_y[cut:]))
 
     def gather_whole(self, parts):
         if not self.square:
             return parts[0]
-        cut, rest = parts[0].shape[0], parts[1].shape[0]
-        rows = cut + rest
-
-        def move(i, first, count, block, offset):
-            return i, first, count, lambda spot: (spot[0] ^ block) * rows + offset
-
-        moves = [
-            move(0, 0, cut, 0, 0),
-            move(1, 0, rest, 0, cut),
-            move(2, 0, cut, 1, 0),
-            move(3, 0, rest, 2, cut),
-            move(4, 0, cut, 2, 0),
-            move(4, cut, cut, 3, 0),
-            move(5, 0, rest, 1, cut),
-            move(5, rest, rest, 3, cut),
-        ]
+        rows, cut = parts[0].shape[0], parts[3].shape[0]
+
+        def move(i, count, block, offset):
+            return i, 0, count, lambda spot: (spot[0] ^ block) * rows + offset
+
+        moves = [move(0, rows, 0, 0), move(1, rows, 1, 0), move(2, rows, 2, 0)]
+        moves += [move(3, cut, 3, 0), move(4, rows - cut, 3, cut)]
         return settle_call(self.spot, parts, moves, 4 * rows)
 
     def interleave(self, mine, theirs, width):
@@ -842,9 +919,11 @@
         return settle_call(self.spot, (mine, theirs), moves, 2 * mine.shape[0], width)
 
 
-    def halves(self, fill, lefts, rights, stride, each, n, step, extra=()):
+    def halves(self, fill, lefts, rights, stride, each, n, step, extra=(), ready=(), hand=None):
         if self.square:
-            return weight_grad(self.spot, fill, lefts, rights, stride, each, n, step, extra)
+            return weight_grad(
+                self.grad_spot, fill, [] if ready else lefts, rights, stride, each, n, step, self.choices, extra, ready, hand
+            )
         products = []
 
         def product(left, right):
@@ -1122,17 +1201,18 @@
     w["gain_a"], w["gain_f"], w["router"] = small[:1], small[1:2], small[2:]
     first = Level(0, place, context, *all_keys(every, rows, place.core))
     first.project(state, w)
-    first.kv, g_part, downs = tie(first.kv, g_part, downs)
+    first.kv, downs, every = tie(first.kv, downs, every)
 
     kvs = place.gather_keys(first.kv)
-    kvs, g_part, downs, every = tie(kvs, g_part, downs, every)
+    later = active_keys(every, rows, place.core, place.square)
+    kvs, g_part, downs, later = tie(kvs, g_part, downs, later)
 
     g_part = place.gather_second(g_part)
     d_part = place.gather_first(downs)
     first.attend(kvs)
     first.widen(w)
-    later = active_keys(every, rows, place.core, place.square)
-    first.normed2, g_part, d_part, later = tie(first.normed2, g_part, d_part, later)
+    first.normed2, g_part, d_part = tie(first.normed2, g_part, d_part)
+    place.fit(rows, later)
     levels = [first] + [Level(r + 1, place, context, *found) for r, found in enumerate(later)]
 
     d_part = place.gather_second(d_part)
@@ -1149,7 +1229,7 @@
         level.project(state, w)
         level.attend(place.gather_keys(level.kv))
         state = level.post(w)
-    activations = place.move_tokens(reorder(order.T, state.astype(BF16)))[None]
+    activations = place.move_wide(reorder(order.T, state.astype(BF16)))
     grad = reorder(order, place.move_tokens(cotangent[0])).astype(F32)
 
     for level in levels[:0:-1]:
@@ -1183,68 +1263,66 @@
     dkv = first.back_attend()
     u, d, dkv = tie(u, d, dkv)
 
-    u = place.scatter_more(u)
     pair = place.scatter_keys_first(dkv)
     (pair,) = tie(pair)
     pair = place.scatter_keys_second(pair)
+    u = place.scatter_more(u)
     lefts, rights = [every("att"), every("normed")], [every("g_attn"), every("dq")]
-    p = place.halves(fill_choice, lefts, rights, each, each, padded, 512)
+    p = place.halves(fill_choice, lefts, rights, each, each, padded, 512, hand=1)
     u, pair, p = tie(u, pair, p)
 
     u = place.scatter_second(u)
-    p_got = place.over_core(p[-1])
-    d = place.z_second(d)
+    p_got = place.over_core(p[4] if place.square else p[1])
     grad = first.back_project(*pair, w)
     vectors = every("g_router") + [sum(every("g_gain_a")), sum(every("g_gain_f"))]
     vectors = jnp.concatenate(vectors + [jnp.zeros((8 - len(vectors), width), F32)], axis=0)
-    k = place.halves(fill_groups, [every("normed")], [every("dkv")], each, each, part + LANES, part + LANES, (vectors,))
+    ready = p[5:] if place.square else ()
+    k = place.halves(
+        fill_groups, [every("normed")], [every("dkv")], each, each, part + LANES, part + LANES, (vectors,), ready=ready
+    )
     p = place.scatter_ready(p, p_got)
-    u, d, p, k, grad = tie(u, d, p, k, grad)
-
-    p = place.scatter_first(p)
+    u, p, k, grad = tie(u, p, k, grad)
+
     k_got = place.over_core(k[-1])
     u, v = place.scatter_rows(u)
     u = place.z_first(u)
-    k = place.scatter_ready(k, k_got)
-    u, v, p, k = tie(u, v, p, k)
-
-    p, k = place.scatter_second(p), place.scatter_first(k)
+    p = place.scatter_first(p)
+    k = place.scatter_first(place.scatter_ready(k, k_got))
+    d = place.z_second(d)
+    u, v, p, k, d = tie(u, v, p, k, d)
+
+    p, k = place.scatter_second(p), place.scatter_second(k)
     u, v = place.z_second(u), place.z_first(v)
-    u, v, p, k = tie(u, v, p, k)
-
-    k = place.scatter_second(k)
+    d = place.z_third(d)
+    input_grad = place.move_wide(reorder(order.T, grad.astype(BF16)))
+    u, v, p, k, d, input_grad, activations = tie(u, v, p, k, d, input_grad, activations)
+
     u, v = place.z_third(u), place.z_second(v)
     a = place.z_first(jnp.concatenate([place.scatter_whole(k), place.scatter_whole(p)], axis=1))
     u, v, a = tie(u, v, a)
 
     a, v = place.z_second(a), place.z_third(v)
-    d = place.z_third(d)
-    input_grad = place.move_tokens(reorder(order.T, grad.astype(BF16)))[None]
-    a, v, d, input_grad = tie(a, v, d, input_grad)
+    d_own = place.z_whole(d)
+    grad_down = finish_rows_call(place.spot, d_own, place.over_core(d_own), width).T
+    input_grad, activations = (b[None, :, :width] for b in (input_grad, activations))
+    a, v, grad_down, input_grad, activations = tie(a, v, grad_down, input_grad, activations)
 
     a = place.z_third(a)
-    d_own = place.z_whole(d)
-    d_other = place.over_core(d_own)
     u_own = jnp.concatenate([place.z_whole(u), place.z_whole(v)], axis=0)
     u_other = place.over_core(u_own)
     grad_gate, grad_up = place.pick(u_own, u_other).astype(F32), place.pick(u_other, u_own).astype(F32)
-    d_own, d_other = d_own[:, :width], d_other[:, :width]
-    grad_down = jnp.concatenate([place.pick(d_own, d_other), place.pick(d_other, d_own)], axis=0).astype(F32)
-    a, grad_gate, grad_up, grad_down = tie(a, grad_gate, grad_up, grad_down)
+    a, grad_gate, grad_up = tie(a, grad_gate, grad_up)
 
     own = place.z_whole(a)
     other = place.over_core(own)
-    low, high = place.pick(own, other).astype(F32), place.pick(other, own).astype(F32)
-    grad_kv = jnp.concatenate([low[:, :part], high[:, 2 * part - both : part]], axis=1)
-    grad_kv = grad_kv.reshape(each, -1, 2, HEAD_DIM)
-    vectors = low[:, part : part + RECUR + 2].T
+    grad_query, grad_key, grad_value, grad_out, vectors = finish_call(place.spot, own, other, part, both, width)
     return (
         activations,
         input_grad,
-        high[:, part + LANES : part + LANES + width],
-        grad_kv[:, :, 0].reshape(each, -1),
-        grad_kv[:, :, 1].reshape(each, -1),
-        low[:, part + LANES : part + LANES + width],
+        grad_query,
+        grad_key.T,
+        grad_value.T,
+        grad_out,
         grad_gate,
         grad_up,
         grad_down,

time: 589 us -> 543 us (0.922)
  local copies, waits for them, and re-layouts: 89.4 us -> 60.7 us
  Pallas kernels: 172 us -> 158 us
  starting transfers between devices: 79.3 us -> 85.3 us
    unnamed x393 -> x301, local copies, waits for them, and re-layouts: 69 us -> 45 us
    ppermute x22, waiting for transfers between devices: 85.4 us -> 77.3 us  [over_x(): return lax.ppermute(a, 'cp', [(i, i ^ 1) for i in range(self.cp)])]
    concatenate x7 -> x1, other arithmetic: 7.75 us -> 0.08 us  [fit(): jnp.concatenate([self.spot, jnp.where(fits, 0, 1)[None].astype(jnp.int32)])]
    pallas_call x4, Pallas kernels: 36.2 us -> 29.9 us  [weight_grad(): pl.pallas_call(functools.partial(weight_grad_kernel, fill, (len(lefts), l...]
    pallas_call x18 -> x20, Pallas kernels: 126 us -> 120 us  [call(): pl.pallas_call(kernel, grid_spec=pltpu.PrefetchScalarGridSpec(num_scalar_...]
    ppermute x22, starting transfers between devices: 21.5 us -> 27.4 us  [over_x(): return lax.ppermute(a, 'cp', [(i, i ^ 1) for i in range(self.cp)])]
  transfers between devices with their start and end apart: 75 -> 75, of which waited for: 36 -> 36; matrix products, arithmetic and copies ran while one was open for 13% -> 13% of each run, Pallas kernels for 17% -> 18%
where the time goes in v4:
time: 543 us; the launch traced here: 536 us
  waiting for transfers between devices  162 us (30%)
  Pallas kernels  158 us (29%)
  starting transfers between devices  85.3 us (16%)
  local copies, waits for them, and re-layouts  60.7 us (11%)
  other arithmetic  54.6 us (10%)
  matrix products  12.6 us (2%)
    pallas_call x20, Pallas kernels, call(): pl.pallas_call(kernel, grid_spec=pltpu.PrefetchScalarGridSpec(num_scalar_...  120 us
    ppermute x22, waiting for transfers between devices, over_x(): return lax.ppermute(a, 'cp', [(i, i ^ 1) for i in range(self.cp)])  77.3 us
    ppermute x12, waiting for transfers between devices, hop(): lax.ppermute(a, 'dp', [(2 * s + c, 2 * t + c) for s, t in moves for c in...  48.7 us
    unnamed x301, local copies, waits for them, and re-layouts  45 us
    convert_element_type x32, other arithmetic, add(): return sum((a.astype(F32) for a in terms)).astype(BF16)  30.3 us
    pallas_call x4, Pallas kernels, weight_grad(): pl.pallas_call(functools.partial(weight_grad_kernel, fill, (len(lefts), l...  29.9 us
    ppermute x22, starting transfers between devices, over_x(): return lax.ppermute(a, 'cp', [(i, i ^ 1) for i in range(self.cp)])  27.4 us
    ppermute x12, starting transfers between devices, hop(): lax.ppermute(a, 'dp', [(2 * s + c, 2 * t + c) for s, t in moves for c in...  26.5 us
  transfers between devices with their start and end apart: 75, of which 36 were waited for; matrix products, arithmetic and copies ran while one was open for 13% of the time, Pallas kernels for 18%

profile of v4, /device:TPU:0, one launch (start us, length us, event | category | flops | bytes accessed | tf_op | source)
XLA Modules:
  0.0 535.9 jit_solution(2428542564423530582)
XLA Ops:
  10.3 6.1 %collective-permute-start.3 = (bf16[288,960]{1,0:T(8,128)(2,1)}, bf16[288,960]{1,0:T(8,128)(2,1)}, u32[]{:S(2)}, u32[]{:S(2)}) collective-permute-start(bf16[288,960]{1,0:T(8,128)(2,1)} %bitcast.286), channel_id=1, source_target_pairs={{0,0},{1,1},{2,4},{3,5},{4,2},{5,3},{6,6},{7,7},{8,8},{9,9},{10,12... | collective-permute-start | bytes 1658888 | tf_op jit(solution)/shard_map/ppermute | solution.py:851
  72.6 5.5 %select_reduce_fusion = s32[2,3,1152]{2,1,0:T(4,128)S(1)} fusion(s32[3,1152]{1,0:T(4,128)S(1)} %broadcast_add_fusion.1, pred[2,1152,1152]{2,1,0:T(8,128)(4,1)} %iota_compare_fusion), kind=kLoop, calls=%fused_computation | loop fusion | flops 15918336 | bytes 2695680 | tf_op jit(solution)/shard_map/reduce_sum | solution.py:1071
  78.2 9.9 %collective-permute-done.10.refs_1_ = bf16[288,640]{1,0:T(8,128)(2,1)} collective-permute-done((bf16[288,640]{1,0:T(8,128)(2,1)}, bf16[288,640]{1,0:T(8,128)(2,1)}, u32[]{:S(2)}, u32[]{:S(2)}) %collective-permute-start.10) | collective-permute-done | bytes 368672 | tf_op jit(solution)/shard_map/ppermute | solution.py:835
  96.4 15.6 %attend.3 = (bf16[288,960]{1,0:T(8,128)(2,1)S(1)}, f32[288,128]{1,0:T(8,128)S(1)}, bf16[1152,640]{1,0:T(8,128)(2,1)S(1)}) custom-call(s32[10]{0:T(128)S(1)} %pad_add_fusion.4.meta_ref, bf16[288,960]{1,0:T(8,128)(2,1)S(1)} %copy-done.74, bf16[288,640]{1,0:T(8,128)(2,1)} %get-tuple-element.320.refs_0_, bf16[288,640]{1,0:T(8,128)(2,1)} %collective-permute-done.10.refs_1_, ...), custom_call_target="tpu_custom_call" | custom-call | flops 2548039680 | bytes 2580480 | tf_op jit(solution)/shard_map/attend/pallas_call | solution.py:54
  114.4 4.8 collective-permute-done.16.refs_4_
  125.4 6.2 %collective-permute-done.19.theirs = bf16[960,2560]{1,0:T(8,128)(2,1)S(1)} collective-permute-done((bf16[960,2560]{1,0:T(8,128)(2,1)S(1)}, bf16[960,2560]{1,0:T(8,128)(2,1)S(1)}, u32[]{:S(2)}, u32[]{:S(2)}) %collective-permute-start.19) | collective-permute-done | bytes 4915232 | tf_op jit(solution)/shard_map/ppermute | solution.py:841
  137.4 4.8 collective-permute-done.22.refs_1_
  149.3 9.1 %collective-permute-done.23.refs_1_ = bf16[288,640]{1,0:T(8,128)(2,1)S(1)} collective-permute-done((bf16[288,640]{1,0:T(8,128)(2,1)S(1)}, bf16[288,640]{1,0:T(8,128)(2,1)S(1)}, u32[]{:S(2)}, u32[]{:S(2)}) %collective-permute-start.23) | collective-permute-done | bytes 368672 | tf_op jit(solution)/shard_map/ppermute | solution.py:835
  160.2 9.3 %attend.4 = (bf16[288,960]{1,0:T(8,128)(2,1)S(1)}, f32[288,128]{1,0:T(8,128)S(1)}, bf16[1152,640]{1,0:T(8,128)(2,1)S(1)}) custom-call(s32[10]{0:T(128)S(1)} %get-tuple-element.317.meta_ref, bf16[288,960]{1,0:T(8,128)(2,1)S(1)} %get-tuple-element.346.q_ref, bf16[288,640]{1,0:T(8,128)(2,1)S(1)} %get-tuple-element.347.refs_0_, ...), custom_call_target="tpu_custom_call" | custom-call | flops 2548039680 | bytes 2580480 | tf_op jit(solution)/shard_map/attend/pallas_call | solution.py:54
  169.6 7.2 %post.2 = (f32[288,960]{1,0:T(8,128)S(1)}, f32[288,960]{1,0:T(8,128)S(1)}, bf16[288,960]{1,0:T(8,128)(2,1)S(1)}, f32[288,960]{1,0:T(8,128)S(1)}, f32[288,1]{1,0:...) custom-call(s32[10]{0:T(128)S(1)} %get-tuple-element.317.meta_ref, ...), custom_call_target="tpu_custom_call" | custom-call | flops 4777574400 | bytes 16588800 | tf_op jit(solution)/shard_map/post/pallas_call | solution.py:54
  180.8 9.3 %collective-permute-done.26.refs_1_ = bf16[288,640]{1,0:T(8,128)(2,1)S(1)} collective-permute-done((bf16[288,640]{1,0:T(8,128)(2,1)S(1)}, bf16[288,640]{1,0:T(8,128)(2,1)S(1)}, u32[]{:S(2)}, u32[]{:S(2)}) %collective-permute-start.26) | collective-permute-done | bytes 368672 | tf_op jit(solution)/shard_map/ppermute | solution.py:835
  197.4 5.5 %post.3 = (f32[288,960]{1,0:T(8,128)S(1)}, f32[288,960]{1,0:T(8,128)S(1)}, bf16[288,960]{1,0:T(8,128)(2,1)S(1)}, f32[288,960]{1,0:T(8,128)S(1)}, f32[288,1]{1,0:...) custom-call(s32[10]{0:T(128)S(1)} %get-tuple-element.318.meta_ref, ...), custom_call_target="tpu_custom_call" | custom-call | flops 4777574400 | bytes 16588800 | tf_op jit(solution)/shard_map/post/pallas_call | solution.py:54
  203.8 8.1 %post_back.2 = (bf16[288,960]{1,0:T(8,128)(2,1)S(1)}, f32[288,960]{1,0:T(8,128)S(1)}, bf16[288,960]{1,0:T(8,128)(2,1)S(1)}, bf16[288,960]{1,0:T(8,128)(2,1)S(1)}...) custom-call(s32[10]{0:T(128)S(1)} %get-tuple-element.318.meta_ref, ...), custom_call_target="tpu_custom_call" | custom-call | flops 4777574400 | bytes 16588800 | tf_op jit(solution)/shard_map/post_back/pallas_call | solution.py:54
  218.2 6.7 %attend_back.3 = (bf16[288,960]{1,0:T(8,128)(2,1)S(1)}, bf16[1152,640]{1,0:T(8,128)(2,1)S(1)}) custom-call(s32[10]{0:T(128)S(1)} %get-tuple-element.318.meta_ref, bf16[288,960]{1,0:T(8,128)(2,1)S(1)} %copy-done.93, bf16[288,960]{1,0:T(8,128)(2,1)S(1)} %get-tuple-element.363.do_ref, bf16[288,960]{1,0:T(8,128)(2,1)S(1)} %get-tuple-element.355.att.att_ref.refs_2_, ...), custom_call_target="tpu_custom_call" | custom-call | flops 6370099200 | bytes 5160960 | tf_op jit(solution)/shard_map/attend_back/pallas_call | solution.py:54
  229.1 9.1 %collective-permute-done.31.got_ref = bf16[288,640]{1,0:T(8,128)(2,1)S(1)} collective-permute-done((bf16[288,640]{1,0:T(8,128)(2,1)S(1)}, bf16[288,640]{1,0:T(8,128)(2,1)S(1)}, u32[]{:S(2)}, u32[]{:S(2)}) %collective-permute-start.31) | collective-permute-done | bytes 368672 | tf_op jit(solution)/shard_map/ppermute | solution.py:835
  240.9 8.7 %post_back.3 = (bf16[288,960]{1,0:T(8,128)(2,1)S(1)}, f32[288,960]{1,0:T(8,128)S(1)}, bf16[288,960]{1,0:T(8,128)(2,1)S(1)}, bf16[288,960]{1,0:T(8,128)(2,1)S(1)}...) custom-call(s32[10]{0:T(128)S(1)} %get-tuple-element.317.meta_ref, ...), custom_call_target="tpu_custom_call" | custom-call | flops 4777574400 | bytes 16588800 | tf_op jit(solution)/shard_map/post_back/pallas_call | solution.py:54
  252.8 11.3 %attend_back.4 = (bf16[288,960]{1,0:T(8,128)(2,1)S(1)}, bf16[1152,640]{1,0:T(8,128)(2,1)S(1)}) custom-call(s32[10]{0:T(128)S(1)} %get-tuple-element.317.meta_ref, bf16[288,960]{1,0:T(8,128)(2,1)S(1)} %copy-done.89, bf16[288,960]{1,0:T(8,128)(2,1)S(1)} %get-tuple-element.375.do_ref, bf16[288,960]{1,0:T(8,128)(2,1)S(1)} %get-tuple-element.349.att.att_ref.refs_1_, ...), custom_call_target="tpu_custom_call" | custom-call | flops 6370099200 | bytes 5160960 | tf_op jit(solution)/shard_map/attend_back/pallas_call | solution.py:54
  268.4 9.7 %collective-permute-done.33.got_ref = bf16[288,640]{1,0:T(8,128)(2,1)S(1)} collective-permute-done((bf16[288,640]{1,0:T(8,128)(2,1)S(1)}, bf16[288,640]{1,0:T(8,128)(2,1)S(1)}, u32[]{:S(2)}, u32[]{:S(2)}) %collective-permute-start.33) | collective-permute-done | bytes 368672 | tf_op jit(solution)/shard_map/ppermute | solution.py:835
  284.5 8.0 %weight_grad.4 = (bf16[2,160,1024]{2,1,0:T(8,128)(2,1)S(1)}, bf16[2,160,1024]{2,1,0:T(8,128)(2,1)S(1)}, bf16[2,160,1024]{2,1,0:T(8,128)(2,1)S(1)}, bf16[2,160,10...) custom-call(s32[3]{0:T(128)S(1)} %pad_add_fusion.6.spot_ref, bf16[288,2560]{1,0:T(8,128)(2,1)S(1)} %copy-done.101, ...), custom_call_target="tpu_custom_call" | custom-call | flops 4246732800 | bytes 11325440 | tf_op jit(solution)/shard_map/weight_grad/pallas_call | solution.py:679
  307.5 12.3 %weight_grad.5 = (bf16[2,128,2560]{2,1,0:T(8,128)(2,1)S(1)}, bf16[2,128,2560]{2,1,0:T(8,128)(2,1)S(1)}, bf16[2,112,2560]{2,1,0:T(8,128)(2,1)S(1)}, bf16[2,112,25...) custom-call(s32[3]{0:T(128)S(1)} %pad_add_fusion.6.spot_ref, bf16[288,960]{1,0:T(8,128)(2,1)S(1)} %copy-done.46, ...), custom_call_target="tpu_custom_call" | custom-call | flops 8493465600 | bytes 20336640 | tf_op jit(solution)/shard_map/weight_grad/pallas_call | solution.py:679
  321.7 4.8 norm_back.1
  330.5 7.8 %collective-permute-done.39 = bf16[160,1024]{1,0:T(8,128)(2,1)S(1)} collective-permute-done((bf16[160,1024]{1,0:T(8,128)(2,1)S(1)}, bf16[160,1024]{1,0:T(8,128)(2,1)S(1)}, u32[]{:S(2)}, u32[]{:S(2)}) %collective-permute-start.39) | collective-permute-done | bytes 327712 | tf_op jit(solution)/shard_map/ppermute | solution.py:835
  345.9 16.7 %attend_back.5 = (bf16[288,960]{1,0:T(8,128)(2,1)S(1)}, bf16[1152,640]{1,0:T(8,128)(2,1)S(1)}) custom-call(s32[10]{0:T(128)S(1)} %pad_add_fusion.4.meta_ref, bf16[288,960]{1,0:T(8,128)(2,1)S(1)} %copy-done.75, bf16[288,960]{1,0:T(8,128)(2,1)S(1)} %get-tuple-element.436.do_ref, bf16[288,960]{1,0:T(8,128)(2,1)S(1)} %copy-done.36, ...), custom_call_target="tpu_custom_call" | custom-call | flops 6370099200 | bytes 5160960 | tf_op jit(solution)/shard_map/attend_back/pallas_call | solution.py:54
  367.3 7.4 %weight_grad.6 = (bf16[2,128,1024]{2,1,0:T(8,128)(2,1)S(1)}, bf16[2,128,1024]{2,1,0:T(8,128)(2,1)S(1)}, bf16[2,112,1024]{2,1,0:T(8,128)(2,1)S(1)}, bf16[2,112,10...) custom-call(s32[3]{0:T(128)S(1)} %pad_add_fusion.6.spot_ref, ...), custom_call_target="tpu_custom_call" | custom-call | flops 3185049600 | bytes 10567680 | tf_op jit(solution)/shard_map/weight_grad/pallas_call | solution.py:679
  382.3 7.1 %collective-permute-done.47.got_ref = bf16[288,640]{1,0:T(8,128)(2,1)S(1)} collective-permute-done((bf16[288,640]{1,0:T(8,128)(2,1)S(1)}, bf16[288,640]{1,0:T(8,128)(2,1)S(1)}, u32[]{:S(2)}, u32[]{:S(2)}) %collective-permute-start.47) | collective-permute-done | bytes 368672 | tf_op jit(solution)/shard_map/ppermute | solution.py:835
  425.4 7.6 %collective-permute-done.51 = bf16[128,2560]{1,0:T(8,128)(2,1)S(1)} collective-permute-done((bf16[128,2560]{1,0:T(8,128)(2,1)S(1)}, bf16[128,2560]{1,0:T(8,128)(2,1)S(1)}, u32[]{:S(2)}, u32[]{:S(2)}) %collective-permute-start.51) | collective-permute-done | bytes 655392 | tf_op jit(solution)/shard_map/ppermute | solution.py:999
  433.6 5.2 collective-permute-start.59
  453.3 4.8 collective-permute-done.61
  467.9 4.8 collective-permute-start.68
  481.0 7.6 %collective-permute-done.68 = bf16[240,1536]{1,0:T(8,128)(2,1)S(1)} collective-permute-done((bf16[240,1536]{1,0:T(8,128)(2,1)S(1)}, bf16[240,1536]{1,0:T(8,128)(2,1)S(1)}, u32[]{:S(2)}, u32[]{:S(2)}) %collective-permute-start.68) | collective-permute-done | bytes 737312 | tf_op jit(solution)/shard_map/ppermute | solution.py:999
  491.0 17.5 %collective-permute-done.70 = bf16[112,2560]{1,0:T(8,128)(2,1)S(1)} collective-permute-done((bf16[112,2560]{1,0:T(8,128)(2,1)S(1)}, bf16[112,2560]{1,0:T(8,128)(2,1)S(1)}, u32[]{:S(2)}, u32[]{:S(2)}) %collective-permute-start.70) | collective-permute-done | bytes 573472 | tf_op jit(solution)/shard_map/ppermute | solution.py:999
  514.6 15.2 %collective-permute-done.72 = bf16[240,1536]{1,0:T(8,128)(2,1)S(1)} collective-permute-done((bf16[240,1536]{1,0:T(8,128)(2,1)S(1)}, bf16[240,1536]{1,0:T(8,128)(2,1)S(1)}, u32[]{:S(2)}, u32[]{:S(2)}) %collective-permute-start.72) | collective-permute-done | bytes 737312 | tf_op jit(solution)/shard_map/ppermute | solution.py:999
  (593 shorter events, 258.8 us)
Async XLA Ops:
  5.1 21.0 %collective-permute-start.1 = (bf16[240,1408]{1,0:T(8,128)(2,1)S(1)}, bf16[240,1408]{1,0:T(8,128)(2,1)S(1)}, u32[]{:S(2)}, u32[]{:S(2)}) collective-permute-start(bf16[240,1408]{1,0:T(8,128)(2,1)S(1)} %concatenate.38.refs_0_), channel_id=1, source_target_pairs={{0,2},{1,3},{2,0},{3,1},{4,6},{5,7},{6,4},{7,5},{8,10},{9,11},{10,... | collective-permute-start | bytes 2027528 | tf_op jit(solution)/shard_map/ppermute | solution.py:838
  8.1 18.0 %collective-permute-start = (bf16[240,1408]{1,0:T(8,128)(2,1)S(1)}, bf16[240,1408]{1,0:T(8,128)(2,1)S(1)}, u32[]{:S(2)}, u32[]{:S(2)}) collective-permute-start(bf16[240,1408]{1,0:T(8,128)(2,1)S(1)} %concatenate.38.refs_0_), channel_id=1, source_target_pairs={{0,1},{1,0},{2,3},{3,2},{4,5},{5,4},{6,7},{7,6},{8,9},{9,8},{10,11... | collective-permute-start | bytes 2027528 | tf_op jit(solution)/shard_map/ppermute | solution.py:835
  49.0 39.1 %collective-permute-start.14 = (bf16[240,2560]{1,0:T(8,128)(2,1)}, bf16[240,2560]{1,0:T(8,128)(2,1)}, u32[]{:S(2)}, u32[]{:S(2)}) collective-permute-start(bf16[240,2560]{1,0:T(8,128)(2,1)} %broadcast_select_fusion.2.refs_0_), channel_id=1, source_target_pairs={{0,2},{1,3},{2,0},{3,1},{4,6},{5,7},{6,4},{7,5},{8,10},{9,11},{10,... | collective-permute-start | bytes 3686408 | tf_op jit(solution)/shard_map/ppermute | solution.py:838
  50.8 37.4 %collective-permute-start.13 = (bf16[240,2560]{1,0:T(8,128)(2,1)}, bf16[240,2560]{1,0:T(8,128)(2,1)}, u32[]{:S(2)}, u32[]{:S(2)}) collective-permute-start(bf16[240,2560]{1,0:T(8,128)(2,1)} %broadcast_select_fusion.2.refs_0_), channel_id=1, source_target_pairs={{0,1},{1,0},{2,3},{3,2},{4,5},{5,4},{6,7},{7,6},{8,9},{9,8},{10,11... | collective-permute-start | bytes 3686408 | tf_op jit(solution)/shard_map/ppermute | solution.py:835
  66.6 21.5 %collective-permute-start.11 = (bf16[288,640]{1,0:T(8,128)(2,1)}, bf16[288,640]{1,0:T(8,128)(2,1)}, u32[]{:S(2)}, u32[]{:S(2)}) collective-permute-start(bf16[288,640]{1,0:T(8,128)(2,1)} %get-tuple-element.320.refs_0_), channel_id=1, source_target_pairs={{0,4},{4,0},{8,12},{12,8},{16,20},{20,16},{24,28},{28,24},{1,5},{5... | collective-permute-start | bytes 1105928 | tf_op jit(solution)/shard_map/ppermute | solution.py:841
  66.8 21.3 %collective-permute-start.10 = (bf16[288,640]{1,0:T(8,128)(2,1)}, bf16[288,640]{1,0:T(8,128)(2,1)}, u32[]{:S(2)}, u32[]{:S(2)}) collective-permute-start(bf16[288,640]{1,0:T(8,128)(2,1)} %get-tuple-element.320.refs_0_), channel_id=1, source_target_pairs={{0,1},{1,0},{2,3},{3,2},{4,5},{5,4},{6,7},{7,6},{8,9},{9,8},{10,11... | collective-permute-start | bytes 1105928 | tf_op jit(solution)/shard_map/ppermute | solution.py:835
  90.0 30.8 %collective-permute-start.18 = (bf16[320,1024]{1,0:T(8,128)(2,1)S(1)}, bf16[320,1024]{1,0:T(8,128)(2,1)S(1)}, u32[]{:S(2)}, u32[]{:S(2)}) collective-permute-start(bf16[320,1024]{1,0:T(8,128)(2,1)S(1)} %copy-done.20), channel_id=1, source_target_pairs={{0,2},{1,3},{2,0},{3,1},{4,6},{5,7},{6,4},{7,5},{8,10},{9,11},{10,... | collective-permute-start | bytes 1966088 | tf_op jit(solution)/shard_map/ppermute | solution.py:838
  90.4 30.5 %collective-permute-start.17 = (bf16[320,1024]{1,0:T(8,128)(2,1)S(1)}, bf16[320,1024]{1,0:T(8,128)(2,1)S(1)}, u32[]{:S(2)}, u32[]{:S(2)}) collective-permute-start(bf16[320,1024]{1,0:T(8,128)(2,1)S(1)} %copy-done.20), channel_id=1, source_target_pairs={{0,1},{1,0},{2,3},{3,2},{4,5},{5,4},{6,7},{7,6},{8,9},{9,8},{10,11... | collective-permute-start | bytes 1966088 | tf_op jit(solution)/shard_map/ppermute | solution.py:835
  93.0 26.2 %collective-permute-start.16 = (bf16[112,2560]{1,0:T(8,128)(2,1)S(1)}, bf16[112,2560]{1,0:T(8,128)(2,1)S(1)}, u32[]{:S(2)}, u32[]{:S(2)}) collective-permute-start(bf16[112,2560]{1,0:T(8,128)(2,1)S(1)} %slice.344), channel_id=1, source_target_pairs={{0,1},{1,0},{2,3},{3,2},{4,5},{5,4},{6,7},{7,6},{8,9},{9,8},{10,11... | collective-permute-start | bytes 1720328 | tf_op jit(solution)/shard_map/ppermute | solution.py:835
  94.7 26.1 %collective-permute-start.15 = (bf16[128,2560]{1,0:T(8,128)(2,1)S(1)}, bf16[128,2560]{1,0:T(8,128)(2,1)S(1)}, u32[]{:S(2)}, u32[]{:S(2)}) collective-permute-start(bf16[128,2560]{1,0:T(8,128)(2,1)S(1)} %slice.343), channel_id=1, source_target_pairs={{0,2},{1,3},{2,0},{3,1},{4,6},{5,7},{6,4},{7,5},{8,10},{9,11},{10,... | collective-permute-start | bytes 1966088 | tf_op jit(solution)/shard_map/ppermute | solution.py:838
  158.5 31.7 %collective-permute-start.29 = (bf16[288,960]{1,0:T(8,128)(2,1)S(1)}, bf16[288,960]{1,0:T(8,128)(2,1)S(1)}, u32[]{:S(2)}, u32[]{:S(2)}) collective-permute-start(bf16[288,960]{1,0:T(8,128)(2,1)S(1)} %bitcast.287), channel_id=1, source_target_pairs={{0,0},{1,1},{2,4},{3,5},{4,2},{5,3},{6,6},{7,7},{8,8},{9,9},{10,12... | collective-permute-start | bytes 1658888 | tf_op jit(solution)/shard_map/ppermute | solution.py:851
  303.2 17.1 %collective-permute-start.36 = (bf16[2,160,1024]{2,1,0:T(8,128)(2,1)}, bf16[2,160,1024]{2,1,0:T(8,128)(2,1)S(1)}, u32[]{:S(2)}, u32[]{:S(2)}) collective-permute-start(bf16[2,160,1024]{2,1,0:T(8,128)(2,1)} %get-tuple-element.396), channel_id=1, source_target_pairs={{0,1},{1,0},{2,3},{3,2},{4,5},{5,4},{6,7},{7,6},{8,9},{9,8},{10,11... | collective-permute-start | bytes 1966088 | tf_op jit(solution)/shard_map/ppermute | solution.py:835
  304.7 16.9 %collective-permute-start.37 = (bf16[2,160,1024]{2,1,0:T(8,128)(2,1)}, bf16[2,160,1024]{2,1,0:T(8,128)(2,1)}, u32[]{:S(2)}, u32[]{:S(2)}) collective-permute-start(bf16[2,160,1024]{2,1,0:T(8,128)(2,1)} %get-tuple-element.397), channel_id=1, source_target_pairs={{0,2},{1,3},{2,0},{3,1},{4,6},{5,7},{6,4},{7,5},{8,10},{9,11},{10,... | collective-permute-start | bytes 1966088 | tf_op jit(solution)/shard_map/ppermute | solution.py:838
  340.4 22.3 %collective-permute-start.43 = (bf16[320,1024]{1,0:T(8,128)(2,1)S(1)}, bf16[320,1024]{1,0:T(8,128)(2,1)S(1)}, u32[]{:S(2)}, u32[]{:S(2)}) collective-permute-start(bf16[320,1024]{1,0:T(8,128)(2,1)S(1)} %pad_maximum_fusion.1), channel_id=1, source_target_pairs={{0,8},{4,12},{24,16},{28,20},{1,9},{5,13},{25,17},{29,21},{2,10},{... | collective-permute-start | bytes 1966088 | tf_op jit(solution)/shard_map/ppermute | solution.py:999
  344.0 18.6 %collective-permute-start.41 = (bf16[128,2560]{1,0:T(8,128)(2,1)S(1)}, bf16[128,2560]{1,0:T(8,128)(2,1)S(1)}, u32[]{:S(2)}, u32[]{:S(2)}) collective-permute-start(bf16[128,2560]{1,0:T(8,128)(2,1)S(1)} %get-tuple-element.426), channel_id=1, source_target_pairs={{0,1},{1,0},{2,3},{3,2},{4,5},{5,4},{6,7},{7,6},{8,9},{9,8},{10,11... | collective-permute-start | bytes 1966088 | tf_op jit(solution)/shard_map/ppermute | solution.py:835
  345.6 17.0 %collective-permute-start.42 = (bf16[112,2560]{1,0:T(8,128)(2,1)S(1)}, bf16[112,2560]{1,0:T(8,128)(2,1)S(1)}, u32[]{:S(2)}, u32[]{:S(2)}) collective-permute-start(bf16[112,2560]{1,0:T(8,128)(2,1)S(1)} %get-tuple-element.428), channel_id=1, source_target_pairs={{0,2},{1,3},{2,0},{3,1},{4,6},{5,7},{6,4},{7,5},{8,10},{9,11},{10,... | collective-permute-start | bytes 1720328 | tf_op jit(solution)/shard_map/ppermute | solution.py:838
  364.8 17.6 %collective-permute-start.44 = (bf16[128,2560]{1,0:T(8,128)(2,1)S(1)}, bf16[128,2560]{1,0:T(8,128)(2,1)S(1)}, u32[]{:S(2)}, u32[]{:S(2)}) collective-permute-start(bf16[128,2560]{1,0:T(8,128)(2,1)S(1)} %get-tuple-element.443), channel_id=1, source_target_pairs={{0,1},{1,0},{2,3},{3,2},{4,5},{5,4},{6,7},{7,6},{8,9},{9,8},{10,11... | collective-permute-start | bytes 1966088 | tf_op jit(solution)/shard_map/ppermute | solution.py:835
  365.6 23.9 %collective-permute-start.47 = (bf16[288,640]{1,0:T(8,128)(2,1)S(1)}, bf16[288,640]{1,0:T(8,128)(2,1)S(1)}, u32[]{:S(2)}, u32[]{:S(2)}) collective-permute-start(bf16[288,640]{1,0:T(8,128)(2,1)S(1)} %get-tuple-element.606), channel_id=1, source_target_pairs={{0,1},{1,0},{2,3},{3,2},{4,5},{5,4},{6,7},{7,6},{8,9},{9,8},{10,11... | collective-permute-start | bytes 1105928 | tf_op jit(solution)/shard_map/ppermute | solution.py:835
  389.5 16.5 %collective-permute-start.50 = (bf16[4,240,1024]{2,1,0:T(8,128)(2,1)}, bf16[4,240,1024]{2,1,0:T(8,128)(2,1)}, u32[]{:S(2)}, u32[]{:S(2)}) collective-permute-start(bf16[4,240,1024]{2,1,0:T(8,128)(2,1)} %get-tuple-element.472), channel_id=1, source_target_pairs={{0,4},{4,0},{8,12},{12,8},{16,20},{20,16},{24,28},{28,24},{1,5},{5... | collective-permute-start | bytes 5898248 | tf_op jit(solution)/shard_map/ppermute | solution.py:841
  390.5 32.1 %collective-permute-start.57 = (bf16[320,1024]{1,0:T(8,128)(2,1)}, bf16[320,1024]{1,0:T(8,128)(2,1)}, u32[]{:S(2)}, u32[]{:S(2)}) collective-permute-start(bf16[320,1024]{1,0:T(8,128)(2,1)} %add_convert_fusion.8), channel_id=1, source_target_pairs={{8,16},{12,20},{16,8},{20,12},{9,17},{13,21},{17,9},{21,13},{10,18... | collective-permute-start | bytes 1966088 | tf_op jit(solution)/shard_map/ppermute | solution.py:999
  394.8 17.2 %collective-permute-start.48 = (bf16[128,2560]{1,0:T(8,128)(2,1)}, bf16[128,2560]{1,0:T(8,128)(2,1)}, u32[]{:S(2)}, u32[]{:S(2)}) collective-permute-start(bf16[128,2560]{1,0:T(8,128)(2,1)} %fusion.8), channel_id=1, source_target_pairs={{0,2},{1,3},{2,0},{3,1},{4,6},{5,7},{6,4},{7,5},{8,10},{9,11},{10,... | collective-permute-start | bytes 1966088 | tf_op jit(solution)/shard_map/ppermute | solution.py:838
  415.4 17.6 %collective-permute-start.51 = (bf16[128,2560]{1,0:T(8,128)(2,1)S(1)}, bf16[128,2560]{1,0:T(8,128)(2,1)S(1)}, u32[]{:S(2)}, u32[]{:S(2)}) collective-permute-start(bf16[128,2560]{1,0:T(8,128)(2,1)S(1)} %fusion.6), channel_id=1, source_target_pairs={{0,8},{4,12},{24,16},{28,20},{1,9},{5,13},{25,17},{29,21},{2,10},{... | collective-permute-start | bytes 1966088 | tf_op jit(solution)/shard_map/ppermute | solution.py:999
  423.9 21.5 %collective-permute-start.65 = (bf16[288,1024]{1,0:T(8,128)(2,1)S(1)}, bf16[288,1024]{1,0:T(8,128)(2,1)}, u32[]{:S(2)}, u32[]{:S(2)}) collective-permute-start(bf16[288,1024]{1,0:T(8,128)(2,1)S(1)} %pad.14), channel_id=1, source_target_pairs={{0,0},{1,1},{2,4},{3,5},{4,2},{5,3},{6,6},{7,7},{8,8},{9,9},{10,12... | collective-permute-start | bytes 1769480 | tf_op jit(solution)/shard_map/ppermute | solution.py:851
  433.6 24.5 %collective-permute-start.59 = (bf16[112,2560]{1,0:T(8,128)(2,1)}, bf16[112,2560]{1,0:T(8,128)(2,1)}, u32[]{:S(2)}, u32[]{:S(2)}) collective-permute-start(bf16[112,2560]{1,0:T(8,128)(2,1)} %fusion.17), channel_id=1, source_target_pairs={{0,8},{4,12},{24,16},{28,20},{1,9},{5,13},{25,17},{29,21},{2,10},{... | collective-permute-start | bytes 1720328 | tf_op jit(solution)/shard_map/ppermute | solution.py:999
  440.4 17.8 %collective-permute-start.64 = (bf16[320,1024]{1,0:T(8,128)(2,1)S(1)}, bf16[320,1024]{1,0:T(8,128)(2,1)S(1)}, u32[]{:S(2)}, u32[]{:S(2)}) collective-permute-start(bf16[320,1024]{1,0:T(8,128)(2,1)S(1)} %add_convert_fusion.6), channel_id=1, source_target_pairs={{8,0},{12,4},{16,24},{20,28},{9,1},{13,5},{17,25},{21,29},{10,2},{... | collective-permute-start | bytes 1966088 | tf_op jit(solution)/shard_map/ppermute | solution.py:999
  442.0 17.1 %collective-permute-start.58 = (bf16[128,2560]{1,0:T(8,128)(2,1)S(1)}, bf16[128,2560]{1,0:T(8,128)(2,1)}, u32[]{:S(2)}, u32[]{:S(2)}) collective-permute-start(bf16[128,2560]{1,0:T(8,128)(2,1)S(1)} %add_convert_fusion.7), channel_id=1, source_target_pairs={{8,16},{12,20},{16,8},{20,12},{9,17},{13,21},{17,9},{21,13},{10,18... | collective-permute-start | bytes 1966088 | tf_op jit(solution)/shard_map/ppermute | solution.py:999
  460.3 17.2 %collective-permute-start.71 = (bf16[320,1024]{1,0:T(8,128)(2,1)S(1)}, bf16[320,1024]{1,0:T(8,128)(2,1)S(1)}, u32[]{:S(2)}, u32[]{:S(2)}) collective-permute-start(bf16[320,1024]{1,0:T(8,128)(2,1)S(1)} %broadcast_select_fusion.5.own), channel_id=1, source_target_pairs={{0,4},{4,0},{8,12},{12,8},{16,20},{20,16},{24,28},{28,24},{1,5},{5... | collective-permute-start | bytes 1966088 | tf_op jit(solution)/shard_map/ppermute | solution.py:841
  462.0 19.0 %collective-permute-start.66 = (bf16[128,2560]{1,0:T(8,128)(2,1)S(1)}, bf16[128,2560]{1,0:T(8,128)(2,1)S(1)}, u32[]{:S(2)}, u32[]{:S(2)}) collective-permute-start(bf16[128,2560]{1,0:T(8,128)(2,1)S(1)} %add_convert_fusion.5), channel_id=1, source_target_pairs={{8,0},{12,4},{16,24},{20,28},{9,1},{13,5},{17,25},{21,29},{10,2},{... | collective-permute-start | bytes 1966088 | tf_op jit(solution)/shard_map/ppermute | solution.py:999
  467.9 20.7 %collective-permute-start.68 = (bf16[240,1536]{1,0:T(8,128)(2,1)S(1)}, bf16[240,1536]{1,0:T(8,128)(2,1)S(1)}, u32[]{:S(2)}, u32[]{:S(2)}) collective-permute-start(bf16[240,1536]{1,0:T(8,128)(2,1)S(1)} %maximum_maximum_fusion), channel_id=1, source_target_pairs={{0,8},{4,12},{24,16},{28,20},{1,9},{5,13},{25,17},{29,21},{2,10},{... | collective-permute-start | bytes 2211848 | tf_op jit(solution)/shard_map/ppermute | solution.py:999
  488.8 19.8 %collective-permute-start.69 = (bf16[240,1536]{1,0:T(8,128)(2,1)S(1)}, bf16[240,1536]{1,0:T(8,128)(2,1)S(1)}, u32[]{:S(2)}, u32[]{:S(2)}) collective-permute-start(bf16[240,1536]{1,0:T(8,128)(2,1)S(1)} %add_convert_fusion.1), channel_id=1, source_target_pairs={{8,16},{12,20},{16,8},{20,12},{9,17},{13,21},{17,9},{21,13},{10,18... | collective-permute-start | bytes 2211848 | tf_op jit(solution)/shard_map/ppermute | solution.py:999
  489.6 18.9 %collective-permute-start.70 = (bf16[112,2560]{1,0:T(8,128)(2,1)S(1)}, bf16[112,2560]{1,0:T(8,128)(2,1)S(1)}, u32[]{:S(2)}, u32[]{:S(2)}) collective-permute-start(bf16[112,2560]{1,0:T(8,128)(2,1)S(1)} %add_convert_fusion.9), channel_id=1, source_target_pairs={{8,0},{12,4},{16,24},{20,28},{9,1},{13,5},{17,25},{21,29},{10,2},{... | collective-permute-start | bytes 1720328 | tf_op jit(solution)/shard_map/ppermute | solution.py:999
  508.9 20.8 %collective-permute-start.72 = (bf16[240,1536]{1,0:T(8,128)(2,1)S(1)}, bf16[240,1536]{1,0:T(8,128)(2,1)S(1)}, u32[]{:S(2)}, u32[]{:S(2)}) collective-permute-start(bf16[240,1536]{1,0:T(8,128)(2,1)S(1)} %add_convert_fusion), channel_id=1, source_target_pairs={{8,0},{12,4},{16,24},{20,28},{9,1},{13,5},{17,25},{21,29},{10,2},{... | collective-permute-start | bytes 2211848 | tf_op jit(solution)/shard_map/ppermute | solution.py:999
  (191 other events, 1702.4 us)

commit v5 on v4

--- a/solution.py
+++ b/solution.py
@@ -173,12 +173,12 @@
             block += 1
 
 
-def by_group(count, do):
+def by_group(count, do, unroll=False):
     def one(g, _):
         do(g, pl.ds(pl.multiple_of(g * LANES, LANES), LANES))
         return 0
 
-    lax.fori_loop(0, count, one, 0)
+    lax.fori_loop(0, count, one, 0, unroll=unroll)
 
 
 def stacked(m):
@@ -199,10 +199,15 @@
         def group(g, cols):
             kv = keys[:n, cols]
             lane = lax.broadcasted_iota(jnp.int32, (m, LANES), 1)
-            for first in range(0, GROUP, at_once):
-                heads = [g * GROUP + first + j for j in range(at_once)]
+            sets = [[g * GROUP + first + j for j in range(at_once)] for first in range(0, GROUP, at_once)]
+
+            def score(heads):
                 queries = jnp.concatenate([q_all[h, :m] for h in heads], axis=0)
-                s = dotf(queries, kv, NT) + jnp.concatenate([bias[:m, :n]] * at_once, axis=0)
+                return dotf(queries, kv, NT) + jnp.concatenate([bias[:m, :n]] * at_once, axis=0)
+
+            s = score(sets[0])
+            for i, heads in enumerate(sets):
+                following = score(sets[i + 1]) if i + 1 < len(sets) else None
                 peak = jnp.max(s, axis=1, keepdims=True)
                 e = jnp.exp(s - peak)
                 total = jnp.sum(e, axis=1, keepdims=True)
@@ -212,8 +217,9 @@
                     here = slice(j * m, (j + 1) * m)
                     o_all[h, :m] = o[here]
                     lse_ref[:m, :] = jnp.where(lane == h, log[here], lse_ref[:m, :])
-
-        by_group(groups, group)
+                s = following
+
+        by_group(groups, group, True)
         join_pairs(o_all, att_ref, False, m)
         clear(m, att_ref)
 
@@ -240,7 +246,7 @@
             pltpu.VMEM((heads, rows, LANES), BF16),
             pltpu.VMEM((heads, rows, LANES), F32),
         ],
-        16,
+        24,
         4 * rows * keys * LANES * heads,
         4 * q.size + 2 * keys * both,
     )
@@ -263,15 +269,20 @@
             kv = keys[:n, cols]
             cos, sin = turns(row_ref[:m], False)
             lane = lax.broadcasted_iota(jnp.int32, (m, LANES), 1)
-            for first in range(0, GROUP, at_once):
-                heads = [g * GROUP + first + j for j in range(at_once)]
-                here = slice(first * m, (first + at_once) * m)
-                stack = lambda parts: jnp.concatenate(parts, axis=0)
+            stack = lambda parts: jnp.concatenate(parts, axis=0)
+            sets = [[g * GROUP + first + j for j in range(at_once)] for first in range(0, GROUP, at_once)]
+
+            def score(heads):
+                s = dotf(stack([q_all[h, :m] for h in heads]), kv, NT) + stack([bias[:m, :n]] * at_once)
+                return s, dotf(stack([do_all[h, :m] for h in heads]), kv, NT)
+
+            s, dp = score(sets[0])
+            for i, heads in enumerate(sets):
+                following = score(sets[i + 1]) if i + 1 < len(sets) else (None, None)
+                here = slice(i * at_once * m, (i + 1) * at_once * m)
                 logs = stack([jnp.sum(jnp.where(lane == h, lse_ref[:m], 0.0), axis=1, keepdims=True) for h in heads])
                 dots = stack([jnp.sum(dq_all[h, :m], axis=1, keepdims=True) for h in heads])
-                s = dotf(stack([q_all[h, :m] for h in heads]), kv, NT) + stack([bias[:m, :n]] * at_once)
                 p = jnp.exp(s - logs)
-                dp = dotf(stack([do_all[h, :m] for h in heads]), kv, NT)
                 ds = (p * (dp - dots)).astype(BF16)
                 p3[here, :n] = p.astype(BF16)
                 ds3[here, :n] = ds
@@ -279,12 +290,13 @@
                 for j, h in enumerate(heads):
                     one = dq[j * m : (j + 1) * m]
                     dq_all[h, :m] = one * cos - turn(one) * sin
+                s, dp = following
             q3 = jnp.concatenate([q_all[g * GROUP + j, :m] for j in range(GROUP)], axis=0)
             do3 = jnp.concatenate([do_all[g * GROUP + j, :m] for j in range(GROUP)], axis=0)
             dkv = dotf(q3, ds3[: GROUP * m, :n], TN) + dotf(do3, p3[: GROUP * m, :n], TN)
             back[:n, cols] = dkv.T
 
-        by_group(groups, group)
+        by_group(groups, group, False)
         join_pairs(dq_all, dq_ref, True, m)
         clear(m, dq_ref)
 
@@ -319,7 +331,7 @@
             pltpu.VMEM((GROUP * rows, keys), BF16),
             pltpu.VMEM((heads, rows, LANES), F32),
         ],
-        24,
+        32,
         10 * rows * keys * LANES * heads,
         8 * q.size + 4 * keys * both,
     )
@@ -974,14 +986,19 @@
         over_x, over_y, from_x, from_y = parts[3:]
         return parts[:3] + ([self.over_x(over_x[0])] + from_x, [self.over_y(over_y[0])] + from_y)
 
-    def scatter_second(self, parts):
+    def scatter_next(self, parts):
         if not self.square:
             return parts
         top, low, got, from_x, from_y = parts
         cut = top.shape[1]
         top_out = add(top[1], got[1, 0, :cut], from_x[1])
         low_out = add(low[1], got[0, 1, cut:], from_y[1])
-        return parts + (self.over_y(top_out), self.over_x(low_out))
+        return parts + (top_out, low_out)
+
+    def scatter_second(self, parts):
+        if not self.square:
+            return parts
+        return parts[:5] + (self.over_y(parts[5]), self.over_x(parts[6]))
 
     def scatter_rows(self, parts):
         if not self.square:
@@ -1253,6 +1270,8 @@
     d, u = tie(d, u)
 
     u_got = place.over_core(u[-1])
+    d = place.scatter_next(d)
+    d, first.g_mine, first.g_theirs = tie(d, first.g_mine, first.g_theirs)
     d = place.scatter_second(d)
     first.back_norm(w)
     u = place.scatter_ready(u, u_got, True)
@@ -1271,6 +1290,8 @@
     p = place.halves(fill_choice, lefts, rights, each, each, padded, 512, hand=1)
     u, pair, p = tie(u, pair, p)
 
+    u = place.scatter_next(u)
+    u, pair = tie(u, pair)
     u = place.scatter_second(u)
     p_got = place.over_core(p[4] if place.square else p[1])
     grad = first.back_project(*pair, w)
@@ -1291,14 +1312,17 @@
     d = place.z_second(d)
     u, v, p, k, d = tie(u, v, p, k, d)
 
+    p, k = place.scatter_next(p), place.scatter_next(k)
+    u, v, p, k, d = tie(u, v, p, k, d)
     p, k = place.scatter_second(p), place.scatter_second(k)
     u, v = place.z_second(u), place.z_first(v)
     d = place.z_third(d)
     input_grad = place.move_wide(reorder(order.T, grad.astype(BF16)))
     u, v, p, k, d, input_grad, activations = tie(u, v, p, k, d, input_grad, activations)
 
-    u, v = place.z_third(u), place.z_second(v)
-    a = place.z_first(jnp.concatenate([place.scatter_whole(k), place.scatter_whole(p)], axis=1))
+    a = jnp.concatenate([place.scatter_whole(k), place.scatter_whole(p)], axis=1)
+    u, v, a = tie(u, v, a)
+    u, v, a = place.z_third(u), place.z_second(v), place.z_first(a)
     u, v, a = tie(u, v, a)
 
     a, v = place.z_second(a), place.z_third(v)

time: 543 us -> 547 us (level)
  waiting for transfers between devices: 162 us -> 153 us
  other arithmetic: 54.6 us -> 60.8 us
    unnamed x301 -> x361, local copies, waits for them, and re-layouts: 45 us -> 48.2 us
  transfers between devices with their start and end apart: 75 -> 75, of which waited for: 36 -> 32; matrix products, arithmetic and copies ran while one was open for 13% -> 14% of each run, Pallas kernels for 18% -> 17%
where the time goes in v5:
time: 547 us; the launch traced here: 538 us
  Pallas kernels  154 us (28%)
  waiting for transfers between devices  153 us (28%)
  starting transfers between devices  89.9 us (16%)
  local copies, waits for them, and re-layouts  64.5 us (12%)
  other arithmetic  60.8 us (11%)
  matrix products  12.7 us (2%)
    pallas_call x20, Pallas kernels, call(): pl.pallas_call(kernel, grid_spec=pltpu.PrefetchScalarGridSpec(num_scalar_...  116 us
    ppermute x22, waiting for transfers between devices, over_x(): return lax.ppermute(a, 'cp', [(i, i ^ 1) for i in range(self.cp)])  75.6 us
    unnamed x361, local copies, waits for them, and re-layouts  48.2 us
    ppermute x12, waiting for transfers between devices, hop(): lax.ppermute(a, 'dp', [(2 * s + c, 2 * t + c) for s, t in moves for c in...  47.2 us
    convert_element_type x32, other arithmetic, add(): return sum((a.astype(F32) for a in terms)).astype(BF16)  35.4 us
    pallas_call x4, Pallas kernels, weight_grad(): pl.pallas_call(functools.partial(weight_grad_kernel, fill, (len(lefts), l...  30.7 us
    ppermute x12, starting transfers between devices, hop(): lax.ppermute(a, 'dp', [(2 * s + c, 2 * t + c) for s, t in moves for c in...  28.2 us
    ppermute x22, starting transfers between devices, over_x(): return lax.ppermute(a, 'cp', [(i, i ^ 1) for i in range(self.cp)])  27 us
  transfers between devices with their start and end apart: 75, of which 32 were waited for; matrix products, arithmetic and copies ran while one was open for 14% of the time, Pallas kernels for 17%

profile of v5, /device:TPU:0, one launch (start us, length us, event | category | flops | bytes accessed | tf_op | source)
XLA Modules:
  0.0 538.2 jit_solution(10755659926760744691)
XLA Ops:
  10.3 6.1 %collective-permute-start.3 = (bf16[288,960]{1,0:T(8,128)(2,1)}, bf16[288,960]{1,0:T(8,128)(2,1)}, u32[]{:S(2)}, u32[]{:S(2)}) collective-permute-start(bf16[288,960]{1,0:T(8,128)(2,1)} %bitcast.280), channel_id=1, source_target_pairs={{0,0},{1,1},{2,4},{3,5},{4,2},{5,3},{6,6},{7,7},{8,8},{9,9},{10,12... | collective-permute-start | bytes 1658888 | tf_op jit(solution)/shard_map/ppermute | solution.py:863
  73.6 5.5 %select_reduce_fusion = s32[2,3,1152]{2,1,0:T(4,128)S(1)} fusion(s32[3,1152]{1,0:T(4,128)S(1)} %broadcast_add_fusion.1, pred[2,1152,1152]{2,1,0:T(8,128)(4,1)} %iota_compare_fusion), kind=kLoop, calls=%fused_computation | loop fusion | flops 15918336 | bytes 2695680 | tf_op jit(solution)/shard_map/reduce_sum | solution.py:1088
  79.2 8.9 %collective-permute-done.10.refs_1_ = bf16[288,640]{1,0:T(8,128)(2,1)} collective-permute-done((bf16[288,640]{1,0:T(8,128)(2,1)}, bf16[288,640]{1,0:T(8,128)(2,1)}, u32[]{:S(2)}, u32[]{:S(2)}) %collective-permute-start.10) | collective-permute-done | bytes 368672 | tf_op jit(solution)/shard_map/ppermute | solution.py:847
  96.5 11.4 %attend.3 = (bf16[288,960]{1,0:T(8,128)(2,1)S(1)}, f32[288,128]{1,0:T(8,128)S(1)}, bf16[1152,640]{1,0:T(8,128)(2,1)S(1)}) custom-call(s32[10]{0:T(128)S(1)} %pad_add_fusion.4.meta_ref, bf16[288,960]{1,0:T(8,128)(2,1)S(1)} %copy-done.94, bf16[288,640]{1,0:T(8,128)(2,1)} %get-tuple-element.362.refs_0_, bf16[288,640]{1,0:T(8,128)(2,1)} %collective-permute-done.10.refs_1_, ...), custom_call_target="tpu_custom_call" | custom-call | flops 2548039680 | bytes 2580480 | tf_op jit(solution)/shard_map/attend/pallas_call | solution.py:54
  110.2 8.9 %collective-permute-done.16.refs_4_ = bf16[112,2560]{1,0:T(8,128)(2,1)S(1)} collective-permute-done((bf16[112,2560]{1,0:T(8,128)(2,1)S(1)}, bf16[112,2560]{1,0:T(8,128)(2,1)S(1)}, u32[]{:S(2)}, u32[]{:S(2)}) %collective-permute-start.16) | collective-permute-done | bytes 573472 | tf_op jit(solution)/shard_map/ppermute | solution.py:847
  125.5 6.2 %collective-permute-done.19.theirs = bf16[960,2560]{1,0:T(8,128)(2,1)S(1)} collective-permute-done((bf16[960,2560]{1,0:T(8,128)(2,1)S(1)}, bf16[960,2560]{1,0:T(8,128)(2,1)S(1)}, u32[]{:S(2)}, u32[]{:S(2)}) %collective-permute-start.19) | collective-permute-done | bytes 4915232 | tf_op jit(solution)/shard_map/ppermute | solution.py:853
  138.0 4.3 collective-permute-done.22.refs_1_
  149.5 9.1 %collective-permute-done.23.refs_1_ = bf16[288,640]{1,0:T(8,128)(2,1)S(1)} collective-permute-done((bf16[288,640]{1,0:T(8,128)(2,1)S(1)}, bf16[288,640]{1,0:T(8,128)(2,1)S(1)}, u32[]{:S(2)}, u32[]{:S(2)}) %collective-permute-start.23) | collective-permute-done | bytes 368672 | tf_op jit(solution)/shard_map/ppermute | solution.py:847
  160.4 7.5 %attend.4 = (bf16[288,960]{1,0:T(8,128)(2,1)S(1)}, f32[288,128]{1,0:T(8,128)S(1)}, bf16[1152,640]{1,0:T(8,128)(2,1)S(1)}) custom-call(s32[10]{0:T(128)S(1)} %get-tuple-element.359.meta_ref, bf16[288,960]{1,0:T(8,128)(2,1)S(1)} %get-tuple-element.388.q_ref, bf16[288,640]{1,0:T(8,128)(2,1)S(1)} %get-tuple-element.389.refs_0_, ...), custom_call_target="tpu_custom_call" | custom-call | flops 2548039680 | bytes 2580480 | tf_op jit(solution)/shard_map/attend/pallas_call | solution.py:54
  167.9 10.2 %post.2 = (f32[288,960]{1,0:T(8,128)S(1)}, f32[288,960]{1,0:T(8,128)S(1)}, bf16[288,960]{1,0:T(8,128)(2,1)S(1)}, f32[288,960]{1,0:T(8,128)S(1)}, f32[288,1]{1,0:...) custom-call(s32[10]{0:T(128)S(1)} %get-tuple-element.359.meta_ref, ...), custom_call_target="tpu_custom_call" | custom-call | flops 4777574400 | bytes 16588800 | tf_op jit(solution)/shard_map/post/pallas_call | solution.py:54
  182.0 9.3 %collective-permute-done.26.refs_1_ = bf16[288,640]{1,0:T(8,128)(2,1)S(1)} collective-permute-done((bf16[288,640]{1,0:T(8,128)(2,1)S(1)}, bf16[288,640]{1,0:T(8,128)(2,1)S(1)}, u32[]{:S(2)}, u32[]{:S(2)}) %collective-permute-start.26) | collective-permute-done | bytes 368672 | tf_op jit(solution)/shard_map/ppermute | solution.py:847
  197.1 7.0 %post.3 = (f32[288,960]{1,0:T(8,128)S(1)}, f32[288,960]{1,0:T(8,128)S(1)}, bf16[288,960]{1,0:T(8,128)(2,1)S(1)}, f32[288,960]{1,0:T(8,128)S(1)}, f32[288,1]{1,0:...) custom-call(s32[10]{0:T(128)S(1)} %get-tuple-element.360.meta_ref, ...), custom_call_target="tpu_custom_call" | custom-call | flops 4777574400 | bytes 16588800 | tf_op jit(solution)/shard_map/post/pallas_call | solution.py:54
  206.2 7.9 %post_back.2 = (bf16[288,960]{1,0:T(8,128)(2,1)S(1)}, f32[288,960]{1,0:T(8,128)S(1)}, bf16[288,960]{1,0:T(8,128)(2,1)S(1)}, bf16[288,960]{1,0:T(8,128)(2,1)S(1)}...) custom-call(s32[10]{0:T(128)S(1)} %get-tuple-element.360.meta_ref, ...), custom_call_target="tpu_custom_call" | custom-call | flops 4777574400 | bytes 16588800 | tf_op jit(solution)/shard_map/post_back/pallas_call | solution.py:54
  220.5 6.4 %attend_back.3 = (bf16[288,960]{1,0:T(8,128)(2,1)S(1)}, bf16[1152,640]{1,0:T(8,128)(2,1)S(1)}) custom-call(s32[10]{0:T(128)S(1)} %get-tuple-element.360.meta_ref, bf16[288,960]{1,0:T(8,128)(2,1)S(1)} %copy-done.115, bf16[288,960]{1,0:T(8,128)(2,1)S(1)} %get-tuple-element.405.do_ref, bf16[288,960]{1,0:T(8,128)(2,1)S(1)} %get-tuple-element.397.att.att_ref.refs_2_, ...), custom_call_target="tpu_custom_call" | custom-call | flops 6370099200 | bytes 5160960 | tf_op jit(solution)/shard_map/attend_back/pallas_call | solution.py:54
  231.1 9.1 %collective-permute-done.31.got_ref = bf16[288,640]{1,0:T(8,128)(2,1)S(1)} collective-permute-done((bf16[288,640]{1,0:T(8,128)(2,1)S(1)}, bf16[288,640]{1,0:T(8,128)(2,1)S(1)}, u32[]{:S(2)}, u32[]{:S(2)}) %collective-permute-start.31) | collective-permute-done | bytes 368672 | tf_op jit(solution)/shard_map/ppermute | solution.py:847
  242.3 8.7 %post_back.3 = (bf16[288,960]{1,0:T(8,128)(2,1)S(1)}, f32[288,960]{1,0:T(8,128)S(1)}, bf16[288,960]{1,0:T(8,128)(2,1)S(1)}, bf16[288,960]{1,0:T(8,128)(2,1)S(1)}...) custom-call(s32[10]{0:T(128)S(1)} %copy-done.71, ...), custom_call_target="tpu_custom_call" | custom-call | flops 4777574400 | bytes 16588800 | tf_op jit(solution)/shard_map/post_back/pallas_call | solution.py:54
  254.9 11.2 %attend_back.4 = (bf16[288,960]{1,0:T(8,128)(2,1)S(1)}, bf16[1152,640]{1,0:T(8,128)(2,1)S(1)}) custom-call(s32[10]{0:T(128)S(1)} %copy-done.71, bf16[288,960]{1,0:T(8,128)(2,1)S(1)} %copy-done.109, bf16[288,960]{1,0:T(8,128)(2,1)S(1)} %get-tuple-element.417.do_ref, bf16[288,960]{1,0:T(8,128)(2,1)S(1)} %get-tuple-element.391.att.att_ref.refs_1_, ...), custom_call_target="tpu_custom_call" | custom-call | flops 6370099200 | bytes 5160960 | tf_op jit(solution)/shard_map/attend_back/pallas_call | solution.py:54
  270.5 9.8 %collective-permute-done.33.got_ref = bf16[288,640]{1,0:T(8,128)(2,1)S(1)} collective-permute-done((bf16[288,640]{1,0:T(8,128)(2,1)S(1)}, bf16[288,640]{1,0:T(8,128)(2,1)S(1)}, u32[]{:S(2)}, u32[]{:S(2)}) %collective-permute-start.33) | collective-permute-done | bytes 368672 | tf_op jit(solution)/shard_map/ppermute | solution.py:847
  286.4 8.7 %weight_grad.4 = (bf16[2,160,1024]{2,1,0:T(8,128)(2,1)S(1)}, bf16[2,160,1024]{2,1,0:T(8,128)(2,1)S(1)}, bf16[2,160,1024]{2,1,0:T(8,128)(2,1)S(1)}, bf16[2,160,10...) custom-call(s32[3]{0:T(128)S(1)} %pad_add_fusion.6.spot_ref, bf16[288,2560]{1,0:T(8,128)(2,1)S(1)} %copy-done.123, ...), custom_call_target="tpu_custom_call" | custom-call | flops 4246732800 | bytes 11325440 | tf_op jit(solution)/shard_map/weight_grad/pallas_call | solution.py:691
  298.0 4.2 expand_back.1
  309.5 12.5 %weight_grad.5 = (bf16[2,128,2560]{2,1,0:T(8,128)(2,1)S(1)}, bf16[2,128,2560]{2,1,0:T(8,128)(2,1)S(1)}, bf16[2,112,2560]{2,1,0:T(8,128)(2,1)S(1)}, bf16[2,112,25...) custom-call(s32[3]{0:T(128)S(1)} %pad_add_fusion.6.spot_ref, bf16[288,960]{1,0:T(8,128)(2,1)S(1)} %copy-done.46, ...), custom_call_target="tpu_custom_call" | custom-call | flops 8493465600 | bytes 20336640 | tf_op jit(solution)/shard_map/weight_grad/pallas_call | solution.py:691
  329.6 4.8 norm_back.1
  345.0 16.2 %attend_back.5 = (bf16[288,960]{1,0:T(8,128)(2,1)S(1)}, bf16[1152,640]{1,0:T(8,128)(2,1)S(1)}) custom-call(s32[10]{0:T(128)S(1)} %copy-done.73, bf16[288,960]{1,0:T(8,128)(2,1)S(1)} %copy-done.95, bf16[288,960]{1,0:T(8,128)(2,1)S(1)} %get-tuple-element.487.do_ref, bf16[288,960]{1,0:T(8,128)(2,1)S(1)} %copy-done.38, bf16[1152,640]{1,0:T(8,128)(2,1)S(1)} %copy-done.127, ...), custom_call_target="tpu_custom_call" | custom-call | flops 6370099200 | bytes 5160960 | tf_op jit(solution)/shard_map/attend_back/pallas_call | solution.py:54
  366.7 7.4 %weight_grad.6 = (bf16[2,128,1024]{2,1,0:T(8,128)(2,1)S(1)}, bf16[2,128,1024]{2,1,0:T(8,128)(2,1)S(1)}, bf16[2,112,1024]{2,1,0:T(8,128)(2,1)S(1)}, bf16[2,112,10...) custom-call(s32[3]{0:T(128)S(1)} %pad_add_fusion.6.spot_ref, ...), custom_call_target="tpu_custom_call" | custom-call | flops 3185049600 | bytes 10567680 | tf_op jit(solution)/shard_map/weight_grad/pallas_call | solution.py:691
  381.1 7.1 %collective-permute-done.47.got_ref = bf16[288,640]{1,0:T(8,128)(2,1)S(1)} collective-permute-done((bf16[288,640]{1,0:T(8,128)(2,1)S(1)}, bf16[288,640]{1,0:T(8,128)(2,1)S(1)}, u32[]{:S(2)}, u32[]{:S(2)}) %collective-permute-start.47) | collective-permute-done | bytes 368672 | tf_op jit(solution)/shard_map/ppermute | solution.py:847
  427.7 6.2 %collective-permute-done.51 = bf16[128,2560]{1,0:T(8,128)(2,1)S(1)} collective-permute-done((bf16[128,2560]{1,0:T(8,128)(2,1)S(1)}, bf16[128,2560]{1,0:T(8,128)(2,1)S(1)}, u32[]{:S(2)}, u32[]{:S(2)}) %collective-permute-start.51) | collective-permute-done | bytes 655392 | tf_op jit(solution)/shard_map/ppermute | solution.py:1016
  441.4 7.8 %collective-permute-start.59 = (bf16[112,2560]{1,0:T(8,128)(2,1)}, bf16[112,2560]{1,0:T(8,128)(2,1)}, u32[]{:S(2)}, u32[]{:S(2)}) collective-permute-start(bf16[112,2560]{1,0:T(8,128)(2,1)} %fusion.17), channel_id=1, source_target_pairs={{0,8},{4,12},{24,16},{28,20},{1,9},{5,13},{25,17},{29,21},{2,10},{... | collective-permute-start | bytes 1720328 | tf_op jit(solution)/shard_map/ppermute | solution.py:1016
  457.1 5.3 collective-permute-done.61
  470.5 4.7 collective-permute-start.68
  482.7 5.4 %collective-permute-done.66 = bf16[128,2560]{1,0:T(8,128)(2,1)S(1)} collective-permute-done((bf16[128,2560]{1,0:T(8,128)(2,1)S(1)}, bf16[128,2560]{1,0:T(8,128)(2,1)S(1)}, u32[]{:S(2)}, u32[]{:S(2)}) %collective-permute-start.66) | collective-permute-done | bytes 655392 | tf_op jit(solution)/shard_map/ppermute | solution.py:1016
  493.5 17.3 %collective-permute-done.70 = bf16[112,2560]{1,0:T(8,128)(2,1)S(1)} collective-permute-done((bf16[112,2560]{1,0:T(8,128)(2,1)S(1)}, bf16[112,2560]{1,0:T(8,128)(2,1)S(1)}, u32[]{:S(2)}, u32[]{:S(2)}) %collective-permute-start.70) | collective-permute-done | bytes 573472 | tf_op jit(solution)/shard_map/ppermute | solution.py:1016
  516.8 15.3 %collective-permute-done.72 = bf16[240,1536]{1,0:T(8,128)(2,1)S(1)} collective-permute-done((bf16[240,1536]{1,0:T(8,128)(2,1)S(1)}, bf16[240,1536]{1,0:T(8,128)(2,1)S(1)}, u32[]{:S(2)}, u32[]{:S(2)}) %collective-permute-start.72) | collective-permute-done | bytes 737312 | tf_op jit(solution)/shard_map/ppermute | solution.py:1016
  (653 shorter events, 264.1 us)
Async XLA Ops:
  5.1 21.0 %collective-permute-start.1 = (bf16[240,1408]{1,0:T(8,128)(2,1)S(1)}, bf16[240,1408]{1,0:T(8,128)(2,1)S(1)}, u32[]{:S(2)}, u32[]{:S(2)}) collective-permute-start(bf16[240,1408]{1,0:T(8,128)(2,1)S(1)} %concatenate.38.refs_0_), channel_id=1, source_target_pairs={{0,2},{1,3},{2,0},{3,1},{4,6},{5,7},{6,4},{7,5},{8,10},{9,11},{10,... | collective-permute-start | bytes 2027528 | tf_op jit(solution)/shard_map/ppermute | solution.py:850
  8.1 18.0 %collective-permute-start = (bf16[240,1408]{1,0:T(8,128)(2,1)S(1)}, bf16[240,1408]{1,0:T(8,128)(2,1)S(1)}, u32[]{:S(2)}, u32[]{:S(2)}) collective-permute-start(bf16[240,1408]{1,0:T(8,128)(2,1)S(1)} %concatenate.38.refs_0_), channel_id=1, source_target_pairs={{0,1},{1,0},{2,3},{3,2},{4,5},{5,4},{6,7},{7,6},{8,9},{9,8},{10,11... | collective-permute-start | bytes 2027528 | tf_op jit(solution)/shard_map/ppermute | solution.py:847
  9.6 16.5 %collective-permute-start.2 = (s32[2,288]{1,0:T(2,128)S(1)}, s32[2,288]{1,0:T(2,128)S(1)}, u32[]{:S(2)}, u32[]{:S(2)}) collective-permute-start(s32[2,288]{1,0:T(2,128)S(1)} %pad_add_fusion.1), channel_id=1, source_target_pairs={{0,0},{1,1},{2,4},{3,5},{4,2},{5,3},{6,6},{7,7},{8,8},{9,9},{10,12... | collective-permute-start | bytes 6920 | tf_op jit(solution)/shard_map/ppermute | solution.py:863
  49.0 39.1 %collective-permute-start.14 = (bf16[240,2560]{1,0:T(8,128)(2,1)}, bf16[240,2560]{1,0:T(8,128)(2,1)}, u32[]{:S(2)}, u32[]{:S(2)}) collective-permute-start(bf16[240,2560]{1,0:T(8,128)(2,1)} %broadcast_select_fusion.2.refs_0_), channel_id=1, source_target_pairs={{0,2},{1,3},{2,0},{3,1},{4,6},{5,7},{6,4},{7,5},{8,10},{9,11},{10,... | collective-permute-start | bytes 3686408 | tf_op jit(solution)/shard_map/ppermute | solution.py:850
  50.8 37.4 %collective-permute-start.13 = (bf16[240,2560]{1,0:T(8,128)(2,1)}, bf16[240,2560]{1,0:T(8,128)(2,1)}, u32[]{:S(2)}, u32[]{:S(2)}) collective-permute-start(bf16[240,2560]{1,0:T(8,128)(2,1)} %broadcast_select_fusion.2.refs_0_), channel_id=1, source_target_pairs={{0,1},{1,0},{2,3},{3,2},{4,5},{5,4},{6,7},{7,6},{8,9},{9,8},{10,11... | collective-permute-start | bytes 3686408 | tf_op jit(solution)/shard_map/ppermute | solution.py:847
  67.1 21.0 %collective-permute-start.11 = (bf16[288,640]{1,0:T(8,128)(2,1)}, bf16[288,640]{1,0:T(8,128)(2,1)}, u32[]{:S(2)}, u32[]{:S(2)}) collective-permute-start(bf16[288,640]{1,0:T(8,128)(2,1)} %get-tuple-element.362.refs_0_), channel_id=1, source_target_pairs={{0,4},{4,0},{8,12},{12,8},{16,20},{20,16},{24,28},{28,24},{1,5},{5... | collective-permute-start | bytes 1105928 | tf_op jit(solution)/shard_map/ppermute | solution.py:853
  67.3 20.8 %collective-permute-start.10 = (bf16[288,640]{1,0:T(8,128)(2,1)}, bf16[288,640]{1,0:T(8,128)(2,1)}, u32[]{:S(2)}, u32[]{:S(2)}) collective-permute-start(bf16[288,640]{1,0:T(8,128)(2,1)} %get-tuple-element.362.refs_0_), channel_id=1, source_target_pairs={{0,1},{1,0},{2,3},{3,2},{4,5},{5,4},{6,7},{7,6},{8,9},{9,8},{10,11... | collective-permute-start | bytes 1105928 | tf_op jit(solution)/shard_map/ppermute | solution.py:847
  90.0 30.8 %collective-permute-start.18 = (bf16[320,1024]{1,0:T(8,128)(2,1)S(1)}, bf16[320,1024]{1,0:T(8,128)(2,1)S(1)}, u32[]{:S(2)}, u32[]{:S(2)}) collective-permute-start(bf16[320,1024]{1,0:T(8,128)(2,1)S(1)} %copy-done.22), channel_id=1, source_target_pairs={{0,2},{1,3},{2,0},{3,1},{4,6},{5,7},{6,4},{7,5},{8,10},{9,11},{10,... | collective-permute-start | bytes 1966088 | tf_op jit(solution)/shard_map/ppermute | solution.py:850
  90.4 30.5 %collective-permute-start.17 = (bf16[320,1024]{1,0:T(8,128)(2,1)S(1)}, bf16[320,1024]{1,0:T(8,128)(2,1)S(1)}, u32[]{:S(2)}, u32[]{:S(2)}) collective-permute-start(bf16[320,1024]{1,0:T(8,128)(2,1)S(1)} %copy-done.22), channel_id=1, source_target_pairs={{0,1},{1,0},{2,3},{3,2},{4,5},{5,4},{6,7},{7,6},{8,9},{9,8},{10,11... | collective-permute-start | bytes 1966088 | tf_op jit(solution)/shard_map/ppermute | solution.py:847
  93.0 26.2 %collective-permute-start.16 = (bf16[112,2560]{1,0:T(8,128)(2,1)S(1)}, bf16[112,2560]{1,0:T(8,128)(2,1)S(1)}, u32[]{:S(2)}, u32[]{:S(2)}) collective-permute-start(bf16[112,2560]{1,0:T(8,128)(2,1)S(1)} %slice.344), channel_id=1, source_target_pairs={{0,1},{1,0},{2,3},{3,2},{4,5},{5,4},{6,7},{7,6},{8,9},{9,8},{10,11... | collective-permute-start | bytes 1720328 | tf_op jit(solution)/shard_map/ppermute | solution.py:847
  94.7 26.1 %collective-permute-start.15 = (bf16[128,2560]{1,0:T(8,128)(2,1)S(1)}, bf16[128,2560]{1,0:T(8,128)(2,1)S(1)}, u32[]{:S(2)}, u32[]{:S(2)}) collective-permute-start(bf16[128,2560]{1,0:T(8,128)(2,1)S(1)} %slice.343), channel_id=1, source_target_pairs={{0,2},{1,3},{2,0},{3,1},{4,6},{5,7},{6,4},{7,5},{8,10},{9,11},{10,... | collective-permute-start | bytes 1966088 | tf_op jit(solution)/shard_map/ppermute | solution.py:850
  158.7 32.7 %collective-permute-start.29 = (bf16[288,960]{1,0:T(8,128)(2,1)S(1)}, bf16[288,960]{1,0:T(8,128)(2,1)S(1)}, u32[]{:S(2)}, u32[]{:S(2)}) collective-permute-start(bf16[288,960]{1,0:T(8,128)(2,1)S(1)} %bitcast.281), channel_id=1, source_target_pairs={{0,0},{1,1},{2,4},{3,5},{4,2},{5,3},{6,6},{7,7},{8,8},{9,9},{10,12... | collective-permute-start | bytes 1658888 | tf_op jit(solution)/shard_map/ppermute | solution.py:863
  305.2 19.1 %collective-permute-start.36 = (bf16[2,160,1024]{2,1,0:T(8,128)(2,1)}, bf16[2,160,1024]{2,1,0:T(8,128)(2,1)}, u32[]{:S(2)}, u32[]{:S(2)}) collective-permute-start(bf16[2,160,1024]{2,1,0:T(8,128)(2,1)} %get-tuple-element.438), channel_id=1, source_target_pairs={{0,1},{1,0},{2,3},{3,2},{4,5},{5,4},{6,7},{7,6},{8,9},{9,8},{10,11... | collective-permute-start | bytes 1966088 | tf_op jit(solution)/shard_map/ppermute | solution.py:847
  306.7 17.6 %collective-permute-start.37 = (bf16[2,160,1024]{2,1,0:T(8,128)(2,1)}, bf16[2,160,1024]{2,1,0:T(8,128)(2,1)}, u32[]{:S(2)}, u32[]{:S(2)}) collective-permute-start(bf16[2,160,1024]{2,1,0:T(8,128)(2,1)} %get-tuple-element.439), channel_id=1, source_target_pairs={{0,2},{1,3},{2,0},{3,1},{4,6},{5,7},{6,4},{7,5},{8,10},{9,11},{10,... | collective-permute-start | bytes 1966088 | tf_op jit(solution)/shard_map/ppermute | solution.py:850
  340.4 20.9 %collective-permute-start.43 = (bf16[320,1024]{1,0:T(8,128)(2,1)S(1)}, bf16[320,1024]{1,0:T(8,128)(2,1)S(1)}, u32[]{:S(2)}, u32[]{:S(2)}) collective-permute-start(bf16[320,1024]{1,0:T(8,128)(2,1)S(1)} %pad_maximum_fusion.1), channel_id=1, source_target_pairs={{0,8},{4,12},{24,16},{28,20},{1,9},{5,13},{25,17},{29,21},{2,10},{... | collective-permute-start | bytes 1966088 | tf_op jit(solution)/shard_map/ppermute | solution.py:1016
  344.0 17.3 %collective-permute-start.41 = (bf16[128,2560]{1,0:T(8,128)(2,1)S(1)}, bf16[128,2560]{1,0:T(8,128)(2,1)S(1)}, u32[]{:S(2)}, u32[]{:S(2)}) collective-permute-start(bf16[128,2560]{1,0:T(8,128)(2,1)S(1)} %get-tuple-element.477), channel_id=1, source_target_pairs={{0,1},{1,0},{2,3},{3,2},{4,5},{5,4},{6,7},{7,6},{8,9},{9,8},{10,11... | collective-permute-start | bytes 1966088 | tf_op jit(solution)/shard_map/ppermute | solution.py:847
  344.9 16.4 %collective-permute-start.42 = (bf16[112,2560]{1,0:T(8,128)(2,1)S(1)}, bf16[112,2560]{1,0:T(8,128)(2,1)S(1)}, u32[]{:S(2)}, u32[]{:S(2)}) collective-permute-start(bf16[112,2560]{1,0:T(8,128)(2,1)S(1)} %get-tuple-element.479), channel_id=1, source_target_pairs={{0,2},{1,3},{2,0},{3,1},{4,6},{5,7},{6,4},{7,5},{8,10},{9,11},{10,... | collective-permute-start | bytes 1720328 | tf_op jit(solution)/shard_map/ppermute | solution.py:850
  363.5 17.6 %collective-permute-start.44 = (bf16[128,2560]{1,0:T(8,128)(2,1)S(1)}, bf16[128,2560]{1,0:T(8,128)(2,1)S(1)}, u32[]{:S(2)}, u32[]{:S(2)}) collective-permute-start(bf16[128,2560]{1,0:T(8,128)(2,1)S(1)} %get-tuple-element.494), channel_id=1, source_target_pairs={{0,1},{1,0},{2,3},{3,2},{4,5},{5,4},{6,7},{7,6},{8,9},{9,8},{10,11... | collective-permute-start | bytes 1966088 | tf_op jit(solution)/shard_map/ppermute | solution.py:847
  365.1 23.1 %collective-permute-start.47 = (bf16[288,640]{1,0:T(8,128)(2,1)S(1)}, bf16[288,640]{1,0:T(8,128)(2,1)S(1)}, u32[]{:S(2)}, u32[]{:S(2)}) collective-permute-start(bf16[288,640]{1,0:T(8,128)(2,1)S(1)} %get-tuple-element.690), channel_id=1, source_target_pairs={{0,1},{1,0},{2,3},{3,2},{4,5},{5,4},{6,7},{7,6},{8,9},{9,8},{10,11... | collective-permute-start | bytes 1105928 | tf_op jit(solution)/shard_map/ppermute | solution.py:847
  388.2 19.4 %collective-permute-start.50 = (bf16[4,240,1024]{2,1,0:T(8,128)(2,1)}, bf16[4,240,1024]{2,1,0:T(8,128)(2,1)}, u32[]{:S(2)}, u32[]{:S(2)}) collective-permute-start(bf16[4,240,1024]{2,1,0:T(8,128)(2,1)} %get-tuple-element.532), channel_id=1, source_target_pairs={{0,4},{4,0},{8,12},{12,8},{16,20},{20,16},{24,28},{28,24},{1,5},{5... | collective-permute-start | bytes 5898248 | tf_op jit(solution)/shard_map/ppermute | solution.py:853
  389.3 34.3 %collective-permute-start.57 = (bf16[320,1024]{1,0:T(8,128)(2,1)}, bf16[320,1024]{1,0:T(8,128)(2,1)}, u32[]{:S(2)}, u32[]{:S(2)}) collective-permute-start(bf16[320,1024]{1,0:T(8,128)(2,1)} %add_convert_fusion.8), channel_id=1, source_target_pairs={{8,16},{12,20},{16,8},{20,12},{9,17},{13,21},{17,9},{21,13},{10,18... | collective-permute-start | bytes 1966088 | tf_op jit(solution)/shard_map/ppermute | solution.py:1016
  396.4 17.2 %collective-permute-start.48 = (bf16[128,2560]{1,0:T(8,128)(2,1)}, bf16[128,2560]{1,0:T(8,128)(2,1)}, u32[]{:S(2)}, u32[]{:S(2)}) collective-permute-start(bf16[128,2560]{1,0:T(8,128)(2,1)} %fusion.8), channel_id=1, source_target_pairs={{0,2},{1,3},{2,0},{3,1},{4,6},{5,7},{6,4},{7,5},{8,10},{9,11},{10,... | collective-permute-start | bytes 1966088 | tf_op jit(solution)/shard_map/ppermute | solution.py:850
  416.3 17.6 %collective-permute-start.51 = (bf16[128,2560]{1,0:T(8,128)(2,1)S(1)}, bf16[128,2560]{1,0:T(8,128)(2,1)S(1)}, u32[]{:S(2)}, u32[]{:S(2)}) collective-permute-start(bf16[128,2560]{1,0:T(8,128)(2,1)S(1)} %fusion.6), channel_id=1, source_target_pairs={{0,8},{4,12},{24,16},{28,20},{1,9},{5,13},{25,17},{29,21},{2,10},{... | collective-permute-start | bytes 1966088 | tf_op jit(solution)/shard_map/ppermute | solution.py:1016
  426.2 24.4 %collective-permute-start.65 = (bf16[288,1024]{1,0:T(8,128)(2,1)S(1)}, bf16[288,1024]{1,0:T(8,128)(2,1)}, u32[]{:S(2)}, u32[]{:S(2)}) collective-permute-start(bf16[288,1024]{1,0:T(8,128)(2,1)S(1)} %pad.14), channel_id=1, source_target_pairs={{0,0},{1,1},{2,4},{3,5},{4,2},{5,3},{6,6},{7,7},{8,8},{9,9},{10,12... | collective-permute-start | bytes 1769480 | tf_op jit(solution)/shard_map/ppermute | solution.py:863
  439.1 23.2 %collective-permute-start.64 = (bf16[320,1024]{1,0:T(8,128)(2,1)S(1)}, bf16[320,1024]{1,0:T(8,128)(2,1)}, u32[]{:S(2)}, u32[]{:S(2)}) collective-permute-start(bf16[320,1024]{1,0:T(8,128)(2,1)S(1)} %add_convert_fusion.6), channel_id=1, source_target_pairs={{8,0},{12,4},{16,24},{20,28},{9,1},{13,5},{17,25},{21,29},{10,2},{... | collective-permute-start | bytes 1966088 | tf_op jit(solution)/shard_map/ppermute | solution.py:1016
  440.7 21.6 %collective-permute-start.58 = (bf16[128,2560]{1,0:T(8,128)(2,1)S(1)}, bf16[128,2560]{1,0:T(8,128)(2,1)S(1)}, u32[]{:S(2)}, u32[]{:S(2)}) collective-permute-start(bf16[128,2560]{1,0:T(8,128)(2,1)S(1)} %add_convert_fusion.7), channel_id=1, source_target_pairs={{8,16},{12,20},{16,8},{20,12},{9,17},{13,21},{17,9},{21,13},{10,18... | collective-permute-start | bytes 1966088 | tf_op jit(solution)/shard_map/ppermute | solution.py:1016
  441.4 20.9 %collective-permute-start.59 = (bf16[112,2560]{1,0:T(8,128)(2,1)}, bf16[112,2560]{1,0:T(8,128)(2,1)}, u32[]{:S(2)}, u32[]{:S(2)}) collective-permute-start(bf16[112,2560]{1,0:T(8,128)(2,1)} %fusion.17), channel_id=1, source_target_pairs={{0,8},{4,12},{24,16},{28,20},{1,9},{5,13},{25,17},{29,21},{2,10},{... | collective-permute-start | bytes 1720328 | tf_op jit(solution)/shard_map/ppermute | solution.py:1016
  469.1 19.0 %collective-permute-start.66 = (bf16[128,2560]{1,0:T(8,128)(2,1)S(1)}, bf16[128,2560]{1,0:T(8,128)(2,1)S(1)}, u32[]{:S(2)}, u32[]{:S(2)}) collective-permute-start(bf16[128,2560]{1,0:T(8,128)(2,1)S(1)} %add_convert_fusion.5), channel_id=1, source_target_pairs={{8,0},{12,4},{16,24},{20,28},{9,1},{13,5},{17,25},{21,29},{10,2},{... | collective-permute-start | bytes 1966088 | tf_op jit(solution)/shard_map/ppermute | solution.py:1016
  470.5 20.6 %collective-permute-start.68 = (bf16[240,1536]{1,0:T(8,128)(2,1)S(1)}, bf16[240,1536]{1,0:T(8,128)(2,1)S(1)}, u32[]{:S(2)}, u32[]{:S(2)}) collective-permute-start(bf16[240,1536]{1,0:T(8,128)(2,1)S(1)} %maximum_maximum_fusion), channel_id=1, source_target_pairs={{0,8},{4,12},{24,16},{28,20},{1,9},{5,13},{25,17},{29,21},{2,10},{... | collective-permute-start | bytes 2211848 | tf_op jit(solution)/shard_map/ppermute | solution.py:1016
  491.2 19.5 %collective-permute-start.69 = (bf16[240,1536]{1,0:T(8,128)(2,1)S(1)}, bf16[240,1536]{1,0:T(8,128)(2,1)S(1)}, u32[]{:S(2)}, u32[]{:S(2)}) collective-permute-start(bf16[240,1536]{1,0:T(8,128)(2,1)S(1)} %add_convert_fusion.1), channel_id=1, source_target_pairs={{8,16},{12,20},{16,8},{20,12},{9,17},{13,21},{17,9},{21,13},{10,18... | collective-permute-start | bytes 2211848 | tf_op jit(solution)/shard_map/ppermute | solution.py:1016
  492.1 18.6 %collective-permute-start.70 = (bf16[112,2560]{1,0:T(8,128)(2,1)S(1)}, bf16[112,2560]{1,0:T(8,128)(2,1)S(1)}, u32[]{:S(2)}, u32[]{:S(2)}) collective-permute-start(bf16[112,2560]{1,0:T(8,128)(2,1)S(1)} %add_convert_fusion.9), channel_id=1, source_target_pairs={{8,0},{12,4},{16,24},{20,28},{9,1},{13,5},{17,25},{21,29},{10,2},{... | collective-permute-start | bytes 1720328 | tf_op jit(solution)/shard_map/ppermute | solution.py:1016
  511.2 20.9 %collective-permute-start.72 = (bf16[240,1536]{1,0:T(8,128)(2,1)S(1)}, bf16[240,1536]{1,0:T(8,128)(2,1)S(1)}, u32[]{:S(2)}, u32[]{:S(2)}) collective-permute-start(bf16[240,1536]{1,0:T(8,128)(2,1)S(1)} %add_convert_fusion), channel_id=1, source_target_pairs={{8,0},{12,4},{16,24},{20,28},{9,1},{13,5},{17,25},{21,29},{10,2},{... | collective-permute-start | bytes 2211848 | tf_op jit(solution)/shard_map/ppermute | solution.py:1016
  (221 other events, 2258.7 us)

commit v6 on v5

--- a/solution.py
+++ b/solution.py
@@ -173,12 +173,12 @@
             block += 1
 
 
-def by_group(count, do, unroll=False):
+def by_group(count, do):
     def one(g, _):
         do(g, pl.ds(pl.multiple_of(g * LANES, LANES), LANES))
         return 0
 
-    lax.fori_loop(0, count, one, 0, unroll=unroll)
+    lax.fori_loop(0, count, one, 0)
 
 
 def stacked(m):
@@ -219,7 +219,7 @@
                     lse_ref[:m, :] = jnp.where(lane == h, log[here], lse_ref[:m, :])
                 s = following
 
-        by_group(groups, group, True)
+        by_group(groups, group)
         join_pairs(o_all, att_ref, False, m)
         clear(m, att_ref)
 
@@ -246,7 +246,7 @@
             pltpu.VMEM((heads, rows, LANES), BF16),
             pltpu.VMEM((heads, rows, LANES), F32),
         ],
-        24,
+        16,
         4 * rows * keys * LANES * heads,
         4 * q.size + 2 * keys * both,
     )
@@ -269,20 +269,15 @@
             kv = keys[:n, cols]
             cos, sin = turns(row_ref[:m], False)
             lane = lax.broadcasted_iota(jnp.int32, (m, LANES), 1)
-            stack = lambda parts: jnp.concatenate(parts, axis=0)
-            sets = [[g * GROUP + first + j for j in range(at_once)] for first in range(0, GROUP, at_once)]
-
-            def score(heads):
-                s = dotf(stack([q_all[h, :m] for h in heads]), kv, NT) + stack([bias[:m, :n]] * at_once)
-                return s, dotf(stack([do_all[h, :m] for h in heads]), kv, NT)
-
-            s, dp = score(sets[0])
-            for i, heads in enumerate(sets):
-                following = score(sets[i + 1]) if i + 1 < len(sets) else (None, None)
-                here = slice(i * at_once * m, (i + 1) * at_once * m)
+            for first in range(0, GROUP, at_once):
+                heads = [g * GROUP + first + j for j in range(at_once)]
+                here = slice(first * m, (first + at_once) * m)
+                stack = lambda parts: jnp.concatenate(parts, axis=0)
                 logs = stack([jnp.sum(jnp.where(lane == h, lse_ref[:m], 0.0), axis=1, keepdims=True) for h in heads])
                 dots = stack([jnp.sum(dq_all[h, :m], axis=1, keepdims=True) for h in heads])
+                s = dotf(stack([q_all[h, :m] for h in heads]), kv, NT) + stack([bias[:m, :n]] * at_once)
                 p = jnp.exp(s - logs)
+                dp = dotf(stack([do_all[h, :m] for h in heads]), kv, NT)
                 ds = (p * (dp - dots)).astype(BF16)
                 p3[here, :n] = p.astype(BF16)
                 ds3[here, :n] = ds
@@ -290,13 +285,12 @@
                 for j, h in enumerate(heads):
                     one = dq[j * m : (j + 1) * m]
                     dq_all[h, :m] = one * cos - turn(one) * sin
-                s, dp = following
             q3 = jnp.concatenate([q_all[g * GROUP + j, :m] for j in range(GROUP)], axis=0)
             do3 = jnp.concatenate([do_all[g * GROUP + j, :m] for j in range(GROUP)], axis=0)
             dkv = dotf(q3, ds3[: GROUP * m, :n], TN) + dotf(do3, p3[: GROUP * m, :n], TN)
             back[:n, cols] = dkv.T
 
-        by_group(groups, group, False)
+        by_group(groups, group)
         join_pairs(dq_all, dq_ref, True, m)
         clear(m, dq_ref)
 
@@ -331,7 +325,7 @@
             pltpu.VMEM((GROUP * rows, keys), BF16),
             pltpu.VMEM((heads, rows, LANES), F32),
         ],
-        32,
+        24,
         10 * rows * keys * LANES * heads,
         8 * q.size + 4 * keys * both,
     )

time: 547 us -> 539 us (0.985)
  waiting for transfers between devices: 153 us -> 161 us
  local copies, waits for them, and re-layouts: 64.5 us -> 57.5 us
  other arithmetic: 60.8 us -> 55.1 us
    unnamed x361 -> x313, local copies, waits for them, and re-layouts: 48.2 us -> 41.8 us
  transfers between devices with their start and end apart: 75 -> 75, of which waited for: 32 -> 36; matrix products, arithmetic and copies ran while one was open for 14% -> 12% of each run, Pallas kernels for 17% -> 17%
where the time goes in v6:
time: 539 us; the launch traced here: 532 us
  waiting for transfers between devices  161 us (30%)
  Pallas kernels  154 us (29%)
  starting transfers between devices  87.9 us (16%)
  local copies, waits for them, and re-layouts  57.5 us (11%)
  other arithmetic  55.1 us (10%)
  matrix products  12.6 us (2%)
    pallas_call x20, Pallas kernels, call(): pl.pallas_call(kernel, grid_spec=pltpu.PrefetchScalarGridSpec(num_scalar_...  116 us
    ppermute x22, waiting for transfers between devices, over_x(): return lax.ppermute(a, 'cp', [(i, i ^ 1) for i in range(self.cp)])  80.6 us
    ppermute x12, waiting for transfers between devices, hop(): lax.ppermute(a, 'dp', [(2 * s + c, 2 * t + c) for s, t in moves for c in...  46.3 us
    unnamed x313, local copies, waits for them, and re-layouts  41.8 us
    convert_element_type x32, other arithmetic, add(): return sum((a.astype(F32) for a in terms)).astype(BF16)  34.5 us
    pallas_call x4, Pallas kernels, weight_grad(): pl.pallas_call(functools.partial(weight_grad_kernel, fill, (len(lefts), l...  30.8 us
    ppermute x12, starting transfers between devices, hop(): lax.ppermute(a, 'dp', [(2 * s + c, 2 * t + c) for s, t in moves for c in...  28.2 us
    ppermute x22, starting transfers between devices, over_x(): return lax.ppermute(a, 'cp', [(i, i ^ 1) for i in range(self.cp)])  26.6 us
  transfers between devices with their start and end apart: 75, of which 36 were waited for; matrix products, arithmetic and copies ran while one was open for 12% of the time, Pallas kernels for 17%

profile of v6, /device:TPU:0, one launch (start us, length us, event | category | flops | bytes accessed | tf_op | source)
XLA Modules:
  0.0 531.7 jit_solution(17922839753510502119)
XLA Ops:
  10.3 6.1 %collective-permute-start.3 = (bf16[288,960]{1,0:T(8,128)(2,1)}, bf16[288,960]{1,0:T(8,128)(2,1)}, u32[]{:S(2)}, u32[]{:S(2)}) collective-permute-start(bf16[288,960]{1,0:T(8,128)(2,1)} %bitcast.280), channel_id=1, source_target_pairs={{0,0},{1,1},{2,4},{3,5},{4,2},{5,3},{6,6},{7,7},{8,8},{9,9},{10,12... | collective-permute-start | bytes 1658888 | tf_op jit(solution)/shard_map/ppermute | solution.py:857
  75.3 12.8 %collective-permute-done.10.refs_1_ = bf16[288,640]{1,0:T(8,128)(2,1)} collective-permute-done((bf16[288,640]{1,0:T(8,128)(2,1)}, bf16[288,640]{1,0:T(8,128)(2,1)}, u32[]{:S(2)}, u32[]{:S(2)}) %collective-permute-start.10) | collective-permute-done | bytes 368672 | tf_op jit(solution)/shard_map/ppermute | solution.py:841
  96.4 13.0 %attend.3 = (bf16[288,960]{1,0:T(8,128)(2,1)S(1)}, f32[288,128]{1,0:T(8,128)S(1)}, bf16[1152,640]{1,0:T(8,128)(2,1)S(1)}) custom-call(s32[10]{0:T(128)S(1)} %pad_add_fusion.4.meta_ref, bf16[288,960]{1,0:T(8,128)(2,1)S(1)} %copy-done.73, bf16[288,640]{1,0:T(8,128)(2,1)} %get-tuple-element.362.refs_0_, bf16[288,640]{1,0:T(8,128)(2,1)} %collective-permute-done.10.refs_1_, ...), custom_call_target="tpu_custom_call" | custom-call | flops 2548039680 | bytes 2580480 | tf_op jit(solution)/shard_map/attend/pallas_call | solution.py:54
  111.8 7.4 %collective-permute-done.16.refs_4_ = bf16[112,2560]{1,0:T(8,128)(2,1)S(1)} collective-permute-done((bf16[112,2560]{1,0:T(8,128)(2,1)S(1)}, bf16[112,2560]{1,0:T(8,128)(2,1)S(1)}, u32[]{:S(2)}, u32[]{:S(2)}) %collective-permute-start.16) | collective-permute-done | bytes 573472 | tf_op jit(solution)/shard_map/ppermute | solution.py:841
  125.4 6.2 %collective-permute-done.19.theirs = bf16[960,2560]{1,0:T(8,128)(2,1)S(1)} collective-permute-done((bf16[960,2560]{1,0:T(8,128)(2,1)S(1)}, bf16[960,2560]{1,0:T(8,128)(2,1)S(1)}, u32[]{:S(2)}, u32[]{:S(2)}) %collective-permute-start.19) | collective-permute-done | bytes 4915232 | tf_op jit(solution)/shard_map/ppermute | solution.py:847
  137.4 4.8 collective-permute-done.22.refs_1_
  149.3 9.1 %collective-permute-done.23.refs_1_ = bf16[288,640]{1,0:T(8,128)(2,1)S(1)} collective-permute-done((bf16[288,640]{1,0:T(8,128)(2,1)S(1)}, bf16[288,640]{1,0:T(8,128)(2,1)S(1)}, u32[]{:S(2)}, u32[]{:S(2)}) %collective-permute-start.23) | collective-permute-done | bytes 368672 | tf_op jit(solution)/shard_map/ppermute | solution.py:841
  160.1 8.1 %attend.4 = (bf16[288,960]{1,0:T(8,128)(2,1)S(1)}, f32[288,128]{1,0:T(8,128)S(1)}, bf16[1152,640]{1,0:T(8,128)(2,1)S(1)}) custom-call(s32[10]{0:T(128)S(1)} %get-tuple-element.359.meta_ref, bf16[288,960]{1,0:T(8,128)(2,1)S(1)} %get-tuple-element.388.q_ref, bf16[288,640]{1,0:T(8,128)(2,1)S(1)} %get-tuple-element.389.refs_0_, ...), custom_call_target="tpu_custom_call" | custom-call | flops 2548039680 | bytes 2580480 | tf_op jit(solution)/shard_map/attend/pallas_call | solution.py:54
  168.3 7.2 %post.2 = (f32[288,960]{1,0:T(8,128)S(1)}, f32[288,960]{1,0:T(8,128)S(1)}, bf16[288,960]{1,0:T(8,128)(2,1)S(1)}, f32[288,960]{1,0:T(8,128)S(1)}, f32[288,1]{1,0:...) custom-call(s32[10]{0:T(128)S(1)} %get-tuple-element.359.meta_ref, ...), custom_call_target="tpu_custom_call" | custom-call | flops 4777574400 | bytes 16588800 | tf_op jit(solution)/shard_map/post/pallas_call | solution.py:54
  179.3 9.3 %collective-permute-done.26.refs_1_ = bf16[288,640]{1,0:T(8,128)(2,1)S(1)} collective-permute-done((bf16[288,640]{1,0:T(8,128)(2,1)S(1)}, bf16[288,640]{1,0:T(8,128)(2,1)S(1)}, u32[]{:S(2)}, u32[]{:S(2)}) %collective-permute-start.26) | collective-permute-done | bytes 368672 | tf_op jit(solution)/shard_map/ppermute | solution.py:841
  190.3 4.6 attend.5
  196.1 5.5 %post.3 = (f32[288,960]{1,0:T(8,128)S(1)}, f32[288,960]{1,0:T(8,128)S(1)}, bf16[288,960]{1,0:T(8,128)(2,1)S(1)}, f32[288,960]{1,0:T(8,128)S(1)}, f32[288,1]{1,0:...) custom-call(s32[10]{0:T(128)S(1)} %get-tuple-element.360.meta_ref, ...), custom_call_target="tpu_custom_call" | custom-call | flops 4777574400 | bytes 16588800 | tf_op jit(solution)/shard_map/post/pallas_call | solution.py:54
  202.7 8.1 %post_back.2 = (bf16[288,960]{1,0:T(8,128)(2,1)S(1)}, f32[288,960]{1,0:T(8,128)S(1)}, bf16[288,960]{1,0:T(8,128)(2,1)S(1)}, bf16[288,960]{1,0:T(8,128)(2,1)S(1)}...) custom-call(s32[10]{0:T(128)S(1)} %get-tuple-element.360.meta_ref, ...), custom_call_target="tpu_custom_call" | custom-call | flops 4777574400 | bytes 16588800 | tf_op jit(solution)/shard_map/post_back/pallas_call | solution.py:54
  217.0 6.7 %attend_back.3 = (bf16[288,960]{1,0:T(8,128)(2,1)S(1)}, bf16[1152,640]{1,0:T(8,128)(2,1)S(1)}) custom-call(s32[10]{0:T(128)S(1)} %get-tuple-element.360.meta_ref, bf16[288,960]{1,0:T(8,128)(2,1)S(1)} %copy-done.94, bf16[288,960]{1,0:T(8,128)(2,1)S(1)} %copy-done.96, bf16[288,960]{1,0:T(8,128)(2,1)S(1)} %get-tuple-element.397.att.att_ref.refs_2_, ...), custom_call_target="tpu_custom_call" | custom-call | flops 6370099200 | bytes 5160960 | tf_op jit(solution)/shard_map/attend_back/pallas_call | solution.py:54
  227.9 9.1 %collective-permute-done.31.got_ref = bf16[288,640]{1,0:T(8,128)(2,1)S(1)} collective-permute-done((bf16[288,640]{1,0:T(8,128)(2,1)S(1)}, bf16[288,640]{1,0:T(8,128)(2,1)S(1)}, u32[]{:S(2)}, u32[]{:S(2)}) %collective-permute-start.31) | collective-permute-done | bytes 368672 | tf_op jit(solution)/shard_map/ppermute | solution.py:841
  239.8 8.6 %post_back.3 = (bf16[288,960]{1,0:T(8,128)(2,1)S(1)}, f32[288,960]{1,0:T(8,128)S(1)}, bf16[288,960]{1,0:T(8,128)(2,1)S(1)}, bf16[288,960]{1,0:T(8,128)(2,1)S(1)}...) custom-call(s32[10]{0:T(128)S(1)} %get-tuple-element.359.meta_ref, ...), custom_call_target="tpu_custom_call" | custom-call | flops 4777574400 | bytes 16588800 | tf_op jit(solution)/shard_map/post_back/pallas_call | solution.py:54
  250.9 11.3 %attend_back.4 = (bf16[288,960]{1,0:T(8,128)(2,1)S(1)}, bf16[1152,640]{1,0:T(8,128)(2,1)S(1)}) custom-call(s32[10]{0:T(128)S(1)} %get-tuple-element.359.meta_ref, bf16[288,960]{1,0:T(8,128)(2,1)S(1)} %copy-done.88, bf16[288,960]{1,0:T(8,128)(2,1)S(1)} %get-tuple-element.417.do_ref, bf16[288,960]{1,0:T(8,128)(2,1)S(1)} %get-tuple-element.391.att.att_ref.refs_1_, ...), custom_call_target="tpu_custom_call" | custom-call | flops 6370099200 | bytes 5160960 | tf_op jit(solution)/shard_map/attend_back/pallas_call | solution.py:54
  266.6 9.7 %collective-permute-done.33.got_ref = bf16[288,640]{1,0:T(8,128)(2,1)S(1)} collective-permute-done((bf16[288,640]{1,0:T(8,128)(2,1)S(1)}, bf16[288,640]{1,0:T(8,128)(2,1)S(1)}, u32[]{:S(2)}, u32[]{:S(2)}) %collective-permute-start.33) | collective-permute-done | bytes 368672 | tf_op jit(solution)/shard_map/ppermute | solution.py:841
  282.3 8.9 %weight_grad.4 = (bf16[2,160,1024]{2,1,0:T(8,128)(2,1)S(1)}, bf16[2,160,1024]{2,1,0:T(8,128)(2,1)S(1)}, bf16[2,160,1024]{2,1,0:T(8,128)(2,1)S(1)}, bf16[2,160,10...) custom-call(s32[3]{0:T(128)S(1)} %pad_add_fusion.6.spot_ref, bf16[288,2560]{1,0:T(8,128)(2,1)S(1)} %copy-done.104, ...), custom_call_target="tpu_custom_call" | custom-call | flops 4246732800 | bytes 11325440 | tf_op jit(solution)/shard_map/weight_grad/pallas_call | solution.py:685
  291.8 4.2 expand_back.1
  303.9 12.3 %weight_grad.5 = (bf16[2,128,2560]{2,1,0:T(8,128)(2,1)S(1)}, bf16[2,128,2560]{2,1,0:T(8,128)(2,1)S(1)}, bf16[2,112,2560]{2,1,0:T(8,128)(2,1)S(1)}, bf16[2,112,25...) custom-call(s32[3]{0:T(128)S(1)} %pad_add_fusion.6.spot_ref, bf16[288,960]{1,0:T(8,128)(2,1)S(1)} %copy-done.41, ...), custom_call_target="tpu_custom_call" | custom-call | flops 8493465600 | bytes 20336640 | tf_op jit(solution)/shard_map/weight_grad/pallas_call | solution.py:685
  321.4 4.8 norm_back.1
  337.6 16.7 %attend_back.5 = (bf16[288,960]{1,0:T(8,128)(2,1)S(1)}, bf16[1152,640]{1,0:T(8,128)(2,1)S(1)}) custom-call(s32[10]{0:T(128)S(1)} %pad_add_fusion.4.meta_ref, bf16[288,960]{1,0:T(8,128)(2,1)S(1)} %copy-done.74, bf16[288,960]{1,0:T(8,128)(2,1)S(1)} %get-tuple-element.487.do_ref, bf16[288,960]{1,0:T(8,128)(2,1)S(1)} %get-tuple-element.366.att_ref.refs_0_, ...), custom_call_target="tpu_custom_call" | custom-call | flops 6370099200 | bytes 5160960 | tf_op jit(solution)/shard_map/attend_back/pallas_call | solution.py:54
  359.4 7.4 %weight_grad.6 = (bf16[2,128,1024]{2,1,0:T(8,128)(2,1)S(1)}, bf16[2,128,1024]{2,1,0:T(8,128)(2,1)S(1)}, bf16[2,112,1024]{2,1,0:T(8,128)(2,1)S(1)}, bf16[2,112,10...) custom-call(s32[3]{0:T(128)S(1)} %pad_add_fusion.6.spot_ref, ...), custom_call_target="tpu_custom_call" | custom-call | flops 3185049600 | bytes 10567680 | tf_op jit(solution)/shard_map/weight_grad/pallas_call | solution.py:685
  373.3 7.1 %collective-permute-done.47.got_ref = bf16[288,640]{1,0:T(8,128)(2,1)S(1)} collective-permute-done((bf16[288,640]{1,0:T(8,128)(2,1)S(1)}, bf16[288,640]{1,0:T(8,128)(2,1)S(1)}, u32[]{:S(2)}, u32[]{:S(2)}) %collective-permute-start.47) | collective-permute-done | bytes 368672 | tf_op jit(solution)/shard_map/ppermute | solution.py:841
  421.5 5.3 collective-permute-done.51
  434.4 7.8 %collective-permute-start.59 = (bf16[112,2560]{1,0:T(8,128)(2,1)}, bf16[112,2560]{1,0:T(8,128)(2,1)}, u32[]{:S(2)}, u32[]{:S(2)}) collective-permute-start(bf16[112,2560]{1,0:T(8,128)(2,1)} %fusion.17), channel_id=1, source_target_pairs={{0,8},{4,12},{24,16},{28,20},{1,9},{5,13},{25,17},{29,21},{2,10},{... | collective-permute-start | bytes 1720328 | tf_op jit(solution)/shard_map/ppermute | solution.py:1010
  449.5 6.3 %collective-permute-done.61 = bf16[112,1024]{1,0:T(8,128)(2,1)} collective-permute-done((bf16[112,1024]{1,0:T(8,128)(2,1)}, bf16[112,1024]{1,0:T(8,128)(2,1)}, u32[]{:S(2)}, u32[]{:S(2)}) %collective-permute-start.61) | collective-permute-done | bytes 229408 | tf_op jit(solution)/shard_map/ppermute | solution.py:841
  464.0 4.7 collective-permute-start.68
  476.1 5.4 %collective-permute-done.66 = bf16[128,2560]{1,0:T(8,128)(2,1)S(1)} collective-permute-done((bf16[128,2560]{1,0:T(8,128)(2,1)S(1)}, bf16[128,2560]{1,0:T(8,128)(2,1)S(1)}, u32[]{:S(2)}, u32[]{:S(2)}) %collective-permute-start.66) | collective-permute-done | bytes 655392 | tf_op jit(solution)/shard_map/ppermute | solution.py:1010
  487.0 17.2 %collective-permute-done.70 = bf16[112,2560]{1,0:T(8,128)(2,1)S(1)} collective-permute-done((bf16[112,2560]{1,0:T(8,128)(2,1)S(1)}, bf16[112,2560]{1,0:T(8,128)(2,1)S(1)}, u32[]{:S(2)}, u32[]{:S(2)}) %collective-permute-start.70) | collective-permute-done | bytes 573472 | tf_op jit(solution)/shard_map/ppermute | solution.py:1010
  510.2 15.3 %collective-permute-done.72 = bf16[240,1536]{1,0:T(8,128)(2,1)S(1)} collective-permute-done((bf16[240,1536]{1,0:T(8,128)(2,1)S(1)}, bf16[240,1536]{1,0:T(8,128)(2,1)S(1)}, u32[]{:S(2)}, u32[]{:S(2)}) %collective-permute-start.72) | collective-permute-done | bytes 737312 | tf_op jit(solution)/shard_map/ppermute | solution.py:1010
  (605 shorter events, 257.2 us)
Async XLA Ops:
  5.1 21.0 %collective-permute-start.1 = (bf16[240,1408]{1,0:T(8,128)(2,1)S(1)}, bf16[240,1408]{1,0:T(8,128)(2,1)S(1)}, u32[]{:S(2)}, u32[]{:S(2)}) collective-permute-start(bf16[240,1408]{1,0:T(8,128)(2,1)S(1)} %concatenate.38.refs_0_), channel_id=1, source_target_pairs={{0,2},{1,3},{2,0},{3,1},{4,6},{5,7},{6,4},{7,5},{8,10},{9,11},{10,... | collective-permute-start | bytes 2027528 | tf_op jit(solution)/shard_map/ppermute | solution.py:844
  8.1 18.0 %collective-permute-start = (bf16[240,1408]{1,0:T(8,128)(2,1)S(1)}, bf16[240,1408]{1,0:T(8,128)(2,1)S(1)}, u32[]{:S(2)}, u32[]{:S(2)}) collective-permute-start(bf16[240,1408]{1,0:T(8,128)(2,1)S(1)} %concatenate.38.refs_0_), channel_id=1, source_target_pairs={{0,1},{1,0},{2,3},{3,2},{4,5},{5,4},{6,7},{7,6},{8,9},{9,8},{10,11... | collective-permute-start | bytes 2027528 | tf_op jit(solution)/shard_map/ppermute | solution.py:841
  9.6 16.5 %collective-permute-start.2 = (s32[2,288]{1,0:T(2,128)S(1)}, s32[2,288]{1,0:T(2,128)S(1)}, u32[]{:S(2)}, u32[]{:S(2)}) collective-permute-start(s32[2,288]{1,0:T(2,128)S(1)} %pad_add_fusion.1), channel_id=1, source_target_pairs={{0,0},{1,1},{2,4},{3,5},{4,2},{5,3},{6,6},{7,7},{8,8},{9,9},{10,12... | collective-permute-start | bytes 6920 | tf_op jit(solution)/shard_map/ppermute | solution.py:857
  49.0 39.1 %collective-permute-start.14 = (bf16[240,2560]{1,0:T(8,128)(2,1)}, bf16[240,2560]{1,0:T(8,128)(2,1)}, u32[]{:S(2)}, u32[]{:S(2)}) collective-permute-start(bf16[240,2560]{1,0:T(8,128)(2,1)} %broadcast_select_fusion.2.refs_0_), channel_id=1, source_target_pairs={{0,2},{1,3},{2,0},{3,1},{4,6},{5,7},{6,4},{7,5},{8,10},{9,11},{10,... | collective-permute-start | bytes 3686408 | tf_op jit(solution)/shard_map/ppermute | solution.py:844
  50.7 37.4 %collective-permute-start.13 = (bf16[240,2560]{1,0:T(8,128)(2,1)}, bf16[240,2560]{1,0:T(8,128)(2,1)}, u32[]{:S(2)}, u32[]{:S(2)}) collective-permute-start(bf16[240,2560]{1,0:T(8,128)(2,1)} %broadcast_select_fusion.2.refs_0_), channel_id=1, source_target_pairs={{0,1},{1,0},{2,3},{3,2},{4,5},{5,4},{6,7},{7,6},{8,9},{9,8},{10,11... | collective-permute-start | bytes 3686408 | tf_op jit(solution)/shard_map/ppermute | solution.py:841
  66.7 21.5 %collective-permute-start.11 = (bf16[288,640]{1,0:T(8,128)(2,1)}, bf16[288,640]{1,0:T(8,128)(2,1)}, u32[]{:S(2)}, u32[]{:S(2)}) collective-permute-start(bf16[288,640]{1,0:T(8,128)(2,1)} %get-tuple-element.362.refs_0_), channel_id=1, source_target_pairs={{0,4},{4,0},{8,12},{12,8},{16,20},{20,16},{24,28},{28,24},{1,5},{5... | collective-permute-start | bytes 1105928 | tf_op jit(solution)/shard_map/ppermute | solution.py:847
  66.8 21.3 %collective-permute-start.10 = (bf16[288,640]{1,0:T(8,128)(2,1)}, bf16[288,640]{1,0:T(8,128)(2,1)}, u32[]{:S(2)}, u32[]{:S(2)}) collective-permute-start(bf16[288,640]{1,0:T(8,128)(2,1)} %get-tuple-element.362.refs_0_), channel_id=1, source_target_pairs={{0,1},{1,0},{2,3},{3,2},{4,5},{5,4},{6,7},{7,6},{8,9},{9,8},{10,11... | collective-permute-start | bytes 1105928 | tf_op jit(solution)/shard_map/ppermute | solution.py:841
  90.0 30.8 %collective-permute-start.18 = (bf16[320,1024]{1,0:T(8,128)(2,1)S(1)}, bf16[320,1024]{1,0:T(8,128)(2,1)S(1)}, u32[]{:S(2)}, u32[]{:S(2)}) collective-permute-start(bf16[320,1024]{1,0:T(8,128)(2,1)S(1)} %copy-done.19), channel_id=1, source_target_pairs={{0,2},{1,3},{2,0},{3,1},{4,6},{5,7},{6,4},{7,5},{8,10},{9,11},{10,... | collective-permute-start | bytes 1966088 | tf_op jit(solution)/shard_map/ppermute | solution.py:844
  90.4 30.5 %collective-permute-start.17 = (bf16[320,1024]{1,0:T(8,128)(2,1)S(1)}, bf16[320,1024]{1,0:T(8,128)(2,1)S(1)}, u32[]{:S(2)}, u32[]{:S(2)}) collective-permute-start(bf16[320,1024]{1,0:T(8,128)(2,1)S(1)} %copy-done.19), channel_id=1, source_target_pairs={{0,1},{1,0},{2,3},{3,2},{4,5},{5,4},{6,7},{7,6},{8,9},{9,8},{10,11... | collective-permute-start | bytes 1966088 | tf_op jit(solution)/shard_map/ppermute | solution.py:841
  93.0 26.2 %collective-permute-start.16 = (bf16[112,2560]{1,0:T(8,128)(2,1)S(1)}, bf16[112,2560]{1,0:T(8,128)(2,1)S(1)}, u32[]{:S(2)}, u32[]{:S(2)}) collective-permute-start(bf16[112,2560]{1,0:T(8,128)(2,1)S(1)} %slice.344), channel_id=1, source_target_pairs={{0,1},{1,0},{2,3},{3,2},{4,5},{5,4},{6,7},{7,6},{8,9},{9,8},{10,11... | collective-permute-start | bytes 1720328 | tf_op jit(solution)/shard_map/ppermute | solution.py:841
  94.7 26.1 %collective-permute-start.15 = (bf16[128,2560]{1,0:T(8,128)(2,1)S(1)}, bf16[128,2560]{1,0:T(8,128)(2,1)S(1)}, u32[]{:S(2)}, u32[]{:S(2)}) collective-permute-start(bf16[128,2560]{1,0:T(8,128)(2,1)S(1)} %slice.343), channel_id=1, source_target_pairs={{0,2},{1,3},{2,0},{3,1},{4,6},{5,7},{6,4},{7,5},{8,10},{9,11},{10,... | collective-permute-start | bytes 1966088 | tf_op jit(solution)/shard_map/ppermute | solution.py:844
  158.4 30.3 %collective-permute-start.29 = (bf16[288,960]{1,0:T(8,128)(2,1)S(1)}, bf16[288,960]{1,0:T(8,128)(2,1)S(1)}, u32[]{:S(2)}, u32[]{:S(2)}) collective-permute-start(bf16[288,960]{1,0:T(8,128)(2,1)S(1)} %bitcast.281), channel_id=1, source_target_pairs={{0,0},{1,1},{2,4},{3,5},{4,2},{5,3},{6,6},{7,7},{8,8},{9,9},{10,12... | collective-permute-start | bytes 1658888 | tf_op jit(solution)/shard_map/ppermute | solution.py:857
  299.6 17.1 %collective-permute-start.36 = (bf16[2,160,1024]{2,1,0:T(8,128)(2,1)}, bf16[2,160,1024]{2,1,0:T(8,128)(2,1)}, u32[]{:S(2)}, u32[]{:S(2)}) collective-permute-start(bf16[2,160,1024]{2,1,0:T(8,128)(2,1)} %get-tuple-element.438), channel_id=1, source_target_pairs={{0,1},{1,0},{2,3},{3,2},{4,5},{5,4},{6,7},{7,6},{8,9},{9,8},{10,11... | collective-permute-start | bytes 1966088 | tf_op jit(solution)/shard_map/ppermute | solution.py:841
  301.1 16.8 %collective-permute-start.37 = (bf16[2,160,1024]{2,1,0:T(8,128)(2,1)}, bf16[2,160,1024]{2,1,0:T(8,128)(2,1)}, u32[]{:S(2)}, u32[]{:S(2)}) collective-permute-start(bf16[2,160,1024]{2,1,0:T(8,128)(2,1)} %get-tuple-element.439), channel_id=1, source_target_pairs={{0,2},{1,3},{2,0},{3,1},{4,6},{5,7},{6,4},{7,5},{8,10},{9,11},{10,... | collective-permute-start | bytes 1966088 | tf_op jit(solution)/shard_map/ppermute | solution.py:844
  332.2 22.2 %collective-permute-start.43 = (bf16[320,1024]{1,0:T(8,128)(2,1)S(1)}, bf16[320,1024]{1,0:T(8,128)(2,1)S(1)}, u32[]{:S(2)}, u32[]{:S(2)}) collective-permute-start(bf16[320,1024]{1,0:T(8,128)(2,1)S(1)} %pad_maximum_fusion.1), channel_id=1, source_target_pairs={{0,8},{4,12},{24,16},{28,20},{1,9},{5,13},{25,17},{29,21},{2,10},{... | collective-permute-start | bytes 1966088 | tf_op jit(solution)/shard_map/ppermute | solution.py:1010
  335.9 18.5 %collective-permute-start.41 = (bf16[128,2560]{1,0:T(8,128)(2,1)S(1)}, bf16[128,2560]{1,0:T(8,128)(2,1)S(1)}, u32[]{:S(2)}, u32[]{:S(2)}) collective-permute-start(bf16[128,2560]{1,0:T(8,128)(2,1)S(1)} %get-tuple-element.477), channel_id=1, source_target_pairs={{0,1},{1,0},{2,3},{3,2},{4,5},{5,4},{6,7},{7,6},{8,9},{9,8},{10,11... | collective-permute-start | bytes 1966088 | tf_op jit(solution)/shard_map/ppermute | solution.py:841
  336.7 17.7 %collective-permute-start.42 = (bf16[112,2560]{1,0:T(8,128)(2,1)S(1)}, bf16[112,2560]{1,0:T(8,128)(2,1)S(1)}, u32[]{:S(2)}, u32[]{:S(2)}) collective-permute-start(bf16[112,2560]{1,0:T(8,128)(2,1)S(1)} %get-tuple-element.479), channel_id=1, source_target_pairs={{0,2},{1,3},{2,0},{3,1},{4,6},{5,7},{6,4},{7,5},{8,10},{9,11},{10,... | collective-permute-start | bytes 1720328 | tf_op jit(solution)/shard_map/ppermute | solution.py:844
  355.7 17.6 %collective-permute-start.44 = (bf16[128,2560]{1,0:T(8,128)(2,1)S(1)}, bf16[128,2560]{1,0:T(8,128)(2,1)S(1)}, u32[]{:S(2)}, u32[]{:S(2)}) collective-permute-start(bf16[128,2560]{1,0:T(8,128)(2,1)S(1)} %get-tuple-element.494), channel_id=1, source_target_pairs={{0,1},{1,0},{2,3},{3,2},{4,5},{5,4},{6,7},{7,6},{8,9},{9,8},{10,11... | collective-permute-start | bytes 1966088 | tf_op jit(solution)/shard_map/ppermute | solution.py:841
  357.3 23.1 %collective-permute-start.47 = (bf16[288,640]{1,0:T(8,128)(2,1)S(1)}, bf16[288,640]{1,0:T(8,128)(2,1)S(1)}, u32[]{:S(2)}, u32[]{:S(2)}) collective-permute-start(bf16[288,640]{1,0:T(8,128)(2,1)S(1)} %get-tuple-element.690), channel_id=1, source_target_pairs={{0,1},{1,0},{2,3},{3,2},{4,5},{5,4},{6,7},{7,6},{8,9},{9,8},{10,11... | collective-permute-start | bytes 1105928 | tf_op jit(solution)/shard_map/ppermute | solution.py:841
  380.4 20.3 %collective-permute-start.50 = (bf16[4,240,1024]{2,1,0:T(8,128)(2,1)}, bf16[4,240,1024]{2,1,0:T(8,128)(2,1)}, u32[]{:S(2)}, u32[]{:S(2)}) collective-permute-start(bf16[4,240,1024]{2,1,0:T(8,128)(2,1)} %get-tuple-element.532), channel_id=1, source_target_pairs={{0,4},{4,0},{8,12},{12,8},{16,20},{20,16},{24,28},{28,24},{1,5},{5... | collective-permute-start | bytes 5898248 | tf_op jit(solution)/shard_map/ppermute | solution.py:847
  381.6 34.2 %collective-permute-start.57 = (bf16[320,1024]{1,0:T(8,128)(2,1)}, bf16[320,1024]{1,0:T(8,128)(2,1)}, u32[]{:S(2)}, u32[]{:S(2)}) collective-permute-start(bf16[320,1024]{1,0:T(8,128)(2,1)} %add_convert_fusion.8), channel_id=1, source_target_pairs={{8,16},{12,20},{16,8},{20,12},{9,17},{13,21},{17,9},{21,13},{10,18... | collective-permute-start | bytes 1966088 | tf_op jit(solution)/shard_map/ppermute | solution.py:1010
  388.7 17.2 %collective-permute-start.48 = (bf16[128,2560]{1,0:T(8,128)(2,1)}, bf16[128,2560]{1,0:T(8,128)(2,1)}, u32[]{:S(2)}, u32[]{:S(2)}) collective-permute-start(bf16[128,2560]{1,0:T(8,128)(2,1)} %fusion.8), channel_id=1, source_target_pairs={{0,2},{1,3},{2,0},{3,1},{4,6},{5,7},{6,4},{7,5},{8,10},{9,11},{10,... | collective-permute-start | bytes 1966088 | tf_op jit(solution)/shard_map/ppermute | solution.py:844
  409.2 17.6 %collective-permute-start.51 = (bf16[128,2560]{1,0:T(8,128)(2,1)S(1)}, bf16[128,2560]{1,0:T(8,128)(2,1)S(1)}, u32[]{:S(2)}, u32[]{:S(2)}) collective-permute-start(bf16[128,2560]{1,0:T(8,128)(2,1)S(1)} %fusion.6), channel_id=1, source_target_pairs={{0,8},{4,12},{24,16},{28,20},{1,9},{5,13},{25,17},{29,21},{2,10},{... | collective-permute-start | bytes 1966088 | tf_op jit(solution)/shard_map/ppermute | solution.py:1010
  417.8 26.0 %collective-permute-start.65 = (bf16[288,1024]{1,0:T(8,128)(2,1)S(1)}, bf16[288,1024]{1,0:T(8,128)(2,1)}, u32[]{:S(2)}, u32[]{:S(2)}) collective-permute-start(bf16[288,1024]{1,0:T(8,128)(2,1)S(1)} %pad.14), channel_id=1, source_target_pairs={{0,0},{1,1},{2,4},{3,5},{4,2},{5,3},{6,6},{7,7},{8,8},{9,9},{10,12... | collective-permute-start | bytes 1769480 | tf_op jit(solution)/shard_map/ppermute | solution.py:857
  432.1 23.7 %collective-permute-start.64 = (bf16[320,1024]{1,0:T(8,128)(2,1)S(1)}, bf16[320,1024]{1,0:T(8,128)(2,1)}, u32[]{:S(2)}, u32[]{:S(2)}) collective-permute-start(bf16[320,1024]{1,0:T(8,128)(2,1)S(1)} %add_convert_fusion.6), channel_id=1, source_target_pairs={{8,0},{12,4},{16,24},{20,28},{9,1},{13,5},{17,25},{21,29},{10,2},{... | collective-permute-start | bytes 1966088 | tf_op jit(solution)/shard_map/ppermute | solution.py:1010
  433.7 22.1 %collective-permute-start.58 = (bf16[128,2560]{1,0:T(8,128)(2,1)S(1)}, bf16[128,2560]{1,0:T(8,128)(2,1)S(1)}, u32[]{:S(2)}, u32[]{:S(2)}) collective-permute-start(bf16[128,2560]{1,0:T(8,128)(2,1)S(1)} %add_convert_fusion.7), channel_id=1, source_target_pairs={{8,16},{12,20},{16,8},{20,12},{9,17},{13,21},{17,9},{21,13},{10,18... | collective-permute-start | bytes 1966088 | tf_op jit(solution)/shard_map/ppermute | solution.py:1010
  434.4 21.4 %collective-permute-start.59 = (bf16[112,2560]{1,0:T(8,128)(2,1)}, bf16[112,2560]{1,0:T(8,128)(2,1)}, u32[]{:S(2)}, u32[]{:S(2)}) collective-permute-start(bf16[112,2560]{1,0:T(8,128)(2,1)} %fusion.17), channel_id=1, source_target_pairs={{0,8},{4,12},{24,16},{28,20},{1,9},{5,13},{25,17},{29,21},{2,10},{... | collective-permute-start | bytes 1720328 | tf_op jit(solution)/shard_map/ppermute | solution.py:1010
  462.5 19.0 %collective-permute-start.66 = (bf16[128,2560]{1,0:T(8,128)(2,1)S(1)}, bf16[128,2560]{1,0:T(8,128)(2,1)S(1)}, u32[]{:S(2)}, u32[]{:S(2)}) collective-permute-start(bf16[128,2560]{1,0:T(8,128)(2,1)S(1)} %add_convert_fusion.5), channel_id=1, source_target_pairs={{8,0},{12,4},{16,24},{20,28},{9,1},{13,5},{17,25},{21,29},{10,2},{... | collective-permute-start | bytes 1966088 | tf_op jit(solution)/shard_map/ppermute | solution.py:1010
  464.0 20.6 %collective-permute-start.68 = (bf16[240,1536]{1,0:T(8,128)(2,1)S(1)}, bf16[240,1536]{1,0:T(8,128)(2,1)S(1)}, u32[]{:S(2)}, u32[]{:S(2)}) collective-permute-start(bf16[240,1536]{1,0:T(8,128)(2,1)S(1)} %maximum_maximum_fusion), channel_id=1, source_target_pairs={{0,8},{4,12},{24,16},{28,20},{1,9},{5,13},{25,17},{29,21},{2,10},{... | collective-permute-start | bytes 2211848 | tf_op jit(solution)/shard_map/ppermute | solution.py:1010
  484.7 19.5 %collective-permute-start.69 = (bf16[240,1536]{1,0:T(8,128)(2,1)S(1)}, bf16[240,1536]{1,0:T(8,128)(2,1)S(1)}, u32[]{:S(2)}, u32[]{:S(2)}) collective-permute-start(bf16[240,1536]{1,0:T(8,128)(2,1)S(1)} %add_convert_fusion.1), channel_id=1, source_target_pairs={{8,16},{12,20},{16,8},{20,12},{9,17},{13,21},{17,9},{21,13},{10,18... | collective-permute-start | bytes 2211848 | tf_op jit(solution)/shard_map/ppermute | solution.py:1010
  485.6 18.6 %collective-permute-start.70 = (bf16[112,2560]{1,0:T(8,128)(2,1)S(1)}, bf16[112,2560]{1,0:T(8,128)(2,1)S(1)}, u32[]{:S(2)}, u32[]{:S(2)}) collective-permute-start(bf16[112,2560]{1,0:T(8,128)(2,1)S(1)} %add_convert_fusion.9), channel_id=1, source_target_pairs={{8,0},{12,4},{16,24},{20,28},{9,1},{13,5},{17,25},{21,29},{10,2},{... | collective-permute-start | bytes 1720328 | tf_op jit(solution)/shard_map/ppermute | solution.py:1010
  504.6 21.0 %collective-permute-start.72 = (bf16[240,1536]{1,0:T(8,128)(2,1)S(1)}, bf16[240,1536]{1,0:T(8,128)(2,1)S(1)}, u32[]{:S(2)}, u32[]{:S(2)}) collective-permute-start(bf16[240,1536]{1,0:T(8,128)(2,1)S(1)} %add_convert_fusion), channel_id=1, source_target_pairs={{8,0},{12,4},{16,24},{20,28},{9,1},{13,5},{17,25},{21,29},{10,2},{... | collective-permute-start | bytes 2211848 | tf_op jit(solution)/shard_map/ppermute | solution.py:1010
  (197 other events, 1867.1 us)

commit v7 on v5

--- a/solution.py
+++ b/solution.py
@@ -173,12 +173,12 @@
             block += 1
 
 
-def by_group(count, do, unroll=False):
+def by_group(count, do):
     def one(g, _):
         do(g, pl.ds(pl.multiple_of(g * LANES, LANES), LANES))
         return 0
 
-    lax.fori_loop(0, count, one, 0, unroll=unroll)
+    lax.fori_loop(0, count, one, 0)
 
 
 def stacked(m):
@@ -219,7 +219,7 @@
                     lse_ref[:m, :] = jnp.where(lane == h, log[here], lse_ref[:m, :])
                 s = following
 
-        by_group(groups, group, True)
+        by_group(groups, group)
         join_pairs(o_all, att_ref, False, m)
         clear(m, att_ref)
 
@@ -246,7 +246,7 @@
             pltpu.VMEM((heads, rows, LANES), BF16),
             pltpu.VMEM((heads, rows, LANES), F32),
         ],
-        24,
+        16,
         4 * rows * keys * LANES * heads,
         4 * q.size + 2 * keys * both,
     )
@@ -296,7 +296,7 @@
             dkv = dotf(q3, ds3[: GROUP * m, :n], TN) + dotf(do3, p3[: GROUP * m, :n], TN)
             back[:n, cols] = dkv.T
 
-        by_group(groups, group, False)
+        by_group(groups, group)
         join_pairs(dq_all, dq_ref, True, m)
         clear(m, dq_ref)
 
@@ -331,7 +331,7 @@
             pltpu.VMEM((GROUP * rows, keys), BF16),
             pltpu.VMEM((heads, rows, LANES), F32),
         ],
-        32,
+        24,
         10 * rows * keys * LANES * heads,
         8 * q.size + 4 * keys * both,
     )

time: 547 us -> 538 us (0.984)
  waiting for transfers between devices: 153 us -> 161 us
  local copies, waits for them, and re-layouts: 64.5 us -> 57.5 us
  other arithmetic: 60.8 us -> 55.1 us
    unnamed x361 -> x313, local copies, waits for them, and re-layouts: 48.2 us -> 41.8 us
  transfers between devices with their start and end apart: 75 -> 75, of which waited for: 32 -> 36; matrix products, arithmetic and copies ran while one was open for 14% -> 12% of each run, Pallas kernels for 17% -> 17%
where the time goes in v7:
time: 538 us; the launch traced here: 531 us
  waiting for transfers between devices  161 us (30%)
  Pallas kernels  154 us (29%)
  starting transfers between devices  88 us (16%)
  local copies, waits for them, and re-layouts  57.5 us (11%)
  other arithmetic  55.1 us (10%)
  matrix products  12.6 us (2%)
    pallas_call x20, Pallas kernels, call(): pl.pallas_call(kernel, grid_spec=pltpu.PrefetchScalarGridSpec(num_scalar_...  115 us
    ppermute x22, waiting for transfers between devices, over_x(): return lax.ppermute(a, 'cp', [(i, i ^ 1) for i in range(self.cp)])  80.5 us
    ppermute x12, waiting for transfers between devices, hop(): lax.ppermute(a, 'dp', [(2 * s + c, 2 * t + c) for s, t in moves for c in...  46.3 us
    unnamed x313, local copies, waits for them, and re-layouts  41.8 us
    convert_element_type x32, other arithmetic, add(): return sum((a.astype(F32) for a in terms)).astype(BF16)  34.5 us
    pallas_call x4, Pallas kernels, weight_grad(): pl.pallas_call(functools.partial(weight_grad_kernel, fill, (len(lefts), l...  30.8 us
    ppermute x12, starting transfers between devices, hop(): lax.ppermute(a, 'dp', [(2 * s + c, 2 * t + c) for s, t in moves for c in...  28.2 us
    ppermute x22, starting transfers between devices, over_x(): return lax.ppermute(a, 'cp', [(i, i ^ 1) for i in range(self.cp)])  26.6 us
  transfers between devices with their start and end apart: 75, of which 36 were waited for; matrix products, arithmetic and copies ran while one was open for 12% of the time, Pallas kernels for 17%

profile of v7, /device:TPU:0, one launch (start us, length us, event | category | flops | bytes accessed | tf_op | source)
XLA Modules:
  0.0 531.0 jit_solution(15995706903385797999)
XLA Ops:
  10.3 6.1 %collective-permute-start.3 = (bf16[288,960]{1,0:T(8,128)(2,1)}, bf16[288,960]{1,0:T(8,128)(2,1)}, u32[]{:S(2)}, u32[]{:S(2)}) collective-permute-start(bf16[288,960]{1,0:T(8,128)(2,1)} %bitcast.280), channel_id=1, source_target_pairs={{0,0},{1,1},{2,4},{3,5},{4,2},{5,3},{6,6},{7,7},{8,8},{9,9},{10,12... | collective-permute-start | bytes 1658888 | tf_op jit(solution)/shard_map/ppermute | solution.py:863
  75.3 12.8 %collective-permute-done.10.refs_1_ = bf16[288,640]{1,0:T(8,128)(2,1)} collective-permute-done((bf16[288,640]{1,0:T(8,128)(2,1)}, bf16[288,640]{1,0:T(8,128)(2,1)}, u32[]{:S(2)}, u32[]{:S(2)}) %collective-permute-start.10) | collective-permute-done | bytes 368672 | tf_op jit(solution)/shard_map/ppermute | solution.py:847
  96.4 13.0 %attend.3 = (bf16[288,960]{1,0:T(8,128)(2,1)S(1)}, f32[288,128]{1,0:T(8,128)S(1)}, bf16[1152,640]{1,0:T(8,128)(2,1)S(1)}) custom-call(s32[10]{0:T(128)S(1)} %pad_add_fusion.4.meta_ref, bf16[288,960]{1,0:T(8,128)(2,1)S(1)} %copy-done.73, bf16[288,640]{1,0:T(8,128)(2,1)} %get-tuple-element.362.refs_0_, bf16[288,640]{1,0:T(8,128)(2,1)} %collective-permute-done.10.refs_1_, ...), custom_call_target="tpu_custom_call" | custom-call | flops 2548039680 | bytes 2580480 | tf_op jit(solution)/shard_map/attend/pallas_call | solution.py:54
  111.8 7.4 %collective-permute-done.16.refs_4_ = bf16[112,2560]{1,0:T(8,128)(2,1)S(1)} collective-permute-done((bf16[112,2560]{1,0:T(8,128)(2,1)S(1)}, bf16[112,2560]{1,0:T(8,128)(2,1)S(1)}, u32[]{:S(2)}, u32[]{:S(2)}) %collective-permute-start.16) | collective-permute-done | bytes 573472 | tf_op jit(solution)/shard_map/ppermute | solution.py:847
  125.4 6.2 %collective-permute-done.19.theirs = bf16[960,2560]{1,0:T(8,128)(2,1)S(1)} collective-permute-done((bf16[960,2560]{1,0:T(8,128)(2,1)S(1)}, bf16[960,2560]{1,0:T(8,128)(2,1)S(1)}, u32[]{:S(2)}, u32[]{:S(2)}) %collective-permute-start.19) | collective-permute-done | bytes 4915232 | tf_op jit(solution)/shard_map/ppermute | solution.py:853
  137.4 4.8 collective-permute-done.22.refs_1_
  149.3 9.1 %collective-permute-done.23.refs_1_ = bf16[288,640]{1,0:T(8,128)(2,1)S(1)} collective-permute-done((bf16[288,640]{1,0:T(8,128)(2,1)S(1)}, bf16[288,640]{1,0:T(8,128)(2,1)S(1)}, u32[]{:S(2)}, u32[]{:S(2)}) %collective-permute-start.23) | collective-permute-done | bytes 368672 | tf_op jit(solution)/shard_map/ppermute | solution.py:847
  160.1 8.1 %attend.4 = (bf16[288,960]{1,0:T(8,128)(2,1)S(1)}, f32[288,128]{1,0:T(8,128)S(1)}, bf16[1152,640]{1,0:T(8,128)(2,1)S(1)}) custom-call(s32[10]{0:T(128)S(1)} %get-tuple-element.359.meta_ref, bf16[288,960]{1,0:T(8,128)(2,1)S(1)} %get-tuple-element.388.q_ref, bf16[288,640]{1,0:T(8,128)(2,1)S(1)} %get-tuple-element.389.refs_0_, ...), custom_call_target="tpu_custom_call" | custom-call | flops 2548039680 | bytes 2580480 | tf_op jit(solution)/shard_map/attend/pallas_call | solution.py:54
  168.3 7.2 %post.2 = (f32[288,960]{1,0:T(8,128)S(1)}, f32[288,960]{1,0:T(8,128)S(1)}, bf16[288,960]{1,0:T(8,128)(2,1)S(1)}, f32[288,960]{1,0:T(8,128)S(1)}, f32[288,1]{1,0:...) custom-call(s32[10]{0:T(128)S(1)} %get-tuple-element.359.meta_ref, ...), custom_call_target="tpu_custom_call" | custom-call | flops 4777574400 | bytes 16588800 | tf_op jit(solution)/shard_map/post/pallas_call | solution.py:54
  179.3 9.3 %collective-permute-done.26.refs_1_ = bf16[288,640]{1,0:T(8,128)(2,1)S(1)} collective-permute-done((bf16[288,640]{1,0:T(8,128)(2,1)S(1)}, bf16[288,640]{1,0:T(8,128)(2,1)S(1)}, u32[]{:S(2)}, u32[]{:S(2)}) %collective-permute-start.26) | collective-permute-done | bytes 368672 | tf_op jit(solution)/shard_map/ppermute | solution.py:847
  190.3 4.6 attend.5
  196.1 5.5 %post.3 = (f32[288,960]{1,0:T(8,128)S(1)}, f32[288,960]{1,0:T(8,128)S(1)}, bf16[288,960]{1,0:T(8,128)(2,1)S(1)}, f32[288,960]{1,0:T(8,128)S(1)}, f32[288,1]{1,0:...) custom-call(s32[10]{0:T(128)S(1)} %get-tuple-element.360.meta_ref, ...), custom_call_target="tpu_custom_call" | custom-call | flops 4777574400 | bytes 16588800 | tf_op jit(solution)/shard_map/post/pallas_call | solution.py:54
  202.7 8.1 %post_back.2 = (bf16[288,960]{1,0:T(8,128)(2,1)S(1)}, f32[288,960]{1,0:T(8,128)S(1)}, bf16[288,960]{1,0:T(8,128)(2,1)S(1)}, bf16[288,960]{1,0:T(8,128)(2,1)S(1)}...) custom-call(s32[10]{0:T(128)S(1)} %get-tuple-element.360.meta_ref, ...), custom_call_target="tpu_custom_call" | custom-call | flops 4777574400 | bytes 16588800 | tf_op jit(solution)/shard_map/post_back/pallas_call | solution.py:54
  217.0 6.7 %attend_back.3 = (bf16[288,960]{1,0:T(8,128)(2,1)S(1)}, bf16[1152,640]{1,0:T(8,128)(2,1)S(1)}) custom-call(s32[10]{0:T(128)S(1)} %get-tuple-element.360.meta_ref, bf16[288,960]{1,0:T(8,128)(2,1)S(1)} %copy-done.94, bf16[288,960]{1,0:T(8,128)(2,1)S(1)} %copy-done.96, bf16[288,960]{1,0:T(8,128)(2,1)S(1)} %get-tuple-element.397.att.att_ref.refs_2_, ...), custom_call_target="tpu_custom_call" | custom-call | flops 6370099200 | bytes 5160960 | tf_op jit(solution)/shard_map/attend_back/pallas_call | solution.py:54
  227.9 9.1 %collective-permute-done.31.got_ref = bf16[288,640]{1,0:T(8,128)(2,1)S(1)} collective-permute-done((bf16[288,640]{1,0:T(8,128)(2,1)S(1)}, bf16[288,640]{1,0:T(8,128)(2,1)S(1)}, u32[]{:S(2)}, u32[]{:S(2)}) %collective-permute-start.31) | collective-permute-done | bytes 368672 | tf_op jit(solution)/shard_map/ppermute | solution.py:847
  239.7 8.6 %post_back.3 = (bf16[288,960]{1,0:T(8,128)(2,1)S(1)}, f32[288,960]{1,0:T(8,128)S(1)}, bf16[288,960]{1,0:T(8,128)(2,1)S(1)}, bf16[288,960]{1,0:T(8,128)(2,1)S(1)}...) custom-call(s32[10]{0:T(128)S(1)} %get-tuple-element.359.meta_ref, ...), custom_call_target="tpu_custom_call" | custom-call | flops 4777574400 | bytes 16588800 | tf_op jit(solution)/shard_map/post_back/pallas_call | solution.py:54
  250.9 11.1 %attend_back.4 = (bf16[288,960]{1,0:T(8,128)(2,1)S(1)}, bf16[1152,640]{1,0:T(8,128)(2,1)S(1)}) custom-call(s32[10]{0:T(128)S(1)} %get-tuple-element.359.meta_ref, bf16[288,960]{1,0:T(8,128)(2,1)S(1)} %copy-done.88, bf16[288,960]{1,0:T(8,128)(2,1)S(1)} %get-tuple-element.417.do_ref, bf16[288,960]{1,0:T(8,128)(2,1)S(1)} %get-tuple-element.391.att.att_ref.refs_1_, ...), custom_call_target="tpu_custom_call" | custom-call | flops 6370099200 | bytes 5160960 | tf_op jit(solution)/shard_map/attend_back/pallas_call | solution.py:54
  266.4 9.7 %collective-permute-done.33.got_ref = bf16[288,640]{1,0:T(8,128)(2,1)S(1)} collective-permute-done((bf16[288,640]{1,0:T(8,128)(2,1)S(1)}, bf16[288,640]{1,0:T(8,128)(2,1)S(1)}, u32[]{:S(2)}, u32[]{:S(2)}) %collective-permute-start.33) | collective-permute-done | bytes 368672 | tf_op jit(solution)/shard_map/ppermute | solution.py:847
  282.0 8.9 %weight_grad.4 = (bf16[2,160,1024]{2,1,0:T(8,128)(2,1)S(1)}, bf16[2,160,1024]{2,1,0:T(8,128)(2,1)S(1)}, bf16[2,160,1024]{2,1,0:T(8,128)(2,1)S(1)}, bf16[2,160,10...) custom-call(s32[3]{0:T(128)S(1)} %pad_add_fusion.6.spot_ref, bf16[288,2560]{1,0:T(8,128)(2,1)S(1)} %copy-done.104, ...), custom_call_target="tpu_custom_call" | custom-call | flops 4246732800 | bytes 11325440 | tf_op jit(solution)/shard_map/weight_grad/pallas_call | solution.py:691
  291.6 4.2 expand_back.1
  303.6 12.3 %weight_grad.5 = (bf16[2,128,2560]{2,1,0:T(8,128)(2,1)S(1)}, bf16[2,128,2560]{2,1,0:T(8,128)(2,1)S(1)}, bf16[2,112,2560]{2,1,0:T(8,128)(2,1)S(1)}, bf16[2,112,25...) custom-call(s32[3]{0:T(128)S(1)} %pad_add_fusion.6.spot_ref, bf16[288,960]{1,0:T(8,128)(2,1)S(1)} %copy-done.41, ...), custom_call_target="tpu_custom_call" | custom-call | flops 8493465600 | bytes 20336640 | tf_op jit(solution)/shard_map/weight_grad/pallas_call | solution.py:691
  321.2 4.8 norm_back.1
  337.4 16.2 %attend_back.5 = (bf16[288,960]{1,0:T(8,128)(2,1)S(1)}, bf16[1152,640]{1,0:T(8,128)(2,1)S(1)}) custom-call(s32[10]{0:T(128)S(1)} %pad_add_fusion.4.meta_ref, bf16[288,960]{1,0:T(8,128)(2,1)S(1)} %copy-done.74, bf16[288,960]{1,0:T(8,128)(2,1)S(1)} %get-tuple-element.487.do_ref, bf16[288,960]{1,0:T(8,128)(2,1)S(1)} %get-tuple-element.366.att_ref.refs_0_, ...), custom_call_target="tpu_custom_call" | custom-call | flops 6370099200 | bytes 5160960 | tf_op jit(solution)/shard_map/attend_back/pallas_call | solution.py:54
  358.7 7.4 %weight_grad.6 = (bf16[2,128,1024]{2,1,0:T(8,128)(2,1)S(1)}, bf16[2,128,1024]{2,1,0:T(8,128)(2,1)S(1)}, bf16[2,112,1024]{2,1,0:T(8,128)(2,1)S(1)}, bf16[2,112,10...) custom-call(s32[3]{0:T(128)S(1)} %pad_add_fusion.6.spot_ref, ...), custom_call_target="tpu_custom_call" | custom-call | flops 3185049600 | bytes 10567680 | tf_op jit(solution)/shard_map/weight_grad/pallas_call | solution.py:691
  372.6 7.1 %collective-permute-done.47.got_ref = bf16[288,640]{1,0:T(8,128)(2,1)S(1)} collective-permute-done((bf16[288,640]{1,0:T(8,128)(2,1)S(1)}, bf16[288,640]{1,0:T(8,128)(2,1)S(1)}, u32[]{:S(2)}, u32[]{:S(2)}) %collective-permute-start.47) | collective-permute-done | bytes 368672 | tf_op jit(solution)/shard_map/ppermute | solution.py:847
  420.9 5.3 collective-permute-done.51
  433.7 7.8 %collective-permute-start.59 = (bf16[112,2560]{1,0:T(8,128)(2,1)}, bf16[112,2560]{1,0:T(8,128)(2,1)}, u32[]{:S(2)}, u32[]{:S(2)}) collective-permute-start(bf16[112,2560]{1,0:T(8,128)(2,1)} %fusion.17), channel_id=1, source_target_pairs={{0,8},{4,12},{24,16},{28,20},{1,9},{5,13},{25,17},{29,21},{2,10},{... | collective-permute-start | bytes 1720328 | tf_op jit(solution)/shard_map/ppermute | solution.py:1016
  448.8 6.3 %collective-permute-done.61 = bf16[112,1024]{1,0:T(8,128)(2,1)} collective-permute-done((bf16[112,1024]{1,0:T(8,128)(2,1)}, bf16[112,1024]{1,0:T(8,128)(2,1)}, u32[]{:S(2)}, u32[]{:S(2)}) %collective-permute-start.61) | collective-permute-done | bytes 229408 | tf_op jit(solution)/shard_map/ppermute | solution.py:847
  463.3 4.7 collective-permute-start.68
  475.4 5.4 %collective-permute-done.66 = bf16[128,2560]{1,0:T(8,128)(2,1)S(1)} collective-permute-done((bf16[128,2560]{1,0:T(8,128)(2,1)S(1)}, bf16[128,2560]{1,0:T(8,128)(2,1)S(1)}, u32[]{:S(2)}, u32[]{:S(2)}) %collective-permute-start.66) | collective-permute-done | bytes 655392 | tf_op jit(solution)/shard_map/ppermute | solution.py:1016
  486.3 17.2 %collective-permute-done.70 = bf16[112,2560]{1,0:T(8,128)(2,1)S(1)} collective-permute-done((bf16[112,2560]{1,0:T(8,128)(2,1)S(1)}, bf16[112,2560]{1,0:T(8,128)(2,1)S(1)}, u32[]{:S(2)}, u32[]{:S(2)}) %collective-permute-start.70) | collective-permute-done | bytes 573472 | tf_op jit(solution)/shard_map/ppermute | solution.py:1016
  509.5 15.3 %collective-permute-done.72 = bf16[240,1536]{1,0:T(8,128)(2,1)S(1)} collective-permute-done((bf16[240,1536]{1,0:T(8,128)(2,1)S(1)}, bf16[240,1536]{1,0:T(8,128)(2,1)S(1)}, u32[]{:S(2)}, u32[]{:S(2)}) %collective-permute-start.72) | collective-permute-done | bytes 737312 | tf_op jit(solution)/shard_map/ppermute | solution.py:1016
  (605 shorter events, 257.2 us)
Async XLA Ops:
  5.1 21.0 %collective-permute-start.1 = (bf16[240,1408]{1,0:T(8,128)(2,1)S(1)}, bf16[240,1408]{1,0:T(8,128)(2,1)S(1)}, u32[]{:S(2)}, u32[]{:S(2)}) collective-permute-start(bf16[240,1408]{1,0:T(8,128)(2,1)S(1)} %concatenate.38.refs_0_), channel_id=1, source_target_pairs={{0,2},{1,3},{2,0},{3,1},{4,6},{5,7},{6,4},{7,5},{8,10},{9,11},{10,... | collective-permute-start | bytes 2027528 | tf_op jit(solution)/shard_map/ppermute | solution.py:850
  8.1 18.0 %collective-permute-start = (bf16[240,1408]{1,0:T(8,128)(2,1)S(1)}, bf16[240,1408]{1,0:T(8,128)(2,1)S(1)}, u32[]{:S(2)}, u32[]{:S(2)}) collective-permute-start(bf16[240,1408]{1,0:T(8,128)(2,1)S(1)} %concatenate.38.refs_0_), channel_id=1, source_target_pairs={{0,1},{1,0},{2,3},{3,2},{4,5},{5,4},{6,7},{7,6},{8,9},{9,8},{10,11... | collective-permute-start | bytes 2027528 | tf_op jit(solution)/shard_map/ppermute | solution.py:847
  9.6 16.5 %collective-permute-start.2 = (s32[2,288]{1,0:T(2,128)S(1)}, s32[2,288]{1,0:T(2,128)S(1)}, u32[]{:S(2)}, u32[]{:S(2)}) collective-permute-start(s32[2,288]{1,0:T(2,128)S(1)} %pad_add_fusion.1), channel_id=1, source_target_pairs={{0,0},{1,1},{2,4},{3,5},{4,2},{5,3},{6,6},{7,7},{8,8},{9,9},{10,12... | collective-permute-start | bytes 6920 | tf_op jit(solution)/shard_map/ppermute | solution.py:863
  49.0 39.1 %collective-permute-start.14 = (bf16[240,2560]{1,0:T(8,128)(2,1)}, bf16[240,2560]{1,0:T(8,128)(2,1)}, u32[]{:S(2)}, u32[]{:S(2)}) collective-permute-start(bf16[240,2560]{1,0:T(8,128)(2,1)} %broadcast_select_fusion.2.refs_0_), channel_id=1, source_target_pairs={{0,2},{1,3},{2,0},{3,1},{4,6},{5,7},{6,4},{7,5},{8,10},{9,11},{10,... | collective-permute-start | bytes 3686408 | tf_op jit(solution)/shard_map/ppermute | solution.py:850
  50.7 37.4 %collective-permute-start.13 = (bf16[240,2560]{1,0:T(8,128)(2,1)}, bf16[240,2560]{1,0:T(8,128)(2,1)}, u32[]{:S(2)}, u32[]{:S(2)}) collective-permute-start(bf16[240,2560]{1,0:T(8,128)(2,1)} %broadcast_select_fusion.2.refs_0_), channel_id=1, source_target_pairs={{0,1},{1,0},{2,3},{3,2},{4,5},{5,4},{6,7},{7,6},{8,9},{9,8},{10,11... | collective-permute-start | bytes 3686408 | tf_op jit(solution)/shard_map/ppermute | solution.py:847
  66.7 21.5 %collective-permute-start.11 = (bf16[288,640]{1,0:T(8,128)(2,1)}, bf16[288,640]{1,0:T(8,128)(2,1)}, u32[]{:S(2)}, u32[]{:S(2)}) collective-permute-start(bf16[288,640]{1,0:T(8,128)(2,1)} %get-tuple-element.362.refs_0_), channel_id=1, source_target_pairs={{0,4},{4,0},{8,12},{12,8},{16,20},{20,16},{24,28},{28,24},{1,5},{5... | collective-permute-start | bytes 1105928 | tf_op jit(solution)/shard_map/ppermute | solution.py:853
  66.8 21.3 %collective-permute-start.10 = (bf16[288,640]{1,0:T(8,128)(2,1)}, bf16[288,640]{1,0:T(8,128)(2,1)}, u32[]{:S(2)}, u32[]{:S(2)}) collective-permute-start(bf16[288,640]{1,0:T(8,128)(2,1)} %get-tuple-element.362.refs_0_), channel_id=1, source_target_pairs={{0,1},{1,0},{2,3},{3,2},{4,5},{5,4},{6,7},{7,6},{8,9},{9,8},{10,11... | collective-permute-start | bytes 1105928 | tf_op jit(solution)/shard_map/ppermute | solution.py:847
  90.0 30.8 %collective-permute-start.18 = (bf16[320,1024]{1,0:T(8,128)(2,1)S(1)}, bf16[320,1024]{1,0:T(8,128)(2,1)S(1)}, u32[]{:S(2)}, u32[]{:S(2)}) collective-permute-start(bf16[320,1024]{1,0:T(8,128)(2,1)S(1)} %copy-done.19), channel_id=1, source_target_pairs={{0,2},{1,3},{2,0},{3,1},{4,6},{5,7},{6,4},{7,5},{8,10},{9,11},{10,... | collective-permute-start | bytes 1966088 | tf_op jit(solution)/shard_map/ppermute | solution.py:850
  90.4 30.5 %collective-permute-start.17 = (bf16[320,1024]{1,0:T(8,128)(2,1)S(1)}, bf16[320,1024]{1,0:T(8,128)(2,1)S(1)}, u32[]{:S(2)}, u32[]{:S(2)}) collective-permute-start(bf16[320,1024]{1,0:T(8,128)(2,1)S(1)} %copy-done.19), channel_id=1, source_target_pairs={{0,1},{1,0},{2,3},{3,2},{4,5},{5,4},{6,7},{7,6},{8,9},{9,8},{10,11... | collective-permute-start | bytes 1966088 | tf_op jit(solution)/shard_map/ppermute | solution.py:847
  93.0 26.2 %collective-permute-start.16 = (bf16[112,2560]{1,0:T(8,128)(2,1)S(1)}, bf16[112,2560]{1,0:T(8,128)(2,1)S(1)}, u32[]{:S(2)}, u32[]{:S(2)}) collective-permute-start(bf16[112,2560]{1,0:T(8,128)(2,1)S(1)} %slice.344), channel_id=1, source_target_pairs={{0,1},{1,0},{2,3},{3,2},{4,5},{5,4},{6,7},{7,6},{8,9},{9,8},{10,11... | collective-permute-start | bytes 1720328 | tf_op jit(solution)/shard_map/ppermute | solution.py:847
  94.7 26.1 %collective-permute-start.15 = (bf16[128,2560]{1,0:T(8,128)(2,1)S(1)}, bf16[128,2560]{1,0:T(8,128)(2,1)S(1)}, u32[]{:S(2)}, u32[]{:S(2)}) collective-permute-start(bf16[128,2560]{1,0:T(8,128)(2,1)S(1)} %slice.343), channel_id=1, source_target_pairs={{0,2},{1,3},{2,0},{3,1},{4,6},{5,7},{6,4},{7,5},{8,10},{9,11},{10,... | collective-permute-start | bytes 1966088 | tf_op jit(solution)/shard_map/ppermute | solution.py:850
  158.4 30.3 %collective-permute-start.29 = (bf16[288,960]{1,0:T(8,128)(2,1)S(1)}, bf16[288,960]{1,0:T(8,128)(2,1)S(1)}, u32[]{:S(2)}, u32[]{:S(2)}) collective-permute-start(bf16[288,960]{1,0:T(8,128)(2,1)S(1)} %bitcast.281), channel_id=1, source_target_pairs={{0,0},{1,1},{2,4},{3,5},{4,2},{5,3},{6,6},{7,7},{8,8},{9,9},{10,12... | collective-permute-start | bytes 1658888 | tf_op jit(solution)/shard_map/ppermute | solution.py:863
  299.3 17.1 %collective-permute-start.36 = (bf16[2,160,1024]{2,1,0:T(8,128)(2,1)}, bf16[2,160,1024]{2,1,0:T(8,128)(2,1)}, u32[]{:S(2)}, u32[]{:S(2)}) collective-permute-start(bf16[2,160,1024]{2,1,0:T(8,128)(2,1)} %get-tuple-element.438), channel_id=1, source_target_pairs={{0,1},{1,0},{2,3},{3,2},{4,5},{5,4},{6,7},{7,6},{8,9},{9,8},{10,11... | collective-permute-start | bytes 1966088 | tf_op jit(solution)/shard_map/ppermute | solution.py:847
  300.8 16.8 %collective-permute-start.37 = (bf16[2,160,1024]{2,1,0:T(8,128)(2,1)}, bf16[2,160,1024]{2,1,0:T(8,128)(2,1)}, u32[]{:S(2)}, u32[]{:S(2)}) collective-permute-start(bf16[2,160,1024]{2,1,0:T(8,128)(2,1)} %get-tuple-element.439), channel_id=1, source_target_pairs={{0,2},{1,3},{2,0},{3,1},{4,6},{5,7},{6,4},{7,5},{8,10},{9,11},{10,... | collective-permute-start | bytes 1966088 | tf_op jit(solution)/shard_map/ppermute | solution.py:850
  332.0 21.7 %collective-permute-start.43 = (bf16[320,1024]{1,0:T(8,128)(2,1)S(1)}, bf16[320,1024]{1,0:T(8,128)(2,1)S(1)}, u32[]{:S(2)}, u32[]{:S(2)}) collective-permute-start(bf16[320,1024]{1,0:T(8,128)(2,1)S(1)} %pad_maximum_fusion.1), channel_id=1, source_target_pairs={{0,8},{4,12},{24,16},{28,20},{1,9},{5,13},{25,17},{29,21},{2,10},{... | collective-permute-start | bytes 1966088 | tf_op jit(solution)/shard_map/ppermute | solution.py:1016
  335.6 18.1 %collective-permute-start.41 = (bf16[128,2560]{1,0:T(8,128)(2,1)S(1)}, bf16[128,2560]{1,0:T(8,128)(2,1)S(1)}, u32[]{:S(2)}, u32[]{:S(2)}) collective-permute-start(bf16[128,2560]{1,0:T(8,128)(2,1)S(1)} %get-tuple-element.477), channel_id=1, source_target_pairs={{0,1},{1,0},{2,3},{3,2},{4,5},{5,4},{6,7},{7,6},{8,9},{9,8},{10,11... | collective-permute-start | bytes 1966088 | tf_op jit(solution)/shard_map/ppermute | solution.py:847
  336.4 17.2 %collective-permute-start.42 = (bf16[112,2560]{1,0:T(8,128)(2,1)S(1)}, bf16[112,2560]{1,0:T(8,128)(2,1)S(1)}, u32[]{:S(2)}, u32[]{:S(2)}) collective-permute-start(bf16[112,2560]{1,0:T(8,128)(2,1)S(1)} %get-tuple-element.479), channel_id=1, source_target_pairs={{0,2},{1,3},{2,0},{3,1},{4,6},{5,7},{6,4},{7,5},{8,10},{9,11},{10,... | collective-permute-start | bytes 1720328 | tf_op jit(solution)/shard_map/ppermute | solution.py:850
  355.0 17.6 %collective-permute-start.44 = (bf16[128,2560]{1,0:T(8,128)(2,1)S(1)}, bf16[128,2560]{1,0:T(8,128)(2,1)S(1)}, u32[]{:S(2)}, u32[]{:S(2)}) collective-permute-start(bf16[128,2560]{1,0:T(8,128)(2,1)S(1)} %get-tuple-element.494), channel_id=1, source_target_pairs={{0,1},{1,0},{2,3},{3,2},{4,5},{5,4},{6,7},{7,6},{8,9},{9,8},{10,11... | collective-permute-start | bytes 1966088 | tf_op jit(solution)/shard_map/ppermute | solution.py:847
  356.6 23.1 %collective-permute-start.47 = (bf16[288,640]{1,0:T(8,128)(2,1)S(1)}, bf16[288,640]{1,0:T(8,128)(2,1)S(1)}, u32[]{:S(2)}, u32[]{:S(2)}) collective-permute-start(bf16[288,640]{1,0:T(8,128)(2,1)S(1)} %get-tuple-element.690), channel_id=1, source_target_pairs={{0,1},{1,0},{2,3},{3,2},{4,5},{5,4},{6,7},{7,6},{8,9},{9,8},{10,11... | collective-permute-start | bytes 1105928 | tf_op jit(solution)/shard_map/ppermute | solution.py:847
  379.7 20.3 %collective-permute-start.50 = (bf16[4,240,1024]{2,1,0:T(8,128)(2,1)}, bf16[4,240,1024]{2,1,0:T(8,128)(2,1)}, u32[]{:S(2)}, u32[]{:S(2)}) collective-permute-start(bf16[4,240,1024]{2,1,0:T(8,128)(2,1)} %get-tuple-element.532), channel_id=1, source_target_pairs={{0,4},{4,0},{8,12},{12,8},{16,20},{20,16},{24,28},{28,24},{1,5},{5... | collective-permute-start | bytes 5898248 | tf_op jit(solution)/shard_map/ppermute | solution.py:853
  380.9 34.2 %collective-permute-start.57 = (bf16[320,1024]{1,0:T(8,128)(2,1)}, bf16[320,1024]{1,0:T(8,128)(2,1)}, u32[]{:S(2)}, u32[]{:S(2)}) collective-permute-start(bf16[320,1024]{1,0:T(8,128)(2,1)} %add_convert_fusion.8), channel_id=1, source_target_pairs={{8,16},{12,20},{16,8},{20,12},{9,17},{13,21},{17,9},{21,13},{10,18... | collective-permute-start | bytes 1966088 | tf_op jit(solution)/shard_map/ppermute | solution.py:1016
  388.0 17.2 %collective-permute-start.48 = (bf16[128,2560]{1,0:T(8,128)(2,1)}, bf16[128,2560]{1,0:T(8,128)(2,1)}, u32[]{:S(2)}, u32[]{:S(2)}) collective-permute-start(bf16[128,2560]{1,0:T(8,128)(2,1)} %fusion.8), channel_id=1, source_target_pairs={{0,2},{1,3},{2,0},{3,1},{4,6},{5,7},{6,4},{7,5},{8,10},{9,11},{10,... | collective-permute-start | bytes 1966088 | tf_op jit(solution)/shard_map/ppermute | solution.py:850
  408.5 17.6 %collective-permute-start.51 = (bf16[128,2560]{1,0:T(8,128)(2,1)S(1)}, bf16[128,2560]{1,0:T(8,128)(2,1)S(1)}, u32[]{:S(2)}, u32[]{:S(2)}) collective-permute-start(bf16[128,2560]{1,0:T(8,128)(2,1)S(1)} %fusion.6), channel_id=1, source_target_pairs={{0,8},{4,12},{24,16},{28,20},{1,9},{5,13},{25,17},{29,21},{2,10},{... | collective-permute-start | bytes 1966088 | tf_op jit(solution)/shard_map/ppermute | solution.py:1016
  417.1 25.9 %collective-permute-start.65 = (bf16[288,1024]{1,0:T(8,128)(2,1)S(1)}, bf16[288,1024]{1,0:T(8,128)(2,1)}, u32[]{:S(2)}, u32[]{:S(2)}) collective-permute-start(bf16[288,1024]{1,0:T(8,128)(2,1)S(1)} %pad.14), channel_id=1, source_target_pairs={{0,0},{1,1},{2,4},{3,5},{4,2},{5,3},{6,6},{7,7},{8,8},{9,9},{10,12... | collective-permute-start | bytes 1769480 | tf_op jit(solution)/shard_map/ppermute | solution.py:863
  431.4 23.7 %collective-permute-start.64 = (bf16[320,1024]{1,0:T(8,128)(2,1)S(1)}, bf16[320,1024]{1,0:T(8,128)(2,1)}, u32[]{:S(2)}, u32[]{:S(2)}) collective-permute-start(bf16[320,1024]{1,0:T(8,128)(2,1)S(1)} %add_convert_fusion.6), channel_id=1, source_target_pairs={{8,0},{12,4},{16,24},{20,28},{9,1},{13,5},{17,25},{21,29},{10,2},{... | collective-permute-start | bytes 1966088 | tf_op jit(solution)/shard_map/ppermute | solution.py:1016
  433.0 22.1 %collective-permute-start.58 = (bf16[128,2560]{1,0:T(8,128)(2,1)S(1)}, bf16[128,2560]{1,0:T(8,128)(2,1)S(1)}, u32[]{:S(2)}, u32[]{:S(2)}) collective-permute-start(bf16[128,2560]{1,0:T(8,128)(2,1)S(1)} %add_convert_fusion.7), channel_id=1, source_target_pairs={{8,16},{12,20},{16,8},{20,12},{9,17},{13,21},{17,9},{21,13},{10,18... | collective-permute-start | bytes 1966088 | tf_op jit(solution)/shard_map/ppermute | solution.py:1016
  433.7 21.4 %collective-permute-start.59 = (bf16[112,2560]{1,0:T(8,128)(2,1)}, bf16[112,2560]{1,0:T(8,128)(2,1)}, u32[]{:S(2)}, u32[]{:S(2)}) collective-permute-start(bf16[112,2560]{1,0:T(8,128)(2,1)} %fusion.17), channel_id=1, source_target_pairs={{0,8},{4,12},{24,16},{28,20},{1,9},{5,13},{25,17},{29,21},{2,10},{... | collective-permute-start | bytes 1720328 | tf_op jit(solution)/shard_map/ppermute | solution.py:1016
  461.8 19.0 %collective-permute-start.66 = (bf16[128,2560]{1,0:T(8,128)(2,1)S(1)}, bf16[128,2560]{1,0:T(8,128)(2,1)S(1)}, u32[]{:S(2)}, u32[]{:S(2)}) collective-permute-start(bf16[128,2560]{1,0:T(8,128)(2,1)S(1)} %add_convert_fusion.5), channel_id=1, source_target_pairs={{8,0},{12,4},{16,24},{20,28},{9,1},{13,5},{17,25},{21,29},{10,2},{... | collective-permute-start | bytes 1966088 | tf_op jit(solution)/shard_map/ppermute | solution.py:1016
  463.3 20.6 %collective-permute-start.68 = (bf16[240,1536]{1,0:T(8,128)(2,1)S(1)}, bf16[240,1536]{1,0:T(8,128)(2,1)S(1)}, u32[]{:S(2)}, u32[]{:S(2)}) collective-permute-start(bf16[240,1536]{1,0:T(8,128)(2,1)S(1)} %maximum_maximum_fusion), channel_id=1, source_target_pairs={{0,8},{4,12},{24,16},{28,20},{1,9},{5,13},{25,17},{29,21},{2,10},{... | collective-permute-start | bytes 2211848 | tf_op jit(solution)/shard_map/ppermute | solution.py:1016
  484.0 19.5 %collective-permute-start.69 = (bf16[240,1536]{1,0:T(8,128)(2,1)S(1)}, bf16[240,1536]{1,0:T(8,128)(2,1)S(1)}, u32[]{:S(2)}, u32[]{:S(2)}) collective-permute-start(bf16[240,1536]{1,0:T(8,128)(2,1)S(1)} %add_convert_fusion.1), channel_id=1, source_target_pairs={{8,16},{12,20},{16,8},{20,12},{9,17},{13,21},{17,9},{21,13},{10,18... | collective-permute-start | bytes 2211848 | tf_op jit(solution)/shard_map/ppermute | solution.py:1016
  484.9 18.6 %collective-permute-start.70 = (bf16[112,2560]{1,0:T(8,128)(2,1)S(1)}, bf16[112,2560]{1,0:T(8,128)(2,1)S(1)}, u32[]{:S(2)}, u32[]{:S(2)}) collective-permute-start(bf16[112,2560]{1,0:T(8,128)(2,1)S(1)} %add_convert_fusion.9), channel_id=1, source_target_pairs={{8,0},{12,4},{16,24},{20,28},{9,1},{13,5},{17,25},{21,29},{10,2},{... | collective-permute-start | bytes 1720328 | tf_op jit(solution)/shard_map/ppermute | solution.py:1016
  503.9 21.0 %collective-permute-start.72 = (bf16[240,1536]{1,0:T(8,128)(2,1)S(1)}, bf16[240,1536]{1,0:T(8,128)(2,1)S(1)}, u32[]{:S(2)}, u32[]{:S(2)}) collective-permute-start(bf16[240,1536]{1,0:T(8,128)(2,1)S(1)} %add_convert_fusion), channel_id=1, source_target_pairs={{8,0},{12,4},{16,24},{20,28},{9,1},{13,5},{17,25},{21,29},{10,2},{... | collective-permute-start | bytes 2211848 | tf_op jit(solution)/shard_map/ppermute | solution.py:1016
  (197 other events, 1864.8 us)
